TPU v7x, 32 devices: a whole 2x2x4 slice. The times are simulated.
32 devices in a mesh: azim: 4 (over x, core), sect: 8 (over z, y).
Axes of the slice: x: 2, y: 2, z: 4, core: 2. Of those that a mesh axis runs over, the one named last changes fastest.
Arguments:
- signals: bfloat16 [1024, 256], P(('azim', 'sect')), may hold values from -6 to 6
- observer_xyz: bfloat16 [1024, 3], P(('azim', 'sect'))
- panel_geometry: float32 [7, 32768], P(None, ('azim', 'sect'))
- delays: int32 [256, 1024], P(('azim', 'sect')), may hold values from 0 to 127
- counts: int32 [32], P(('azim', 'sect')), may hold values from 1 to 1024, as said below
- connectivity: int32 [4, 32768], P(None, ('azim', 'sect')), may hold values from 0 to 1160, as said below
- owners: int32 [32768], P(('azim', 'sect')), may hold values from 0 to 2047, as said below
Outputs:
- node_grad: float32 [33024, 128], P(('azim', 'sect'))
- cell_grad: float32 [8192, 128], P(('azim', 'sect'))
Inputs may be any that keep to these rules, and one draw needn't show every extreme that they name: counts[d] panels of device d are live, the first ones of its 1024 slots; the others are padding. In every azim group the last section holds 1024. `connectivity`: A value k below 1032 is node k of the panel's own device; otherwise k - 1032 is below 129 and names that node of the next device along sect, the last section's next being the first. owners[p] // 256 is the section and owners[p] % 256 the cell within the panel's azim group. The four panels of each aligned group of four slots share one owner. At most 64 groups of one device have owners in one section, and every device reaches that number.
All inputs are finite; a program needn't handle non-finite values.
Results may differ from a plain program's by a relative error of at most 0.006.
Values may be sent and summed in bfloat16 or wider, within the bound.
No kernel may reach another device: no remote copies, remote signals or barrier semaphores. Data moves between devices by JAX's collectives and lax.ppermute only.
A program may use at most 64 MiB of HBM per device.

v0:
```python
import jax
import jax.numpy as jnp
from jax import lax
from jax.sharding import PartitionSpec as P

NPU = 128
BLK = 128
TW = 128
DMAX = 127
CELL_DEV = 256
NODE_DEV = 1032


RADIUS = 4.0


def passed_along(array, axis, by):
    peers = lax.axis_size(axis)
    return lax.ppermute(array, axis, [(i, (i + by) % peers) for i in range(peers)])


def delayed_window(signal, shift):
    window = signal
    for bit in range(DMAX.bit_length()):
        step_size = 1 << bit
        taken = shift // step_size % 2 == 1
        window = jnp.where(taken[:, None], jnp.roll(window, -step_size, axis=1), window)
    return window[:, : TW + 1]


def block_sources(geometry, signal, observers, shift):
    points = observers.astype(jnp.float32)
    delta_x = points[:, 0][None, :] - geometry[0][:, None]
    delta_y = points[:, 1][None, :] - geometry[1][:, None]
    delta_z = points[:, 2][None, :] - geometry[2][:, None]
    distance = jnp.sqrt(delta_x * delta_x + delta_y * delta_y + delta_z * delta_z)
    inverse = RADIUS / distance
    facing = (
        geometry[3][:, None] * delta_x
        + geometry[4][:, None] * delta_y
        + geometry[5][:, None] * delta_z
    ) / distance
    near_weight = (facing * inverse * inverse).astype(jnp.bfloat16)
    far_weight = (facing * inverse).astype(jnp.bfloat16)
    thick_weight = (geometry[6][:, None] * inverse).astype(jnp.bfloat16)
    window = delayed_window(signal, shift)
    current = window[:, :TW]
    change = (window[:, 1:].astype(jnp.float32) - current.astype(jnp.float32)).astype(jnp.bfloat16)
    loading = jnp.dot(near_weight, current, preferred_element_type=jnp.float32)
    loading = loading + jnp.dot(far_weight, change, preferred_element_type=jnp.float32)
    thickness = jnp.dot(thick_weight, change, preferred_element_type=jnp.float32)
    return (loading, thickness)


def group_sources(geometry, signal, observers, shifts, live_rows):
    panel_rows = geometry.shape[1]
    group_rows = 4 * BLK
    live_rows = jnp.maximum(live_rows, 0)
    used_groups = (live_rows + group_rows - 1) // group_rows
    empty = jnp.zeros((panel_rows, TW), jnp.float32)
    batched = jax.vmap(block_sources, in_axes=(0, None, None, 0))

    def advance(group_index, carried):
        offset = group_index * group_rows
        pieces = (
            lax.dynamic_slice_in_dim(geometry, offset, group_rows, 1)
            .reshape(7, 4, BLK)
            .transpose(1, 0, 2)
        )
        shift_rows = lax.dynamic_slice_in_dim(shifts, group_index * 4, 4, 0)
        loading, thickness = batched(pieces, signal, observers, shift_rows)
        row_index = offset + lax.broadcasted_iota(jnp.int32, (group_rows, 1), 0)
        keep_mask = (row_index < live_rows).astype(jnp.float32)
        new_loading = lax.dynamic_update_slice_in_dim(
            carried[0], loading.reshape(group_rows, TW) * keep_mask, offset, 0
        )
        new_thickness = lax.dynamic_update_slice_in_dim(
            carried[1], thickness.reshape(group_rows, TW) * keep_mask, offset, 0
        )
        return (new_loading, new_thickness)

    return lax.fori_loop(0, used_groups, advance, (empty, empty))


def per_device(signals, observer_xyz, panel_geometry, delays, counts, connectivity, owners):
    live_rows = counts[0]
    signal_all, xyz_all = (
        lax.all_gather(signals, ("azim", "sect"), axis=0, tiled=True),
        lax.all_gather(observer_xyz, ("azim", "sect"), axis=0, tiled=True),
    )
    loading, thickness = group_sources(panel_geometry, signal_all, xyz_all, delays, live_rows)
    rim_count = NPU + 1
    buffer = jnp.zeros((NODE_DEV + rim_count, TW), jnp.float32)
    quarter = 0.25 * loading
    for corner in range(4):
        buffer = buffer.at[connectivity[corner]].add(quarter)
    received = passed_along(buffer[NODE_DEV:], "sect", 1)
    node_grad = jnp.concatenate([buffer[:rim_count] + received, buffer[rim_count:NODE_DEV]], 0)
    sections = lax.axis_size("sect")
    group_cap = 2 * CELL_DEV // sections
    values = thickness.reshape(CELL_DEV, 4, TW).sum(axis=1)
    target = owners.reshape(CELL_DEV, 4)[:, 0]
    destination = target // CELL_DEV
    one_hot = (destination[:, None] == lax.broadcasted_iota(jnp.int32, (1, sections), 1)).astype(
        jnp.int32
    )
    position = jnp.cumsum(one_hot, axis=0)
    slot_index = jnp.sum(position * one_hot, axis=1) - 1
    outgoing = (
        jnp.zeros((sections, group_cap, TW), jnp.float32).at[destination, slot_index].set(values)
    )
    cell_index = jnp.full((sections, group_cap), float(CELL_DEV), jnp.float32)
    cell_index = cell_index.at[destination, slot_index].set((target % CELL_DEV).astype(jnp.float32))
    incoming, incoming_ids = (
        lax.all_to_all(outgoing, "sect", split_axis=0, concat_axis=0, tiled=True),
        lax.all_to_all(cell_index, "sect", split_axis=0, concat_axis=0, tiled=True),
    )
    row_targets = incoming_ids.reshape(-1).astype(jnp.int32)
    cell_sums = (
        jnp.zeros((CELL_DEV + 1, TW), jnp.float32).at[row_targets].add(incoming.reshape(-1, TW))
    )
    return (node_grad, cell_sums[:CELL_DEV])


def solution(mesh):
    in_specs = (
        P(("azim", "sect"), None),
        P(("azim", "sect"), None),
        P(None, ("azim", "sect")),
        P(("azim", "sect"), None),
        P(("azim", "sect")),
        P(None, ("azim", "sect")),
        P(("azim", "sect")),
    )
    out_specs = (P(("azim", "sect"), None), P(("azim", "sect"), None))
    return jax.shard_map(
        per_device, mesh=mesh, in_specs=in_specs, out_specs=out_specs, check_vma=False
    )
```

profile of v0, /device:TPU:0, one launch (start us, length us, event | category | flops | bytes accessed | tf_op | source)
XLA Modules:
  0.0 309.8 jit_solution(5773276448960741617)
XLA Ops:
  3.2 38.7 %scatter_fusion = f32[8,64]{1,0:T(8,128)} fusion(f32[8,64]{1,0:T(8,128)} %broadcast_in_dim.120, s32[256]{0:T(256)S(1)} %bitcast.69, f32[256]{0:T(256)S(1)} %fusion.58), kind=kCustom, calls=%fused_computation.4 | custom fusion | bytes 5120 | tf_op jit(solution)/shard_map/scatter | solution.py:113
  41.8 7.3 %all-to-all-start = ((f32[8,1,64]{2,1,0:T(1,128)}), f32[8,1,64]{2,1,0:T(1,128)}, u32[]{:S(2)}, u32[]{:S(2)}) async-start(f32[8,1,64]{2,1,0:T(1,128)} %bitcast.32), calls=%async_computation | async-start | bytes 8192 | tf_op jit(solution)/shard_map/all_to_all | solution.py:116
  49.8 70.7 %all_gather.7 = bf16[1024,256]{1,0:T(8,128)(2,1)S(1)} all-gather(bf16[32,256]{1,0:T(8,128)(2,1)S(1)} %copy-done.10), channel_id=1, replica_groups=mesh['azim'=4,'sect'=8] {'azim','sect'}, dimensions={0}, use_global_device_ids=true | all-gather | bytes 540672 | tf_op jit(solution)/shard_map/all_gather | solution.py:88
  120.8 63.4 %all-gather = bf16[32,32,3]{1,2,0:T(4,128)(2,1)S(1)} all-gather(bf16[1,32,3]{1,2,0:T(4,128)(2,1)S(1)} %bitcast.94), channel_id=1, replica_groups=mesh['azim'=4,'sect'=8] {'azim','sect'}, dimensions={0}, use_global_device_ids=true | all-gather | bytes 6336 | tf_op jit(solution)/shard_map/all_gather | solution.py:89
  186.2 29.3 %while.15 = (s32[]{:T(128)}, f32[1024,128]{1,0:T(8,128)}, f32[1024,128]{1,0:T(8,128)}, s32[]{:T(128)}, f32[7,1024]{1,0:T(8,128)S(1)}, /*index=5*/bf16[1024,3]{0,...) while((s32[]{:T(128)}, f32[1024,128]{1,0:T(8,128)}, ...), condition=%wide.region_1.2_spmd, body=%wide.region_0.1_spmd.sunk | while | flops 465307136 | bytes 82084224 | solution.py:82
  186.4 1.2 broadcast_select_fusion.2
  188.8 2.3 maximum_select_fusion.12
  192.4 2.0 maximum_select_fusion.13
  195.6 2.0 maximum_select_fusion.14
  198.8 2.0 maximum_select_fusion.15
  202.0 2.0 maximum_select_fusion.16
  205.2 2.0 maximum_select_fusion.17
  207.2 2.0 fusion.76
  209.2 2.5 convolution_add_fusion.2
  211.7 2.0 fusion.74
  215.5 6.1 %scatter_custom_fusion = f32[1161,128]{1,0:T(8,128)S(1)} fusion(s32[1024]{0:T(1024)S(1)} %bitcast.92, f32[1024,128]{1,0:T(8,128)} %get-tuple-element.177, f32[]{:T(128)} %constant.292.clone.1, f32[]{:T(128)} %constant.300.clone.1), kind=kCustom, calls=%fused_computation.121 | custom fusion | flops 262144 | bytes 1118728 | tf_op jit(solution)/shard_map/scatter-add | solution.py:96
  221.6 6.7 %scatter_custom_fusion.1 = f32[1161,128]{1,0:T(8,128)S(1)} fusion(f32[1161,128]{1,0:T(8,128)S(1)} %scatter_custom_fusion, s32[1024]{0:T(1024)S(1)} %bitcast.91, f32[1024,128]{1,0:T(8,128)} %get-tuple-element.177, f32[]{:T(128)} %constant.300.clone.1), kind=kCustom, calls=%fused_computation.119 | custom fusion | flops 262144 | bytes 1118724 | tf_op jit(solution)/shard_map/scatter-add | solution.py:96
  228.3 6.3 %scatter_custom_fusion.2 = f32[1161,128]{1,0:T(8,128)S(1)} fusion(f32[1161,128]{1,0:T(8,128)S(1)} %scatter_custom_fusion.1, s32[1024]{0:T(1024)S(1)} %bitcast.90, f32[1024,128]{1,0:T(8,128)S(1)} %copy-done.4, f32[]{:T(128)} %constant.300.clone.1), kind=kCustom, calls=%fused_computation.117 | custom fusion | flops 262144 | bytes 1118724 | tf_op jit(solution)/shard_map/scatter-add | solution.py:96
  234.6 6.3 %scatter_custom_fusion.3 = f32[1161,128]{1,0:T(8,128)S(1)} fusion(f32[1161,128]{1,0:T(8,128)S(1)} %scatter_custom_fusion.2, s32[1024]{0:T(1024)S(1)} %bitcast.89, f32[1024,128]{1,0:T(8,128)S(1)} %copy-done.4, f32[]{:T(128)} %constant.300.clone.1), kind=kCustom, calls=%fused_computation.115 | custom fusion | flops 262144 | bytes 1118724 | tf_op jit(solution)/shard_map/scatter-add | solution.py:96
  240.9 2.3 collective-permute-start
  244.3 27.5 %scatter_fusion.1 = f32[8,64,128]{2,1,0:T(8,128)} fusion(f32[8,64,128]{2,1,0:T(8,128)} %broadcast_in_dim.121, s32[256]{0:T(256)S(1)} %bitcast.70, f32[256,128]{1,0:T(8,128)S(1)} %reduce_sum.19), kind=kCustom, calls=%fused_computation.5 | custom fusion | bytes 395264 | tf_op jit(solution)/shard_map/scatter | solution.py:110
  271.8 25.9 %all-to-all-start.1 = ((f32[8,64,128]{2,1,0:T(8,128)}), f32[8,64,128]{2,1,0:T(8,128)S(1)}, u32[]{:S(2)}, u32[]{:S(2)}) async-start(f32[8,64,128]{2,1,0:T(8,128)} %scatter_fusion.1), calls=%async_computation.1 | async-start | bytes 524288 | tf_op jit(solution)/shard_map/all_to_all | solution.py:115
  299.3 6.7 %all-to-all-done.1 = f32[8,64,128]{2,1,0:T(8,128)S(1)} async-done(((f32[8,64,128]{2,1,0:T(8,128)}), f32[8,64,128]{2,1,0:T(8,128)S(1)}, u32[]{:S(2)}, u32[]{:S(2)}) %all-to-all-start.1) | async-done | bytes 262176 | tf_op jit(solution)/shard_map/all_to_all | solution.py:115
  306.0 3.1 scatter_custom_fusion.6
  (80 shorter events, 17.4 us)
Async XLA Ops:
  0.6 49.2 %copy-start.10 = (bf16[32,256]{1,0:T(8,128)(2,1)S(1)}, bf16[32,256]{1,0:T(8,128)(2,1)}, u32[]{:S(2)}) copy-start(bf16[32,256]{1,0:T(8,128)(2,1)} %param.9) | copy-start | bytes 49156
  2.6 47.2 %copy-start = (s32[256,1]{0,1:T(1,128)}, s32[256,1]{0,1:T(1,128)S(1)}, u32[]{:S(2)}) copy-start(s32[256,1]{0,1:T(1,128)S(1)} %or_select_fusion) | copy-start | bytes 3076
  3.2 117.7 %copy-start.12 = (bf16[32,3]{0,1:T(4,128)(2,1)S(1)}, bf16[32,3]{0,1:T(4,128)(2,1)}, u32[]{:S(2)}) copy-start(bf16[32,3]{0,1:T(4,128)(2,1)} %param.10) | copy-start | bytes 580
  41.8 229.9 %all-to-all-start = ((f32[8,1,64]{2,1,0:T(1,128)}), f32[8,1,64]{2,1,0:T(1,128)}, u32[]{:S(2)}, u32[]{:S(2)}) async-start(f32[8,1,64]{2,1,0:T(1,128)} %bitcast.32), calls=%async_computation | async-start | bytes 8192 | tf_op jit(solution)/shard_map/all_to_all | solution.py:116
  120.5 65.7 %copy-start.8 = (s32[8,1024]{1,0:T(8,128)S(1)}, s32[8,1024]{1,0:T(8,128)}, u32[]{:S(2)}) copy-start(s32[8,1024]{1,0:T(8,128)} %param.12) | copy-start | bytes 98308
  120.5 65.7 %copy-start.9 = (f32[7,1024]{1,0:T(8,128)S(1)}, f32[7,1024]{1,0:T(8,128)}, u32[]{:S(2)}) copy-start(f32[7,1024]{1,0:T(8,128)} %param.11) | copy-start | bytes 86020
  186.2 29.3 %copy-start.11 = (s32[4,1024]{1,0:T(4,128)S(1)}, s32[4,1024]{1,0:T(4,128)}, u32[]{:S(2)}) copy-start(s32[4,1024]{1,0:T(4,128)} %param.14) | copy-start | bytes 49156
  211.7 2.2 copy-start.2
  211.7 2.2 copy-start.5
  213.9 0.8 copy-start.3
  214.7 0.8 copy-start.6
  215.5 12.8 %copy-start.4 = (f32[1024,128]{1,0:T(8,128)S(1)}, f32[1024,128]{1,0:T(8,128)}, u32[]{:S(2)}) copy-start(f32[1024,128]{1,0:T(8,128)} %get-tuple-element.177) | copy-start | bytes 1572868
  221.6 21.6 %copy-start.7 = (f32[1024,128]{1,0:T(8,128)S(1)}, f32[1024,128]{1,0:T(8,128)}, u32[]{:S(2)}) copy-start(f32[1024,128]{1,0:T(8,128)} %get-tuple-element.178) | copy-start | bytes 1572868
  228.3 16.0 %copy-start.1 = (s32[256,1]{0,1:T(1,128)S(1)}, s32[256,1]{0,1:T(1,128)}, u32[]{:S(2)}) copy-start(s32[256,1]{0,1:T(1,128)} %copy-done) | copy-start | bytes 3076
  240.9 57.6 %collective-permute-start = (f32[129,128]{1,0:T(8,128)S(1)}, f32[129,128]{1,0:T(8,128)S(1)}, u32[]{:S(2)}, u32[]{:S(2)}) collective-permute-start(f32[129,128]{1,0:T(8,128)S(1)} %slice.272), channel_id=1, source_target_pairs={{0,1},{1,2},{2,3},{3,4},{4,5},{5,6},{6,7},{7,0},{8,9},{9,10},{10,1... | collective-permute-start | bytes 198152 | tf_op jit(solution)/shard_map/ppermute | solution.py:19
  271.8 34.2 %all-to-all-start.1 = ((f32[8,64,128]{2,1,0:T(8,128)}), f32[8,64,128]{2,1,0:T(8,128)S(1)}, u32[]{:S(2)}, u32[]{:S(2)}) async-start(f32[8,64,128]{2,1,0:T(8,128)} %scatter_fusion.1), calls=%async_computation.1 | async-start | bytes 524288 | tf_op jit(solution)/shard_map/all_to_all | solution.py:115
where the time goes:
time: 314 us; the launch traced here: 310 us
  blocking collectives  134 us (43%)
  local copies, waits for them, and re-layouts  80.3 us (26%)
  other arithmetic  44.9 us (14%)
  starting transfers between devices  35.5 us (11%)
  waiting for transfers between devices  6.69 us (2%)
  matrix products  6.43 us (2%)
    all_gather x1, blocking collectives, per_device(): lax.all_gather(signals, ('azim', 'sect'), axis=0, tiled=True)  70.7 us
    all_gather x1, blocking collectives, per_device(): lax.all_gather(observer_xyz, ('azim', 'sect'), axis=0, tiled=True)  63.4 us
    scatter x1, local copies, waits for them, and re-layouts, per_device(): cell_index.at[destination, slot_index]  38.7 us
    scatter x1, local copies, waits for them, and re-layouts, per_device(): jnp.zeros((sections, group_cap, TW), jnp.float32)  27.5 us
    all_to_all x1, starting transfers between devices, per_device(): lax.all_to_all(outgoing, 'sect', split_axis=0, concat_axis=0, tiled=True)  25.9 us
    scatter-add x4, other arithmetic, per_device(): buffer = buffer.at[connectivity[corner]].add(quarter)  25.3 us
    select_n x7, other arithmetic, delayed_window(): jnp.where(taken[:, None], jnp.roll(window, -step_size, axis=1), window)  13.4 us
    slice x14, local copies, waits for them, and re-layouts, delayed_window(): jnp.roll(window, -step_size, axis=1)  7.51 us
  transfers between devices with their start and end apart: 3, of which 1 were waited for; matrix products, arithmetic and copies ran while one was open for 27% of the time, Pallas kernels for 0%

commit v1 on v0

v1 whole, which is shorter than its diff:
```python
import functools

import jax
import jax.numpy as jnp
from jax import lax
from jax.experimental import pallas as pl
from jax.experimental.pallas import tpu as pltpu
from jax.sharding import PartitionSpec as P

NPU = 128
BLK = 128
TW = 128
CELL_DEV = 256
NODE_DEV = 1032
RIM = NPU + 1
NODE_ROWS = 1168
EXTRA = 16
F32 = jnp.float32
BF16 = jnp.bfloat16
VMEM = pltpu.VMEM
SMEM = pltpu.SMEM


def params(mib=24):
    return pltpu.CompilerParams(vmem_limit_bytes=mib * 1024 * 1024)


def route_kernel(cap, place_ref, conn_ref, owner_ref, corner_ref, slot_ref, ids_ref):
    panels = conn_ref.shape[1]
    sections = ids_ref.shape[0] // EXTRA * EXTRA
    live = place_ref[1]

    def corner_rows(step, carried):
        row = pl.multiple_of(step * 16, 16)
        node = row + lax.broadcasted_iota(jnp.int32, (16, panels), 0)
        panel = lax.broadcasted_iota(jnp.int32, (16, panels), 1)
        node = jnp.where(panel < live, node, -1)
        total = jnp.zeros((16, panels), F32)
        for corner in range(4):
            total = total + jnp.where(conn_ref[corner : corner + 1, :] == node, 0.25, 0.0)
        corner_ref[pl.ds(row, 16), :] = total.astype(BF16)
        return carried

    lax.fori_loop(0, NODE_ROWS // 16, corner_rows, 0)

    owner = owner_ref[...]
    dest = owner // CELL_DEV
    lane = lax.broadcasted_iota(jnp.int32, (sections, panels), 1)
    mine = dest == lax.broadcasted_iota(jnp.int32, (sections, panels), 0)
    count = jnp.where(mine, 1, 0)
    span = 1
    while span < panels:
        count = count + jnp.where(lane >= span, pltpu.roll(count, span, 1), 0)
        span *= 2
    before = jnp.sum(jnp.where(mine, count - 1, 0), axis=0, keepdims=True)
    rank = before // 4
    slot = dest * cap + rank

    def slot_rows(step, carried):
        row = pl.multiple_of(step * 16, 16)
        number = row + lax.broadcasted_iota(jnp.int32, (16, panels), 0)
        panel = lax.broadcasted_iota(jnp.int32, (16, panels), 1)
        number = jnp.where(panel < live, number, -1)
        slot_ref[pl.ds(row, 16), :] = jnp.where(slot == number, 1.0, 0.0).astype(BF16)
        return carried

    lax.fori_loop(0, slot_ref.shape[0] // 16, slot_rows, 0)

    first = place_ref[0] * cap % 128
    at_lane = rank + first == lax.broadcasted_iota(jnp.int32, (128, panels), 0)
    at_lane = jnp.where(at_lane, 1.0, 0.0).astype(BF16)
    cell = jnp.where(mine & (lane % 4 == 0), owner % CELL_DEV, 0).astype(F32).astype(BF16)
    ids = lax.dot_general(cell, at_lane, (((1,), (1,)), ((), ())), preferred_element_type=F32)
    ids_ref[...] = ids.astype(BF16)


def route_matrices(sections, place, connectivity, owners):
    panels = connectivity.shape[1]
    cap = 2 * CELL_DEV // sections
    padded = -(-sections // EXTRA) * EXTRA
    return pl.pallas_call(
        functools.partial(route_kernel, cap),
        out_shape=(
            jax.ShapeDtypeStruct((NODE_ROWS, panels), BF16),
            jax.ShapeDtypeStruct((sections * cap, panels), BF16),
            jax.ShapeDtypeStruct((padded, 128), BF16),
        ),
        in_specs=[
            pl.BlockSpec(memory_space=SMEM),
            pl.BlockSpec(memory_space=VMEM),
            pl.BlockSpec(memory_space=VMEM),
        ],
        out_specs=[pl.BlockSpec(memory_space=VMEM)] * 3,
        compiler_params=params(),
        cost_estimate=pl.CostEstimate(flops=20_000_000, bytes_accessed=4_000_000, transcendentals=0),
        name="route",
    )(place, connectivity, owners.reshape(1, panels))


def sources_kernel(chunk_order, cap, place_ref, *refs):
    chunks = refs[: len(chunk_order)]
    (delay_ref, geometry_ref, corner_ref, slot_ref, ids_ref) = refs[len(chunk_order) : len(chunk_order) + 5]
    (node_ref, rim_ref, message_ref) = refs[len(chunk_order) + 5 : len(chunk_order) + 8]
    (low_ref, high_ref, shift_ref, panel_ref, weight_ref, window_ref, loading_ref, thick_ref) = refs[len(chunk_order) + 8 :]
    span = chunks[0].shape[0] - EXTRA
    observers = span * len(chunks)
    panels = geometry_ref.shape[1]
    live = place_ref[1]
    azim = place_ref[2]

    points = []
    for number, chunk in enumerate(chunks):
        rows = pl.ds(number * span, span)
        low_ref[rows, :] = chunk[:span, :128].astype(F32)
        high_ref[rows, :] = chunk[:span, 128:].astype(F32)
        points.append(chunk[span : span + EXTRA, :].astype(F32) * 0.25)
        begin = pl.multiple_of((azim ^ chunk_order[number]) * span, span)
        for row in range(delay_ref.shape[0]):
            shift_ref[row, :, rows] = delay_ref[row : row + 1, pl.ds(begin, span)]

    lanes = lax.broadcasted_iota(jnp.int32, (128, 128), 1)

    def column(row):
        return jnp.broadcast_to(row, (128, 128)).T

    def block(index, carried):
        start = pl.multiple_of(index * BLK, BLK)
        for part in range(7):
            scale = 0.25 if part < 3 else 1.0
            panel_ref[part] = column(geometry_ref[part : part + 1, pl.ds(start, BLK)] * scale)
        for number in range(len(chunk_order)):
            for piece in range(span // 128):
                here = number * span + piece * 128
                cols = pl.ds(here, 128)
                shift = column(shift_ref[index, :, cols])
                source = shift + lanes
                at = source & 127
                low = jnp.take_along_axis(low_ref[cols, :], at, axis=1, mode="promise_in_bounds")
                high = jnp.take_along_axis(high_ref[cols, :], at, axis=1, mode="promise_in_bounds")
                current = jnp.where(source < 128, low, high)
                following = pltpu.roll(jnp.where(lanes == 0, high, current), 127, 1)
                window_ref[cols, :128] = current.astype(BF16)
                window_ref[cols, 128:] = (following - current).astype(BF16)

                at_x, at_y, at_z = (points[number][i : i + 1, piece * 128 : piece * 128 + 128] for i in range(3))
                for strip in range(BLK // 32):
                    rows = pl.ds(strip * 32, 32)
                    delta_x = at_x - panel_ref[0, rows, :]
                    delta_y = at_y - panel_ref[1, rows, :]
                    delta_z = at_z - panel_ref[2, rows, :]
                    inverse = lax.rsqrt(delta_x * delta_x + delta_y * delta_y + delta_z * delta_z)
                    flux = (
                        panel_ref[3, rows, :] * delta_x
                        + panel_ref[4, rows, :] * delta_y
                        + panel_ref[5, rows, :] * delta_z
                    )
                    far = flux * inverse * inverse
                    weight_ref[pl.ds(strip * 32, 32), cols] = (far * inverse).astype(BF16)
                    weight_ref[pl.ds(BLK + strip * 32, 32), cols] = far.astype(BF16)
                    weight_ref[pl.ds(2 * BLK + strip * 32, 32), cols] = (panel_ref[6, rows, :] * inverse).astype(BF16)
        products = jnp.dot(weight_ref[...], window_ref[...], preferred_element_type=F32)
        alive = start + lax.broadcasted_iota(jnp.int32, (BLK, TW), 0) < live
        loading = products[:BLK, :TW] + products[BLK : 2 * BLK, TW:]
        loading_ref[pl.ds(start, BLK), :] = jnp.where(alive, loading, 0.0).astype(BF16)
        thick_ref[pl.ds(start, BLK), :] = jnp.where(alive, products[2 * BLK :, TW:], 0.0).astype(BF16)
        return carried

    lax.fori_loop(0, panels // BLK, block, 0)

    nodes = jnp.dot(corner_ref[...], loading_ref[...], preferred_element_type=F32)
    node_ref[...] = nodes[:NODE_DEV]
    rim_ref[...] = nodes[NODE_DEV : NODE_DEV + RIM]
    slots = jnp.dot(slot_ref[...], thick_ref[...], preferred_element_type=F32).astype(BF16)
    for section in range(message_ref.shape[0]):
        message_ref[section, :cap, :] = slots[section * cap : (section + 1) * cap]
        message_ref[section, cap:, :] = jnp.broadcast_to(
            ids_ref[section : section + 1, :].astype(F32), (EXTRA, 128)
        ).astype(BF16)


def sources(sections, chunk_order, place, chunks, delays, geometry, corners, slots, ids):
    panels = geometry.shape[1]
    observers = delays.shape[1]
    cap = 2 * CELL_DEV // sections
    return pl.pallas_call(
        functools.partial(sources_kernel, chunk_order, cap),
        out_shape=(
            jax.ShapeDtypeStruct((NODE_DEV, TW), F32),
            jax.ShapeDtypeStruct((RIM, TW), F32),
            jax.ShapeDtypeStruct((sections, cap + EXTRA, TW), BF16),
        ),
        in_specs=[pl.BlockSpec(memory_space=SMEM)] + [pl.BlockSpec(memory_space=VMEM)] * (len(chunks) + 5),
        out_specs=[pl.BlockSpec(memory_space=VMEM)] * 3,
        scratch_shapes=[
            VMEM((observers, 128), F32),
            VMEM((observers, 128), F32),
            VMEM((panels // BLK, 1, observers), jnp.int32),
            VMEM((7, BLK, 128), F32),
            VMEM((3 * BLK, observers), BF16),
            VMEM((observers, 2 * TW), BF16),
            VMEM((panels, TW), BF16),
            VMEM((panels, TW), BF16),
        ],
        compiler_params=params(),
        cost_estimate=pl.CostEstimate(flops=2_000_000_000, bytes_accessed=6_000_000, transcendentals=1_000_000),
        name="sources",
    )(place, *chunks, delays, geometry, corners, slots, ids)


def finish_kernel(cap, message_ref, rim_ref, node_in_ref, node_ref, cell_ref, rows_ref):
    sections = message_ref.shape[0]
    per = 128 // cap
    node_ref[...] = node_in_ref[...]
    node_ref[:RIM, :] = node_in_ref[:RIM, :] + rim_ref[...]
    total = jnp.zeros((CELL_DEV, TW), F32)
    for group in range(sections // per):
        ids = jnp.zeros((8, 128), F32)
        for inner in range(per):
            section = group * per + inner
            ids = ids + message_ref[section, cap : cap + EXTRA, :].astype(F32)[:8]
            rows_ref[group * 128 + inner * cap : group * 128 + (inner + 1) * cap, :] = message_ref[section, :cap, :]
        cell = lax.broadcasted_iota(jnp.int32, (CELL_DEV, 128), 0)
        match = jnp.where(ids[:1].astype(jnp.int32) == cell, 1.0, 0.0).astype(BF16)
        total = total + jnp.dot(match, rows_ref[group * 128 : (group + 1) * 128, :], preferred_element_type=F32)
    cell_ref[...] = total


def finish(sections, message, rim, nodes):
    cap = 2 * CELL_DEV // sections
    head = 136
    return pl.pallas_call(
        functools.partial(finish_kernel, cap),
        grid=(1,),
        out_shape=(
            jax.ShapeDtypeStruct((NODE_DEV, TW), F32),
            jax.ShapeDtypeStruct((CELL_DEV, TW), F32),
        ),
        in_specs=[
            pl.BlockSpec(message.shape, lambda i: (0, 0, 0)),
            pl.BlockSpec(rim.shape, lambda i: (0, 0)),
            pl.BlockSpec((head, TW), lambda i: (0, 0)),
        ],
        out_specs=[
            pl.BlockSpec((head, TW), lambda i: (0, 0)),
            pl.BlockSpec((CELL_DEV, TW), lambda i: (0, 0)),
        ],
        scratch_shapes=[VMEM((sections * cap, TW), BF16)],
        input_output_aliases={2: 0},
        compiler_params=params(),
        name="finish",
    )(message, rim, nodes)


def swapped(array, axis, bit):
    peers = lax.axis_size(axis)
    return lax.ppermute(array, axis, [(i, i ^ bit) for i in range(peers)])


def gathered(signals, xyz):
    count = signals.shape[0]
    sections = lax.axis_size("sect")
    section = lax.axis_index("sect")
    extra = jnp.zeros((EXTRA, signals.shape[1]), BF16)
    extra = lax.dynamic_update_slice(extra, xyz.T, (0, section * count))
    payload = jnp.concatenate([signals, extra], 0)
    everyone = jnp.broadcast_to(payload[None], (sections,) + payload.shape)
    received = lax.all_to_all(everyone, "sect", split_axis=0, concat_axis=0, tiled=True)
    span = sections * count
    chunk = jnp.concatenate(
        [received[:, :count].reshape(span, -1), received[:, count:].astype(F32).sum(0).astype(BF16)], 0
    )
    chunks = {0: chunk}
    bit = lax.axis_size("azim") // 2
    while bit:
        for offset in list(chunks):
            chunks[offset ^ bit] = swapped(chunks[offset], "azim", bit)
        bit //= 2
    return tuple(chunks), tuple(chunks.values())


def per_device(signals, observer_xyz, panel_geometry, delays, counts, connectivity, owners):
    sections = lax.axis_size("sect")
    section = lax.axis_index("sect")
    place = jnp.stack([section, counts[0], lax.axis_index("azim")]).astype(jnp.int32)
    chunk_order, chunks = gathered(signals, observer_xyz)
    corners, slots, ids = route_matrices(sections, place, connectivity, owners)
    nodes, rim, message = sources(
        sections, chunk_order, place, chunks, delays, panel_geometry, corners, slots, ids
    )
    rim = lax.ppermute(rim, "sect", [(i, (i + 1) % sections) for i in range(sections)])
    message = lax.all_to_all(message, "sect", split_axis=0, concat_axis=0, tiled=True)
    return finish(sections, message, rim, nodes)


def solution(mesh):
    in_specs = (
        P(("azim", "sect"), None),
        P(("azim", "sect"), None),
        P(None, ("azim", "sect")),
        P(("azim", "sect"), None),
        P(("azim", "sect")),
        P(None, ("azim", "sect")),
        P(("azim", "sect")),
    )
    out_specs = (P(("azim", "sect"), None), P(("azim", "sect"), None))
    return jax.shard_map(
        per_device, mesh=mesh, in_specs=in_specs, out_specs=out_specs, check_vma=False
    )
```

time: 314 us -> 67.3 us (0.21); the launches traced: 310 us -> 66.6 us
  blocking collectives: 134 us -> 15.2 us
  local copies, waits for them, and re-layouts: 80.3 us -> 4.49 us
  other arithmetic: 44.9 us -> 0.82 us
  starting transfers between devices: 35.5 us -> 6.86 us
  Pallas kernels: 0 us -> 26.2 us
  matrix products: 6.43 us -> 0 us
  waiting for transfers between devices: 6.69 us -> 11.7 us
    all_gather x2 -> x0, blocking collectives: 134 us -> none  [the longest x1 70.7 us: per_device(): lax.all_gather(signals, ('azim', 'sect'), axis=0, tiled=True)]
    scatter x2 -> x0, local copies, waits for them, and re-layouts: 66.2 us -> none  [the longest x1 38.7 us: per_device(): cell_index.at[destination, slot_index]]
    all_to_all x2 -> x1, starting transfers between devices: 33.2 us -> 3.38 us  [per_device(): lax.all_to_all(message, 'sect', split_axis=0, concat_axis=0, tiled=True)]
    scatter-add x5 -> x0, other arithmetic: 28.4 us -> none  [the longest x4 25.3 us: per_device(): buffer = buffer.at[connectivity[corner]].add(quarter)]
    pallas_call x0 -> x3, Pallas kernels: none -> 26.2 us  [the longest x1 20.1 us: sources(): pl.pallas_call(functools.partial(sources_kernel, chunk_order, cap), out_s...]
    all_to_all x0 -> x1, blocking collectives: none -> 15.2 us  [gathered(): lax.all_to_all(everyone, 'sect', split_axis=0, concat_axis=0, tiled=True)]
    select_n x10 -> x0, other arithmetic: 13.4 us -> none  [the longest x7 13.4 us: delayed_window(): jnp.where(taken[:, None], jnp.roll(window, -step_size, axis=1), window)]
    ppermute x1 -> x4, waiting for transfers between devices: 0.01 us -> 11.7 us  [the longest x1 8.14 us: per_device(): lax.ppermute(rim, 'sect', [(i, (i + 1) % sections) for i in range(section...]
  transfers between devices with their start and end apart: 3 -> 5, of which waited for: 1 -> 2; matrix products, arithmetic and copies ran while one was open for 27% -> 0% of each run, Pallas kernels for 0% -> 6%
where the time goes in v1:
time: 67.3 us; the launch traced here: 66.6 us
  Pallas kernels  26.2 us (39%)
  blocking collectives  15.2 us (23%)
  waiting for transfers between devices  11.7 us (17%)
  starting transfers between devices  6.86 us (10%)
  local copies, waits for them, and re-layouts  4.49 us (7%)
  between operations  1.36 us (2%)
  other arithmetic  0.82 us (1%)
    pallas_call x1, Pallas kernels, sources(): pl.pallas_call(functools.partial(sources_kernel, chunk_order, cap), out_s...  20.1 us
    all_to_all x1, blocking collectives, gathered(): lax.all_to_all(everyone, 'sect', split_axis=0, concat_axis=0, tiled=True)  15.2 us
    ppermute x1, waiting for transfers between devices, per_device(): lax.ppermute(rim, 'sect', [(i, (i + 1) % sections) for i in range(section...  8.14 us
    pallas_call x1, Pallas kernels, route_matrices(): pl.pallas_call(functools.partial(route_kernel, cap), out_shape=(jax.Shape...  4.3 us
    ppermute x3, waiting for transfers between devices, swapped(): return lax.ppermute(array, axis, [(i, i ^ bit) for i in range(peers)])  3.57 us
    all_to_all x1, starting transfers between devices, per_device(): lax.all_to_all(message, 'sect', split_axis=0, concat_axis=0, tiled=True)  3.38 us
    unnamed x8, local copies, waits for them, and re-layouts  2.92 us
    ppermute x1, starting transfers between devices, per_device(): lax.ppermute(rim, 'sect', [(i, (i + 1) % sections) for i in range(section...  1.92 us
  transfers between devices with their start and end apart: 5, of which 2 were waited for; matrix products, arithmetic and copies ran while one was open for 0% of the time, Pallas kernels for 6%

profile of v1, /device:TPU:0, one launch (start us, length us, event | category | flops | bytes accessed | tf_op | source)
XLA Modules:
  0.0 66.6 jit_solution(12923359034044517953)
XLA Ops:
  0.6 1.5 %dynamic_update_slice.3 = bf16[16,256]{1,0:T(8,128)(2,1)S(1)} dynamic-update-slice(bf16[16,256]{1,0:T(8,128)(2,1)S(1)} %broadcast_in_dim.4, bf16[3,32]{1,0:T(4,128)(2,1)} %bitcast.7, s32[]{:T(128)} %constant.5.clone.1, s32[]{:T(128)S(6)} %select_n.3) | dynamic-update-slice | bytes 388 | tf_op jit(solution)/shard_map/dynamic_update_slice | solution.py:264
  2.2 0.7 %pad_maximum_fusion.1 = bf16[48,256]{1,0:T(8,128)(2,1)S(1)} fusion(bf16[16,256]{1,0:T(8,128)(2,1)S(1)} %dynamic_update_slice.3, bf16[32,256]{1,0:T(8,128)(2,1)} %param.7), kind=kLoop, calls=%fused_computation.2 | loop fusion | flops 49152 | bytes 49152 | tf_op jit(solution)/shard_map/concatenate | solution.py:265
  2.9 15.2 %all_to_all.10 = bf16[8,48,256]{2,1,0:T(8,128)(2,1)S(1)} all-to-all(bf16[8,48,256]{2,1,0:T(8,128)(2,1)S(1)} %broadcast_in_dim.10), channel_id=1, replica_groups=mesh['azim'=4,'sect'=8] {'sect'}, dimensions={0} | all-to-all | bytes 393216 | tf_op jit(solution)/shard_map/all_to_all | solution.py:267
  18.1 1.6 %collective-permute-start = (bf16[272,256]{1,0:T(8,128)(2,1)S(1)}, bf16[272,256]{1,0:T(8,128)(2,1)S(1)}, u32[]{:S(2)}, u32[]{:S(2)}) collective-permute-start(bf16[272,256]{1,0:T(8,128)(2,1)S(1)} %pad_maximum_fusion.refs_0_), channel_id=1, source_target_pairs={{0,16},{8,24},{16,0},{24,8},{1,17},{9,25},{17,1},{25,9},{2,18},{10... | collective-permute-start | bytes 417800 | tf_op jit(solution)/shard_map/ppermute | solution.py:256
  19.7 0.0 collective-permute-start.1
  19.7 3.6 %collective-permute-done.refs_1_ = bf16[272,256]{1,0:T(8,128)(2,1)S(1)} collective-permute-done((bf16[272,256]{1,0:T(8,128)(2,1)S(1)}, bf16[272,256]{1,0:T(8,128)(2,1)S(1)}, u32[]{:S(2)}, u32[]{:S(2)}) %collective-permute-start) | collective-permute-done | bytes 139296 | tf_op jit(solution)/shard_map/ppermute | solution.py:256
  23.3 0.0 collective-permute-start.2
  23.9 0.1 pad_add_fusion.place_ref
  24.0 0.0 copy-start.2
  24.0 0.7 %copy-done.2 = s32[4,1024]{1,0:T(4,128)S(1)} copy-done((s32[4,1024]{1,0:T(4,128)S(1)}, s32[4,1024]{1,0:T(4,128)}, u32[]{:S(2)}) %copy-start.2) | copy-done | bytes 16408
  24.7 0.0 copy-start.3
  24.7 0.7 %copy-done.3 = s32[1024]{0:T(1024)S(1)} copy-done((s32[1024]{0:T(1024)S(1)}, s32[1024]{0:T(1024)}, u32[]{:S(2)}) %copy-start.3) | copy-done | bytes 4120
  25.4 4.3 %route.1 = (bf16[1168,1024]{1,0:T(8,128)(2,1)S(1)}, bf16[512,1024]{1,0:T(8,128)(2,1)S(1)}, bf16[16,128]{1,0:T(8,128)(2,1)S(1)}) custom-call(s32[3]{0:T(128)S(1)} %pad_add_fusion.place_ref, s32[4,1024]{1,0:T(4,128)S(1)} %copy-done.2, s32[1,1024]{1,0:T(1,128)S(1)} %bitcast.5), custom_call_target="tpu_custom_call" | custom-call | flops 20000000 | bytes 4000000 | tf_op jit(solution)/shard_map/route/pallas_call | solution.py:81
  29.7 0.0 collective-permute-done.1.refs_2_
  29.7 0.0 collective-permute-done.2.refs_3_
  29.7 0.0 copy-start
  29.7 0.7 %copy-done = s32[8,1024]{1,0:T(8,128)S(1)} copy-done((s32[8,1024]{1,0:T(8,128)S(1)}, s32[8,1024]{1,0:T(8,128)}, u32[]{:S(2)}) %copy-start) | copy-done | bytes 32792
  30.5 0.8 %copy-done.1 = f32[7,1024]{1,0:T(8,128)S(1)} copy-done((f32[7,1024]{1,0:T(8,128)S(1)}, f32[7,1024]{1,0:T(8,128)}, u32[]{:S(2)}) %copy-start.1) | copy-done | bytes 28696
  31.3 20.1 %sources.1 = (f32[1032,128]{1,0:T(8,128)}, f32[129,128]{1,0:T(8,128)S(1)}, bf16[8,80,128]{2,1,0:T(8,128)(2,1)}) custom-call(s32[3]{0:T(128)S(1)} %pad_add_fusion.place_ref, bf16[272,256]{1,0:T(8,128)(2,1)S(1)} %pad_maximum_fusion.refs_0_, bf16[272,256]{1,0:T(8,128)(2,1)S(1)} %collective-permute-done.refs_1_, ...), custom_call_target="tpu_custom_call" | custom-call | flops 2000000000 | bytes 6000000 | tf_op jit(solution)/shard_map/sources/pallas_call | solution.py:185
  51.4 3.4 %all-to-all-start.1 = ((bf16[8,80,128]{2,1,0:T(8,128)(2,1)}), bf16[8,80,128]{2,1,0:T(8,128)(2,1)S(1)}, u32[]{:S(2)}, u32[]{:S(2)}) async-start(bf16[8,80,128]{2,1,0:T(8,128)(2,1)} %get-tuple-element.11), calls=%async_computation.1 | async-start | bytes 327680 | tf_op jit(solution)/shard_map/all_to_all | solution.py:291
  54.8 1.9 %collective-permute-start.3 = (f32[129,128]{1,0:T(8,128)S(1)}, f32[129,128]{1,0:T(8,128)S(1)}, u32[]{:S(2)}, u32[]{:S(2)}) collective-permute-start(f32[129,128]{1,0:T(8,128)S(1)} %get-tuple-element.12), channel_id=1, source_target_pairs={{0,1},{1,2},{2,3},{3,4},{4,5},{5,6},{6,7},{7,0},{8,9},{9,10},{10,1... | collective-permute-start | bytes 198152 | tf_op jit(solution)/shard_map/ppermute | solution.py:290
  56.7 8.1 %collective-permute-done.3.rim_ref = f32[129,128]{1,0:T(8,128)S(1)} collective-permute-done((f32[129,128]{1,0:T(8,128)S(1)}, f32[129,128]{1,0:T(8,128)S(1)}, u32[]{:S(2)}, u32[]{:S(2)}) %collective-permute-start.3) | collective-permute-done | bytes 66080 | tf_op jit(solution)/shard_map/ppermute | solution.py:290
  64.8 0.0 all-to-all-done.1.message_ref
  64.9 1.8 %finish.1 = (f32[1032,128]{1,0:T(8,128)}, f32[256,128]{1,0:T(8,128)}) custom-call(bf16[8,80,128]{2,1,0:T(8,128)(2,1)S(1)} %all-to-all-done.1.message_ref, f32[129,128]{1,0:T(8,128)S(1)} %collective-permute-done.3.rim_ref, f32[1032,128]{1,0:T(8,128)} %get-tuple-element.13.node_in_ref), custom_call_target="tpu_custom_call", output_to_operand_aliasing={{0}: (2, {})} | custom-call | tf_op jit(solution)/shard_map/finish/pallas_call | solution.py:231
  (6 shorter events, 0.1 us)
Async XLA Ops:
  18.1 5.1 %collective-permute-start = (bf16[272,256]{1,0:T(8,128)(2,1)S(1)}, bf16[272,256]{1,0:T(8,128)(2,1)S(1)}, u32[]{:S(2)}, u32[]{:S(2)}) collective-permute-start(bf16[272,256]{1,0:T(8,128)(2,1)S(1)} %pad_maximum_fusion.refs_0_), channel_id=1, source_target_pairs={{0,16},{8,24},{16,0},{24,8},{1,17},{9,25},{17,1},{25,9},{2,18},{10... | collective-permute-start | bytes 417800 | tf_op jit(solution)/shard_map/ppermute | solution.py:256
  19.7 10.0 %collective-permute-start.1 = (bf16[272,256]{1,0:T(8,128)(2,1)S(1)}, bf16[272,256]{1,0:T(8,128)(2,1)S(1)}, u32[]{:S(2)}, u32[]{:S(2)}) collective-permute-start(bf16[272,256]{1,0:T(8,128)(2,1)S(1)} %pad_maximum_fusion.refs_0_), channel_id=1, source_target_pairs={{0,8},{8,0},{16,24},{24,16},{1,9},{9,1},{17,25},{25,17},{2,10},{10... | collective-permute-start | bytes 417800 | tf_op jit(solution)/shard_map/ppermute | solution.py:256
  23.3 6.5 %collective-permute-start.2 = (bf16[272,256]{1,0:T(8,128)(2,1)S(1)}, bf16[272,256]{1,0:T(8,128)(2,1)S(1)}, u32[]{:S(2)}, u32[]{:S(2)}) collective-permute-start(bf16[272,256]{1,0:T(8,128)(2,1)S(1)} %collective-permute-done.refs_1_), channel_id=1, source_target_pairs={{0,8},{8,0},{16,24},{24,16},{1,9},{9,1},{17,25},{25,17},{2,10},{10... | collective-permute-start | bytes 417800 | tf_op jit(solution)/shard_map/ppermute | solution.py:256
  24.0 0.7 %copy-start.2 = (s32[4,1024]{1,0:T(4,128)S(1)}, s32[4,1024]{1,0:T(4,128)}, u32[]{:S(2)}) copy-start(s32[4,1024]{1,0:T(4,128)} %conn_ref.1) | copy-start | bytes 49156
  24.7 0.7 %copy-start.3 = (s32[1024]{0:T(1024)S(1)}, s32[1024]{0:T(1024)}, u32[]{:S(2)}) copy-start(s32[1024]{0:T(1024)} %param.13) | copy-start | bytes 12292
  29.7 0.8 %copy-start = (s32[8,1024]{1,0:T(8,128)S(1)}, s32[8,1024]{1,0:T(8,128)}, u32[]{:S(2)}) copy-start(s32[8,1024]{1,0:T(8,128)} %refs_4_.1) | copy-start | bytes 98308
  30.5 0.8 %copy-start.1 = (f32[7,1024]{1,0:T(8,128)S(1)}, f32[7,1024]{1,0:T(8,128)}, u32[]{:S(2)}) copy-start(f32[7,1024]{1,0:T(8,128)} %refs_5_.1) | copy-start | bytes 86020
  51.4 13.5 %all-to-all-start.1 = ((bf16[8,80,128]{2,1,0:T(8,128)(2,1)}), bf16[8,80,128]{2,1,0:T(8,128)(2,1)S(1)}, u32[]{:S(2)}, u32[]{:S(2)}) async-start(bf16[8,80,128]{2,1,0:T(8,128)(2,1)} %get-tuple-element.11), calls=%async_computation.1 | async-start | bytes 327680 | tf_op jit(solution)/shard_map/all_to_all | solution.py:291
  54.8 10.1 %collective-permute-start.3 = (f32[129,128]{1,0:T(8,128)S(1)}, f32[129,128]{1,0:T(8,128)S(1)}, u32[]{:S(2)}, u32[]{:S(2)}) collective-permute-start(f32[129,128]{1,0:T(8,128)S(1)} %get-tuple-element.12), channel_id=1, source_target_pairs={{0,1},{1,2},{2,3},{3,4},{4,5},{5,6},{6,7},{7,0},{8,9},{9,10},{10,1... | collective-permute-start | bytes 198152 | tf_op jit(solution)/shard_map/ppermute | solution.py:290

commit v2 on v1

v2 whole, which is shorter than its diff:
```python
import functools

import jax
import jax.numpy as jnp
from jax import lax
from jax.experimental import pallas as pl
from jax.experimental.pallas import tpu as pltpu
from jax.sharding import PartitionSpec as P

NPU = 128
BLK = 128
TW = 128
CELL_DEV = 256
NODE_DEV = 1032
RIM = NPU + 1
HEAD = 136
NODE_ROWS = 1168
EXTRA = 16
F32 = jnp.float32
BF16 = jnp.bfloat16
VMEM = pltpu.VMEM
SMEM = pl.BlockSpec(memory_space=pltpu.SMEM)
WHOLE = pl.BlockSpec(memory_space=pltpu.VMEM)
PLACE = pl.BlockSpec(memory_space=pl.ANY)
COPY = pltpu.SemaphoreType.DMA


def call(kernel, name, out_shape, in_specs, out_specs, scratch_shapes=(), aliases=None, work=1_000_000):
    return pl.pallas_call(
        kernel,
        out_shape=out_shape,
        in_specs=in_specs,
        out_specs=out_specs,
        scratch_shapes=list(scratch_shapes),
        input_output_aliases=aliases or {},
        compiler_params=pltpu.CompilerParams(vmem_limit_bytes=24 * 1024 * 1024),
        cost_estimate=pl.CostEstimate(flops=work, bytes_accessed=4_000_000, transcendentals=0),
        name=name,
    )


def route_kernel(
    sections, place_ref, conn_at, owner_at, delay_at, geometry_at,
    corner_ref, slot_ref, ids_ref, source_ref, panel_ref,
    conn_ref, owner_ref, delay_ref, geometry_ref, sems,
):
    copies = [
        pltpu.make_async_copy(source, target, sems.at[number])
        for number, (source, target) in enumerate(
            ((delay_at, delay_ref), (geometry_at, geometry_ref), (conn_at, conn_ref), (owner_at, owner_ref))
        )
    ]
    for copy in copies:
        copy.start()
    for copy in copies:
        copy.wait()
    panels = conn_ref.shape[1]
    cap = slot_ref.shape[0] // sections
    padded = ids_ref.shape[0]
    section = place_ref[0]
    live = place_ref[1]
    groups, blocks, span, _ = source_ref.shape

    lanes = lax.broadcasted_iota(jnp.int32, (128, 128), 1)
    for piece in range(groups * span // 128):
        columns = delay_ref[:, piece * 128 : (piece + 1) * 128].T
        begin = piece * 128 % span
        for block in range(blocks):
            source = jnp.broadcast_to(columns[:, block : block + 1], (128, 128)) + lanes
            source_ref[piece * 128 // span, block, begin : begin + 128, :] = source
    for block in range(blocks):
        values = geometry_ref[:, block * BLK : (block + 1) * BLK]
        columns = jnp.concatenate([values, values[:1]], 0).T
        for part in range(7):
            column = columns[:, part : part + 1] * (0.25 if part < 3 else 1.0)
            panel_ref[block, part] = jnp.broadcast_to(column, (BLK, 128))

    def corner_rows(step, carried):
        row = pl.multiple_of(step * 16, 16)
        node = row + lax.broadcasted_iota(jnp.int32, (16, panels), 0)
        panel = lax.broadcasted_iota(jnp.int32, (16, panels), 1)
        node = jnp.where(panel < live, node, -1)
        total = jnp.zeros((16, panels), F32)
        for corner in range(4):
            total = total + jnp.where(conn_ref[corner : corner + 1, :] == node, 0.25, 0.0)
        corner_ref[pl.ds(row, 16), :] = total.astype(BF16)
        return carried

    lax.fori_loop(0, NODE_ROWS // 16, corner_rows, 0)

    owner = owner_ref[...]
    away = owner // CELL_DEV - section
    away = jnp.where(away < 0, away + sections, away)
    lane = lax.broadcasted_iota(jnp.int32, (padded, panels), 1)
    mine = away == lax.broadcasted_iota(jnp.int32, (padded, panels), 0)
    count = jnp.where(mine, 1, 0)
    span = 1
    while span < panels:
        count = count + jnp.where(lane >= span, pltpu.roll(count, span, 1), 0)
        span *= 2
    before = jnp.sum(jnp.where(mine, count - 1, 0), axis=0, keepdims=True)
    slot = away * cap + before // 4

    def slot_rows(step, carried):
        row = pl.multiple_of(step * 16, 16)
        number = row + lax.broadcasted_iota(jnp.int32, (16, panels), 0)
        panel = lax.broadcasted_iota(jnp.int32, (16, panels), 1)
        number = jnp.where(panel < live, number, -1)
        slot_ref[pl.ds(row, 16), :] = jnp.where(slot == number, 1.0, 0.0).astype(BF16)
        return carried

    lax.fori_loop(0, slot_ref.shape[0] // 16, slot_rows, 0)

    at_lane = slot % 128 == lax.broadcasted_iota(jnp.int32, (128, panels), 0)
    at_lane = jnp.where(at_lane, 1.0, 0.0).astype(BF16)
    cell = jnp.where(mine & (lane % 4 == 0), owner % CELL_DEV, 0).astype(F32).astype(BF16)
    ids_ref[...] = lax.dot_general(cell, at_lane, (((1,), (1,)), ((), ())), preferred_element_type=F32)


def route(sections, groups, place, connectivity, owners, delays, geometry):
    panels = connectivity.shape[1]
    blocks, observers = delays.shape
    cap = 2 * CELL_DEV // sections
    padded = -(-sections // EXTRA) * EXTRA
    return call(
        functools.partial(route_kernel, sections),
        "route",
        (
            jax.ShapeDtypeStruct((NODE_ROWS, panels), BF16),
            jax.ShapeDtypeStruct((sections * cap, panels), BF16),
            jax.ShapeDtypeStruct((padded, 128), F32),
            jax.ShapeDtypeStruct((groups, blocks, observers // groups, 128), jnp.int32),
            jax.ShapeDtypeStruct((blocks, 7, BLK, 128), F32),
        ),
        [SMEM] + [PLACE] * 4,
        [WHOLE] * 5,
        [
            VMEM(connectivity.shape, jnp.int32),
            VMEM((1, panels), jnp.int32),
            VMEM(delays.shape, jnp.int32),
            VMEM(geometry.shape, F32),
            COPY((4,)),
        ],
        work=4_000_000_000,
    )(place, connectivity, owners.reshape(1, panels), delays, geometry)


def join_kernel(sections, place_ref, *refs):
    signals = refs[:sections]
    points = refs[sections : 2 * sections]
    chunk_ref, wide_ref = refs[2 * sections :]
    count = signals[0].shape[0]
    span = sections * count
    wide_ref[...] = jnp.zeros_like(wide_ref)
    total = jnp.zeros(wide_ref.shape, F32)
    for number in range(sections):
        origin = place_ref[0] - number
        origin = jnp.where(origin < 0, origin + sections, origin)
        chunk_ref[pl.ds(pl.multiple_of(origin * count, count), count), :] = signals[number][...]
        wide_ref[:3, :count] = points[number][...].astype(F32)
        total = total + pltpu.roll(wide_ref[...], origin * count, 1)
    chunk_ref[span : span + EXTRA, :] = total.astype(BF16)


def join(sections, place, signals, points):
    count, width = signals[0].shape
    return call(
        functools.partial(join_kernel, sections),
        "join",
        jax.ShapeDtypeStruct((sections * count + EXTRA, width), BF16),
        [SMEM] + [WHOLE] * (2 * sections),
        WHOLE,
        [VMEM((EXTRA, width), F32)],
    )(place, *signals, *points)


def sources_kernel(offsets, first, sections, place_ref, *refs):
    refs = list(refs)

    def take(number):
        taken = refs[:number]
        del refs[:number]
        return taken

    parts = len(offsets)
    chunks = take(parts)
    source_ref, panel_ref = take(2)
    loading_in, thick_in = (None, None) if first else take(2)
    final = sections is not None
    if final:
        corner_ref, slot_ref, ids_ref = take(3)
        node_ref, head_ref = take(2)
        messages = take(sections)
        loading_ref, thick_ref = take(2)
    else:
        loading_ref, thick_ref = take(2)
    low_ref, high_ref, pair_ref, mass_ref, window_ref = take(5)

    blocks, span = source_ref.shape[1:3]
    panels = panel_ref.shape[0] * BLK
    observers = parts * span
    points = []
    for number, chunk in enumerate(chunks):
        low_ref[number * span : (number + 1) * span, :] = chunk[:span, :128].astype(F32)
        high_ref[number * span : (number + 1) * span, :] = chunk[:span, 128:].astype(F32)
        points.append(chunk[span : span + EXTRA, :].astype(F32) * 0.25)

    lanes = lax.broadcasted_iota(jnp.int32, (128, 128), 1)
    for block in range(blocks):
        for number, offset in enumerate(offsets):
            group = place_ref[2] ^ offset
            for piece in range(span // 128):
                here = number * span + piece * 128
                source = source_ref[group, block, piece * 128 : (piece + 1) * 128, :]
                at = source & 127
                low = jnp.take_along_axis(low_ref[here : here + 128, :], at, axis=1, mode="promise_in_bounds")
                high = jnp.take_along_axis(high_ref[here : here + 128, :], at, axis=1, mode="promise_in_bounds")
                current = jnp.where(source < 128, low, high)
                following = pltpu.roll(jnp.where(lanes == 0, high, current), 127, 1)
                window_ref[block, here : here + 128, :] = current.astype(BF16)
                window_ref[block, observers + here : observers + here + 128, :] = (following - current).astype(BF16)

                at_x, at_y, at_z = (points[number][i : i + 1, piece * 128 : piece * 128 + 128] for i in range(3))
                for strip in range(BLK // 16):
                    rows = slice(strip * 16, strip * 16 + 16)
                    delta_x = at_x - panel_ref[block, 0, rows, :]
                    delta_y = at_y - panel_ref[block, 1, rows, :]
                    delta_z = at_z - panel_ref[block, 2, rows, :]
                    inverse = lax.rsqrt(delta_x * delta_x + delta_y * delta_y + delta_z * delta_z)
                    flux = (
                        panel_ref[block, 3, rows, :] * delta_x
                        + panel_ref[block, 4, rows, :] * delta_y
                        + panel_ref[block, 5, rows, :] * delta_z
                    )
                    far = flux * inverse * inverse
                    pair_ref[block, rows, here : here + 128] = (far * inverse).astype(BF16)
                    pair_ref[block, rows, observers + here : observers + here + 128] = far.astype(BF16)
                    mass_ref[block, rows, here : here + 128] = (panel_ref[block, 6, rows, :] * inverse).astype(BF16)
        rows = slice(block * BLK, (block + 1) * BLK)
        loading = jnp.dot(pair_ref[block], window_ref[block], preferred_element_type=F32)
        thick = jnp.dot(mass_ref[block], window_ref[block, observers:, :], preferred_element_type=F32)
        if not first:
            loading = loading + loading_in[rows, :]
            thick = thick + thick_in[rows, :]
        if final:
            alive = block * BLK + lax.broadcasted_iota(jnp.int32, (BLK, TW), 0) < place_ref[1]
            loading = jnp.where(alive, loading, 0.0).astype(BF16)
            thick = jnp.where(alive, thick, 0.0).astype(BF16)
        loading_ref[rows, :] = loading
        thick_ref[rows, :] = thick

    if final:
        nodes = jnp.dot(corner_ref[...], loading_ref[...], preferred_element_type=F32)
        head_ref[...] = nodes[:HEAD]
        node_ref[...] = nodes[:NODE_DEV]
        cap = slot_ref.shape[0] // sections
        slots = jnp.dot(slot_ref[...], thick_ref[...], preferred_element_type=F32).astype(BF16)
        for away, message_ref in enumerate(messages):
            message_ref[:cap, :] = slots[away * cap : (away + 1) * cap]
            message_ref[cap : cap + EXTRA, :] = jnp.broadcast_to(ids_ref[away : away + 1, :], (EXTRA, 128)).astype(BF16)
            if away == 1:
                message_ref[cap + EXTRA :, :] = nodes[NODE_DEV:].astype(BF16)


def sources(offsets, place, chunks, source, panel_values, sums, matrices=None, sections=None):
    blocks, span = source.shape[1:3]
    panels = panel_values.shape[0] * BLK
    observers = len(offsets) * span
    first = sums is None
    operands = [place, *chunks, source, panel_values] + ([] if first else list(sums))
    in_specs = [SMEM] + [WHOLE] * (len(operands) - 1)
    scratch = [
        VMEM((observers, 128), F32),
        VMEM((observers, 128), F32),
        VMEM((blocks, BLK, 2 * observers), BF16),
        VMEM((blocks, BLK, observers), BF16),
        VMEM((blocks, 2 * observers, TW), BF16),
    ]
    aliases = {}
    if matrices is None:
        out_shape = [jax.ShapeDtypeStruct((panels, TW), F32)] * 2
        if not first:
            aliases = {len(operands) - 2: 0, len(operands) - 1: 1}
    else:
        operands += list(matrices)
        in_specs += [WHOLE] * 3
        cap = 2 * CELL_DEV // sections
        out_shape = [jax.ShapeDtypeStruct((NODE_DEV, TW), F32), jax.ShapeDtypeStruct((HEAD, TW), F32)]
        for away in range(sections):
            rows = cap + EXTRA + (HEAD if away == 1 else 0)
            out_shape.append(jax.ShapeDtypeStruct((rows, TW), BF16))
        scratch = [VMEM((panels, TW), BF16)] * 2 + scratch
    return call(
        functools.partial(sources_kernel, offsets, first, sections),
        "sources",
        out_shape,
        in_specs,
        [WHOLE] * len(out_shape),
        scratch,
        aliases,
        work=3_000_000_000,
    )(*operands)


def finish_kernel(*refs):
    sections = len(refs) - 8
    messages = refs[:sections]
    head_ref, _, node_ref, cell_ref, rows_ref, top_ref, total_ref, sems = refs[sections:]
    rim_rows = messages[1].shape[0] - HEAD
    cap = rim_rows - EXTRA
    per = 128 // cap
    top_ref[...] = head_ref[...] + messages[1][rim_rows:, :].astype(F32)
    top_copy = pltpu.make_async_copy(top_ref, node_ref.at[pl.ds(0, HEAD), :], sems.at[0])
    top_copy.start()
    total = jnp.zeros((CELL_DEV, TW), F32)
    cell = lax.broadcasted_iota(jnp.int32, (CELL_DEV, 128), 0).astype(F32)
    for group in range(sections // per):
        ids = jnp.zeros((EXTRA, 128), F32)
        for inner in range(per):
            message = messages[group * per + inner]
            ids = ids + message[cap : cap + EXTRA, :].astype(F32)
            rows_ref[group * 128 + inner * cap : group * 128 + (inner + 1) * cap, :] = message[:cap, :]
        match = jnp.where(ids[:1] == cell, 1.0, 0.0).astype(BF16)
        total = total + jnp.dot(match, rows_ref[group * 128 : (group + 1) * 128, :], preferred_element_type=F32)
    total_ref[...] = total
    cell_copy = pltpu.make_async_copy(total_ref, cell_ref, sems.at[1])
    cell_copy.start()
    top_copy.wait()
    cell_copy.wait()


def finish(messages, head, nodes):
    sections = len(messages)
    cap = messages[0].shape[0] - EXTRA
    return call(
        finish_kernel,
        "finish",
        (
            jax.ShapeDtypeStruct((NODE_DEV, TW), F32),
            jax.ShapeDtypeStruct((CELL_DEV, TW), F32),
        ),
        [WHOLE] * (sections + 1) + [PLACE],
        [PLACE] * 2,
        [VMEM((sections * cap, TW), BF16), VMEM((HEAD, TW), F32), VMEM((CELL_DEV, TW), F32), COPY((2,))],
        {sections + 1: 0},
    )(*messages, head, nodes)


def swapped(array, axis, bit):
    peers = lax.axis_size(axis)
    return lax.ppermute(array, axis, [(i, i ^ bit) for i in range(peers)])


def shifted(array, axis, by):
    peers = lax.axis_size(axis)
    return lax.ppermute(array, axis, [(i, (i + by) % peers) for i in range(peers)])


def section_chunk(place, signals, xyz):
    count, width = signals.shape
    sections = lax.axis_size("sect")
    if count % 16 == 0:
        turned = xyz.T
        pieces = [signals] + [shifted(signals, "sect", by) for by in range(1, sections)]
        points = [turned] + [shifted(turned, "sect", by) for by in range(1, sections)]
        return join(sections, place, pieces, points)
    extra = jnp.zeros((EXTRA, width), BF16)
    extra = lax.dynamic_update_slice(extra, xyz.T, (0, lax.axis_index("sect") * count))
    payload = jnp.concatenate([signals, extra], 0)
    everyone = jnp.broadcast_to(payload[None], (sections,) + payload.shape)
    received = lax.all_to_all(everyone, "sect", split_axis=0, concat_axis=0, tiled=True)
    return jnp.concatenate(
        [received[:, :count].reshape(sections * count, -1), received[:, count:].astype(F32).sum(0).astype(BF16)], 0
    )


def per_device(signals, observer_xyz, panel_geometry, delays, counts, connectivity, owners):
    sections = lax.axis_size("sect")
    groups = lax.axis_size("azim")
    place = jnp.stack([lax.axis_index("sect"), counts[0], lax.axis_index("azim")]).astype(jnp.int32)
    chunks = {0: section_chunk(place, signals, observer_xyz)}
    bit = groups // 2
    while bit:
        for offset in list(chunks):
            chunks[offset ^ bit] = swapped(chunks[offset], "azim", bit)
        bit //= 2
    order = list(chunks)
    corners, slots, ids, source, panel_values = route(
        sections, groups, place, connectivity, owners, delays, panel_geometry
    )
    sums = None
    half = groups // 2 + 1
    for offsets in (order[:1], order[1:half]):
        sums = sources(offsets, place, [chunks[o] for o in offsets], source, panel_values, sums)
    offsets = order[half:]
    nodes, head, *messages = sources(
        offsets, place, [chunks[o] for o in offsets], source, panel_values, sums, (corners, slots, ids), sections
    )
    messages = messages[:1] + [shifted(m, "sect", by) for by, m in enumerate(messages) if by]
    return finish(messages, head, nodes)


def solution(mesh):
    in_specs = (
        P(("azim", "sect"), None),
        P(("azim", "sect"), None),
        P(None, ("azim", "sect")),
        P(("azim", "sect"), None),
        P(("azim", "sect")),
        P(None, ("azim", "sect")),
        P(("azim", "sect")),
    )
    out_specs = (P(("azim", "sect"), None), P(("azim", "sect"), None))
    return jax.shard_map(
        per_device, mesh=mesh, in_specs=in_specs, out_specs=out_specs, check_vma=False
    )
```

time: 67.3 us -> 67.4 us (level)
  starting transfers between devices: 6.86 us -> 34.9 us
  blocking collectives: 15.2 us -> 0 us
  Pallas kernels: 26.2 us -> 20.8 us
  waiting for transfers between devices: 11.7 us -> 6.96 us
  local copies, waits for them, and re-layouts: 4.49 us -> 2.93 us
  other arithmetic: 0.82 us -> 0.08 us
    ppermute x1 -> x21, starting transfers between devices: 1.92 us -> 33.4 us  [shifted(): lax.ppermute(array, axis, [(i, (i + by) % peers) for i in range(peers)])]
    all_to_all x1 -> x0, blocking collectives: 15.2 us -> none  [gathered(): lax.all_to_all(everyone, 'sect', split_axis=0, concat_axis=0, tiled=True)]
    pallas_call x3 -> x6, Pallas kernels: 26.2 us -> 20.8 us  [the longest x3 12.3 us: sources(): call(functools.partial(sources_kernel, offsets, first, sections), 'source...]
    all_to_all x1 -> x0, starting transfers between devices: 3.38 us -> none  [per_device(): lax.all_to_all(message, 'sect', split_axis=0, concat_axis=0, tiled=True)]
    ppermute x3, waiting for transfers between devices: 3.57 us -> 0.76 us  [swapped(): return lax.ppermute(array, axis, [(i, i ^ bit) for i in range(peers)])]
    ppermute x1 -> x21, waiting for transfers between devices: 8.14 us -> 6.2 us  [shifted(): lax.ppermute(array, axis, [(i, (i + by) % peers) for i in range(peers)])]
    dynamic_update_slice x1 -> x0, local copies, waits for them, and re-layouts: 1.55 us -> none  [gathered(): extra = lax.dynamic_update_slice(extra, xyz.T, (0, section * count))]
    concatenate x2 -> x0, other arithmetic: 0.73 us -> none  [the longest x1 0.72 us: gathered(): payload = jnp.concatenate([signals, extra], 0)]
  transfers between devices with their start and end apart: 5 -> 24, of which waited for: 2 -> 6; matrix products, arithmetic and copies ran while one was open for 0% -> 0% of each run, Pallas kernels for 6% -> 22%
where the time goes in v2:
time: 67.4 us; the launch traced here: 67.1 us
  starting transfers between devices  34.9 us (52%)
  Pallas kernels  20.8 us (31%)
  waiting for transfers between devices  6.96 us (10%)
  local copies, waits for them, and re-layouts  2.93 us (4%)
  between operations  1.4 us (2%)
    ppermute x21, starting transfers between devices, shifted(): lax.ppermute(array, axis, [(i, (i + by) % peers) for i in range(peers)])  33.4 us
    pallas_call x3, Pallas kernels, sources(): call(functools.partial(sources_kernel, offsets, first, sections), 'source...  12.3 us
    pallas_call x1, Pallas kernels, route(): call(functools.partial(route_kernel, sections), 'route', (jax.ShapeDtypeS...  6.95 us
    ppermute x21, waiting for transfers between devices, shifted(): lax.ppermute(array, axis, [(i, (i + by) % peers) for i in range(peers)])  6.2 us
    unnamed x12, local copies, waits for them, and re-layouts  2.93 us
    ppermute x3, starting transfers between devices, swapped(): return lax.ppermute(array, axis, [(i, i ^ bit) for i in range(peers)])  1.56 us
  transfers between devices with their start and end apart: 24, of which 6 were waited for; matrix products, arithmetic and copies ran while one was open for 0% of the time, Pallas kernels for 22%

profile of v2, /device:TPU:0, one launch (start us, length us, event | category | flops | bytes accessed | tf_op | source)
XLA Modules:
  0.0 67.1 jit_solution(14639860611362543837)
XLA Ops:
  0.6 4.1 %collective-permute-start.10 = (bf16[3,32]{1,0:T(4,128)(2,1)}, bf16[3,32]{1,0:T(4,128)(2,1)S(1)}, u32[]{:S(2)}, u32[]{:S(2)}) collective-permute-start(bf16[3,32]{1,0:T(4,128)(2,1)} %bitcast.4), channel_id=1, source_target_pairs={{0,4},{1,5},{2,6},{3,7},{4,0},{5,1},{6,2},{7,3},{8,12},{9,13},{10,... | collective-permute-start | bytes 584 | tf_op jit(solution)/shard_map/ppermute | solution.py:356
  4.7 1.3 %collective-permute-start.11 = (bf16[3,32]{1,0:T(4,128)(2,1)}, bf16[3,32]{1,0:T(4,128)(2,1)S(1)}, u32[]{:S(2)}, u32[]{:S(2)}) collective-permute-start(bf16[3,32]{1,0:T(4,128)(2,1)} %bitcast.5), channel_id=1, source_target_pairs={{0,5},{1,6},{2,7},{3,0},{4,1},{5,2},{6,3},{7,4},{8,13},{9,14},{10,... | collective-permute-start | bytes 584 | tf_op jit(solution)/shard_map/ppermute | solution.py:356
  6.0 3.6 %collective-permute-start.12 = (bf16[3,32]{1,0:T(4,128)(2,1)}, bf16[3,32]{1,0:T(4,128)(2,1)S(1)}, u32[]{:S(2)}, u32[]{:S(2)}) collective-permute-start(bf16[3,32]{1,0:T(4,128)(2,1)} %bitcast.6), channel_id=1, source_target_pairs={{0,6},{1,7},{2,0},{3,1},{4,2},{5,3},{6,4},{7,5},{8,14},{9,15},{10,... | collective-permute-start | bytes 584 | tf_op jit(solution)/shard_map/ppermute | solution.py:356
  10.4 4.7 %collective-permute-start.13 = (bf16[3,32]{1,0:T(4,128)(2,1)}, bf16[3,32]{1,0:T(4,128)(2,1)S(1)}, u32[]{:S(2)}, u32[]{:S(2)}) collective-permute-start(bf16[3,32]{1,0:T(4,128)(2,1)} %bitcast.7), channel_id=1, source_target_pairs={{0,7},{1,0},{2,1},{3,2},{4,3},{5,4},{6,5},{7,6},{8,15},{9,8},{10,9... | collective-permute-start | bytes 584 | tf_op jit(solution)/shard_map/ppermute | solution.py:356
  15.2 1.4 %collective-permute-done.13.refs_15_ = bf16[3,32]{1,0:T(4,128)(2,1)S(1)} collective-permute-done((bf16[3,32]{1,0:T(4,128)(2,1)}, bf16[3,32]{1,0:T(4,128)(2,1)S(1)}, u32[]{:S(2)}, u32[]{:S(2)}) %collective-permute-start.13) | collective-permute-done | bytes 224 | tf_op jit(solution)/shard_map/ppermute | solution.py:356
  16.6 2.6 %collective-permute-start.9 = (bf16[3,32]{1,0:T(4,128)(2,1)}, bf16[3,32]{1,0:T(4,128)(2,1)S(1)}, u32[]{:S(2)}, u32[]{:S(2)}) collective-permute-start(bf16[3,32]{1,0:T(4,128)(2,1)} %bitcast.10), channel_id=1, source_target_pairs={{0,3},{1,4},{2,5},{3,6},{4,7},{5,0},{6,1},{7,2},{8,11},{9,12},{10,... | collective-permute-start | bytes 584 | tf_op jit(solution)/shard_map/ppermute | solution.py:356
  19.1 2.4 %collective-permute-done.7.refs_9_ = bf16[3,32]{1,0:T(4,128)(2,1)S(1)} collective-permute-done((bf16[3,32]{1,0:T(4,128)(2,1)}, bf16[3,32]{1,0:T(4,128)(2,1)S(1)}, u32[]{:S(2)}, u32[]{:S(2)}) %collective-permute-start.7) | collective-permute-done | bytes 224 | tf_op jit(solution)/shard_map/ppermute | solution.py:356
  22.2 3.8 %collective-permute-start.4 = (bf16[32,256]{1,0:T(8,128)(2,1)}, bf16[32,256]{1,0:T(8,128)(2,1)S(1)}, u32[]{:S(2)}, u32[]{:S(2)}) collective-permute-start(bf16[32,256]{1,0:T(8,128)(2,1)} %refs_0_.1), channel_id=1, source_target_pairs={{0,5},{1,6},{2,7},{3,0},{4,1},{5,2},{6,3},{7,4},{8,13},{9,14},{10,... | collective-permute-start | bytes 49160 | tf_op jit(solution)/shard_map/ppermute | solution.py:356
  26.0 1.2 %collective-permute-start.5 = (bf16[32,256]{1,0:T(8,128)(2,1)}, bf16[32,256]{1,0:T(8,128)(2,1)S(1)}, u32[]{:S(2)}, u32[]{:S(2)}) collective-permute-start(bf16[32,256]{1,0:T(8,128)(2,1)} %refs_0_.1), channel_id=1, source_target_pairs={{0,6},{1,7},{2,0},{3,1},{4,2},{5,3},{6,4},{7,5},{8,14},{9,15},{10,... | collective-permute-start | bytes 49160 | tf_op jit(solution)/shard_map/ppermute | solution.py:356
  30.6 6.9 %route.1 = (bf16[1168,1024]{1,0:T(8,128)(2,1)S(1)}, bf16[512,1024]{1,0:T(8,128)(2,1)S(1)}, f32[16,128]{1,0:T(8,128)S(1)}, s32[4,8,256,128]{3,2,1,0:T(8,128)S(1)}, f32[8,7,128,128]{3,2,1,0:T(8,128)S(1)}) custom-call(s32[3]{0:T(128)S(1)} %pad_add_fusion.place_ref, s32[4,1024]{1,0:T(4,128)S(1)} %copy-done.4, s32[1,1024]{1,0:T(1,128)S(1)} %bitcast.12, ...), custom_call_target="tpu_custom_call" | custom-call | flops 4000000000 | bytes 4000000 | tf_op jit(solution)/shard_map/route/pallas_call | solution.py:125
  38.3 1.6 %collective-permute-start.14 = (bf16[272,256]{1,0:T(8,128)(2,1)S(1)}, bf16[272,256]{1,0:T(8,128)(2,1)S(1)}, u32[]{:S(2)}, u32[]{:S(2)}) collective-permute-start(bf16[272,256]{1,0:T(8,128)(2,1)S(1)} %join.1.refs_0_), channel_id=1, source_target_pairs={{0,16},{8,24},{16,0},{24,8},{1,17},{9,25},{17,1},{25,9},{2,18},{10... | collective-permute-start | bytes 417800 | tf_op jit(solution)/shard_map/ppermute | solution.py:351
  39.9 2.8 %sources.3 = (f32[1024,128]{1,0:T(8,128)S(1)}, f32[1024,128]{1,0:T(8,128)S(1)}) custom-call(s32[3]{0:T(128)S(1)} %pad_add_fusion.place_ref, bf16[272,256]{1,0:T(8,128)(2,1)S(1)} %join.1.refs_0_, s32[4,8,256,128]{3,2,1,0:T(8,128)S(1)} %get-tuple-element.21.refs_1_.refs_2_, f32[8,7,128,128]{3,2,1,0:T(8,128)S(1)} %get-tuple-element.22.refs_2_.refs_3_), custom_call_target="tpu_custom_call" | custom-call | flops 3000000000 | bytes 4000000 | tf_op jit(solution)/shard_map/sources/pallas_call | solution.py:293
  43.5 5.2 %sources.4 = (f32[1024,128]{1,0:T(8,128)S(1)}, f32[1024,128]{1,0:T(8,128)S(1)}) custom-call(s32[3]{0:T(128)S(1)} %pad_add_fusion.place_ref, bf16[272,256]{1,0:T(8,128)(2,1)S(1)} %collective-permute-done.14.refs_0_, bf16[272,256]{1,0:T(8,128)(2,1)S(1)} %collective-permute-done.16.refs_1_, ...), custom_call_target="tpu_custom_call", output_to_operand_aliasing={{0}: (5, {}), {1}: (6, {})} | custom-call | flops 3000000000 | bytes 4000000 | tf_op jit(solution)/shard_map/sources/pallas_call | solution.py:293
  48.7 4.3 %sources.5 = (f32[1032,128]{1,0:T(8,128)}, f32[136,128]{1,0:T(8,128)S(1)}, bf16[80,128]{1,0:T(8,128)(2,1)S(1)}, bf16[216,128]{1,0:T(8,128)(2,1)S(1)}, bf16[80,12...) custom-call(s32[3]{0:T(128)S(1)} %pad_add_fusion.place_ref, ...), custom_call_target="tpu_custom_call" | custom-call | flops 3000000000 | bytes 4000000 | tf_op jit(solution)/shard_map/sources/pallas_call | solution.py:293
  52.9 1.5 %collective-permute-start.17 = (bf16[216,128]{1,0:T(8,128)(2,1)S(1)}, bf16[216,128]{1,0:T(8,128)(2,1)S(1)}, u32[]{:S(2)}, u32[]{:S(2)}) collective-permute-start(bf16[216,128]{1,0:T(8,128)(2,1)S(1)} %get-tuple-element.31), channel_id=1, source_target_pairs={{0,1},{1,2},{2,3},{3,4},{4,5},{5,6},{6,7},{7,0},{8,9},{9,10},{10,1... | collective-permute-start | bytes 165896 | tf_op jit(solution)/shard_map/ppermute | solution.py:356
  54.4 0.8 %collective-permute-start.18 = (bf16[80,128]{1,0:T(8,128)(2,1)S(1)}, bf16[80,128]{1,0:T(8,128)(2,1)S(1)}, u32[]{:S(2)}, u32[]{:S(2)}) collective-permute-start(bf16[80,128]{1,0:T(8,128)(2,1)S(1)} %get-tuple-element.32), channel_id=1, source_target_pairs={{0,2},{1,3},{2,4},{3,5},{4,6},{5,7},{6,0},{7,1},{8,10},{9,11},{10,... | collective-permute-start | bytes 61448 | tf_op jit(solution)/shard_map/ppermute | solution.py:356
  55.2 1.8 %collective-permute-start.19 = (bf16[80,128]{1,0:T(8,128)(2,1)S(1)}, bf16[80,128]{1,0:T(8,128)(2,1)S(1)}, u32[]{:S(2)}, u32[]{:S(2)}) collective-permute-start(bf16[80,128]{1,0:T(8,128)(2,1)S(1)} %get-tuple-element.33), channel_id=1, source_target_pairs={{0,3},{1,4},{2,5},{3,6},{4,7},{5,0},{6,1},{7,2},{8,11},{9,12},{10,... | collective-permute-start | bytes 61448 | tf_op jit(solution)/shard_map/ppermute | solution.py:356
  57.1 2.4 %collective-permute-start.20 = (bf16[80,128]{1,0:T(8,128)(2,1)S(1)}, bf16[80,128]{1,0:T(8,128)(2,1)S(1)}, u32[]{:S(2)}, u32[]{:S(2)}) collective-permute-start(bf16[80,128]{1,0:T(8,128)(2,1)S(1)} %get-tuple-element.34), channel_id=1, source_target_pairs={{0,4},{1,5},{2,6},{3,7},{4,0},{5,1},{6,2},{7,3},{8,12},{9,13},{10,... | collective-permute-start | bytes 61448 | tf_op jit(solution)/shard_map/ppermute | solution.py:356
  59.4 2.0 %collective-permute-start.21 = (bf16[80,128]{1,0:T(8,128)(2,1)S(1)}, bf16[80,128]{1,0:T(8,128)(2,1)S(1)}, u32[]{:S(2)}, u32[]{:S(2)}) collective-permute-start(bf16[80,128]{1,0:T(8,128)(2,1)S(1)} %get-tuple-element.35), channel_id=1, source_target_pairs={{0,5},{1,6},{2,7},{3,0},{4,1},{5,2},{6,3},{7,4},{8,13},{9,14},{10,... | collective-permute-start | bytes 61448 | tf_op jit(solution)/shard_map/ppermute | solution.py:356
  61.4 1.0 %collective-permute-start.22 = (bf16[80,128]{1,0:T(8,128)(2,1)S(1)}, bf16[80,128]{1,0:T(8,128)(2,1)S(1)}, u32[]{:S(2)}, u32[]{:S(2)}) collective-permute-start(bf16[80,128]{1,0:T(8,128)(2,1)S(1)} %get-tuple-element.36), channel_id=1, source_target_pairs={{0,6},{1,7},{2,0},{3,1},{4,2},{5,3},{6,4},{7,5},{8,14},{9,15},{10,... | collective-permute-start | bytes 61448 | tf_op jit(solution)/shard_map/ppermute | solution.py:356
  62.4 1.5 %collective-permute-start.23 = (bf16[80,128]{1,0:T(8,128)(2,1)S(1)}, bf16[80,128]{1,0:T(8,128)(2,1)S(1)}, u32[]{:S(2)}, u32[]{:S(2)}) collective-permute-start(bf16[80,128]{1,0:T(8,128)(2,1)S(1)} %get-tuple-element.37), channel_id=1, source_target_pairs={{0,7},{1,0},{2,1},{3,2},{4,3},{5,4},{6,5},{7,6},{8,15},{9,8},{10,9... | collective-permute-start | bytes 61448 | tf_op jit(solution)/shard_map/ppermute | solution.py:356
  64.3 1.0 %collective-permute-done.22.refs_6_ = bf16[80,128]{1,0:T(8,128)(2,1)S(1)} collective-permute-done((bf16[80,128]{1,0:T(8,128)(2,1)S(1)}, bf16[80,128]{1,0:T(8,128)(2,1)S(1)}, u32[]{:S(2)}, u32[]{:S(2)}) %collective-permute-start.22) | collective-permute-done | bytes 20512 | tf_op jit(solution)/shard_map/ppermute | solution.py:356
  65.2 1.0 %collective-permute-done.23.refs_7_ = bf16[80,128]{1,0:T(8,128)(2,1)S(1)} collective-permute-done((bf16[80,128]{1,0:T(8,128)(2,1)S(1)}, bf16[80,128]{1,0:T(8,128)(2,1)S(1)}, u32[]{:S(2)}, u32[]{:S(2)}) %collective-permute-start.23) | collective-permute-done | bytes 20512 | tf_op jit(solution)/shard_map/ppermute | solution.py:356
  66.2 0.9 %finish.1 = (f32[1032,128]{1,0:T(8,128)}, f32[256,128]{1,0:T(8,128)}) custom-call(bf16[80,128]{1,0:T(8,128)(2,1)S(1)} %get-tuple-element.30.refs_0_, bf16[216,128]{1,0:T(8,128)(2,1)S(1)} %collective-permute-done.17.refs_1_, bf16[80,128]{1,0:T(8,128)(2,1)S(1)} %collective-permute-done.18.refs_2_, ...), custom_call_target="tpu_custom_call", output_to_operand_aliasing={{0}: (9, {})} | custom-call | flops 1000000 | bytes 4000000 | tf_op jit(solution)/shard_map/finish/pallas_call | solution.py:335
  (43 shorter events, 6.1 us)
Async XLA Ops:
  0.6 9.7 %collective-permute-start.10 = (bf16[3,32]{1,0:T(4,128)(2,1)}, bf16[3,32]{1,0:T(4,128)(2,1)S(1)}, u32[]{:S(2)}, u32[]{:S(2)}) collective-permute-start(bf16[3,32]{1,0:T(4,128)(2,1)} %bitcast.4), channel_id=1, source_target_pairs={{0,4},{1,5},{2,6},{3,7},{4,0},{5,1},{6,2},{7,3},{8,12},{9,13},{10,... | collective-permute-start | bytes 584 | tf_op jit(solution)/shard_map/ppermute | solution.py:356
  4.7 10.4 %collective-permute-start.11 = (bf16[3,32]{1,0:T(4,128)(2,1)}, bf16[3,32]{1,0:T(4,128)(2,1)S(1)}, u32[]{:S(2)}, u32[]{:S(2)}) collective-permute-start(bf16[3,32]{1,0:T(4,128)(2,1)} %bitcast.5), channel_id=1, source_target_pairs={{0,5},{1,6},{2,7},{3,0},{4,1},{5,2},{6,3},{7,4},{8,13},{9,14},{10,... | collective-permute-start | bytes 584 | tf_op jit(solution)/shard_map/ppermute | solution.py:356
  6.0 9.1 %collective-permute-start.12 = (bf16[3,32]{1,0:T(4,128)(2,1)}, bf16[3,32]{1,0:T(4,128)(2,1)S(1)}, u32[]{:S(2)}, u32[]{:S(2)}) collective-permute-start(bf16[3,32]{1,0:T(4,128)(2,1)} %bitcast.6), channel_id=1, source_target_pairs={{0,6},{1,7},{2,0},{3,1},{4,2},{5,3},{6,4},{7,5},{8,14},{9,15},{10,... | collective-permute-start | bytes 584 | tf_op jit(solution)/shard_map/ppermute | solution.py:356
  9.6 16.3 %collective-permute-start = (bf16[32,256]{1,0:T(8,128)(2,1)}, bf16[32,256]{1,0:T(8,128)(2,1)S(1)}, u32[]{:S(2)}, u32[]{:S(2)}) collective-permute-start(bf16[32,256]{1,0:T(8,128)(2,1)} %refs_0_.1), channel_id=1, source_target_pairs={{0,1},{1,2},{2,3},{3,4},{4,5},{5,6},{6,7},{7,0},{8,9},{9,10},{10,1... | collective-permute-start | bytes 49160 | tf_op jit(solution)/shard_map/ppermute | solution.py:356
  9.6 17.5 %collective-permute-start.1 = (bf16[32,256]{1,0:T(8,128)(2,1)}, bf16[32,256]{1,0:T(8,128)(2,1)S(1)}, u32[]{:S(2)}, u32[]{:S(2)}) collective-permute-start(bf16[32,256]{1,0:T(8,128)(2,1)} %refs_0_.1), channel_id=1, source_target_pairs={{0,2},{1,3},{2,4},{3,5},{4,6},{5,7},{6,0},{7,1},{8,10},{9,11},{10,... | collective-permute-start | bytes 49160 | tf_op jit(solution)/shard_map/ppermute | solution.py:356
  10.4 6.2 %collective-permute-start.13 = (bf16[3,32]{1,0:T(4,128)(2,1)}, bf16[3,32]{1,0:T(4,128)(2,1)S(1)}, u32[]{:S(2)}, u32[]{:S(2)}) collective-permute-start(bf16[3,32]{1,0:T(4,128)(2,1)} %bitcast.7), channel_id=1, source_target_pairs={{0,7},{1,0},{2,1},{3,2},{4,3},{5,4},{6,5},{7,6},{8,15},{9,8},{10,9... | collective-permute-start | bytes 584 | tf_op jit(solution)/shard_map/ppermute | solution.py:356
  15.1 6.5 %collective-permute-start.7 = (bf16[3,32]{1,0:T(4,128)(2,1)}, bf16[3,32]{1,0:T(4,128)(2,1)S(1)}, u32[]{:S(2)}, u32[]{:S(2)}) collective-permute-start(bf16[3,32]{1,0:T(4,128)(2,1)} %bitcast.8), channel_id=1, source_target_pairs={{0,1},{1,2},{2,3},{3,4},{4,5},{5,6},{6,7},{7,0},{8,9},{9,10},{10,1... | collective-permute-start | bytes 584 | tf_op jit(solution)/shard_map/ppermute | solution.py:356
  15.1 6.5 %collective-permute-start.8 = (bf16[3,32]{1,0:T(4,128)(2,1)}, bf16[3,32]{1,0:T(4,128)(2,1)S(1)}, u32[]{:S(2)}, u32[]{:S(2)}) collective-permute-start(bf16[3,32]{1,0:T(4,128)(2,1)} %bitcast.9), channel_id=1, source_target_pairs={{0,2},{1,3},{2,4},{3,5},{4,6},{5,7},{6,0},{7,1},{8,10},{9,11},{10,... | collective-permute-start | bytes 584 | tf_op jit(solution)/shard_map/ppermute | solution.py:356
  16.6 5.6 %collective-permute-start.9 = (bf16[3,32]{1,0:T(4,128)(2,1)}, bf16[3,32]{1,0:T(4,128)(2,1)S(1)}, u32[]{:S(2)}, u32[]{:S(2)}) collective-permute-start(bf16[3,32]{1,0:T(4,128)(2,1)} %bitcast.10), channel_id=1, source_target_pairs={{0,3},{1,4},{2,5},{3,6},{4,7},{5,0},{6,1},{7,2},{8,11},{9,12},{10,... | collective-permute-start | bytes 584 | tf_op jit(solution)/shard_map/ppermute | solution.py:356
  21.6 16.0 %collective-permute-start.2 = (bf16[32,256]{1,0:T(8,128)(2,1)}, bf16[32,256]{1,0:T(8,128)(2,1)S(1)}, u32[]{:S(2)}, u32[]{:S(2)}) collective-permute-start(bf16[32,256]{1,0:T(8,128)(2,1)} %refs_0_.1), channel_id=1, source_target_pairs={{0,3},{1,4},{2,5},{3,6},{4,7},{5,0},{6,1},{7,2},{8,11},{9,12},{10,... | collective-permute-start | bytes 49160 | tf_op jit(solution)/shard_map/ppermute | solution.py:356
  21.6 16.0 %collective-permute-start.3 = (bf16[32,256]{1,0:T(8,128)(2,1)}, bf16[32,256]{1,0:T(8,128)(2,1)S(1)}, u32[]{:S(2)}, u32[]{:S(2)}) collective-permute-start(bf16[32,256]{1,0:T(8,128)(2,1)} %refs_0_.1), channel_id=1, source_target_pairs={{0,4},{1,5},{2,6},{3,7},{4,0},{5,1},{6,2},{7,3},{8,12},{9,13},{10,... | collective-permute-start | bytes 49160 | tf_op jit(solution)/shard_map/ppermute | solution.py:356
  22.2 15.4 %collective-permute-start.4 = (bf16[32,256]{1,0:T(8,128)(2,1)}, bf16[32,256]{1,0:T(8,128)(2,1)S(1)}, u32[]{:S(2)}, u32[]{:S(2)}) collective-permute-start(bf16[32,256]{1,0:T(8,128)(2,1)} %refs_0_.1), channel_id=1, source_target_pairs={{0,5},{1,6},{2,7},{3,0},{4,1},{5,2},{6,3},{7,4},{8,13},{9,14},{10,... | collective-permute-start | bytes 49160 | tf_op jit(solution)/shard_map/ppermute | solution.py:356
  26.0 11.7 %collective-permute-start.5 = (bf16[32,256]{1,0:T(8,128)(2,1)}, bf16[32,256]{1,0:T(8,128)(2,1)S(1)}, u32[]{:S(2)}, u32[]{:S(2)}) collective-permute-start(bf16[32,256]{1,0:T(8,128)(2,1)} %refs_0_.1), channel_id=1, source_target_pairs={{0,6},{1,7},{2,0},{3,1},{4,2},{5,3},{6,4},{7,5},{8,14},{9,15},{10,... | collective-permute-start | bytes 49160 | tf_op jit(solution)/shard_map/ppermute | solution.py:356
  27.2 10.5 %collective-permute-start.6 = (bf16[32,256]{1,0:T(8,128)(2,1)}, bf16[32,256]{1,0:T(8,128)(2,1)S(1)}, u32[]{:S(2)}, u32[]{:S(2)}) collective-permute-start(bf16[32,256]{1,0:T(8,128)(2,1)} %refs_0_.1), channel_id=1, source_target_pairs={{0,7},{1,0},{2,1},{3,2},{4,3},{5,4},{6,5},{7,6},{8,15},{9,8},{10,9... | collective-permute-start | bytes 49160 | tf_op jit(solution)/shard_map/ppermute | solution.py:356
  38.3 5.1 %collective-permute-start.14 = (bf16[272,256]{1,0:T(8,128)(2,1)S(1)}, bf16[272,256]{1,0:T(8,128)(2,1)S(1)}, u32[]{:S(2)}, u32[]{:S(2)}) collective-permute-start(bf16[272,256]{1,0:T(8,128)(2,1)S(1)} %join.1.refs_0_), channel_id=1, source_target_pairs={{0,16},{8,24},{16,0},{24,8},{1,17},{9,25},{17,1},{25,9},{2,18},{10... | collective-permute-start | bytes 417800 | tf_op jit(solution)/shard_map/ppermute | solution.py:351
  39.9 3.6 %collective-permute-start.16 = (bf16[272,256]{1,0:T(8,128)(2,1)S(1)}, bf16[272,256]{1,0:T(8,128)(2,1)S(1)}, u32[]{:S(2)}, u32[]{:S(2)}) collective-permute-start(bf16[272,256]{1,0:T(8,128)(2,1)S(1)} %join.1.refs_0_), channel_id=1, source_target_pairs={{0,8},{8,0},{16,24},{24,16},{1,9},{9,1},{17,25},{25,17},{2,10},{10... | collective-permute-start | bytes 417800 | tf_op jit(solution)/shard_map/ppermute | solution.py:351
  43.5 5.2 %collective-permute-start.15 = (bf16[272,256]{1,0:T(8,128)(2,1)S(1)}, bf16[272,256]{1,0:T(8,128)(2,1)S(1)}, u32[]{:S(2)}, u32[]{:S(2)}) collective-permute-start(bf16[272,256]{1,0:T(8,128)(2,1)S(1)} %collective-permute-done.14.refs_0_), channel_id=1, source_target_pairs={{0,8},{8,0},{16,24},{24,16},{1,9},{9,1},{17,25},{25,17},{2,10},{10... | collective-permute-start | bytes 417800 | tf_op jit(solution)/shard_map/ppermute | solution.py:351
  52.9 13.2 %collective-permute-start.17 = (bf16[216,128]{1,0:T(8,128)(2,1)S(1)}, bf16[216,128]{1,0:T(8,128)(2,1)S(1)}, u32[]{:S(2)}, u32[]{:S(2)}) collective-permute-start(bf16[216,128]{1,0:T(8,128)(2,1)S(1)} %get-tuple-element.31), channel_id=1, source_target_pairs={{0,1},{1,2},{2,3},{3,4},{4,5},{5,6},{6,7},{7,0},{8,9},{9,10},{10,1... | collective-permute-start | bytes 165896 | tf_op jit(solution)/shard_map/ppermute | solution.py:356
  54.4 7.0 %collective-permute-start.18 = (bf16[80,128]{1,0:T(8,128)(2,1)S(1)}, bf16[80,128]{1,0:T(8,128)(2,1)S(1)}, u32[]{:S(2)}, u32[]{:S(2)}) collective-permute-start(bf16[80,128]{1,0:T(8,128)(2,1)S(1)} %get-tuple-element.32), channel_id=1, source_target_pairs={{0,2},{1,3},{2,4},{3,5},{4,6},{5,7},{6,0},{7,1},{8,10},{9,11},{10,... | collective-permute-start | bytes 61448 | tf_op jit(solution)/shard_map/ppermute | solution.py:356
  55.2 7.1 %collective-permute-start.19 = (bf16[80,128]{1,0:T(8,128)(2,1)S(1)}, bf16[80,128]{1,0:T(8,128)(2,1)S(1)}, u32[]{:S(2)}, u32[]{:S(2)}) collective-permute-start(bf16[80,128]{1,0:T(8,128)(2,1)S(1)} %get-tuple-element.33), channel_id=1, source_target_pairs={{0,3},{1,4},{2,5},{3,6},{4,7},{5,0},{6,1},{7,2},{8,11},{9,12},{10,... | collective-permute-start | bytes 61448 | tf_op jit(solution)/shard_map/ppermute | solution.py:356
  57.1 6.8 %collective-permute-start.20 = (bf16[80,128]{1,0:T(8,128)(2,1)S(1)}, bf16[80,128]{1,0:T(8,128)(2,1)S(1)}, u32[]{:S(2)}, u32[]{:S(2)}) collective-permute-start(bf16[80,128]{1,0:T(8,128)(2,1)S(1)} %get-tuple-element.34), channel_id=1, source_target_pairs={{0,4},{1,5},{2,6},{3,7},{4,0},{5,1},{6,2},{7,3},{8,12},{9,13},{10,... | collective-permute-start | bytes 61448 | tf_op jit(solution)/shard_map/ppermute | solution.py:356
  59.4 4.8 %collective-permute-start.21 = (bf16[80,128]{1,0:T(8,128)(2,1)S(1)}, bf16[80,128]{1,0:T(8,128)(2,1)S(1)}, u32[]{:S(2)}, u32[]{:S(2)}) collective-permute-start(bf16[80,128]{1,0:T(8,128)(2,1)S(1)} %get-tuple-element.35), channel_id=1, source_target_pairs={{0,5},{1,6},{2,7},{3,0},{4,1},{5,2},{6,3},{7,4},{8,13},{9,14},{10,... | collective-permute-start | bytes 61448 | tf_op jit(solution)/shard_map/ppermute | solution.py:356
  61.4 3.8 %collective-permute-start.22 = (bf16[80,128]{1,0:T(8,128)(2,1)S(1)}, bf16[80,128]{1,0:T(8,128)(2,1)S(1)}, u32[]{:S(2)}, u32[]{:S(2)}) collective-permute-start(bf16[80,128]{1,0:T(8,128)(2,1)S(1)} %get-tuple-element.36), channel_id=1, source_target_pairs={{0,6},{1,7},{2,0},{3,1},{4,2},{5,3},{6,4},{7,5},{8,14},{9,15},{10,... | collective-permute-start | bytes 61448 | tf_op jit(solution)/shard_map/ppermute | solution.py:356
  62.4 3.8 %collective-permute-start.23 = (bf16[80,128]{1,0:T(8,128)(2,1)S(1)}, bf16[80,128]{1,0:T(8,128)(2,1)S(1)}, u32[]{:S(2)}, u32[]{:S(2)}) collective-permute-start(bf16[80,128]{1,0:T(8,128)(2,1)S(1)} %get-tuple-element.37), channel_id=1, source_target_pairs={{0,7},{1,0},{2,1},{3,2},{4,3},{5,4},{6,5},{7,6},{8,15},{9,8},{10,9... | collective-permute-start | bytes 61448 | tf_op jit(solution)/shard_map/ppermute | solution.py:356
  (6 other events, 17.0 us)

commit v3 on v2

v3 whole, which is shorter than its diff:
```python
import functools

import jax
import jax.numpy as jnp
from jax import lax
from jax.experimental import pallas as pl
from jax.experimental.pallas import tpu as pltpu
from jax.sharding import PartitionSpec as P

NPU = 128
BLK = 128
TW = 128
CELL_DEV = 256
NODE_DEV = 1032
RIM = NPU + 1
HEAD = 136
NODE_ROWS = 1168
EXTRA = 16
F32 = jnp.float32
BF16 = jnp.bfloat16
VMEM = pltpu.VMEM
SMEM = pl.BlockSpec(memory_space=pltpu.SMEM)
WHOLE = pl.BlockSpec(memory_space=pltpu.VMEM)
PLACE = pl.BlockSpec(memory_space=pl.ANY)
FAR = pl.BlockSpec(memory_space=pltpu.HBM)
COPY = pltpu.SemaphoreType.DMA


def call(kernel, name, out_shape, in_specs, out_specs, scratch_shapes=(), aliases=None, work=1_000_000):
    return pl.pallas_call(
        kernel,
        out_shape=out_shape,
        in_specs=in_specs,
        out_specs=out_specs,
        scratch_shapes=list(scratch_shapes),
        input_output_aliases=aliases or {},
        compiler_params=pltpu.CompilerParams(vmem_limit_bytes=24 * 1024 * 1024),
        cost_estimate=pl.CostEstimate(flops=work, bytes_accessed=4_000_000, transcendentals=0),
        name=name,
    )


def fetch(pairs, sems):
    copies = [pltpu.make_async_copy(source, target, sems.at[i]) for i, (source, target) in enumerate(pairs)]
    for copy in copies:
        copy.start()
    for copy in copies:
        copy.wait()


def window_kernel(sections, paired, place_ref, delay_at, source_ref, delay_ref, sems):
    fetch([(delay_at, delay_ref)], sems)
    groups, blocks, span, _ = source_ref.shape
    count = span // sections
    piece_rows = count if paired else 128
    lanes = lax.broadcasted_iota(jnp.int32, (piece_rows, 128), 1)
    for piece in range(groups * span // 128):
        columns = delay_ref[:, piece * 128 : (piece + 1) * 128].T
        for part in range(128 // piece_rows):
            row = piece * 128 + part * piece_rows
            begin = row % span
            if paired:
                apart = place_ref[0] ^ (begin // count)
                begin = pl.multiple_of((apart // 2 + apart % 2 * (sections // 2)) * count, count)
            for block in range(blocks):
                column = columns[part * piece_rows : (part + 1) * piece_rows, block : block + 1]
                source_ref[row // span, block, pl.ds(begin, piece_rows), :] = (
                    jnp.broadcast_to(column, (piece_rows, 128)) + lanes
                )


def window_index(sections, groups, paired, place, delays):
    blocks, observers = delays.shape
    return call(
        functools.partial(window_kernel, sections, paired),
        "windows",
        jax.ShapeDtypeStruct((groups, blocks, observers // groups, 128), jnp.int32),
        [SMEM, FAR],
        WHOLE,
        [VMEM(delays.shape, jnp.int32), COPY((1,))],
        work=2_000_000_000,
    )(place, delays)


def column_kernel(
    sections, place_ref, geometry_at, owner_at, panel_ref, slot_ref, ids_ref, geometry_ref, owner_ref, sems
):
    fetch([(geometry_at, geometry_ref), (owner_at, owner_ref)], sems)
    panels = geometry_ref.shape[1]
    for block in range(panels // BLK):
        values = geometry_ref[:, block * BLK : (block + 1) * BLK]
        columns = jnp.concatenate([values, values[:1]], 0).T
        for part in range(7):
            column = columns[:, part : part + 1] * (0.25 if part < 3 else 1.0)
            panel_ref[block, part] = jnp.broadcast_to(column, (BLK, 128))

    cap = slot_ref.shape[0] // sections
    padded = ids_ref.shape[0]
    section = place_ref[0]
    live = place_ref[1]
    owner = owner_ref[...]
    dest = owner // CELL_DEV
    lane = lax.broadcasted_iota(jnp.int32, (padded, panels), 1)
    mine = dest == lax.broadcasted_iota(jnp.int32, (padded, panels), 0)
    count = jnp.where(mine, 1, 0)
    span = 1
    while span < panels:
        count = count + jnp.where(lane >= span, pltpu.roll(count, span, 1), 0)
        span *= 2
    before = jnp.sum(jnp.where(mine, count - 1, 0), axis=0, keepdims=True)
    rank = before // 4
    slot = dest * cap + rank

    def slot_rows(step, carried):
        row = pl.multiple_of(step * 16, 16)
        number = row + lax.broadcasted_iota(jnp.int32, (16, panels), 0)
        panel = lax.broadcasted_iota(jnp.int32, (16, panels), 1)
        number = jnp.where(panel < live, number, -1)
        slot_ref[pl.ds(row, 16), :] = jnp.where(slot == number, 1.0, 0.0).astype(BF16)
        return carried

    lax.fori_loop(0, slot_ref.shape[0] // 16, slot_rows, 0)

    at_lane = rank + section * cap % 128 == lax.broadcasted_iota(jnp.int32, (128, panels), 0)
    at_lane = jnp.where(at_lane, 1.0, 0.0).astype(BF16)
    cell = jnp.where(mine & (lane % 4 == 0), owner % CELL_DEV, 0).astype(F32).astype(BF16)
    ids_ref[...] = lax.dot_general(cell, at_lane, (((1,), (1,)), ((), ())), preferred_element_type=F32)


def panel_columns(sections, place, geometry, owners):
    panels = geometry.shape[1]
    cap = 2 * CELL_DEV // sections
    padded = -(-sections // EXTRA) * EXTRA
    return call(
        functools.partial(column_kernel, sections),
        "columns",
        (
            jax.ShapeDtypeStruct((panels // BLK, 7, BLK, 128), F32),
            jax.ShapeDtypeStruct((sections * cap, panels), BF16),
            jax.ShapeDtypeStruct((padded, 128), F32),
        ),
        [SMEM, FAR, FAR],
        [WHOLE] * 3,
        [VMEM(geometry.shape, F32), VMEM((1, panels), jnp.int32), COPY((2,))],
        work=2_000_000_000,
    )(place, geometry, owners.reshape(1, panels))


def corner_kernel(place_ref, conn_at, corner_ref, conn_ref, sems):
    fetch([(conn_at, conn_ref)], sems)
    panels = conn_ref.shape[1]
    live = place_ref[1]

    def corner_rows(step, carried):
        row = pl.multiple_of(step * 16, 16)
        node = row + lax.broadcasted_iota(jnp.int32, (16, panels), 0)
        panel = lax.broadcasted_iota(jnp.int32, (16, panels), 1)
        node = jnp.where(panel < live, node, -1)
        total = jnp.zeros((16, panels), F32)
        for corner in range(4):
            total = total + jnp.where(conn_ref[corner : corner + 1, :] == node, 0.25, 0.0)
        corner_ref[pl.ds(row, 16), :] = total.astype(BF16)
        return carried

    lax.fori_loop(0, NODE_ROWS // 16, corner_rows, 0)


def corner_matrix(place, connectivity):
    return call(
        corner_kernel,
        "corners",
        jax.ShapeDtypeStruct((NODE_ROWS, connectivity.shape[1]), BF16),
        [SMEM, FAR],
        WHOLE,
        [VMEM(connectivity.shape, jnp.int32), COPY((1,))],
        work=2_000_000_000,
    )(place, connectivity)


def first_join_kernel(mine_ref, other_ref, my_points_ref, other_points_ref, chunk_ref, wide_ref):
    count = mine_ref.shape[0]
    chunk_ref[:count, :] = mine_ref[...]
    chunk_ref[count : 2 * count, :] = other_ref[...]
    wide_ref[...] = jnp.zeros_like(wide_ref)
    wide_ref[:3, :count] = other_points_ref[...].astype(F32)
    moved = pltpu.roll(wide_ref[...], count, 1)
    wide_ref[:3, :count] = my_points_ref[...].astype(F32)
    wide_ref[3:, :count] = jnp.zeros((EXTRA - 3, count), F32)
    chunk_ref[2 * count :, :] = (moved + wide_ref[...]).astype(BF16)


def join_kernel(mine_ref, other_ref, chunk_ref):
    span = mine_ref.shape[0] - EXTRA
    chunk_ref[:span, :] = mine_ref[:span, :]
    chunk_ref[span : 2 * span, :] = other_ref[:span, :]
    moved = pltpu.roll(other_ref[span:, :].astype(F32), span, 1)
    chunk_ref[2 * span :, :] = (mine_ref[span:, :].astype(F32) + moved).astype(BF16)


def sources_kernel(offsets, first, final, place_ref, *refs):
    refs = list(refs)

    def take(number):
        taken = refs[:number]
        del refs[:number]
        return taken

    parts = len(offsets)
    chunks = take(parts)
    source_ref, panel_ref = take(2)
    loading_in, thick_in = (None, None) if first else take(2)
    if final:
        corner_ref, node_ref, head_ref, rim_ref, thick_ref, loading_ref = take(6)
    else:
        loading_ref, thick_ref = take(2)
    low_ref, high_ref, pair_ref, mass_ref, window_ref = take(5)

    blocks, span = source_ref.shape[1:3]
    panels = panel_ref.shape[0] * BLK
    observers = parts * span
    points = []
    for number, chunk in enumerate(chunks):
        low_ref[number * span : (number + 1) * span, :] = chunk[:span, :128].astype(F32)
        high_ref[number * span : (number + 1) * span, :] = chunk[:span, 128:].astype(F32)
        points.append(chunk[span : span + EXTRA, :].astype(F32) * 0.25)

    lanes = lax.broadcasted_iota(jnp.int32, (128, 128), 1)
    for block in range(blocks):
        for number, offset in enumerate(offsets):
            group = place_ref[2] ^ offset
            for piece in range(span // 128):
                here = number * span + piece * 128
                source = source_ref[group, block, piece * 128 : (piece + 1) * 128, :]
                at = source & 127
                low = jnp.take_along_axis(low_ref[here : here + 128, :], at, axis=1, mode="promise_in_bounds")
                high = jnp.take_along_axis(high_ref[here : here + 128, :], at, axis=1, mode="promise_in_bounds")
                current = jnp.where(source < 128, low, high)
                following = pltpu.roll(jnp.where(lanes == 0, high, current), 127, 1)
                window_ref[block, here : here + 128, :] = current.astype(BF16)
                window_ref[block, observers + here : observers + here + 128, :] = (following - current).astype(BF16)

                at_x, at_y, at_z = (points[number][i : i + 1, piece * 128 : piece * 128 + 128] for i in range(3))
                for strip in range(BLK // 16):
                    rows = slice(strip * 16, strip * 16 + 16)
                    delta_x = at_x - panel_ref[block, 0, rows, :]
                    delta_y = at_y - panel_ref[block, 1, rows, :]
                    delta_z = at_z - panel_ref[block, 2, rows, :]
                    inverse = lax.rsqrt(delta_x * delta_x + delta_y * delta_y + delta_z * delta_z)
                    flux = (
                        panel_ref[block, 3, rows, :] * delta_x
                        + panel_ref[block, 4, rows, :] * delta_y
                        + panel_ref[block, 5, rows, :] * delta_z
                    )
                    far = flux * inverse * inverse
                    pair_ref[block, rows, here : here + 128] = (far * inverse).astype(BF16)
                    pair_ref[block, rows, observers + here : observers + here + 128] = far.astype(BF16)
                    mass_ref[block, rows, here : here + 128] = (panel_ref[block, 6, rows, :] * inverse).astype(BF16)
        rows = slice(block * BLK, (block + 1) * BLK)
        loading = jnp.dot(pair_ref[block], window_ref[block], preferred_element_type=F32)
        thick = jnp.dot(mass_ref[block], window_ref[block, observers:, :], preferred_element_type=F32)
        if not first:
            loading = loading + loading_in[rows, :]
            thick = thick + thick_in[rows, :]
        if final:
            alive = block * BLK + lax.broadcasted_iota(jnp.int32, (BLK, TW), 0) < place_ref[1]
            loading = jnp.where(alive, loading, 0.0).astype(BF16)
            thick = jnp.where(alive, thick, 0.0).astype(BF16)
        loading_ref[rows, :] = loading
        thick_ref[rows, :] = thick

    if final:
        nodes = jnp.dot(corner_ref[...], loading_ref[...], preferred_element_type=F32)
        head_ref[...] = nodes[:HEAD]
        rim_ref[...] = nodes[NODE_DEV:].astype(BF16)
        node_ref[...] = nodes[:NODE_DEV]


def sources(offsets, place, chunks, source, panel_values, sums, corners=None):
    blocks, span = source.shape[1:3]
    panels = panel_values.shape[0] * BLK
    observers = len(offsets) * span
    first = sums is None
    operands = [place, *chunks, source, panel_values] + ([] if first else list(sums))
    in_specs = [SMEM] + [WHOLE] * (len(operands) - 1)
    scratch = [
        VMEM((observers, 128), F32),
        VMEM((observers, 128), F32),
        VMEM((blocks, BLK, 2 * observers), BF16),
        VMEM((blocks, BLK, observers), BF16),
        VMEM((blocks, 2 * observers, TW), BF16),
    ]
    aliases = {}
    if corners is None:
        out_shape = [jax.ShapeDtypeStruct((panels, TW), F32)] * 2
        if not first:
            aliases = {len(operands) - 2: 0, len(operands) - 1: 1}
    else:
        operands.append(corners)
        in_specs.append(WHOLE)
        out_shape = [
            jax.ShapeDtypeStruct((NODE_DEV, TW), F32),
            jax.ShapeDtypeStruct((HEAD, TW), F32),
            jax.ShapeDtypeStruct((HEAD, TW), BF16),
            jax.ShapeDtypeStruct((panels, TW), BF16),
        ]
        scratch = [VMEM((panels, TW), BF16)] + scratch
    return call(
        functools.partial(sources_kernel, offsets, first, corners is not None),
        "sources",
        out_shape,
        in_specs,
        [WHOLE] * len(out_shape),
        scratch,
        aliases,
        work=3_000_000_000,
    )(*operands)


def slot_kernel(slot_ref, ids_ref, thick_ref, message_ref):
    sections = message_ref.shape[0]
    cap = slot_ref.shape[0] // sections
    slots = jnp.dot(slot_ref[...], thick_ref[...], preferred_element_type=F32).astype(BF16)
    for section in range(sections):
        message_ref[section, :cap, :] = slots[section * cap : (section + 1) * cap]
        ids = jnp.broadcast_to(ids_ref[section : section + 1, :], (EXTRA, 128))
        message_ref[section, cap:, :] = ids.astype(BF16)


def slot_messages(sections, slots, ids, thick):
    cap = 2 * CELL_DEV // sections
    return call(
        slot_kernel,
        "slots",
        jax.ShapeDtypeStruct((sections, cap + EXTRA, TW), BF16),
        [WHOLE] * 3,
        WHOLE,
    )(slots, ids, thick)


def finish_kernel(message_ref, rim_ref, head_ref, _, node_ref, cell_ref, rows_ref, top_ref, total_ref, sems):
    sections = message_ref.shape[0]
    cap = message_ref.shape[1] - EXTRA
    per = 128 // cap
    top_ref[...] = head_ref[...] + rim_ref[...].astype(F32)
    top_copy = pltpu.make_async_copy(top_ref, node_ref.at[pl.ds(0, HEAD), :], sems.at[0])
    top_copy.start()
    total = jnp.zeros((CELL_DEV, TW), F32)
    cell = lax.broadcasted_iota(jnp.int32, (CELL_DEV, 128), 0).astype(F32)
    for group in range(sections // per):
        ids = jnp.zeros((EXTRA, 128), F32)
        for inner in range(per):
            section = group * per + inner
            ids = ids + message_ref[section, cap:, :].astype(F32)
            rows_ref[section * cap : (section + 1) * cap, :] = message_ref[section, :cap, :]
        match = jnp.where(ids[:1] == cell, 1.0, 0.0).astype(BF16)
        total = total + jnp.dot(match, rows_ref[group * 128 : (group + 1) * 128, :], preferred_element_type=F32)
    total_ref[...] = total
    cell_copy = pltpu.make_async_copy(total_ref, cell_ref, sems.at[1])
    cell_copy.start()
    top_copy.wait()
    cell_copy.wait()


def finish(message, rim, head, nodes):
    sections = message.shape[0]
    cap = message.shape[1] - EXTRA
    return call(
        finish_kernel,
        "finish",
        (
            jax.ShapeDtypeStruct((NODE_DEV, TW), F32),
            jax.ShapeDtypeStruct((CELL_DEV, TW), F32),
        ),
        [WHOLE] * 3 + [PLACE],
        [PLACE] * 2,
        [VMEM((sections * cap, TW), BF16), VMEM((HEAD, TW), F32), VMEM((CELL_DEV, TW), F32), COPY((2,))],
        {3: 0},
    )(message, rim, head, nodes)


def swapped(array, axis, bit):
    peers = lax.axis_size(axis)
    return lax.ppermute(array, axis, [(i, i ^ bit) for i in range(peers)])


def joined(mine, other):
    span = mine.shape[0] - EXTRA
    shape = jax.ShapeDtypeStruct((2 * span + EXTRA, mine.shape[1]), BF16)
    return call(join_kernel, "join", shape, [WHOLE] * 2, WHOLE)(mine, other)


def paired_chunk(signals, xyz, sections, local):
    count, width = signals.shape
    turned = xyz.T
    bit = 2
    other, other_points = swapped(signals, "sect", bit), swapped(turned, "sect", bit)
    shape = jax.ShapeDtypeStruct((2 * count + EXTRA, width), BF16)
    done = [local[0]()]
    chunk = call(first_join_kernel, "pair", shape, [WHOLE] * 4, WHOLE, [VMEM((EXTRA, width), F32)])(
        signals, other, turned, other_points
    )
    for step in range(2, sections.bit_length()):
        bit = bit * 2 if bit * 2 < sections else 1
        other = swapped(chunk, "sect", bit)
        done.append(local[step - 1](chunk) if step <= len(local) else None)
        chunk = joined(chunk, other)
    return chunk, done


def spread_chunk(signals, xyz, sections):
    count, width = signals.shape
    extra = jnp.zeros((EXTRA, width), BF16)
    extra = lax.dynamic_update_slice(extra, xyz.T, (0, lax.axis_index("sect") * count))
    payload = jnp.concatenate([signals, extra], 0)
    everyone = jnp.broadcast_to(payload[None], (sections,) + payload.shape)
    received = lax.all_to_all(everyone, "sect", split_axis=0, concat_axis=0, tiled=True)
    return jnp.concatenate(
        [received[:, :count].reshape(sections * count, -1), received[:, count:].astype(F32).sum(0).astype(BF16)], 0
    )


def per_device(signals, observer_xyz, panel_geometry, delays, counts, connectivity, owners):
    sections = lax.axis_size("sect")
    groups = lax.axis_size("azim")
    place = jnp.stack([lax.axis_index("sect"), counts[0], lax.axis_index("azim")]).astype(jnp.int32)
    paired = sections == 8 and signals.shape[0] % 16 == 0

    def windows():
        return window_index(sections, groups, paired, place, delays)

    def columns(after=None):
        geometry = panel_geometry
        if after is not None:
            geometry, _ = lax.optimization_barrier((geometry, after))
        return panel_columns(sections, place, geometry, owners)

    def corners(after=None):
        nodes = connectivity
        if after is not None:
            nodes, _ = lax.optimization_barrier((nodes, after))
        return corner_matrix(place, nodes)

    if paired:
        chunk, done = paired_chunk(signals, observer_xyz, sections, (windows, columns, corners))
        source, (panel_values, slots, ids), corner_values = done
    else:
        chunk = spread_chunk(signals, observer_xyz, sections)
        source, (panel_values, slots, ids), corner_values = windows(), columns(), corners()
    chunks = {0: chunk}
    bit = groups // 2
    while bit:
        for offset in list(chunks):
            chunks[offset ^ bit] = swapped(chunks[offset], "azim", bit)
        bit //= 2
    sums = None
    for offsets in ([0], [1]):
        sums = sources(offsets, place, [chunks[o] for o in offsets], source, panel_values, sums)
    offsets = [o for o in chunks if o > 1]
    nodes, head, rim, thick = sources(
        offsets, place, [chunks[o] for o in offsets], source, panel_values, sums, corner_values
    )
    rim = lax.ppermute(rim, "sect", [(i, (i + 1) % sections) for i in range(sections)])
    message = slot_messages(sections, slots, ids, thick)
    message = lax.all_to_all(message, "sect", split_axis=0, concat_axis=0, tiled=True)
    return finish(message, rim, head, nodes)


def solution(mesh):
    in_specs = (
        P(("azim", "sect"), None),
        P(("azim", "sect"), None),
        P(None, ("azim", "sect")),
        P(("azim", "sect"), None),
        P(("azim", "sect")),
        P(None, ("azim", "sect")),
        P(("azim", "sect")),
    )
    out_specs = (P(("azim", "sect"), None), P(("azim", "sect"), None))
    return jax.shard_map(
        per_device, mesh=mesh, in_specs=in_specs, out_specs=out_specs, check_vma=False
    )
```

time: 67.4 us -> 49.6 us (0.74)
  starting transfers between devices: 34.9 us -> 16.2 us
  Pallas kernels: 20.8 us -> 23 us
  local copies, waits for them, and re-layouts: 2.93 us -> 0.78 us
  waiting for transfers between devices: 6.96 us -> 7.85 us
    ppermute x21 -> x1, starting transfers between devices: 33.4 us -> 2.02 us  [per_device(): lax.ppermute(rim, 'sect', [(i, (i + 1) % sections) for i in range(section...]
    ppermute x3 -> x7, starting transfers between devices: 1.56 us -> 9.23 us  [swapped(): return lax.ppermute(array, axis, [(i, i ^ bit) for i in range(peers)])]
    all_to_all x0 -> x1, starting transfers between devices: none -> 4.96 us  [per_device(): lax.all_to_all(message, 'sect', split_axis=0, concat_axis=0, tiled=True)]
    pallas_call x5 -> x10, Pallas kernels: 19.9 us -> 22.1 us  [the longest x3 12.2 us: sources(): call(functools.partial(sources_kernel, offsets, first, corners is not Non...]
    unnamed x12, local copies, waits for them, and re-layouts: 2.93 us -> 0.78 us
    ppermute x21 -> x1, waiting for transfers between devices: 6.2 us -> 7.08 us  [per_device(): lax.ppermute(rim, 'sect', [(i, (i + 1) % sections) for i in range(section...]
  transfers between devices with their start and end apart: 24 -> 9, of which waited for: 6 -> 2; matrix products, arithmetic and copies ran while one was open for 0% -> 0% of each run, Pallas kernels for 22% -> 29%
where the time goes in v3:
time: 49.6 us; the launch traced here: 49.3 us
  Pallas kernels  23 us (46%)
  starting transfers between devices  16.2 us (33%)
  waiting for transfers between devices  7.85 us (16%)
  between operations  1.4 us (3%)
  local copies, waits for them, and re-layouts  0.78 us (2%)
    pallas_call x3, Pallas kernels, sources(): call(functools.partial(sources_kernel, offsets, first, corners is not Non...  12.2 us
    ppermute x7, starting transfers between devices, swapped(): return lax.ppermute(array, axis, [(i, i ^ bit) for i in range(peers)])  9.23 us
    ppermute x1, waiting for transfers between devices, per_device(): lax.ppermute(rim, 'sect', [(i, (i + 1) % sections) for i in range(section...  7.08 us
    all_to_all x1, starting transfers between devices, per_device(): lax.all_to_all(message, 'sect', split_axis=0, concat_axis=0, tiled=True)  4.96 us
    pallas_call x1, Pallas kernels, panel_columns(): call(functools.partial(column_kernel, sections), 'columns', (jax.ShapeDty...  3.26 us
    pallas_call x1, Pallas kernels, corner_matrix(): call(corner_kernel, 'corners', jax.ShapeDtypeStruct((NODE_ROWS, connectiv...  3.03 us
    pallas_call x1, Pallas kernels, window_index(): call(functools.partial(window_kernel, sections, paired), 'windows', jax.S...  2.38 us
    ppermute x1, starting transfers between devices, per_device(): lax.ppermute(rim, 'sect', [(i, (i + 1) % sections) for i in range(section...  2.02 us
  transfers between devices with their start and end apart: 9, of which 2 were waited for; matrix products, arithmetic and copies ran while one was open for 0% of the time, Pallas kernels for 29%

profile of v3, /device:TPU:0, one launch (start us, length us, event | category | flops | bytes accessed | tf_op | source)
XLA Modules:
  0.0 49.3 jit_solution(6970804525595359284)
XLA Ops:
  0.6 3.1 %collective-permute-start = (bf16[32,256]{1,0:T(8,128)(2,1)}, bf16[32,256]{1,0:T(8,128)(2,1)S(1)}, u32[]{:S(2)}, u32[]{:S(2)}) collective-permute-start(bf16[32,256]{1,0:T(8,128)(2,1)} %mine_ref.1), channel_id=1, source_target_pairs={{0,2},{1,3},{2,0},{3,1},{4,6},{5,7},{6,4},{7,5},{8,10},{9,11},{10,... | collective-permute-start | bytes 49160 | tf_op jit(solution)/shard_map/ppermute | solution.py:383
  3.7 0.1 collective-permute-start.1
  4.5 0.1 pad_add_fusion.place_ref
  4.5 0.8 %copy-done.2 = s32[8,1024]{1,0:T(8,128)S(1)} copy-done((s32[8,1024]{1,0:T(8,128)S(1)}, s32[8,1024]{1,0:T(8,128)}, u32[]{:S(2)}) %copy-start.2) | copy-done | bytes 32792
  5.3 2.4 %windows.1.refs_1_.refs_2_ = s32[4,8,256,128]{3,2,1,0:T(8,128)S(1)} custom-call(s32[3]{0:T(128)S(1)} %pad_add_fusion.place_ref, s32[8,1024]{1,0:T(8,128)S(1)} %copy-done.2), custom_call_target="tpu_custom_call" | custom-call | flops 2000000000 | bytes 4000000 | tf_op jit(solution)/shard_map/windows/pallas_call | solution.py:74
  7.7 0.0 collective-permute-done.1.other_points_ref
  7.7 0.1 pair.1.mine_ref
  7.8 3.0 %collective-permute-start.2 = (bf16[80,256]{1,0:T(8,128)(2,1)S(1)}, bf16[80,256]{1,0:T(8,128)(2,1)S(1)}, u32[]{:S(2)}, u32[]{:S(2)}) collective-permute-start(bf16[80,256]{1,0:T(8,128)(2,1)S(1)} %pair.1.mine_ref), channel_id=1, source_target_pairs={{0,4},{1,5},{2,6},{3,7},{4,0},{5,1},{6,2},{7,3},{8,12},{9,13},{10,... | collective-permute-start | bytes 122888 | tf_op jit(solution)/shard_map/ppermute | solution.py:383
  10.8 3.3 %columns.1 = (f32[8,7,128,128]{3,2,1,0:T(8,128)S(1)}, bf16[512,1024]{1,0:T(8,128)(2,1)S(1)}, f32[16,128]{1,0:T(8,128)S(1)}) custom-call(s32[3]{0:T(128)S(1)} %pad_add_fusion.place_ref, f32[7,1024]{1,0:T(8,128)S(1)} %copy-done.3, s32[1,1024]{1,0:T(1,128)S(1)} %bitcast.6), custom_call_target="tpu_custom_call" | custom-call | flops 2000000000 | bytes 4000000 | tf_op jit(solution)/shard_map/columns/pallas_call | solution.py:134
  14.0 0.0 collective-permute-done.2.other_ref
  14.1 0.1 join.2.mine_ref
  14.1 1.5 %collective-permute-start.3 = (bf16[144,256]{1,0:T(8,128)(2,1)S(1)}, bf16[144,256]{1,0:T(8,128)(2,1)S(1)}, u32[]{:S(2)}, u32[]{:S(2)}) collective-permute-start(bf16[144,256]{1,0:T(8,128)(2,1)S(1)} %join.2.mine_ref), channel_id=1, source_target_pairs={{0,1},{1,0},{2,3},{3,2},{4,5},{5,4},{6,7},{7,6},{8,9},{9,8},{10,11... | collective-permute-start | bytes 221192 | tf_op jit(solution)/shard_map/ppermute | solution.py:383
  15.7 3.0 %corners.1.refs_6_ = bf16[1168,1024]{1,0:T(8,128)(2,1)S(1)} custom-call(s32[3]{0:T(128)S(1)} %pad_add_fusion.place_ref, s32[4,1024]{1,0:T(4,128)S(1)} %copy-done.4), custom_call_target="tpu_custom_call" | custom-call | flops 2000000000 | bytes 4000000 | tf_op jit(solution)/shard_map/corners/pallas_call | solution.py:169
  18.7 0.0 collective-permute-done.3.other_ref
  18.7 1.6 %collective-permute-start.4 = (bf16[272,256]{1,0:T(8,128)(2,1)S(1)}, bf16[272,256]{1,0:T(8,128)(2,1)S(1)}, u32[]{:S(2)}, u32[]{:S(2)}) collective-permute-start(bf16[272,256]{1,0:T(8,128)(2,1)S(1)} %join.3.refs_0_), channel_id=1, source_target_pairs={{0,16},{8,24},{16,0},{24,8},{1,17},{9,25},{17,1},{25,9},{2,18},{10... | collective-permute-start | bytes 417800 | tf_op jit(solution)/shard_map/ppermute | solution.py:383
  20.3 2.8 %sources.3 = (f32[1024,128]{1,0:T(8,128)S(1)}, f32[1024,128]{1,0:T(8,128)S(1)}) custom-call(s32[3]{0:T(128)S(1)} %pad_add_fusion.place_ref, bf16[272,256]{1,0:T(8,128)(2,1)S(1)} %join.3.refs_0_, s32[4,8,256,128]{3,2,1,0:T(8,128)S(1)} %windows.1.refs_1_.refs_2_, f32[8,7,128,128]{3,2,1,0:T(8,128)S(1)} %get-tuple-element.18.refs_2_.refs_3_), custom_call_target="tpu_custom_call" | custom-call | flops 3000000000 | bytes 4000000 | tf_op jit(solution)/shard_map/sources/pallas_call | solution.py:307
  23.1 0.8 %collective-permute-done.4.refs_0_ = bf16[272,256]{1,0:T(8,128)(2,1)S(1)} collective-permute-done((bf16[272,256]{1,0:T(8,128)(2,1)S(1)}, bf16[272,256]{1,0:T(8,128)(2,1)S(1)}, u32[]{:S(2)}, u32[]{:S(2)}) %collective-permute-start.4) | collective-permute-done | bytes 139296 | tf_op jit(solution)/shard_map/ppermute | solution.py:383
  23.9 2.9 %sources.4 = (f32[1024,128]{1,0:T(8,128)S(1)}, f32[1024,128]{1,0:T(8,128)S(1)}) custom-call(s32[3]{0:T(128)S(1)} %pad_add_fusion.place_ref, bf16[272,256]{1,0:T(8,128)(2,1)S(1)} %collective-permute-done.6.refs_0_, s32[4,8,256,128]{3,2,1,0:T(8,128)S(1)} %windows.1.refs_1_.refs_2_, ...), custom_call_target="tpu_custom_call", output_to_operand_aliasing={{0}: (4, {}), {1}: (5, {})} | custom-call | flops 3000000000 | bytes 4000000 | tf_op jit(solution)/shard_map/sources/pallas_call | solution.py:307
  26.8 6.5 %sources.5 = (f32[1032,128]{1,0:T(8,128)}, f32[136,128]{1,0:T(8,128)S(1)}, bf16[136,128]{1,0:T(8,128)(2,1)S(1)}, bf16[1024,128]{1,0:T(8,128)(2,1)S(1)}) custom-call(s32[3]{0:T(128)S(1)} %pad_add_fusion.place_ref, bf16[272,256]{1,0:T(8,128)(2,1)S(1)} %collective-permute-done.4.refs_0_, bf16[272,256]{1,0:T(8,128)(2,1)S(1)} %collective-permute-done.5.refs_1_, ...), custom_call_target="tpu_custom_call" | custom-call | flops 3000000000 | bytes 4000000 | tf_op jit(solution)/shard_map/sources/pallas_call | solution.py:307
  33.3 1.1 %slots.1 = bf16[8,80,128]{2,1,0:T(8,128)(2,1)} custom-call(bf16[512,1024]{1,0:T(8,128)(2,1)S(1)} %get-tuple-element.16.slot_ref, f32[16,128]{1,0:T(8,128)S(1)} %get-tuple-element.17.ids_ref, bf16[1024,128]{1,0:T(8,128)(2,1)S(1)} %get-tuple-element.24.thick_ref), custom_call_target="tpu_custom_call" | custom-call | flops 1000000 | bytes 4000000 | tf_op jit(solution)/shard_map/slots/pallas_call | solution.py:331
  34.4 5.0 %all-to-all-start = ((bf16[8,80,128]{2,1,0:T(8,128)(2,1)}), bf16[8,80,128]{2,1,0:T(8,128)(2,1)S(1)}, u32[]{:S(2)}, u32[]{:S(2)}) async-start(bf16[8,80,128]{2,1,0:T(8,128)(2,1)} %slots.1), calls=%async_computation | async-start | bytes 327680 | tf_op jit(solution)/shard_map/all_to_all | solution.py:464
  39.3 2.0 %collective-permute-start.7 = (bf16[136,128]{1,0:T(8,128)(2,1)S(1)}, bf16[136,128]{1,0:T(8,128)(2,1)S(1)}, u32[]{:S(2)}, u32[]{:S(2)}) collective-permute-start(bf16[136,128]{1,0:T(8,128)(2,1)S(1)} %get-tuple-element.25), channel_id=1, source_target_pairs={{0,1},{1,2},{2,3},{3,4},{4,5},{5,6},{6,7},{7,0},{8,9},{9,10},{10,1... | collective-permute-start | bytes 104456 | tf_op jit(solution)/shard_map/ppermute | solution.py:462
  41.3 7.1 %collective-permute-done.7.rim_ref = bf16[136,128]{1,0:T(8,128)(2,1)S(1)} collective-permute-done((bf16[136,128]{1,0:T(8,128)(2,1)S(1)}, bf16[136,128]{1,0:T(8,128)(2,1)S(1)}, u32[]{:S(2)}, u32[]{:S(2)}) %collective-permute-start.7) | collective-permute-done | bytes 34848 | tf_op jit(solution)/shard_map/ppermute | solution.py:462
  48.4 0.9 %finish.1 = (f32[1032,128]{1,0:T(8,128)}, f32[256,128]{1,0:T(8,128)}) custom-call(bf16[8,80,128]{2,1,0:T(8,128)(2,1)S(1)} %all-to-all-done.message_ref, bf16[136,128]{1,0:T(8,128)(2,1)S(1)} %collective-permute-done.7.rim_ref, f32[136,128]{1,0:T(8,128)S(1)} %get-tuple-element.26.head_ref, ...), custom_call_target="tpu_custom_call", output_to_operand_aliasing={{0}: (3, {})} | custom-call | flops 1000000 | bytes 4000000 | tf_op jit(solution)/shard_map/finish/pallas_call | solution.py:367
  (18 shorter events, 0.1 us)
Async XLA Ops:
  0.6 7.1 %collective-permute-start = (bf16[32,256]{1,0:T(8,128)(2,1)}, bf16[32,256]{1,0:T(8,128)(2,1)S(1)}, u32[]{:S(2)}, u32[]{:S(2)}) collective-permute-start(bf16[32,256]{1,0:T(8,128)(2,1)} %mine_ref.1), channel_id=1, source_target_pairs={{0,2},{1,3},{2,0},{3,1},{4,6},{5,7},{6,4},{7,5},{8,10},{9,11},{10,... | collective-permute-start | bytes 49160 | tf_op jit(solution)/shard_map/ppermute | solution.py:383
  3.7 4.0 %collective-permute-start.1 = (bf16[3,32]{1,0:T(4,128)(2,1)}, bf16[3,32]{1,0:T(4,128)(2,1)S(1)}, u32[]{:S(2)}, u32[]{:S(2)}) collective-permute-start(bf16[3,32]{1,0:T(4,128)(2,1)} %bitcast.4), channel_id=1, source_target_pairs={{0,2},{1,3},{2,0},{3,1},{4,6},{5,7},{6,4},{7,5},{8,10},{9,11},{10,... | collective-permute-start | bytes 584 | tf_op jit(solution)/shard_map/ppermute | solution.py:383
  4.5 0.8 %copy-start.2 = (s32[8,1024]{1,0:T(8,128)S(1)}, s32[8,1024]{1,0:T(8,128)}, u32[]{:S(2)}) copy-start(s32[8,1024]{1,0:T(8,128)} %delay_at.1) | copy-start | bytes 98308
  5.3 2.4 %copy-start = (bf16[32,256]{1,0:T(8,128)(2,1)S(1)}, bf16[32,256]{1,0:T(8,128)(2,1)}, u32[]{:S(2)}) copy-start(bf16[32,256]{1,0:T(8,128)(2,1)} %mine_ref.1) | copy-start | bytes 49156
  5.3 2.4 %copy-start.1 = (bf16[32,3]{0,1:T(4,128)(2,1)S(1)}, bf16[32,3]{0,1:T(4,128)(2,1)}, u32[]{:S(2)}) copy-start(bf16[32,3]{0,1:T(4,128)(2,1)} %param.8) | copy-start | bytes 580
  5.3 5.5 %copy-start.3 = (f32[7,1024]{1,0:T(8,128)S(1)}, f32[7,1024]{1,0:T(8,128)}, u32[]{:S(2)}) copy-start(f32[7,1024]{1,0:T(8,128)} %geometry_at) | copy-start | bytes 86020
  5.3 5.5 %copy-start.5 = (s32[1024]{0:T(1024)S(1)}, s32[1024]{0:T(1024)}, u32[]{:S(2)}) copy-start(s32[1024]{0:T(1024)} %param.13) | copy-start | bytes 12292
  7.8 6.2 %collective-permute-start.2 = (bf16[80,256]{1,0:T(8,128)(2,1)S(1)}, bf16[80,256]{1,0:T(8,128)(2,1)S(1)}, u32[]{:S(2)}, u32[]{:S(2)}) collective-permute-start(bf16[80,256]{1,0:T(8,128)(2,1)S(1)} %pair.1.mine_ref), channel_id=1, source_target_pairs={{0,4},{1,5},{2,6},{3,7},{4,0},{5,1},{6,2},{7,3},{8,12},{9,13},{10,... | collective-permute-start | bytes 122888 | tf_op jit(solution)/shard_map/ppermute | solution.py:383
  10.8 4.9 %copy-start.4 = (s32[4,1024]{1,0:T(4,128)S(1)}, s32[4,1024]{1,0:T(4,128)}, u32[]{:S(2)}) copy-start(s32[4,1024]{1,0:T(4,128)} %conn_at) | copy-start | bytes 49156
  14.1 4.6 %collective-permute-start.3 = (bf16[144,256]{1,0:T(8,128)(2,1)S(1)}, bf16[144,256]{1,0:T(8,128)(2,1)S(1)}, u32[]{:S(2)}, u32[]{:S(2)}) collective-permute-start(bf16[144,256]{1,0:T(8,128)(2,1)S(1)} %join.2.mine_ref), channel_id=1, source_target_pairs={{0,1},{1,0},{2,3},{3,2},{4,5},{5,4},{6,7},{7,6},{8,9},{9,8},{10,11... | collective-permute-start | bytes 221192 | tf_op jit(solution)/shard_map/ppermute | solution.py:383
  18.7 5.1 %collective-permute-start.4 = (bf16[272,256]{1,0:T(8,128)(2,1)S(1)}, bf16[272,256]{1,0:T(8,128)(2,1)S(1)}, u32[]{:S(2)}, u32[]{:S(2)}) collective-permute-start(bf16[272,256]{1,0:T(8,128)(2,1)S(1)} %join.3.refs_0_), channel_id=1, source_target_pairs={{0,16},{8,24},{16,0},{24,8},{1,17},{9,25},{17,1},{25,9},{2,18},{10... | collective-permute-start | bytes 417800 | tf_op jit(solution)/shard_map/ppermute | solution.py:383
  20.3 3.6 %collective-permute-start.6 = (bf16[272,256]{1,0:T(8,128)(2,1)S(1)}, bf16[272,256]{1,0:T(8,128)(2,1)S(1)}, u32[]{:S(2)}, u32[]{:S(2)}) collective-permute-start(bf16[272,256]{1,0:T(8,128)(2,1)S(1)} %join.3.refs_0_), channel_id=1, source_target_pairs={{0,8},{8,0},{16,24},{24,16},{1,9},{9,1},{17,25},{25,17},{2,10},{10... | collective-permute-start | bytes 417800 | tf_op jit(solution)/shard_map/ppermute | solution.py:383
  23.9 3.0 %collective-permute-start.5 = (bf16[272,256]{1,0:T(8,128)(2,1)S(1)}, bf16[272,256]{1,0:T(8,128)(2,1)S(1)}, u32[]{:S(2)}, u32[]{:S(2)}) collective-permute-start(bf16[272,256]{1,0:T(8,128)(2,1)S(1)} %collective-permute-done.4.refs_0_), channel_id=1, source_target_pairs={{0,8},{8,0},{16,24},{24,16},{1,9},{9,1},{17,25},{25,17},{2,10},{10... | collective-permute-start | bytes 417800 | tf_op jit(solution)/shard_map/ppermute | solution.py:383
  34.4 14.1 %all-to-all-start = ((bf16[8,80,128]{2,1,0:T(8,128)(2,1)}), bf16[8,80,128]{2,1,0:T(8,128)(2,1)S(1)}, u32[]{:S(2)}, u32[]{:S(2)}) async-start(bf16[8,80,128]{2,1,0:T(8,128)(2,1)} %slots.1), calls=%async_computation | async-start | bytes 327680 | tf_op jit(solution)/shard_map/all_to_all | solution.py:464
  39.3 9.1 %collective-permute-start.7 = (bf16[136,128]{1,0:T(8,128)(2,1)S(1)}, bf16[136,128]{1,0:T(8,128)(2,1)S(1)}, u32[]{:S(2)}, u32[]{:S(2)}) collective-permute-start(bf16[136,128]{1,0:T(8,128)(2,1)S(1)} %get-tuple-element.25), channel_id=1, source_target_pairs={{0,1},{1,2},{2,3},{3,4},{4,5},{5,6},{6,7},{7,0},{8,9},{9,10},{10,1... | collective-permute-start | bytes 104456 | tf_op jit(solution)/shard_map/ppermute | solution.py:462

commit v4 on v3

v4 whole, which is shorter than its diff:
```python
import functools

import jax
import jax.numpy as jnp
from jax import lax
from jax.experimental import pallas as pl
from jax.experimental.pallas import tpu as pltpu
from jax.sharding import PartitionSpec as P

NPU = 128
BLK = 128
TW = 128
CELL_DEV = 256
NODE_DEV = 1032
RIM = NPU + 1
HEAD = 136
NODE_ROWS = 1168
EXTRA = 16
F32 = jnp.float32
BF16 = jnp.bfloat16
VMEM = pltpu.VMEM
SMEM = pl.BlockSpec(memory_space=pltpu.SMEM)
WHOLE = pl.BlockSpec(memory_space=pltpu.VMEM)
PLACE = pl.BlockSpec(memory_space=pl.ANY)
COPY = pltpu.SemaphoreType.DMA


def call(kernel, name, out_shape, in_specs, out_specs, scratch_shapes=(), aliases=None, work=1_000_000):
    return pl.pallas_call(
        kernel,
        out_shape=out_shape,
        in_specs=in_specs,
        out_specs=out_specs,
        scratch_shapes=list(scratch_shapes),
        input_output_aliases=aliases or {},
        compiler_params=pltpu.CompilerParams(vmem_limit_bytes=24 * 1024 * 1024),
        cost_estimate=pl.CostEstimate(flops=work, bytes_accessed=4_000_000, transcendentals=0),
        name=name,
    )


def window_kernel(sections, paired, delay_ref, source_ref):
    groups, blocks, span, _ = source_ref.shape
    count = span // sections
    piece_rows = count if paired else 128
    padded = -(-blocks // 16) * 16
    delay = delay_ref[...].astype(F32)
    delay = jnp.concatenate([delay, jnp.zeros((padded - blocks, delay.shape[1]), F32)], 0).astype(BF16)
    spread = (padded, blocks * 128)
    spread = lax.broadcasted_iota(jnp.int32, spread, 1) // 128 == lax.broadcasted_iota(jnp.int32, spread, 0)
    spread = jnp.where(spread, 1.0, 0.0).astype(BF16)
    lanes = lax.broadcasted_iota(jnp.int32, (128, 128), 1)
    for piece in range(groups * span // 128):
        columns = lax.dot_general(
            delay[:, piece * 128 : (piece + 1) * 128], spread, (((0,), (0,)), ((), ())), preferred_element_type=F32
        )
        for block in range(blocks):
            source = columns[:, block * 128 : (block + 1) * 128].astype(jnp.int32) + lanes
            for part in range(128 // piece_rows):
                row = piece * 128 + part * piece_rows
                begin = row % span
                if paired:
                    apart = lax.axis_index("sect") ^ (begin // count)
                    begin = pl.multiple_of((apart // 2 + apart % 2 * (sections // 2)) * count, count)
                source_ref[row // span, block, pl.ds(begin, piece_rows), :] = source[
                    part * piece_rows : (part + 1) * piece_rows
                ]


def window_index(sections, groups, paired, delays):
    blocks, observers = delays.shape
    return call(
        functools.partial(window_kernel, sections, paired),
        "windows",
        jax.ShapeDtypeStruct((groups, blocks, observers // groups, 128), jnp.int32),
        [WHOLE],
        WHOLE,
        work=2_000_000_000,
    )(delays)


def column_kernel(sections, count_ref, geometry_ref, owner_ref, panel_ref, slot_ref, ids_ref):
    panels = geometry_ref.shape[1]
    spread = (32, 7 * 128)
    number = lax.broadcasted_iota(jnp.int32, spread, 0)
    spread = (lax.broadcasted_iota(jnp.int32, spread, 1) // 128 == number % 8) & (number < 24)
    spread = jnp.where(spread, 1.0, 0.0).astype(BF16)
    scale = jnp.where(lax.broadcasted_iota(jnp.int32, (8, BLK), 0) < 3, 0.25, 1.0)
    for block in range(panels // BLK):
        values = geometry_ref[:, block * BLK : (block + 1) * BLK]
        values = jnp.concatenate([values, values[:1]], 0) * scale
        high = values.astype(BF16).astype(F32)
        middle = (values - high).astype(BF16).astype(F32)
        parts = jnp.concatenate([high, middle, values - high - middle, jnp.zeros_like(values)], 0).astype(BF16)
        columns = lax.dot_general(parts, spread, (((0,), (0,)), ((), ())), preferred_element_type=F32)
        for part in range(7):
            panel_ref[block, part] = columns[:, part * 128 : (part + 1) * 128]

    cap = slot_ref.shape[0] // sections
    padded = ids_ref.shape[0]
    owner = owner_ref[...]
    dest = owner // CELL_DEV
    lane = lax.broadcasted_iota(jnp.int32, (padded, panels), 1)
    mine = dest == lax.broadcasted_iota(jnp.int32, (padded, panels), 0)
    ones = jnp.where(mine, 1.0, 0.0).astype(BF16)
    square = (128, 128)
    upto = lax.broadcasted_iota(jnp.int32, square, 0) <= lax.broadcasted_iota(jnp.int32, square, 1)
    upto = jnp.where(upto, 1.0, 0.0).astype(BF16)
    every = jnp.ones(square, BF16)
    carry = jnp.zeros((padded, 128), F32)
    counts = []
    for begin in range(0, panels, 128):
        piece = ones[:, begin : begin + 128]
        counts.append(carry + jnp.dot(piece, upto, preferred_element_type=F32))
        carry = carry + jnp.dot(piece, every, preferred_element_type=F32)
    count = jnp.concatenate(counts, 1).astype(jnp.int32)
    before = jnp.sum(jnp.where(mine, count - 1, 0), axis=0, keepdims=True)
    rank = before // 4
    slot = jnp.where(lane[:1] < count_ref[0], dest * cap + rank, -1)
    slot = jnp.broadcast_to(slot, (16, panels)).astype(jnp.int16)
    number = lax.broadcasted_iota(jnp.int16, (16, panels), 0)
    one, zero = jnp.array(1, BF16), jnp.array(0, BF16)
    for row in range(0, slot_ref.shape[0], 16):
        slot_ref[row : row + 16, :] = jnp.where(slot == number + jnp.int16(row), one, zero)

    at_lane = rank + lax.axis_index("sect") * cap % 128 == lax.broadcasted_iota(jnp.int32, (128, panels), 0)
    at_lane = jnp.where(at_lane, 1.0, 0.0).astype(BF16)
    cell = jnp.where(mine & (lane % 4 == 0), owner % CELL_DEV, 0).astype(F32).astype(BF16)
    ids_ref[...] = lax.dot_general(cell, at_lane, (((1,), (1,)), ((), ())), preferred_element_type=F32)


def panel_columns(sections, counts, geometry, owners):
    panels = geometry.shape[1]
    cap = 2 * CELL_DEV // sections
    padded = -(-sections // EXTRA) * EXTRA
    return call(
        functools.partial(column_kernel, sections),
        "columns",
        (
            jax.ShapeDtypeStruct((panels // BLK, 7, BLK, 128), F32),
            jax.ShapeDtypeStruct((sections * cap, panels), BF16),
            jax.ShapeDtypeStruct((padded, 128), F32),
        ),
        [SMEM, WHOLE, WHOLE],
        [WHOLE] * 3,
        work=2_000_000_000,
    )(counts, geometry, owners.reshape(1, panels))


def corner_kernel(count_ref, conn_ref, corner_ref):
    panels = conn_ref.shape[1]
    live = lax.broadcasted_iota(jnp.int32, (16, panels), 1) < count_ref[0]
    corners = [
        jnp.where(live, jnp.broadcast_to(conn_ref[i : i + 1, :], (16, panels)), -1).astype(jnp.int16) for i in range(4)
    ]
    number = lax.broadcasted_iota(jnp.int16, (16, panels), 0)
    share, zero = jnp.array(0.25, BF16), jnp.array(0, BF16)
    for row in range(0, NODE_ROWS, 16):
        node = number + jnp.int16(row)
        total = jnp.where(corners[0] == node, share, zero)
        for corner in corners[1:]:
            total = total + jnp.where(corner == node, share, zero)
        corner_ref[row : row + 16, :] = total


def corner_matrix(counts, connectivity):
    return call(
        corner_kernel,
        "corners",
        jax.ShapeDtypeStruct((NODE_ROWS, connectivity.shape[1]), BF16),
        [SMEM, WHOLE],
        WHOLE,
        work=2_000_000_000,
    )(counts, connectivity)


def first_join_kernel(mine_ref, other_ref, my_points_ref, other_points_ref, chunk_ref, wide_ref):
    count = mine_ref.shape[0]
    chunk_ref[:count, :] = mine_ref[...]
    chunk_ref[count : 2 * count, :] = other_ref[...]
    wide_ref[...] = jnp.zeros_like(wide_ref)
    wide_ref[:3, :count] = other_points_ref[...].astype(F32)
    moved = pltpu.roll(wide_ref[...], count, 1)
    wide_ref[:3, :count] = my_points_ref[...].astype(F32)
    wide_ref[3:, :count] = jnp.zeros((EXTRA - 3, count), F32)
    chunk_ref[2 * count :, :] = (moved + wide_ref[...]).astype(BF16)


def join_kernel(mine_ref, other_ref, chunk_ref):
    span = mine_ref.shape[0] - EXTRA
    chunk_ref[:span, :] = mine_ref[:span, :]
    chunk_ref[span : 2 * span, :] = other_ref[:span, :]
    moved = pltpu.roll(other_ref[span:, :].astype(F32), span, 1)
    chunk_ref[2 * span :, :] = (mine_ref[span:, :].astype(F32) + moved).astype(BF16)


def sources_kernel(offsets, first, last, count_ref, *refs):
    refs = list(refs)

    def take(number):
        taken = refs[:number]
        del refs[:number]
        return taken

    parts = len(offsets)
    chunks = take(parts)
    source_ref, panel_ref = take(2)
    if last:
        thick_in, slot_ref, ids_ref, pair_ref, window_ref, message_ref, thick_ref = take(7)
        low_ref, high_ref, mass_ref = take(3)
    else:
        loading_in, thick_in = (None, None) if first else take(2)
        loading_ref, thick_ref = take(2)
        low_ref, high_ref, mass_ref, pair_ref, window_ref = take(5)

    blocks, span = source_ref.shape[1:3]
    observers = parts * span
    points = []
    for number, chunk in enumerate(chunks):
        low_ref[number * span : (number + 1) * span, :] = chunk[:span, :128].astype(F32)
        high_ref[number * span : (number + 1) * span, :] = chunk[:span, 128:].astype(F32)
        points.append(chunk[span : span + EXTRA, :].astype(F32) * 0.25)

    lanes = lax.broadcasted_iota(jnp.int32, (128, 128), 1)
    for block in range(blocks):
        for number, offset in enumerate(offsets):
            group = lax.axis_index("azim") ^ offset
            for piece in range(span // 128):
                here = number * span + piece * 128
                source = source_ref[group, block, piece * 128 : (piece + 1) * 128, :]
                at = source & 127
                low = jnp.take_along_axis(low_ref[here : here + 128, :], at, axis=1, mode="promise_in_bounds")
                high = jnp.take_along_axis(high_ref[here : here + 128, :], at, axis=1, mode="promise_in_bounds")
                current = jnp.where(source < 128, low, high)
                following = pltpu.roll(jnp.where(lanes == 0, high, current).astype(BF16), 127, 1)
                current = current.astype(BF16)
                window_ref[block, here : here + 128, :] = current
                window_ref[block, observers + here : observers + here + 128, :] = following - current

                at_x, at_y, at_z = (points[number][i : i + 1, piece * 128 : piece * 128 + 128] for i in range(3))
                for strip in range(BLK // 16):
                    rows = slice(strip * 16, strip * 16 + 16)
                    delta_x = at_x - panel_ref[block, 0, rows, :]
                    delta_y = at_y - panel_ref[block, 1, rows, :]
                    delta_z = at_z - panel_ref[block, 2, rows, :]
                    inverse = lax.rsqrt(delta_x * delta_x + delta_y * delta_y + delta_z * delta_z)
                    flux = (
                        panel_ref[block, 3, rows, :] * delta_x
                        + panel_ref[block, 4, rows, :] * delta_y
                        + panel_ref[block, 5, rows, :] * delta_z
                    )
                    far = flux * inverse * inverse
                    pair_ref[block, rows, here : here + 128] = (far * inverse).astype(BF16)
                    pair_ref[block, rows, observers + here : observers + here + 128] = far.astype(BF16)
                    mass_ref[block, rows, here : here + 128] = (panel_ref[block, 6, rows, :] * inverse).astype(BF16)
        rows = slice(block * BLK, (block + 1) * BLK)
        thick = jnp.dot(mass_ref[block], window_ref[block, observers:, :], preferred_element_type=F32)
        if not first:
            thick = thick + thick_in[rows, :]
        if last:
            alive = block * BLK + lax.broadcasted_iota(jnp.int32, (BLK, TW), 0) < count_ref[0]
            thick_ref[rows, :] = jnp.where(alive, thick, 0.0).astype(BF16)
            continue
        thick_ref[rows, :] = thick
        loading = jnp.dot(pair_ref[block], window_ref[block], preferred_element_type=F32)
        loading_ref[rows, :] = loading if first else loading + loading_in[rows, :]

    if last:
        sections = message_ref.shape[0]
        cap = slot_ref.shape[0] // sections
        slots = jnp.dot(slot_ref[...], thick_ref[...], preferred_element_type=F32).astype(BF16)
        for section in range(sections):
            message_ref[section, :cap, :] = slots[section * cap : (section + 1) * cap]
            ids = jnp.broadcast_to(ids_ref[section : section + 1, :], (EXTRA, 128))
            message_ref[section, cap:, :] = ids.astype(BF16)


def sources(offsets, counts, chunks, source, panel_values, sums=(), slots=None, sections=None):
    blocks, span = source.shape[1:3]
    panels = panel_values.shape[0] * BLK
    observers = len(offsets) * span
    last = slots is not None
    operands = [counts, *chunks, source, panel_values, *sums]
    scratch = [
        VMEM((observers, 128), F32),
        VMEM((observers, 128), F32),
        VMEM((blocks, BLK, observers), BF16),
    ]
    pair, window = (blocks, BLK, 2 * observers), (blocks, 2 * observers, TW)
    aliases = {}
    if last:
        operands += slots
        cap = 2 * CELL_DEV // sections
        out_shape = [
            jax.ShapeDtypeStruct(pair, BF16),
            jax.ShapeDtypeStruct(window, BF16),
            jax.ShapeDtypeStruct((sections, cap + EXTRA, TW), BF16),
        ]
        scratch = [VMEM((panels, TW), BF16)] + scratch
    else:
        out_shape = [jax.ShapeDtypeStruct((panels, TW), F32)] * 2
        scratch += [VMEM(pair, BF16), VMEM(window, BF16)]
        if sums:
            aliases = {len(operands) - 2: 0, len(operands) - 1: 1}
    return call(
        functools.partial(sources_kernel, offsets, not sums, last),
        "sources",
        out_shape,
        [SMEM] + [WHOLE] * (len(operands) - 1),
        [WHOLE] * len(out_shape),
        scratch,
        aliases,
        work=3_000_000_000,
    )(*operands)


def loading_kernel(count_ref, pair_ref, window_ref, sum_ref, corner_ref, loading_ref, rim_ref):
    for block in range(pair_ref.shape[0]):
        rows = slice(block * BLK, (block + 1) * BLK)
        loading = sum_ref[rows, :] + jnp.dot(pair_ref[block], window_ref[block], preferred_element_type=F32)
        alive = block * BLK + lax.broadcasted_iota(jnp.int32, (BLK, TW), 0) < count_ref[0]
        loading_ref[rows, :] = jnp.where(alive, loading, 0.0).astype(BF16)
    rim = jnp.dot(corner_ref[NODE_DEV - 8 :, :], loading_ref[...], preferred_element_type=F32)
    rim_ref[...] = rim[8:].astype(BF16)


def loading_sums(counts, pair, window, sums, corners):
    panels = sums.shape[0]
    return call(
        loading_kernel,
        "loading",
        (jax.ShapeDtypeStruct((panels, TW), BF16), jax.ShapeDtypeStruct((HEAD, TW), BF16)),
        [SMEM] + [WHOLE] * 4,
        [WHOLE] * 2,
        work=2_000_000_000,
    )(counts, pair, window, sums, corners)


def node_kernel(corner_ref, loading_ref, node_ref, head_ref):
    nodes = jnp.dot(corner_ref[: NODE_DEV + 8, :], loading_ref[...], preferred_element_type=F32)
    head_ref[...] = nodes[:HEAD]
    node_ref[...] = nodes[:NODE_DEV]


def node_sums(corners, loading):
    return call(
        node_kernel,
        "nodes",
        (jax.ShapeDtypeStruct((NODE_DEV, TW), F32), jax.ShapeDtypeStruct((HEAD, TW), F32)),
        [WHOLE] * 2,
        [WHOLE] * 2,
        work=2_000_000_000,
    )(corners, loading)


def finish_kernel(message_ref, rim_ref, head_ref, _, node_ref, cell_ref, rows_ref, top_ref, total_ref, sems):
    sections = message_ref.shape[0]
    cap = message_ref.shape[1] - EXTRA
    per = 128 // cap
    top_ref[...] = head_ref[...] + rim_ref[...].astype(F32)
    top_copy = pltpu.make_async_copy(top_ref, node_ref.at[pl.ds(0, HEAD), :], sems.at[0])
    top_copy.start()
    total = jnp.zeros((CELL_DEV, TW), F32)
    cell = lax.broadcasted_iota(jnp.int32, (CELL_DEV, 128), 0).astype(F32)
    for group in range(sections // per):
        ids = jnp.zeros((EXTRA, 128), F32)
        for inner in range(per):
            section = group * per + inner
            ids = ids + message_ref[section, cap:, :].astype(F32)
            rows_ref[section * cap : (section + 1) * cap, :] = message_ref[section, :cap, :]
        match = jnp.where(ids[:1] == cell, 1.0, 0.0).astype(BF16)
        total = total + jnp.dot(match, rows_ref[group * 128 : (group + 1) * 128, :], preferred_element_type=F32)
    total_ref[...] = total
    cell_copy = pltpu.make_async_copy(total_ref, cell_ref, sems.at[1])
    cell_copy.start()
    top_copy.wait()
    cell_copy.wait()


def finish(message, rim, head, nodes):
    sections = message.shape[0]
    cap = message.shape[1] - EXTRA
    return call(
        finish_kernel,
        "finish",
        (
            jax.ShapeDtypeStruct((NODE_DEV, TW), F32),
            jax.ShapeDtypeStruct((CELL_DEV, TW), F32),
        ),
        [WHOLE] * 3 + [PLACE],
        [PLACE] * 2,
        [VMEM((sections * cap, TW), BF16), VMEM((HEAD, TW), F32), VMEM((CELL_DEV, TW), F32), COPY((2,))],
        {3: 0},
    )(message, rim, head, nodes)


def swapped(array, axis, bit):
    peers = lax.axis_size(axis)
    return lax.ppermute(array, axis, [(i, i ^ bit) for i in range(peers)])


def joined(mine, other):
    span = mine.shape[0] - EXTRA
    shape = jax.ShapeDtypeStruct((2 * span + EXTRA, mine.shape[1]), BF16)
    return call(join_kernel, "join", shape, [WHOLE] * 2, WHOLE)(mine, other)


def paired_chunk(signals, xyz, sections, local):
    count, width = signals.shape
    turned = xyz.T
    bit = 2
    other, other_points = swapped(signals, "sect", bit), swapped(turned, "sect", bit)
    shape = jax.ShapeDtypeStruct((2 * count + EXTRA, width), BF16)
    done = [local[0]()]
    chunk = call(first_join_kernel, "pair", shape, [WHOLE] * 4, WHOLE, [VMEM((EXTRA, width), F32)])(
        signals, other, turned, other_points
    )
    for step in range(2, sections.bit_length()):
        bit = bit * 2 if bit * 2 < sections else 1
        other = swapped(chunk, "sect", bit)
        done.append(local[step - 1](chunk) if step <= len(local) else None)
        chunk = joined(chunk, other)
    return chunk, done


def spread_chunk(signals, xyz, sections):
    count, width = signals.shape
    extra = jnp.zeros((EXTRA, width), BF16)
    extra = lax.dynamic_update_slice(extra, xyz.T, (0, lax.axis_index("sect") * count))
    payload = jnp.concatenate([signals, extra], 0)
    everyone = jnp.broadcast_to(payload[None], (sections,) + payload.shape)
    received = lax.all_to_all(everyone, "sect", split_axis=0, concat_axis=0, tiled=True)
    return jnp.concatenate(
        [received[:, :count].reshape(sections * count, -1), received[:, count:].astype(F32).sum(0).astype(BF16)], 0
    )


def per_device(signals, observer_xyz, panel_geometry, delays, counts, connectivity, owners):
    sections = lax.axis_size("sect")
    groups = lax.axis_size("azim")
    paired = sections == 8 and signals.shape[0] % 16 == 0

    def windows():
        return window_index(sections, groups, paired, delays)

    def columns(after=None):
        geometry = panel_geometry
        if after is not None:
            geometry, _ = lax.optimization_barrier((geometry, after))
        return panel_columns(sections, counts, geometry, owners)

    def corners(after=None):
        nodes = connectivity
        if after is not None:
            nodes, _ = lax.optimization_barrier((nodes, after))
        return corner_matrix(counts, nodes)

    if paired:
        chunk, done = paired_chunk(signals, observer_xyz, sections, (windows, columns, corners))
        source, (panel_values, slots, ids), corner_values = done
    else:
        chunk = spread_chunk(signals, observer_xyz, sections)
        source, (panel_values, slots, ids), corner_values = windows(), columns(), corners()
    chunks = {0: chunk}
    bit = groups // 2
    while bit:
        for offset in list(chunks):
            chunks[offset ^ bit] = swapped(chunks[offset], "azim", bit)
        bit //= 2
    sums = ()
    for offsets in ([0], [1]):
        sums = sources(offsets, counts, [chunks[o] for o in offsets], source, panel_values, sums)
    offsets = [o for o in chunks if o > 1]
    pair, window, message = sources(
        offsets, counts, [chunks[o] for o in offsets], source, panel_values, sums[1:], [slots, ids], sections
    )
    message = lax.all_to_all(message, "sect", split_axis=0, concat_axis=0, tiled=True)
    loading, rim = loading_sums(counts, pair, window, sums[0], corner_values)
    rim = lax.ppermute(rim, "sect", [(i, (i + 1) % sections) for i in range(sections)])
    nodes, head = node_sums(corner_values, loading)
    return finish(message, rim, head, nodes)


def solution(mesh):
    in_specs = (
        P(("azim", "sect"), None),
        P(("azim", "sect"), None),
        P(None, ("azim", "sect")),
        P(("azim", "sect"), None),
        P(("azim", "sect")),
        P(None, ("azim", "sect")),
        P(("azim", "sect")),
    )
    out_specs = (P(("azim", "sect"), None), P(("azim", "sect"), None))
    return jax.shard_map(
        per_device, mesh=mesh, in_specs=in_specs, out_specs=out_specs, check_vma=False
    )
```

time: 49.6 us -> 50.3 us (1.014)
  Pallas kernels: 23 us -> 16 us
  local copies, waits for them, and re-layouts: 0.78 us -> 6.59 us
  waiting for transfers between devices: 7.85 us -> 9.98 us
    ppermute x7, waiting for transfers between devices: 0.77 us -> 6.88 us  [swapped(): return lax.ppermute(array, axis, [(i, i ^ bit) for i in range(peers)])]
    unnamed x12 -> x20, local copies, waits for them, and re-layouts: 0.78 us -> 6.59 us
    ppermute x1, waiting for transfers between devices: 7.08 us -> 3.1 us  [per_device(): lax.ppermute(rim, 'sect', [(i, (i + 1) % sections) for i in range(section...]
    pallas_call x1, Pallas kernels: 3.26 us -> 1.11 us  [panel_columns(): call(functools.partial(column_kernel, sections), 'columns', (jax.ShapeDty...]
    pallas_call x1, Pallas kernels: 3.03 us -> 0.96 us  [corner_matrix(): call(corner_kernel, 'corners', jax.ShapeDtypeStruct((NODE_ROWS, connectiv...]
    pallas_call x1, Pallas kernels: 2.38 us -> 0.74 us  [window_index(): call(functools.partial(window_kernel, sections, paired), 'windows', jax.S...]
    pallas_call x4 -> x5, Pallas kernels: 13.3 us -> 12.1 us  [the longest x3 9.73 us: sources(): call(functools.partial(sources_kernel, offsets, not sums, last), 'sources...]
  transfers between devices with their start and end apart: 9 -> 9, of which waited for: 2 -> 5; matrix products, arithmetic and copies ran while one was open for 0% -> 0% of each run, Pallas kernels for 29% -> 19%
where the time goes in v4:
time: 50.3 us; the launch traced here: 50 us
  starting transfers between devices  16 us (32%)
  Pallas kernels  16 us (32%)
  waiting for transfers between devices  9.98 us (20%)
  local copies, waits for them, and re-layouts  6.59 us (13%)
  between operations  1.37 us (3%)
    pallas_call x3, Pallas kernels, sources(): call(functools.partial(sources_kernel, offsets, not sums, last), 'sources...  9.73 us
    ppermute x7, starting transfers between devices, swapped(): return lax.ppermute(array, axis, [(i, i ^ bit) for i in range(peers)])  9.28 us
    ppermute x7, waiting for transfers between devices, swapped(): return lax.ppermute(array, axis, [(i, i ^ bit) for i in range(peers)])  6.88 us
    unnamed x20, local copies, waits for them, and re-layouts  6.59 us
    all_to_all x1, starting transfers between devices, per_device(): lax.all_to_all(message, 'sect', split_axis=0, concat_axis=0, tiled=True)  4.67 us
    ppermute x1, waiting for transfers between devices, per_device(): lax.ppermute(rim, 'sect', [(i, (i + 1) % sections) for i in range(section...  3.1 us
    ppermute x1, starting transfers between devices, per_device(): lax.ppermute(rim, 'sect', [(i, (i + 1) % sections) for i in range(section...  2.07 us
    pallas_call x1, Pallas kernels, node_sums(): call(node_kernel, 'nodes', (jax.ShapeDtypeStruct((NODE_DEV, TW), F32), ja...  1.51 us
  transfers between devices with their start and end apart: 9, of which 5 were waited for; matrix products, arithmetic and copies ran while one was open for 0% of the time, Pallas kernels for 19%

profile of v4, /device:TPU:0, one launch (start us, length us, event | category | flops | bytes accessed | tf_op | source)
XLA Modules:
  0.0 50.0 jit_solution(9139344743839790855)
XLA Ops:
  0.7 3.1 %collective-permute-start.1 = (bf16[3,32]{1,0:T(4,128)(2,1)}, bf16[3,32]{1,0:T(4,128)(2,1)S(1)}, u32[]{:S(2)}, u32[]{:S(2)}) collective-permute-start(bf16[3,32]{1,0:T(4,128)(2,1)} %bitcast.2), channel_id=1, source_target_pairs={{0,2},{1,3},{2,0},{3,1},{4,6},{5,7},{6,4},{7,5},{8,10},{9,11},{10,... | collective-permute-start | bytes 584 | tf_op jit(solution)/shard_map/ppermute | solution.py:399
  3.8 0.8 %copy-done.2 = s32[8,1024]{1,0:T(8,128)S(1)} copy-done((s32[8,1024]{1,0:T(8,128)S(1)}, s32[8,1024]{1,0:T(8,128)}, u32[]{:S(2)}) %copy-start.2) | copy-done | bytes 32792
  6.0 1.7 %collective-permute-done.other_ref = bf16[32,256]{1,0:T(8,128)(2,1)S(1)} collective-permute-done((bf16[32,256]{1,0:T(8,128)(2,1)}, bf16[32,256]{1,0:T(8,128)(2,1)S(1)}, u32[]{:S(2)}, u32[]{:S(2)}) %collective-permute-start) | collective-permute-done | bytes 16416 | tf_op jit(solution)/shard_map/ppermute | solution.py:399
  7.8 2.6 %collective-permute-start.2 = (bf16[80,256]{1,0:T(8,128)(2,1)S(1)}, bf16[80,256]{1,0:T(8,128)(2,1)S(1)}, u32[]{:S(2)}, u32[]{:S(2)}) collective-permute-start(bf16[80,256]{1,0:T(8,128)(2,1)S(1)} %pair.1.mine_ref), channel_id=1, source_target_pairs={{0,4},{1,5},{2,6},{3,7},{4,0},{5,1},{6,2},{7,3},{8,12},{9,13},{10,... | collective-permute-start | bytes 122888 | tf_op jit(solution)/shard_map/ppermute | solution.py:399
  10.4 1.1 %columns.1 = (f32[8,7,128,128]{3,2,1,0:T(8,128)S(1)}, bf16[512,1024]{1,0:T(8,128)(2,1)S(1)}, f32[16,128]{1,0:T(8,128)S(1)}) custom-call(s32[1]{0:T(128)S(6)} %copy.15.count_ref, f32[7,1024]{1,0:T(8,128)S(1)} %copy-done.3, s32[1,1024]{1,0:T(1,128)S(1)} %bitcast.4), custom_call_target="tpu_custom_call" | custom-call | flops 2000000000 | bytes 4000000 | tf_op jit(solution)/shard_map/columns/pallas_call | solution.py:136
  11.5 1.3 %collective-permute-done.2.other_ref = bf16[80,256]{1,0:T(8,128)(2,1)S(1)} collective-permute-done((bf16[80,256]{1,0:T(8,128)(2,1)S(1)}, bf16[80,256]{1,0:T(8,128)(2,1)S(1)}, u32[]{:S(2)}, u32[]{:S(2)}) %collective-permute-start.2) | collective-permute-done | bytes 40992 | tf_op jit(solution)/shard_map/ppermute | solution.py:399
  12.9 1.7 %collective-permute-start.3 = (bf16[144,256]{1,0:T(8,128)(2,1)S(1)}, bf16[144,256]{1,0:T(8,128)(2,1)S(1)}, u32[]{:S(2)}, u32[]{:S(2)}) collective-permute-start(bf16[144,256]{1,0:T(8,128)(2,1)S(1)} %join.2.mine_ref), channel_id=1, source_target_pairs={{0,1},{1,0},{2,3},{3,2},{4,5},{5,4},{6,7},{7,6},{8,9},{9,8},{10,11... | collective-permute-start | bytes 221192 | tf_op jit(solution)/shard_map/ppermute | solution.py:399
  14.6 1.0 %corners.1.corner_ref = bf16[1168,1024]{1,0:T(8,128)(2,1)S(1)} custom-call(s32[1]{0:T(128)S(6)} %copy.15.count_ref, s32[4,1024]{1,0:T(4,128)S(1)} %copy-done.4), custom_call_target="tpu_custom_call" | custom-call | flops 2000000000 | bytes 4000000 | tf_op jit(solution)/shard_map/corners/pallas_call | solution.py:167
  15.6 1.7 %collective-permute-done.3.other_ref = bf16[144,256]{1,0:T(8,128)(2,1)S(1)} collective-permute-done((bf16[144,256]{1,0:T(8,128)(2,1)S(1)}, bf16[144,256]{1,0:T(8,128)(2,1)S(1)}, u32[]{:S(2)}, u32[]{:S(2)}) %collective-permute-start.3) | collective-permute-done | bytes 73760 | tf_op jit(solution)/shard_map/ppermute | solution.py:399
  17.4 1.7 %collective-permute-start.4 = (bf16[272,256]{1,0:T(8,128)(2,1)S(1)}, bf16[272,256]{1,0:T(8,128)(2,1)S(1)}, u32[]{:S(2)}, u32[]{:S(2)}) collective-permute-start(bf16[272,256]{1,0:T(8,128)(2,1)S(1)} %join.3.refs_0_), channel_id=1, source_target_pairs={{0,16},{8,24},{16,0},{24,8},{1,17},{9,25},{17,1},{25,9},{2,18},{10... | collective-permute-start | bytes 417800 | tf_op jit(solution)/shard_map/ppermute | solution.py:399
  19.1 2.2 %sources.3 = (f32[1024,128]{1,0:T(8,128)S(1)}, f32[1024,128]{1,0:T(8,128)S(1)}) custom-call(s32[1]{0:T(128)S(6)} %copy.15.count_ref, bf16[272,256]{1,0:T(8,128)(2,1)S(1)} %join.3.refs_0_, s32[4,8,256,128]{3,2,1,0:T(8,128)S(1)} %windows.1.refs_1_.refs_2_, f32[8,7,128,128]{3,2,1,0:T(8,128)S(1)} %get-tuple-element.19.refs_2_.refs_3_), custom_call_target="tpu_custom_call" | custom-call | flops 3000000000 | bytes 4000000 | tf_op jit(solution)/shard_map/sources/pallas_call | solution.py:305
  21.3 2.1 %collective-permute-done.4.refs_0_ = bf16[272,256]{1,0:T(8,128)(2,1)S(1)} collective-permute-done((bf16[272,256]{1,0:T(8,128)(2,1)S(1)}, bf16[272,256]{1,0:T(8,128)(2,1)S(1)}, u32[]{:S(2)}, u32[]{:S(2)}) %collective-permute-start.4) | collective-permute-done | bytes 139296 | tf_op jit(solution)/shard_map/ppermute | solution.py:399
  23.5 2.3 %sources.4 = (f32[1024,128]{1,0:T(8,128)S(1)}, f32[1024,128]{1,0:T(8,128)S(1)}) custom-call(s32[1]{0:T(128)S(6)} %copy.15.count_ref, bf16[272,256]{1,0:T(8,128)(2,1)S(1)} %collective-permute-done.6.refs_0_, s32[4,8,256,128]{3,2,1,0:T(8,128)S(1)} %windows.1.refs_1_.refs_2_, ...), custom_call_target="tpu_custom_call", output_to_operand_aliasing={{0}: (4, {}), {1}: (5, {})} | custom-call | flops 3000000000 | bytes 4000000 | tf_op jit(solution)/shard_map/sources/pallas_call | solution.py:305
  25.8 5.2 %sources.5 = (bf16[8,128,1024]{2,1,0:T(8,128)(2,1)S(1)}, bf16[8,1024,128]{2,1,0:T(8,128)(2,1)S(1)}, bf16[8,80,128]{2,1,0:T(8,128)(2,1)}) custom-call(s32[1]{0:T(128)S(6)} %copy.15.count_ref, bf16[272,256]{1,0:T(8,128)(2,1)S(1)} %collective-permute-done.4.refs_0_, bf16[272,256]{1,0:T(8,128)(2,1)S(1)} %collective-permute-done.5.refs_1_, ...), custom_call_target="tpu_custom_call" | custom-call | flops 3000000000 | bytes 4000000 | tf_op jit(solution)/shard_map/sources/pallas_call | solution.py:305
  31.0 1.3 %copy-done.6 = bf16[8,128,1024]{2,1,0:T(8,128)(2,1)} copy-done((bf16[8,128,1024]{2,1,0:T(8,128)(2,1)}, bf16[8,128,1024]{2,1,0:T(8,128)(2,1)S(1)}, u32[]{:S(2)}) %copy-start.6) | copy-done | bytes 2097176
  32.3 1.3 %copy-done.8 = bf16[8,1024,128]{2,1,0:T(8,128)(2,1)} copy-done((bf16[8,1024,128]{2,1,0:T(8,128)(2,1)}, bf16[8,1024,128]{2,1,0:T(8,128)(2,1)S(1)}, u32[]{:S(2)}) %copy-start.8) | copy-done | bytes 2097176
  33.6 4.7 %all-to-all-start = ((bf16[8,80,128]{2,1,0:T(8,128)(2,1)}), bf16[8,80,128]{2,1,0:T(8,128)(2,1)S(1)}, u32[]{:S(2)}, u32[]{:S(2)}) async-start(bf16[8,80,128]{2,1,0:T(8,128)(2,1)} %get-tuple-element.25), calls=%async_computation | async-start | bytes 327680 | tf_op jit(solution)/shard_map/all_to_all | solution.py:477
  38.3 1.6 %copy-done.7 = bf16[8,128,1024]{2,1,0:T(8,128)(2,1)S(1)} copy-done((bf16[8,128,1024]{2,1,0:T(8,128)(2,1)S(1)}, bf16[8,128,1024]{2,1,0:T(8,128)(2,1)}, u32[]{:S(2)}) %copy-start.7) | copy-done | bytes 2097176
  39.9 1.6 %copy-done.9 = bf16[8,1024,128]{2,1,0:T(8,128)(2,1)S(1)} copy-done((bf16[8,1024,128]{2,1,0:T(8,128)(2,1)S(1)}, bf16[8,1024,128]{2,1,0:T(8,128)(2,1)}, u32[]{:S(2)}) %copy-start.9) | copy-done | bytes 2097176
  41.5 0.9 %loading.1 = (bf16[1024,128]{1,0:T(8,128)(2,1)S(1)}, bf16[136,128]{1,0:T(8,128)(2,1)S(1)}) custom-call(s32[1]{0:T(128)S(6)} %copy.15.count_ref, bf16[8,128,1024]{2,1,0:T(8,128)(2,1)S(1)} %copy-done.7, bf16[8,1024,128]{2,1,0:T(8,128)(2,1)S(1)} %copy-done.9, f32[1024,128]{1,0:T(8,128)S(1)} %get-tuple-element.28.sum_ref, bf16[1168,1024]{1,0:T(8,128)(2,1)S(1)} %corners.1.corner_ref), custom_call_target="tpu_custom_call" | custom-call | flops 2000000000 | bytes 4000000 | tf_op jit(solution)/shard_map/loading/pallas_call | solution.py:329
  42.4 2.1 %collective-permute-start.7 = (bf16[136,128]{1,0:T(8,128)(2,1)S(1)}, bf16[136,128]{1,0:T(8,128)(2,1)S(1)}, u32[]{:S(2)}, u32[]{:S(2)}) collective-permute-start(bf16[136,128]{1,0:T(8,128)(2,1)S(1)} %get-tuple-element.30), channel_id=1, source_target_pairs={{0,1},{1,2},{2,3},{3,4},{4,5},{5,6},{6,7},{7,0},{8,9},{9,10},{10,1... | collective-permute-start | bytes 104456 | tf_op jit(solution)/shard_map/ppermute | solution.py:479
  44.4 1.5 %nodes.1 = (f32[1032,128]{1,0:T(8,128)}, f32[136,128]{1,0:T(8,128)S(1)}) custom-call(bf16[1168,1024]{1,0:T(8,128)(2,1)S(1)} %corners.1.corner_ref, bf16[1024,128]{1,0:T(8,128)(2,1)S(1)} %get-tuple-element.31.loading_ref), custom_call_target="tpu_custom_call" | custom-call | flops 2000000000 | bytes 4000000 | tf_op jit(solution)/shard_map/nodes/pallas_call | solution.py:346
  45.9 3.1 %collective-permute-done.7.rim_ref = bf16[136,128]{1,0:T(8,128)(2,1)S(1)} collective-permute-done((bf16[136,128]{1,0:T(8,128)(2,1)S(1)}, bf16[136,128]{1,0:T(8,128)(2,1)S(1)}, u32[]{:S(2)}, u32[]{:S(2)}) %collective-permute-start.7) | collective-permute-done | bytes 34848 | tf_op jit(solution)/shard_map/ppermute | solution.py:479
  49.1 0.9 %finish.1 = (f32[1032,128]{1,0:T(8,128)}, f32[256,128]{1,0:T(8,128)}) custom-call(bf16[8,80,128]{2,1,0:T(8,128)(2,1)S(1)} %all-to-all-done.message_ref, bf16[136,128]{1,0:T(8,128)(2,1)S(1)} %collective-permute-done.7.rim_ref, f32[136,128]{1,0:T(8,128)S(1)} %get-tuple-element.32.head_ref, ...), custom_call_target="tpu_custom_call", output_to_operand_aliasing={{0}: (3, {})} | custom-call | flops 1000000 | bytes 4000000 | tf_op jit(solution)/shard_map/finish/pallas_call | solution.py:383
  (26 shorter events, 1.1 us)
Async XLA Ops:
  0.6 7.1 %copy-start = (bf16[32,256]{1,0:T(8,128)(2,1)S(1)}, bf16[32,256]{1,0:T(8,128)(2,1)}, u32[]{:S(2)}) copy-start(bf16[32,256]{1,0:T(8,128)(2,1)} %mine_ref.1) | copy-start | bytes 49156
  0.6 7.1 %copy-start.1 = (bf16[32,3]{0,1:T(4,128)(2,1)S(1)}, bf16[32,3]{0,1:T(4,128)(2,1)}, u32[]{:S(2)}) copy-start(bf16[32,3]{0,1:T(4,128)(2,1)} %param.8) | copy-start | bytes 580
  0.7 5.3 %collective-permute-start.1 = (bf16[3,32]{1,0:T(4,128)(2,1)}, bf16[3,32]{1,0:T(4,128)(2,1)S(1)}, u32[]{:S(2)}, u32[]{:S(2)}) collective-permute-start(bf16[3,32]{1,0:T(4,128)(2,1)} %bitcast.2), channel_id=1, source_target_pairs={{0,2},{1,3},{2,0},{3,1},{4,6},{5,7},{6,4},{7,5},{8,10},{9,11},{10,... | collective-permute-start | bytes 584 | tf_op jit(solution)/shard_map/ppermute | solution.py:399
  3.7 3.9 %collective-permute-start = (bf16[32,256]{1,0:T(8,128)(2,1)}, bf16[32,256]{1,0:T(8,128)(2,1)S(1)}, u32[]{:S(2)}, u32[]{:S(2)}) collective-permute-start(bf16[32,256]{1,0:T(8,128)(2,1)} %mine_ref.1), channel_id=1, source_target_pairs={{0,2},{1,3},{2,0},{3,1},{4,6},{5,7},{6,4},{7,5},{8,10},{9,11},{10,... | collective-permute-start | bytes 49160 | tf_op jit(solution)/shard_map/ppermute | solution.py:399
  3.8 0.8 %copy-start.2 = (s32[8,1024]{1,0:T(8,128)S(1)}, s32[8,1024]{1,0:T(8,128)}, u32[]{:S(2)}) copy-start(s32[8,1024]{1,0:T(8,128)} %delay_ref.1) | copy-start | bytes 98308
  4.6 5.8 %copy-start.3 = (f32[7,1024]{1,0:T(8,128)S(1)}, f32[7,1024]{1,0:T(8,128)}, u32[]{:S(2)}) copy-start(f32[7,1024]{1,0:T(8,128)} %geometry_ref) | copy-start | bytes 86020
  4.6 5.8 %copy-start.5 = (s32[1024]{0:T(1024)S(1)}, s32[1024]{0:T(1024)}, u32[]{:S(2)}) copy-start(s32[1024]{0:T(1024)} %param.13) | copy-start | bytes 12292
  7.8 5.1 %collective-permute-start.2 = (bf16[80,256]{1,0:T(8,128)(2,1)S(1)}, bf16[80,256]{1,0:T(8,128)(2,1)S(1)}, u32[]{:S(2)}, u32[]{:S(2)}) collective-permute-start(bf16[80,256]{1,0:T(8,128)(2,1)S(1)} %pair.1.mine_ref), channel_id=1, source_target_pairs={{0,4},{1,5},{2,6},{3,7},{4,0},{5,1},{6,2},{7,3},{8,12},{9,13},{10,... | collective-permute-start | bytes 122888 | tf_op jit(solution)/shard_map/ppermute | solution.py:399
  10.4 4.2 %copy-start.4 = (s32[4,1024]{1,0:T(4,128)S(1)}, s32[4,1024]{1,0:T(4,128)}, u32[]{:S(2)}) copy-start(s32[4,1024]{1,0:T(4,128)} %conn_ref) | copy-start | bytes 49156
  12.9 4.4 %collective-permute-start.3 = (bf16[144,256]{1,0:T(8,128)(2,1)S(1)}, bf16[144,256]{1,0:T(8,128)(2,1)S(1)}, u32[]{:S(2)}, u32[]{:S(2)}) collective-permute-start(bf16[144,256]{1,0:T(8,128)(2,1)S(1)} %join.2.mine_ref), channel_id=1, source_target_pairs={{0,1},{1,0},{2,3},{3,2},{4,5},{5,4},{6,7},{7,6},{8,9},{9,8},{10,11... | collective-permute-start | bytes 221192 | tf_op jit(solution)/shard_map/ppermute | solution.py:399
  17.3 6.2 %collective-permute-start.6 = (bf16[272,256]{1,0:T(8,128)(2,1)S(1)}, bf16[272,256]{1,0:T(8,128)(2,1)S(1)}, u32[]{:S(2)}, u32[]{:S(2)}) collective-permute-start(bf16[272,256]{1,0:T(8,128)(2,1)S(1)} %join.3.refs_0_), channel_id=1, source_target_pairs={{0,8},{8,0},{16,24},{24,16},{1,9},{9,1},{17,25},{25,17},{2,10},{10... | collective-permute-start | bytes 417800 | tf_op jit(solution)/shard_map/ppermute | solution.py:399
  17.4 6.1 %collective-permute-start.4 = (bf16[272,256]{1,0:T(8,128)(2,1)S(1)}, bf16[272,256]{1,0:T(8,128)(2,1)S(1)}, u32[]{:S(2)}, u32[]{:S(2)}) collective-permute-start(bf16[272,256]{1,0:T(8,128)(2,1)S(1)} %join.3.refs_0_), channel_id=1, source_target_pairs={{0,16},{8,24},{16,0},{24,8},{1,17},{9,25},{17,1},{25,9},{2,18},{10... | collective-permute-start | bytes 417800 | tf_op jit(solution)/shard_map/ppermute | solution.py:399
  23.4 2.3 %collective-permute-start.5 = (bf16[272,256]{1,0:T(8,128)(2,1)S(1)}, bf16[272,256]{1,0:T(8,128)(2,1)S(1)}, u32[]{:S(2)}, u32[]{:S(2)}) collective-permute-start(bf16[272,256]{1,0:T(8,128)(2,1)S(1)} %collective-permute-done.4.refs_0_), channel_id=1, source_target_pairs={{0,8},{8,0},{16,24},{24,16},{1,9},{9,1},{17,25},{25,17},{2,10},{10... | collective-permute-start | bytes 417800 | tf_op jit(solution)/shard_map/ppermute | solution.py:399
  31.0 1.3 %copy-start.6 = (bf16[8,128,1024]{2,1,0:T(8,128)(2,1)}, bf16[8,128,1024]{2,1,0:T(8,128)(2,1)S(1)}, u32[]{:S(2)}) copy-start(bf16[8,128,1024]{2,1,0:T(8,128)(2,1)S(1)} %get-tuple-element.26.pair_ref) | copy-start | bytes 6291460
  32.3 1.3 %copy-start.8 = (bf16[8,1024,128]{2,1,0:T(8,128)(2,1)}, bf16[8,1024,128]{2,1,0:T(8,128)(2,1)S(1)}, u32[]{:S(2)}) copy-start(bf16[8,1024,128]{2,1,0:T(8,128)(2,1)S(1)} %get-tuple-element.27.window_ref) | copy-start | bytes 6291460
  33.6 15.4 %all-to-all-start = ((bf16[8,80,128]{2,1,0:T(8,128)(2,1)}), bf16[8,80,128]{2,1,0:T(8,128)(2,1)S(1)}, u32[]{:S(2)}, u32[]{:S(2)}) async-start(bf16[8,80,128]{2,1,0:T(8,128)(2,1)} %get-tuple-element.25), calls=%async_computation | async-start | bytes 327680 | tf_op jit(solution)/shard_map/all_to_all | solution.py:477
  38.3 1.6 %copy-start.7 = (bf16[8,128,1024]{2,1,0:T(8,128)(2,1)S(1)}, bf16[8,128,1024]{2,1,0:T(8,128)(2,1)}, u32[]{:S(2)}) copy-start(bf16[8,128,1024]{2,1,0:T(8,128)(2,1)} %copy-done.6) | copy-start | bytes 6291460
  39.9 1.6 %copy-start.9 = (bf16[8,1024,128]{2,1,0:T(8,128)(2,1)S(1)}, bf16[8,1024,128]{2,1,0:T(8,128)(2,1)}, u32[]{:S(2)}) copy-start(bf16[8,1024,128]{2,1,0:T(8,128)(2,1)} %copy-done.8) | copy-start | bytes 6291460
  42.4 6.7 %collective-permute-start.7 = (bf16[136,128]{1,0:T(8,128)(2,1)S(1)}, bf16[136,128]{1,0:T(8,128)(2,1)S(1)}, u32[]{:S(2)}, u32[]{:S(2)}) collective-permute-start(bf16[136,128]{1,0:T(8,128)(2,1)S(1)} %get-tuple-element.30), channel_id=1, source_target_pairs={{0,1},{1,2},{2,3},{3,4},{4,5},{5,6},{6,7},{7,0},{8,9},{9,10},{10,1... | collective-permute-start | bytes 104456 | tf_op jit(solution)/shard_map/ppermute | solution.py:479

commit v5 on v4

--- a/solution.py
+++ b/solution.py
@@ -174,16 +174,17 @@
     )(counts, connectivity)
 
 
-def first_join_kernel(mine_ref, other_ref, my_points_ref, other_points_ref, chunk_ref, wide_ref):
-    count = mine_ref.shape[0]
-    chunk_ref[:count, :] = mine_ref[...]
-    chunk_ref[count : 2 * count, :] = other_ref[...]
+def first_join_kernel(*refs):
+    *inputs, chunk_ref, wide_ref = refs
+    parts = len(inputs) // 2
+    count = inputs[0].shape[0]
     wide_ref[...] = jnp.zeros_like(wide_ref)
-    wide_ref[:3, :count] = other_points_ref[...].astype(F32)
-    moved = pltpu.roll(wide_ref[...], count, 1)
-    wide_ref[:3, :count] = my_points_ref[...].astype(F32)
-    wide_ref[3:, :count] = jnp.zeros((EXTRA - 3, count), F32)
-    chunk_ref[2 * count :, :] = (moved + wide_ref[...]).astype(BF16)
+    total = jnp.zeros(wide_ref.shape, F32)
+    for part in range(parts):
+        chunk_ref[part * count : (part + 1) * count, :] = inputs[part][...]
+        wide_ref[:3, :count] = inputs[parts + part][...].astype(F32)
+        total = total + (pltpu.roll(wide_ref[...], part * count, 1) if part else wide_ref[...])
+    chunk_ref[parts * count :, :] = total.astype(BF16)
 
 
 def join_kernel(mine_ref, other_ref, chunk_ref):
@@ -194,7 +195,7 @@
     chunk_ref[2 * span :, :] = (mine_ref[span:, :].astype(F32) + moved).astype(BF16)
 
 
-def sources_kernel(offsets, first, last, count_ref, *refs):
+def sources_kernel(places, first, last, count_ref, *refs):
     refs = list(refs)
 
     def take(number):
@@ -202,18 +203,18 @@
         del refs[:number]
         return taken
 
-    parts = len(offsets)
+    parts = len(places)
     chunks = take(parts)
     source_ref, panel_ref = take(2)
     if last:
-        thick_in, slot_ref, ids_ref, pair_ref, window_ref, message_ref, thick_ref = take(7)
-        low_ref, high_ref, mass_ref = take(3)
+        loading_in, thick_in, slot_ref, ids_ref, loading_ref, message_ref, thick_ref = take(7)
     else:
         loading_in, thick_in = (None, None) if first else take(2)
         loading_ref, thick_ref = take(2)
-        low_ref, high_ref, mass_ref, pair_ref, window_ref = take(5)
-
-    blocks, span = source_ref.shape[1:3]
+    low_ref, high_ref, mass_ref, pair_ref, window_ref = take(5)
+
+    blocks = source_ref.shape[1]
+    span = chunks[0].shape[0] - EXTRA
     observers = parts * span
     points = []
     for number, chunk in enumerate(chunks):
@@ -223,11 +224,11 @@
 
     lanes = lax.broadcasted_iota(jnp.int32, (128, 128), 1)
     for block in range(blocks):
-        for number, offset in enumerate(offsets):
+        for number, (offset, begin) in enumerate(places):
             group = lax.axis_index("azim") ^ offset
             for piece in range(span // 128):
                 here = number * span + piece * 128
-                source = source_ref[group, block, piece * 128 : (piece + 1) * 128, :]
+                source = source_ref[group, block, begin + piece * 128 : begin + (piece + 1) * 128, :]
                 at = source & 127
                 low = jnp.take_along_axis(low_ref[here : here + 128, :], at, axis=1, mode="promise_in_bounds")
                 high = jnp.take_along_axis(high_ref[here : here + 128, :], at, axis=1, mode="promise_in_bounds")
@@ -255,15 +256,16 @@
                     mass_ref[block, rows, here : here + 128] = (panel_ref[block, 6, rows, :] * inverse).astype(BF16)
         rows = slice(block * BLK, (block + 1) * BLK)
         thick = jnp.dot(mass_ref[block], window_ref[block, observers:, :], preferred_element_type=F32)
+        loading = jnp.dot(pair_ref[block], window_ref[block], preferred_element_type=F32)
         if not first:
             thick = thick + thick_in[rows, :]
+            loading = loading + loading_in[rows, :]
         if last:
             alive = block * BLK + lax.broadcasted_iota(jnp.int32, (BLK, TW), 0) < count_ref[0]
-            thick_ref[rows, :] = jnp.where(alive, thick, 0.0).astype(BF16)
-            continue
+            thick = jnp.where(alive, thick, 0.0).astype(BF16)
+            loading = jnp.where(alive, loading, 0.0).astype(BF16)
         thick_ref[rows, :] = thick
-        loading = jnp.dot(pair_ref[block], window_ref[block], preferred_element_type=F32)
-        loading_ref[rows, :] = loading if first else loading + loading_in[rows, :]
+        loading_ref[rows, :] = loading
 
     if last:
         sections = message_ref.shape[0]
@@ -275,35 +277,34 @@
             message_ref[section, cap:, :] = ids.astype(BF16)
 
 
-def sources(offsets, counts, chunks, source, panel_values, sums=(), slots=None, sections=None):
-    blocks, span = source.shape[1:3]
+def sources(places, counts, chunks, source, panel_values, sums=(), slots=None, sections=None):
+    blocks = source.shape[1]
     panels = panel_values.shape[0] * BLK
-    observers = len(offsets) * span
+    observers = len(places) * (chunks[0].shape[0] - EXTRA)
     last = slots is not None
     operands = [counts, *chunks, source, panel_values, *sums]
     scratch = [
         VMEM((observers, 128), F32),
         VMEM((observers, 128), F32),
         VMEM((blocks, BLK, observers), BF16),
+        VMEM((blocks, BLK, 2 * observers), BF16),
+        VMEM((blocks, 2 * observers, TW), BF16),
     ]
-    pair, window = (blocks, BLK, 2 * observers), (blocks, 2 * observers, TW)
     aliases = {}
     if last:
         operands += slots
         cap = 2 * CELL_DEV // sections
         out_shape = [
-            jax.ShapeDtypeStruct(pair, BF16),
-            jax.ShapeDtypeStruct(window, BF16),
+            jax.ShapeDtypeStruct((panels, TW), BF16),
             jax.ShapeDtypeStruct((sections, cap + EXTRA, TW), BF16),
         ]
         scratch = [VMEM((panels, TW), BF16)] + scratch
     else:
         out_shape = [jax.ShapeDtypeStruct((panels, TW), F32)] * 2
-        scratch += [VMEM(pair, BF16), VMEM(window, BF16)]
         if sums:
             aliases = {len(operands) - 2: 0, len(operands) - 1: 1}
     return call(
-        functools.partial(sources_kernel, offsets, not sums, last),
+        functools.partial(sources_kernel, places, not sums, last),
         "sources",
         out_shape,
         [SMEM] + [WHOLE] * (len(operands) - 1),
@@ -314,26 +315,15 @@
     )(*operands)
 
 
-def loading_kernel(count_ref, pair_ref, window_ref, sum_ref, corner_ref, loading_ref, rim_ref):
-    for block in range(pair_ref.shape[0]):
-        rows = slice(block * BLK, (block + 1) * BLK)
-        loading = sum_ref[rows, :] + jnp.dot(pair_ref[block], window_ref[block], preferred_element_type=F32)
-        alive = block * BLK + lax.broadcasted_iota(jnp.int32, (BLK, TW), 0) < count_ref[0]
-        loading_ref[rows, :] = jnp.where(alive, loading, 0.0).astype(BF16)
+def rim_kernel(corner_ref, loading_ref, rim_ref):
     rim = jnp.dot(corner_ref[NODE_DEV - 8 :, :], loading_ref[...], preferred_element_type=F32)
     rim_ref[...] = rim[8:].astype(BF16)
 
 
-def loading_sums(counts, pair, window, sums, corners):
-    panels = sums.shape[0]
-    return call(
-        loading_kernel,
-        "loading",
-        (jax.ShapeDtypeStruct((panels, TW), BF16), jax.ShapeDtypeStruct((HEAD, TW), BF16)),
-        [SMEM] + [WHOLE] * 4,
-        [WHOLE] * 2,
-        work=2_000_000_000,
-    )(counts, pair, window, sums, corners)
+def rim_sums(corners, loading):
+    return call(
+        rim_kernel, "rim", jax.ShapeDtypeStruct((HEAD, TW), BF16), [WHOLE] * 2, WHOLE, work=1_000_000_000
+    )(corners, loading)
 
 
 def node_kernel(corner_ref, loading_ref, node_ref, head_ref):
@@ -405,22 +395,21 @@
     return call(join_kernel, "join", shape, [WHOLE] * 2, WHOLE)(mine, other)
 
 
-def paired_chunk(signals, xyz, sections, local):
+def half_chunk(signals, xyz, sections):
     count, width = signals.shape
     turned = xyz.T
-    bit = 2
-    other, other_points = swapped(signals, "sect", bit), swapped(turned, "sect", bit)
-    shape = jax.ShapeDtypeStruct((2 * count + EXTRA, width), BF16)
-    done = [local[0]()]
-    chunk = call(first_join_kernel, "pair", shape, [WHOLE] * 4, WHOLE, [VMEM((EXTRA, width), F32)])(
-        signals, other, turned, other_points
-    )
-    for step in range(2, sections.bit_length()):
-        bit = bit * 2 if bit * 2 < sections else 1
-        other = swapped(chunk, "sect", bit)
-        done.append(local[step - 1](chunk) if step <= len(local) else None)
-        chunk = joined(chunk, other)
-    return chunk, done
+    pieces, points = [signals], [turned]
+    for apart in range(2, sections, 2):
+        pieces.append(swapped(signals, "sect", apart))
+        points.append(swapped(turned, "sect", apart))
+    shape = jax.ShapeDtypeStruct((len(pieces) * count + EXTRA, width), BF16)
+    return call(
+        first_join_kernel, "first", shape, [WHOLE] * (2 * len(pieces)), WHOLE, [VMEM((EXTRA, width), F32)]
+    )(*pieces, *points)
+
+
+def after(array, other):
+    return lax.optimization_barrier((array, other))[0]
 
 
 def spread_chunk(signals, xyz, sections):
@@ -438,46 +427,47 @@
 def per_device(signals, observer_xyz, panel_geometry, delays, counts, connectivity, owners):
     sections = lax.axis_size("sect")
     groups = lax.axis_size("azim")
-    paired = sections == 8 and signals.shape[0] % 16 == 0
-
-    def windows():
-        return window_index(sections, groups, paired, delays)
-
-    def columns(after=None):
-        geometry = panel_geometry
-        if after is not None:
-            geometry, _ = lax.optimization_barrier((geometry, after))
-        return panel_columns(sections, counts, geometry, owners)
-
-    def corners(after=None):
-        nodes = connectivity
-        if after is not None:
-            nodes, _ = lax.optimization_barrier((nodes, after))
-        return corner_matrix(counts, nodes)
+    count = signals.shape[0]
+    paired = count % 16 == 0 and sections % 2 == 0 and sections // 2 * count == 128
+
+    source = window_index(sections, groups, paired, delays)
+    panel_values, slots, ids = panel_columns(sections, counts, panel_geometry, owners)
+
+    def add(sums, places, chunks, *rest):
+        return sources(places, counts, chunks, source, panel_values, sums, *rest)
 
     if paired:
-        chunk, done = paired_chunk(signals, observer_xyz, sections, (windows, columns, corners))
-        source, (panel_values, slots, ids), corner_values = done
+        half = half_chunk(signals, observer_xyz, sections)
+        other = swapped(half, "sect", 1)
+        corners = corner_matrix(counts, after(connectivity, half))
+        sums = add((), [(0, 0)], [half])
+        chunk = joined(half, other)
     else:
         chunk = spread_chunk(signals, observer_xyz, sections)
-        source, (panel_values, slots, ids), corner_values = windows(), columns(), corners()
+        corners = corner_matrix(counts, connectivity)
+    near = swapped(chunk, "azim", 1)
     chunks = {0: chunk}
     bit = groups // 2
-    while bit:
+    while bit > 1:
         for offset in list(chunks):
             chunks[offset ^ bit] = swapped(chunks[offset], "azim", bit)
         bit //= 2
-    sums = ()
-    for offsets in ([0], [1]):
-        sums = sources(offsets, counts, [chunks[o] for o in offsets], source, panel_values, sums)
-    offsets = [o for o in chunks if o > 1]
-    pair, window, message = sources(
-        offsets, counts, [chunks[o] for o in offsets], source, panel_values, sums[1:], [slots, ids], sections
-    )
+    if paired:
+        sums = add(sums, [(0, 128)], [other])
+    else:
+        sums = add((), [(0, 0)], [chunk])
+    sums = add(sums, [(1, 0)], [near])
+    rest = [offset for offset in chunks if offset]
+    for offset in rest:
+        chunks[offset] = after(chunks[offset], sums[0])
+        chunks[offset ^ 1] = swapped(chunks[offset], "azim", 1)
+    sums = add(sums, [(o, 0) for o in rest], [chunks[o] for o in rest])
+    rest = [offset ^ 1 for offset in rest]
+    loading, message = add(sums, [(o, 0) for o in rest], [chunks[o] for o in rest], [slots, ids], sections)
     message = lax.all_to_all(message, "sect", split_axis=0, concat_axis=0, tiled=True)
-    loading, rim = loading_sums(counts, pair, window, sums[0], corner_values)
+    rim = rim_sums(corners, loading)
     rim = lax.ppermute(rim, "sect", [(i, (i + 1) % sections) for i in range(sections)])
-    nodes, head = node_sums(corner_values, loading)
+    nodes, head = node_sums(corners, loading)
     return finish(message, rim, head, nodes)
 
 

time: 50.3 us -> 48.6 us (0.966)
  local copies, waits for them, and re-layouts: 6.59 us -> 0.78 us
  starting transfers between devices: 16 us -> 18.7 us
  waiting for transfers between devices: 9.98 us -> 11.8 us
    unnamed x20 -> x12, local copies, waits for them, and re-layouts: 6.59 us -> 0.78 us
    ppermute x7 -> x10, starting transfers between devices: 9.28 us -> 13.3 us  [swapped(): return lax.ppermute(array, axis, [(i, i ^ bit) for i in range(peers)])]
    ppermute x1, waiting for transfers between devices: 3.1 us -> 4.63 us  [per_device(): lax.ppermute(rim, 'sect', [(i, (i + 1) % sections) for i in range(section...]
    all_to_all x1, starting transfers between devices: 4.67 us -> 3.38 us  [per_device(): lax.all_to_all(message, 'sect', split_axis=0, concat_axis=0, tiled=True)]
    pallas_call x5 -> x7, Pallas kernels: 10.7 us -> 10.3 us  [the longest x5 9.97 us: sources(): call(functools.partial(sources_kernel, places, not sums, last), 'sources'...]
    ppermute x7 -> x10, waiting for transfers between devices: 6.88 us -> 7.21 us  [swapped(): return lax.ppermute(array, axis, [(i, i ^ bit) for i in range(peers)])]
  transfers between devices with their start and end apart: 9 -> 12, of which waited for: 5 -> 4; matrix products, arithmetic and copies ran while one was open for 0% -> 0% of each run, Pallas kernels for 19% -> 24%
where the time goes in v5:
time: 48.6 us; the launch traced here: 48.3 us
  starting transfers between devices  18.7 us (38%)
  Pallas kernels  15.5 us (32%)
  waiting for transfers between devices  11.8 us (24%)
  between operations  1.45 us (3%)
  local copies, waits for them, and re-layouts  0.78 us (2%)
    ppermute x10, starting transfers between devices, swapped(): return lax.ppermute(array, axis, [(i, i ^ bit) for i in range(peers)])  13.3 us
    pallas_call x5, Pallas kernels, sources(): call(functools.partial(sources_kernel, places, not sums, last), 'sources'...  9.97 us
    ppermute x10, waiting for transfers between devices, swapped(): return lax.ppermute(array, axis, [(i, i ^ bit) for i in range(peers)])  7.21 us
    ppermute x1, waiting for transfers between devices, per_device(): lax.ppermute(rim, 'sect', [(i, (i + 1) % sections) for i in range(section...  4.63 us
    all_to_all x1, starting transfers between devices, per_device(): lax.all_to_all(message, 'sect', split_axis=0, concat_axis=0, tiled=True)  3.38 us
    ppermute x1, starting transfers between devices, per_device(): lax.ppermute(rim, 'sect', [(i, (i + 1) % sections) for i in range(section...  1.96 us
    pallas_call x1, Pallas kernels, node_sums(): call(node_kernel, 'nodes', (jax.ShapeDtypeStruct((NODE_DEV, TW), F32), ja...  1.51 us
    pallas_call x1, Pallas kernels, panel_columns(): call(functools.partial(column_kernel, sections), 'columns', (jax.ShapeDty...  1.11 us
  transfers between devices with their start and end apart: 12, of which 4 were waited for; matrix products, arithmetic and copies ran while one was open for 0% of the time, Pallas kernels for 24%

profile of v5, /device:TPU:0, one launch (start us, length us, event | category | flops | bytes accessed | tf_op | source)
XLA Modules:
  0.0 48.3 jit_solution(5669144419284742041)
XLA Ops:
  0.6 3.1 %collective-permute-start.3 = (bf16[3,32]{1,0:T(4,128)(2,1)}, bf16[3,32]{1,0:T(4,128)(2,1)S(1)}, u32[]{:S(2)}, u32[]{:S(2)}) collective-permute-start(bf16[3,32]{1,0:T(4,128)(2,1)} %bitcast.2), channel_id=1, source_target_pairs={{0,2},{1,3},{2,0},{3,1},{4,6},{5,7},{6,4},{7,5},{8,10},{9,11},{10,... | collective-permute-start | bytes 584 | tf_op jit(solution)/shard_map/ppermute | solution.py:389
  3.7 2.6 %collective-permute-start.4 = (bf16[3,32]{1,0:T(4,128)(2,1)}, bf16[3,32]{1,0:T(4,128)(2,1)S(1)}, u32[]{:S(2)}, u32[]{:S(2)}) collective-permute-start(bf16[3,32]{1,0:T(4,128)(2,1)} %bitcast.3), channel_id=1, source_target_pairs={{0,4},{1,5},{2,6},{3,7},{4,0},{5,1},{6,2},{7,3},{8,12},{9,13},{10,... | collective-permute-start | bytes 584 | tf_op jit(solution)/shard_map/ppermute | solution.py:389
  6.3 0.9 %collective-permute-start = (bf16[32,256]{1,0:T(8,128)(2,1)}, bf16[32,256]{1,0:T(8,128)(2,1)S(1)}, u32[]{:S(2)}, u32[]{:S(2)}) collective-permute-start(bf16[32,256]{1,0:T(8,128)(2,1)} %refs_0_.1), channel_id=1, source_target_pairs={{0,2},{1,3},{2,0},{3,1},{4,6},{5,7},{6,4},{7,5},{8,10},{9,11},{10,... | collective-permute-start | bytes 49160 | tf_op jit(solution)/shard_map/ppermute | solution.py:389
  7.2 3.5 %collective-permute-start.1 = (bf16[32,256]{1,0:T(8,128)(2,1)}, bf16[32,256]{1,0:T(8,128)(2,1)S(1)}, u32[]{:S(2)}, u32[]{:S(2)}) collective-permute-start(bf16[32,256]{1,0:T(8,128)(2,1)} %refs_0_.1), channel_id=1, source_target_pairs={{0,4},{1,5},{2,6},{3,7},{4,0},{5,1},{6,2},{7,3},{8,12},{9,13},{10,... | collective-permute-start | bytes 49160 | tf_op jit(solution)/shard_map/ppermute | solution.py:389
  10.7 0.8 %copy-done.2 = s32[8,1024]{1,0:T(8,128)S(1)} copy-done((s32[8,1024]{1,0:T(8,128)S(1)}, s32[8,1024]{1,0:T(8,128)}, u32[]{:S(2)}) %copy-start.2) | copy-done | bytes 32792
  11.5 0.7 %windows.1.refs_1_ = s32[4,8,256,128]{3,2,1,0:T(8,128)S(1)} custom-call(s32[8,1024]{1,0:T(8,128)S(1)} %copy-done.2), custom_call_target="tpu_custom_call" | custom-call | flops 2000000000 | bytes 4000000 | tf_op jit(solution)/shard_map/windows/pallas_call | solution.py:72
  13.0 1.1 %columns.1 = (f32[8,7,128,128]{3,2,1,0:T(8,128)S(1)}, bf16[512,1024]{1,0:T(8,128)(2,1)S(1)}, f32[16,128]{1,0:T(8,128)S(1)}) custom-call(s32[1]{0:T(128)S(6)} %copy.23.count_ref, f32[7,1024]{1,0:T(8,128)S(1)} %copy-done.3, s32[1,1024]{1,0:T(1,128)S(1)} %bitcast.6), custom_call_target="tpu_custom_call" | custom-call | flops 2000000000 | bytes 4000000 | tf_op jit(solution)/shard_map/columns/pallas_call | solution.py:136
  14.1 4.4 %collective-permute-done.2.refs_3_ = bf16[32,256]{1,0:T(8,128)(2,1)S(1)} collective-permute-done((bf16[32,256]{1,0:T(8,128)(2,1)S(1)}, bf16[32,256]{1,0:T(8,128)(2,1)S(1)}, u32[]{:S(2)}, u32[]{:S(2)}) %collective-permute-start.2) | collective-permute-done | bytes 16416 | tf_op jit(solution)/shard_map/ppermute | solution.py:389
  18.6 1.6 %collective-permute-start.6 = (bf16[144,256]{1,0:T(8,128)(2,1)S(1)}, bf16[144,256]{1,0:T(8,128)(2,1)S(1)}, u32[]{:S(2)}, u32[]{:S(2)}) collective-permute-start(bf16[144,256]{1,0:T(8,128)(2,1)S(1)} %first.1.mine_ref.refs_0_), channel_id=1, source_target_pairs={{0,1},{1,0},{2,3},{3,2},{4,5},{5,4},{6,7},{7,6},{8,9},{9,8},{10,11... | collective-permute-start | bytes 221192 | tf_op jit(solution)/shard_map/ppermute | solution.py:389
  20.2 1.1 %sources.5 = (f32[1024,128]{1,0:T(8,128)S(1)}, f32[1024,128]{1,0:T(8,128)S(1)}) custom-call(s32[1]{0:T(128)S(6)} %copy.23.count_ref, bf16[144,256]{1,0:T(8,128)(2,1)S(1)} %first.1.mine_ref.refs_0_, s32[4,8,256,128]{3,2,1,0:T(8,128)S(1)} %windows.1.refs_1_, f32[8,7,128,128]{3,2,1,0:T(8,128)S(1)} %get-tuple-element.19.refs_2_), custom_call_target="tpu_custom_call" | custom-call | flops 3000000000 | bytes 4000000 | tf_op jit(solution)/shard_map/sources/pallas_call | solution.py:306
  21.2 1.8 %collective-permute-done.6.other_ref.refs_0_ = bf16[144,256]{1,0:T(8,128)(2,1)S(1)} collective-permute-done((bf16[144,256]{1,0:T(8,128)(2,1)S(1)}, bf16[144,256]{1,0:T(8,128)(2,1)S(1)}, u32[]{:S(2)}, u32[]{:S(2)}) %collective-permute-start.6) | collective-permute-done | bytes 73760 | tf_op jit(solution)/shard_map/ppermute | solution.py:389
  23.1 1.6 %collective-permute-start.7 = (bf16[272,256]{1,0:T(8,128)(2,1)S(1)}, bf16[272,256]{1,0:T(8,128)(2,1)S(1)}, u32[]{:S(2)}, u32[]{:S(2)}) collective-permute-start(bf16[272,256]{1,0:T(8,128)(2,1)S(1)} %join.1), channel_id=1, source_target_pairs={{0,16},{8,24},{16,0},{24,8},{1,17},{9,25},{17,1},{25,9},{2,18},{10... | collective-permute-start | bytes 417800 | tf_op jit(solution)/shard_map/ppermute | solution.py:389
  24.7 1.1 %sources.6 = (f32[1024,128]{1,0:T(8,128)S(1)}, f32[1024,128]{1,0:T(8,128)S(1)}) custom-call(s32[1]{0:T(128)S(6)} %copy.23.count_ref, bf16[144,256]{1,0:T(8,128)(2,1)S(1)} %collective-permute-done.6.other_ref.refs_0_, s32[4,8,256,128]{3,2,1,0:T(8,128)S(1)} %windows.1.refs_1_, ...), custom_call_target="tpu_custom_call", output_to_operand_aliasing={{0}: (4, {}), {1}: (5, {})} | custom-call | flops 3000000000 | bytes 4000000 | tf_op jit(solution)/shard_map/sources/pallas_call | solution.py:306
  25.8 2.4 %sources.7 = (f32[1024,128]{1,0:T(8,128)S(1)}, f32[1024,128]{1,0:T(8,128)S(1)}) custom-call(s32[1]{0:T(128)S(6)} %copy.23.count_ref, bf16[272,256]{1,0:T(8,128)(2,1)S(1)} %collective-permute-done.8.refs_0_, s32[4,8,256,128]{3,2,1,0:T(8,128)S(1)} %windows.1.refs_1_, ...), custom_call_target="tpu_custom_call", output_to_operand_aliasing={{0}: (4, {}), {1}: (5, {})} | custom-call | flops 3000000000 | bytes 4000000 | tf_op jit(solution)/shard_map/sources/pallas_call | solution.py:306
  28.1 1.1 %collective-permute-done.7.refs_0_ = bf16[272,256]{1,0:T(8,128)(2,1)S(1)} collective-permute-done((bf16[272,256]{1,0:T(8,128)(2,1)S(1)}, bf16[272,256]{1,0:T(8,128)(2,1)S(1)}, u32[]{:S(2)}, u32[]{:S(2)}) %collective-permute-start.7) | collective-permute-done | bytes 139296 | tf_op jit(solution)/shard_map/ppermute | solution.py:389
  29.2 2.4 %sources.8 = (f32[1024,128]{1,0:T(8,128)S(1)}, f32[1024,128]{1,0:T(8,128)S(1)}) custom-call(s32[1]{0:T(128)S(6)} %copy.23.count_ref, bf16[272,256]{1,0:T(8,128)(2,1)S(1)} %collective-permute-done.7.refs_0_, s32[4,8,256,128]{3,2,1,0:T(8,128)S(1)} %windows.1.refs_1_, ...), custom_call_target="tpu_custom_call", output_to_operand_aliasing={{0}: (4, {}), {1}: (5, {})} | custom-call | flops 3000000000 | bytes 4000000 | tf_op jit(solution)/shard_map/sources/pallas_call | solution.py:306
  31.6 3.1 %sources.9 = (bf16[1024,128]{1,0:T(8,128)(2,1)S(1)}, bf16[8,80,128]{2,1,0:T(8,128)(2,1)}) custom-call(s32[1]{0:T(128)S(6)} %copy.23.count_ref, bf16[272,256]{1,0:T(8,128)(2,1)S(1)} %collective-permute-done.9.refs_0_, s32[4,8,256,128]{3,2,1,0:T(8,128)S(1)} %windows.1.refs_1_, f32[8,7,128,128]{3,2,1,0:T(8,128)S(1)} %get-tuple-element.19.refs_2_, ...), custom_call_target="tpu_custom_call" | custom-call | flops 3000000000 | bytes 4000000 | tf_op jit(solution)/shard_map/sources/pallas_call | solution.py:306
  34.7 3.4 %all-to-all-start = ((bf16[8,80,128]{2,1,0:T(8,128)(2,1)}), bf16[8,80,128]{2,1,0:T(8,128)(2,1)S(1)}, u32[]{:S(2)}, u32[]{:S(2)}) async-start(bf16[8,80,128]{2,1,0:T(8,128)(2,1)} %get-tuple-element.31), calls=%async_computation | async-start | bytes 327680 | tf_op jit(solution)/shard_map/all_to_all | solution.py:467
  38.1 1.0 %corners.1.corner_ref = bf16[1168,1024]{1,0:T(8,128)(2,1)S(1)} custom-call(s32[1]{0:T(128)S(6)} %copy.23.count_ref, s32[4,1024]{1,0:T(4,128)S(1)} %copy-done.4), custom_call_target="tpu_custom_call" | custom-call | flops 2000000000 | bytes 4000000 | tf_op jit(solution)/shard_map/corners/pallas_call | solution.py:167
  39.0 0.2 rim.1
  39.3 2.0 %collective-permute-start.10 = (bf16[136,128]{1,0:T(8,128)(2,1)S(1)}, bf16[136,128]{1,0:T(8,128)(2,1)S(1)}, u32[]{:S(2)}, u32[]{:S(2)}) collective-permute-start(bf16[136,128]{1,0:T(8,128)(2,1)S(1)} %rim.1), channel_id=1, source_target_pairs={{0,1},{1,2},{2,3},{3,4},{4,5},{5,6},{6,7},{7,0},{8,9},{9,10},{10,1... | collective-permute-start | bytes 104456 | tf_op jit(solution)/shard_map/ppermute | solution.py:469
  41.2 1.5 %nodes.1 = (f32[1032,128]{1,0:T(8,128)}, f32[136,128]{1,0:T(8,128)S(1)}) custom-call(bf16[1168,1024]{1,0:T(8,128)(2,1)S(1)} %corners.1.corner_ref, bf16[1024,128]{1,0:T(8,128)(2,1)S(1)} %get-tuple-element.33.loading_ref), custom_call_target="tpu_custom_call" | custom-call | flops 2000000000 | bytes 4000000 | tf_op jit(solution)/shard_map/nodes/pallas_call | solution.py:336
  42.8 4.6 %collective-permute-done.10.rim_ref = bf16[136,128]{1,0:T(8,128)(2,1)S(1)} collective-permute-done((bf16[136,128]{1,0:T(8,128)(2,1)S(1)}, bf16[136,128]{1,0:T(8,128)(2,1)S(1)}, u32[]{:S(2)}, u32[]{:S(2)}) %collective-permute-start.10) | collective-permute-done | bytes 34848 | tf_op jit(solution)/shard_map/ppermute | solution.py:469
  47.4 0.9 %finish.1 = (f32[1032,128]{1,0:T(8,128)}, f32[256,128]{1,0:T(8,128)}) custom-call(bf16[8,80,128]{2,1,0:T(8,128)(2,1)S(1)} %all-to-all-done.message_ref, bf16[136,128]{1,0:T(8,128)(2,1)S(1)} %collective-permute-done.10.rim_ref, f32[136,128]{1,0:T(8,128)S(1)} %get-tuple-element.34.head_ref, ...), custom_call_target="tpu_custom_call", output_to_operand_aliasing={{0}: (3, {})} | custom-call | flops 1000000 | bytes 4000000 | tf_op jit(solution)/shard_map/finish/pallas_call | solution.py:373
  (25 shorter events, 0.3 us)
Async XLA Ops:
  0.6 12.3 %copy-start = (bf16[32,256]{1,0:T(8,128)(2,1)S(1)}, bf16[32,256]{1,0:T(8,128)(2,1)}, u32[]{:S(2)}) copy-start(bf16[32,256]{1,0:T(8,128)(2,1)} %refs_0_.1) | copy-start | bytes 49156
  0.6 12.2 %collective-permute-start.3 = (bf16[3,32]{1,0:T(4,128)(2,1)}, bf16[3,32]{1,0:T(4,128)(2,1)S(1)}, u32[]{:S(2)}, u32[]{:S(2)}) collective-permute-start(bf16[3,32]{1,0:T(4,128)(2,1)} %bitcast.2), channel_id=1, source_target_pairs={{0,2},{1,3},{2,0},{3,1},{4,6},{5,7},{6,4},{7,5},{8,10},{9,11},{10,... | collective-permute-start | bytes 584 | tf_op jit(solution)/shard_map/ppermute | solution.py:389
  3.7 10.4 %collective-permute-start.4 = (bf16[3,32]{1,0:T(4,128)(2,1)}, bf16[3,32]{1,0:T(4,128)(2,1)S(1)}, u32[]{:S(2)}, u32[]{:S(2)}) collective-permute-start(bf16[3,32]{1,0:T(4,128)(2,1)} %bitcast.3), channel_id=1, source_target_pairs={{0,4},{1,5},{2,6},{3,7},{4,0},{5,1},{6,2},{7,3},{8,12},{9,13},{10,... | collective-permute-start | bytes 584 | tf_op jit(solution)/shard_map/ppermute | solution.py:389
  6.3 7.8 %collective-permute-start.5 = (bf16[3,32]{1,0:T(4,128)(2,1)}, bf16[3,32]{1,0:T(4,128)(2,1)S(1)}, u32[]{:S(2)}, u32[]{:S(2)}) collective-permute-start(bf16[3,32]{1,0:T(4,128)(2,1)} %bitcast.4), channel_id=1, source_target_pairs={{0,6},{1,7},{2,4},{3,5},{4,2},{5,3},{6,0},{7,1},{8,14},{9,15},{10,... | collective-permute-start | bytes 584 | tf_op jit(solution)/shard_map/ppermute | solution.py:389
  6.3 7.8 %collective-permute-start = (bf16[32,256]{1,0:T(8,128)(2,1)}, bf16[32,256]{1,0:T(8,128)(2,1)S(1)}, u32[]{:S(2)}, u32[]{:S(2)}) collective-permute-start(bf16[32,256]{1,0:T(8,128)(2,1)} %refs_0_.1), channel_id=1, source_target_pairs={{0,2},{1,3},{2,0},{3,1},{4,6},{5,7},{6,4},{7,5},{8,10},{9,11},{10,... | collective-permute-start | bytes 49160 | tf_op jit(solution)/shard_map/ppermute | solution.py:389
  7.2 6.9 %collective-permute-start.1 = (bf16[32,256]{1,0:T(8,128)(2,1)}, bf16[32,256]{1,0:T(8,128)(2,1)S(1)}, u32[]{:S(2)}, u32[]{:S(2)}) collective-permute-start(bf16[32,256]{1,0:T(8,128)(2,1)} %refs_0_.1), channel_id=1, source_target_pairs={{0,4},{1,5},{2,6},{3,7},{4,0},{5,1},{6,2},{7,3},{8,12},{9,13},{10,... | collective-permute-start | bytes 49160 | tf_op jit(solution)/shard_map/ppermute | solution.py:389
  10.7 0.8 %copy-start.2 = (s32[8,1024]{1,0:T(8,128)S(1)}, s32[8,1024]{1,0:T(8,128)}, u32[]{:S(2)}) copy-start(s32[8,1024]{1,0:T(8,128)} %delay_ref.1) | copy-start | bytes 98308
  11.5 1.5 %copy-start.3 = (f32[7,1024]{1,0:T(8,128)S(1)}, f32[7,1024]{1,0:T(8,128)}, u32[]{:S(2)}) copy-start(f32[7,1024]{1,0:T(8,128)} %geometry_ref.1) | copy-start | bytes 86020
  11.5 1.5 %copy-start.5 = (s32[1024]{0:T(1024)S(1)}, s32[1024]{0:T(1024)}, u32[]{:S(2)}) copy-start(s32[1024]{0:T(1024)} %param.13) | copy-start | bytes 12292
  12.9 5.6 %collective-permute-start.2 = (bf16[32,256]{1,0:T(8,128)(2,1)S(1)}, bf16[32,256]{1,0:T(8,128)(2,1)S(1)}, u32[]{:S(2)}, u32[]{:S(2)}) collective-permute-start(bf16[32,256]{1,0:T(8,128)(2,1)S(1)} %copy-done), channel_id=1, source_target_pairs={{0,6},{1,7},{2,4},{3,5},{4,2},{5,3},{6,0},{7,1},{8,14},{9,15},{10,... | collective-permute-start | bytes 49160 | tf_op jit(solution)/shard_map/ppermute | solution.py:389
  13.0 5.5 %copy-start.1 = (bf16[32,3]{0,1:T(4,128)(2,1)S(1)}, bf16[32,3]{0,1:T(4,128)(2,1)}, u32[]{:S(2)}) copy-start(bf16[32,3]{0,1:T(4,128)(2,1)} %param.8) | copy-start | bytes 580
  18.6 4.4 %collective-permute-start.6 = (bf16[144,256]{1,0:T(8,128)(2,1)S(1)}, bf16[144,256]{1,0:T(8,128)(2,1)S(1)}, u32[]{:S(2)}, u32[]{:S(2)}) collective-permute-start(bf16[144,256]{1,0:T(8,128)(2,1)S(1)} %first.1.mine_ref.refs_0_), channel_id=1, source_target_pairs={{0,1},{1,0},{2,3},{3,2},{4,5},{5,4},{6,7},{7,6},{8,9},{9,8},{10,11... | collective-permute-start | bytes 221192 | tf_op jit(solution)/shard_map/ppermute | solution.py:389
  23.0 2.7 %collective-permute-start.8 = (bf16[272,256]{1,0:T(8,128)(2,1)S(1)}, bf16[272,256]{1,0:T(8,128)(2,1)S(1)}, u32[]{:S(2)}, u32[]{:S(2)}) collective-permute-start(bf16[272,256]{1,0:T(8,128)(2,1)S(1)} %join.1), channel_id=1, source_target_pairs={{0,8},{8,0},{16,24},{24,16},{1,9},{9,1},{17,25},{25,17},{2,10},{10... | collective-permute-start | bytes 417800 | tf_op jit(solution)/shard_map/ppermute | solution.py:389
  23.1 6.1 %collective-permute-start.7 = (bf16[272,256]{1,0:T(8,128)(2,1)S(1)}, bf16[272,256]{1,0:T(8,128)(2,1)S(1)}, u32[]{:S(2)}, u32[]{:S(2)}) collective-permute-start(bf16[272,256]{1,0:T(8,128)(2,1)S(1)} %join.1), channel_id=1, source_target_pairs={{0,16},{8,24},{16,0},{24,8},{1,17},{9,25},{17,1},{25,9},{2,18},{10... | collective-permute-start | bytes 417800 | tf_op jit(solution)/shard_map/ppermute | solution.py:389
  29.2 2.4 %collective-permute-start.9 = (bf16[272,256]{1,0:T(8,128)(2,1)S(1)}, bf16[272,256]{1,0:T(8,128)(2,1)S(1)}, u32[]{:S(2)}, u32[]{:S(2)}) collective-permute-start(bf16[272,256]{1,0:T(8,128)(2,1)S(1)} %collective-permute-done.7.refs_0_), channel_id=1, source_target_pairs={{0,8},{8,0},{16,24},{24,16},{1,9},{9,1},{17,25},{25,17},{2,10},{10... | collective-permute-start | bytes 417800 | tf_op jit(solution)/shard_map/ppermute | solution.py:389
  31.6 6.5 %copy-start.4 = (s32[4,1024]{1,0:T(4,128)S(1)}, s32[4,1024]{1,0:T(4,128)}, u32[]{:S(2)}) copy-start(s32[4,1024]{1,0:T(4,128)} %conn_ref) | copy-start | bytes 49156
  34.7 12.7 %all-to-all-start = ((bf16[8,80,128]{2,1,0:T(8,128)(2,1)}), bf16[8,80,128]{2,1,0:T(8,128)(2,1)S(1)}, u32[]{:S(2)}, u32[]{:S(2)}) async-start(bf16[8,80,128]{2,1,0:T(8,128)(2,1)} %get-tuple-element.31), calls=%async_computation | async-start | bytes 327680 | tf_op jit(solution)/shard_map/all_to_all | solution.py:467
  39.3 8.1 %collective-permute-start.10 = (bf16[136,128]{1,0:T(8,128)(2,1)S(1)}, bf16[136,128]{1,0:T(8,128)(2,1)S(1)}, u32[]{:S(2)}, u32[]{:S(2)}) collective-permute-start(bf16[136,128]{1,0:T(8,128)(2,1)S(1)} %rim.1), channel_id=1, source_target_pairs={{0,1},{1,2},{2,3},{3,4},{4,5},{5,6},{6,7},{7,0},{8,9},{9,10},{10,1... | collective-permute-start | bytes 104456 | tf_op jit(solution)/shard_map/ppermute | solution.py:469

commit v6 on v5

--- a/solution.py
+++ b/solution.py
@@ -16,6 +16,7 @@
 HEAD = 136
 NODE_ROWS = 1168
 EXTRA = 16
+FIXED = 32000.0
 F32 = jnp.float32
 BF16 = jnp.bfloat16
 VMEM = pltpu.VMEM
@@ -207,19 +208,26 @@
     chunks = take(parts)
     source_ref, panel_ref = take(2)
     if last:
-        loading_in, thick_in, slot_ref, ids_ref, loading_ref, message_ref, thick_ref = take(7)
+        loading_in, thick_in, slot_ref, ids_ref, corner_ref = take(5)
+        loading_ref, message_ref, rim_ref, thick_ref = take(4)
     else:
         loading_in, thick_in = (None, None) if first else take(2)
         loading_ref, thick_ref = take(2)
-    low_ref, high_ref, mass_ref, pair_ref, window_ref = take(5)
+    code_ref, scale_ref, mass_ref, pair_ref, window_ref = take(5)
 
     blocks = source_ref.shape[1]
     span = chunks[0].shape[0] - EXTRA
     observers = parts * span
     points = []
     for number, chunk in enumerate(chunks):
-        low_ref[number * span : (number + 1) * span, :] = chunk[:span, :128].astype(F32)
-        high_ref[number * span : (number + 1) * span, :] = chunk[:span, 128:].astype(F32)
+        low = chunk[:span, :128].astype(F32)
+        high = chunk[:span, 128:].astype(F32)
+        most = jnp.max(jnp.maximum(jnp.abs(low), jnp.abs(high)), axis=1, keepdims=True)
+        most = jnp.maximum(jnp.broadcast_to(most, (span, 128)), 1e-30)
+        low = jnp.floor(low * (FIXED / most) + 0.5).astype(jnp.int32)
+        high = jnp.floor(high * (FIXED / most) + 0.5).astype(jnp.int32)
+        code_ref[number * span : (number + 1) * span, :] = (high << 16) | (low & 0xFFFF)
+        scale_ref[number * span : (number + 1) * span, :] = most * (1 / (FIXED * 65536))
         points.append(chunk[span : span + EXTRA, :].astype(F32) * 0.25)
 
     lanes = lax.broadcasted_iota(jnp.int32, (128, 128), 1)
@@ -230,11 +238,12 @@
                 here = number * span + piece * 128
                 source = source_ref[group, block, begin + piece * 128 : begin + (piece + 1) * 128, :]
                 at = source & 127
-                low = jnp.take_along_axis(low_ref[here : here + 128, :], at, axis=1, mode="promise_in_bounds")
-                high = jnp.take_along_axis(high_ref[here : here + 128, :], at, axis=1, mode="promise_in_bounds")
-                current = jnp.where(source < 128, low, high)
-                following = pltpu.roll(jnp.where(lanes == 0, high, current).astype(BF16), 127, 1)
-                current = current.astype(BF16)
+                code = jnp.take_along_axis(code_ref[here : here + 128, :], at, axis=1, mode="promise_in_bounds")
+                scale = scale_ref[here : here + 128, :]
+                current = jnp.where(source < 128, code << 16, code)
+                following = (jnp.where(lanes == 0, code, current).astype(F32) * scale).astype(BF16)
+                following = pltpu.roll(following, 127, 1)
+                current = (current.astype(F32) * scale).astype(BF16)
                 window_ref[block, here : here + 128, :] = current
                 window_ref[block, observers + here : observers + here + 128, :] = following - current
 
@@ -275,6 +284,8 @@
             message_ref[section, :cap, :] = slots[section * cap : (section + 1) * cap]
             ids = jnp.broadcast_to(ids_ref[section : section + 1, :], (EXTRA, 128))
             message_ref[section, cap:, :] = ids.astype(BF16)
+        rim = jnp.dot(corner_ref[NODE_DEV - 8 :, :], loading_ref[...], preferred_element_type=F32)
+        rim_ref[...] = rim[8:].astype(BF16)
 
 
 def sources(places, counts, chunks, source, panel_values, sums=(), slots=None, sections=None):
@@ -284,7 +295,7 @@
     last = slots is not None
     operands = [counts, *chunks, source, panel_values, *sums]
     scratch = [
-        VMEM((observers, 128), F32),
+        VMEM((observers, 128), jnp.int32),
         VMEM((observers, 128), F32),
         VMEM((blocks, BLK, observers), BF16),
         VMEM((blocks, BLK, 2 * observers), BF16),
@@ -297,6 +308,7 @@
         out_shape = [
             jax.ShapeDtypeStruct((panels, TW), BF16),
             jax.ShapeDtypeStruct((sections, cap + EXTRA, TW), BF16),
+            jax.ShapeDtypeStruct((HEAD, TW), BF16),
         ]
         scratch = [VMEM((panels, TW), BF16)] + scratch
     else:
@@ -313,17 +325,6 @@
         aliases,
         work=3_000_000_000,
     )(*operands)
-
-
-def rim_kernel(corner_ref, loading_ref, rim_ref):
-    rim = jnp.dot(corner_ref[NODE_DEV - 8 :, :], loading_ref[...], preferred_element_type=F32)
-    rim_ref[...] = rim[8:].astype(BF16)
-
-
-def rim_sums(corners, loading):
-    return call(
-        rim_kernel, "rim", jax.ShapeDtypeStruct((HEAD, TW), BF16), [WHOLE] * 2, WHOLE, work=1_000_000_000
-    )(corners, loading)
 
 
 def node_kernel(corner_ref, loading_ref, node_ref, head_ref):
@@ -398,14 +399,15 @@
 def half_chunk(signals, xyz, sections):
     count, width = signals.shape
     turned = xyz.T
-    pieces, points = [signals], [turned]
-    for apart in range(2, sections, 2):
-        pieces.append(swapped(signals, "sect", apart))
-        points.append(swapped(turned, "sect", apart))
-    shape = jax.ShapeDtypeStruct((len(pieces) * count + EXTRA, width), BF16)
-    return call(
-        first_join_kernel, "first", shape, [WHOLE] * (2 * len(pieces)), WHOLE, [VMEM((EXTRA, width), F32)]
-    )(*pieces, *points)
+    shape = jax.ShapeDtypeStruct((2 * count + EXTRA, width), BF16)
+    chunk = call(first_join_kernel, "first", shape, [WHOLE] * 4, WHOLE, [VMEM((EXTRA, width), F32)])(
+        signals, swapped(signals, "sect", 2), turned, swapped(turned, "sect", 2)
+    )
+    bit = 4
+    while bit < sections:
+        chunk = joined(chunk, swapped(chunk, "sect", bit))
+        bit *= 2
+    return chunk
 
 
 def after(array, other):
@@ -431,7 +433,7 @@
     paired = count % 16 == 0 and sections % 2 == 0 and sections // 2 * count == 128
 
     source = window_index(sections, groups, paired, delays)
-    panel_values, slots, ids = panel_columns(sections, counts, panel_geometry, owners)
+    panel_values, slots, ids = panel_columns(sections, counts, after(panel_geometry, source), owners)
 
     def add(sums, places, chunks, *rest):
         return sources(places, counts, chunks, source, panel_values, sums, *rest)
@@ -441,6 +443,7 @@
         other = swapped(half, "sect", 1)
         corners = corner_matrix(counts, after(connectivity, half))
         sums = add((), [(0, 0)], [half])
+        sums = after(sums, corners)
         chunk = joined(half, other)
     else:
         chunk = spread_chunk(signals, observer_xyz, sections)
@@ -463,9 +466,9 @@
         chunks[offset ^ 1] = swapped(chunks[offset], "azim", 1)
     sums = add(sums, [(o, 0) for o in rest], [chunks[o] for o in rest])
     rest = [offset ^ 1 for offset in rest]
-    loading, message = add(sums, [(o, 0) for o in rest], [chunks[o] for o in rest], [slots, ids], sections)
+    matrices = [slots, ids, corners]
+    loading, message, rim = add(sums, [(o, 0) for o in rest], [chunks[o] for o in rest], matrices, sections)
     message = lax.all_to_all(message, "sect", split_axis=0, concat_axis=0, tiled=True)
-    rim = rim_sums(corners, loading)
     rim = lax.ppermute(rim, "sect", [(i, (i + 1) % sections) for i in range(sections)])
     nodes, head = node_sums(corners, loading)
     return finish(message, rim, head, nodes)

time: 48.6 us -> 44 us (0.905)
  starting transfers between devices: 18.7 us -> 16 us
  waiting for transfers between devices: 11.8 us -> 9.97 us
    ppermute x10 -> x7, starting transfers between devices: 13.3 us -> 9.29 us  [swapped(): return lax.ppermute(array, axis, [(i, i ^ bit) for i in range(peers)])]
    ppermute x10 -> x7, waiting for transfers between devices: 7.21 us -> 4.4 us  [swapped(): return lax.ppermute(array, axis, [(i, i ^ bit) for i in range(peers)])]
    all_to_all x1, starting transfers between devices: 3.38 us -> 4.68 us  [per_device(): lax.all_to_all(message, 'sect', split_axis=0, concat_axis=0, tiled=True)]
    ppermute x1, waiting for transfers between devices: 4.63 us -> 5.57 us  [per_device(): lax.ppermute(rim, 'sect', [(i, (i + 1) % sections) for i in range(section...]
  transfers between devices with their start and end apart: 12 -> 9, of which waited for: 4 -> 5; matrix products, arithmetic and copies ran while one was open for 0% -> 0% of each run, Pallas kernels for 24% -> 26%
where the time goes in v6:
time: 44 us; the launch traced here: 43.7 us
  starting transfers between devices  16 us (36%)
  Pallas kernels  15.6 us (35%)
  waiting for transfers between devices  9.97 us (23%)
  between operations  1.39 us (3%)
  local copies, waits for them, and re-layouts  0.78 us (2%)
    pallas_call x5, Pallas kernels, sources(): call(functools.partial(sources_kernel, places, not sums, last), 'sources'...  10.2 us
    ppermute x7, starting transfers between devices, swapped(): return lax.ppermute(array, axis, [(i, i ^ bit) for i in range(peers)])  9.29 us
    ppermute x1, waiting for transfers between devices, per_device(): lax.ppermute(rim, 'sect', [(i, (i + 1) % sections) for i in range(section...  5.57 us
    all_to_all x1, starting transfers between devices, per_device(): lax.all_to_all(message, 'sect', split_axis=0, concat_axis=0, tiled=True)  4.68 us
    ppermute x7, waiting for transfers between devices, swapped(): return lax.ppermute(array, axis, [(i, i ^ bit) for i in range(peers)])  4.4 us
    ppermute x1, starting transfers between devices, per_device(): lax.ppermute(rim, 'sect', [(i, (i + 1) % sections) for i in range(section...  2.02 us
    pallas_call x1, Pallas kernels, node_sums(): call(node_kernel, 'nodes', (jax.ShapeDtypeStruct((NODE_DEV, TW), F32), ja...  1.51 us
    pallas_call x1, Pallas kernels, panel_columns(): call(functools.partial(column_kernel, sections), 'columns', (jax.ShapeDty...  1.11 us
  transfers between devices with their start and end apart: 9, of which 5 were waited for; matrix products, arithmetic and copies ran while one was open for 0% of the time, Pallas kernels for 26%

profile of v6, /device:TPU:0, one launch (start us, length us, event | category | flops | bytes accessed | tf_op | source)
XLA Modules:
  0.0 43.7 jit_solution(13563164207493841876)
XLA Ops:
  0.7 3.1 %collective-permute-start.1 = (bf16[3,32]{1,0:T(4,128)(2,1)}, bf16[3,32]{1,0:T(4,128)(2,1)S(1)}, u32[]{:S(2)}, u32[]{:S(2)}) collective-permute-start(bf16[3,32]{1,0:T(4,128)(2,1)} %bitcast.2), channel_id=1, source_target_pairs={{0,2},{1,3},{2,0},{3,1},{4,6},{5,7},{6,4},{7,5},{8,10},{9,11},{10,... | collective-permute-start | bytes 584 | tf_op jit(solution)/shard_map/ppermute | solution.py:390
  3.7 0.1 collective-permute-start
  3.8 0.8 %copy-done.2 = s32[8,1024]{1,0:T(8,128)S(1)} copy-done((s32[8,1024]{1,0:T(8,128)S(1)}, s32[8,1024]{1,0:T(8,128)}, u32[]{:S(2)}) %copy-start.2) | copy-done | bytes 32792
  4.6 0.7 %windows.1.refs_1_ = s32[4,8,256,128]{3,2,1,0:T(8,128)S(1)} custom-call(s32[8,1024]{1,0:T(8,128)S(1)} %copy-done.2), custom_call_target="tpu_custom_call" | custom-call | flops 2000000000 | bytes 4000000 | tf_op jit(solution)/shard_map/windows/pallas_call | solution.py:73
  6.0 1.7 %collective-permute-done.refs_1_ = bf16[32,256]{1,0:T(8,128)(2,1)S(1)} collective-permute-done((bf16[32,256]{1,0:T(8,128)(2,1)}, bf16[32,256]{1,0:T(8,128)(2,1)S(1)}, u32[]{:S(2)}, u32[]{:S(2)}) %collective-permute-start) | collective-permute-done | bytes 16416 | tf_op jit(solution)/shard_map/ppermute | solution.py:390
  7.8 2.6 %collective-permute-start.2 = (bf16[80,256]{1,0:T(8,128)(2,1)S(1)}, bf16[80,256]{1,0:T(8,128)(2,1)S(1)}, u32[]{:S(2)}, u32[]{:S(2)}) collective-permute-start(bf16[80,256]{1,0:T(8,128)(2,1)S(1)} %first.1.mine_ref), channel_id=1, source_target_pairs={{0,4},{1,5},{2,6},{3,7},{4,0},{5,1},{6,2},{7,3},{8,12},{9,13},{10,... | collective-permute-start | bytes 122888 | tf_op jit(solution)/shard_map/ppermute | solution.py:390
  10.4 1.1 %columns.1 = (f32[8,7,128,128]{3,2,1,0:T(8,128)S(1)}, bf16[512,1024]{1,0:T(8,128)(2,1)S(1)}, f32[16,128]{1,0:T(8,128)S(1)}) custom-call(s32[1]{0:T(128)S(6)} %copy.23.count_ref, f32[7,1024]{1,0:T(8,128)S(1)} %copy-done.3, s32[1,1024]{1,0:T(1,128)S(1)} %bitcast.4), custom_call_target="tpu_custom_call" | custom-call | flops 2000000000 | bytes 4000000 | tf_op jit(solution)/shard_map/columns/pallas_call | solution.py:137
  11.5 1.3 %collective-permute-done.2.other_ref = bf16[80,256]{1,0:T(8,128)(2,1)S(1)} collective-permute-done((bf16[80,256]{1,0:T(8,128)(2,1)S(1)}, bf16[80,256]{1,0:T(8,128)(2,1)S(1)}, u32[]{:S(2)}, u32[]{:S(2)}) %collective-permute-start.2) | collective-permute-done | bytes 40992 | tf_op jit(solution)/shard_map/ppermute | solution.py:390
  12.8 0.1 join.2.mine_ref.refs_0_
  12.9 1.7 %collective-permute-start.3 = (bf16[144,256]{1,0:T(8,128)(2,1)S(1)}, bf16[144,256]{1,0:T(8,128)(2,1)S(1)}, u32[]{:S(2)}, u32[]{:S(2)}) collective-permute-start(bf16[144,256]{1,0:T(8,128)(2,1)S(1)} %join.2.mine_ref.refs_0_), channel_id=1, source_target_pairs={{0,1},{1,0},{2,3},{3,2},{4,5},{5,4},{6,7},{7,6},{8,9},{9,8},{10,11... | collective-permute-start | bytes 221192 | tf_op jit(solution)/shard_map/ppermute | solution.py:390
  14.6 1.2 %sources.5 = (f32[1024,128]{1,0:T(8,128)S(1)}, f32[1024,128]{1,0:T(8,128)S(1)}) custom-call(s32[1]{0:T(128)S(6)} %copy.23.count_ref, bf16[144,256]{1,0:T(8,128)(2,1)S(1)} %join.2.mine_ref.refs_0_, s32[4,8,256,128]{3,2,1,0:T(8,128)S(1)} %windows.1.refs_1_, f32[8,7,128,128]{3,2,1,0:T(8,128)S(1)} %get-tuple-element.24.refs_2_), custom_call_target="tpu_custom_call" | custom-call | flops 3000000000 | bytes 4000000 | tf_op jit(solution)/shard_map/sources/pallas_call | solution.py:318
  15.8 1.0 %corners.1.refs_7_.corner_ref = bf16[1168,1024]{1,0:T(8,128)(2,1)S(1)} custom-call(s32[1]{0:T(128)S(6)} %copy.23.count_ref, s32[4,1024]{1,0:T(4,128)S(1)} %copy-done.4), custom_call_target="tpu_custom_call" | custom-call | flops 2000000000 | bytes 4000000 | tf_op jit(solution)/shard_map/corners/pallas_call | solution.py:168
  16.8 0.5 %collective-permute-done.3.other_ref.refs_0_ = bf16[144,256]{1,0:T(8,128)(2,1)S(1)} collective-permute-done((bf16[144,256]{1,0:T(8,128)(2,1)S(1)}, bf16[144,256]{1,0:T(8,128)(2,1)S(1)}, u32[]{:S(2)}, u32[]{:S(2)}) %collective-permute-start.3) | collective-permute-done | bytes 73760 | tf_op jit(solution)/shard_map/ppermute | solution.py:390
  17.4 1.7 %collective-permute-start.4 = (bf16[272,256]{1,0:T(8,128)(2,1)S(1)}, bf16[272,256]{1,0:T(8,128)(2,1)S(1)}, u32[]{:S(2)}, u32[]{:S(2)}) collective-permute-start(bf16[272,256]{1,0:T(8,128)(2,1)S(1)} %join.3), channel_id=1, source_target_pairs={{0,16},{8,24},{16,0},{24,8},{1,17},{9,25},{17,1},{25,9},{2,18},{10... | collective-permute-start | bytes 417800 | tf_op jit(solution)/shard_map/ppermute | solution.py:390
  19.1 1.2 %sources.6 = (f32[1024,128]{1,0:T(8,128)S(1)}, f32[1024,128]{1,0:T(8,128)S(1)}) custom-call(s32[1]{0:T(128)S(6)} %copy.23.count_ref, bf16[144,256]{1,0:T(8,128)(2,1)S(1)} %collective-permute-done.3.other_ref.refs_0_, s32[4,8,256,128]{3,2,1,0:T(8,128)S(1)} %windows.1.refs_1_, ...), custom_call_target="tpu_custom_call", output_to_operand_aliasing={{0}: (4, {}), {1}: (5, {})} | custom-call | flops 3000000000 | bytes 4000000 | tf_op jit(solution)/shard_map/sources/pallas_call | solution.py:318
  20.4 2.2 %sources.7 = (f32[1024,128]{1,0:T(8,128)S(1)}, f32[1024,128]{1,0:T(8,128)S(1)}) custom-call(s32[1]{0:T(128)S(6)} %copy.23.count_ref, bf16[272,256]{1,0:T(8,128)(2,1)S(1)} %collective-permute-done.5.refs_0_, s32[4,8,256,128]{3,2,1,0:T(8,128)S(1)} %windows.1.refs_1_, ...), custom_call_target="tpu_custom_call", output_to_operand_aliasing={{0}: (4, {}), {1}: (5, {})} | custom-call | flops 3000000000 | bytes 4000000 | tf_op jit(solution)/shard_map/sources/pallas_call | solution.py:318
  22.6 0.8 %collective-permute-done.4.refs_0_ = bf16[272,256]{1,0:T(8,128)(2,1)S(1)} collective-permute-done((bf16[272,256]{1,0:T(8,128)(2,1)S(1)}, bf16[272,256]{1,0:T(8,128)(2,1)S(1)}, u32[]{:S(2)}, u32[]{:S(2)}) %collective-permute-start.4) | collective-permute-done | bytes 139296 | tf_op jit(solution)/shard_map/ppermute | solution.py:390
  23.5 2.2 %sources.8 = (f32[1024,128]{1,0:T(8,128)S(1)}, f32[1024,128]{1,0:T(8,128)S(1)}) custom-call(s32[1]{0:T(128)S(6)} %copy.23.count_ref, bf16[272,256]{1,0:T(8,128)(2,1)S(1)} %collective-permute-done.4.refs_0_, s32[4,8,256,128]{3,2,1,0:T(8,128)S(1)} %windows.1.refs_1_, ...), custom_call_target="tpu_custom_call", output_to_operand_aliasing={{0}: (4, {}), {1}: (5, {})} | custom-call | flops 3000000000 | bytes 4000000 | tf_op jit(solution)/shard_map/sources/pallas_call | solution.py:318
  25.7 3.3 %sources.9 = (bf16[1024,128]{1,0:T(8,128)(2,1)S(1)}, bf16[8,80,128]{2,1,0:T(8,128)(2,1)}, bf16[136,128]{1,0:T(8,128)(2,1)S(1)}) custom-call(s32[1]{0:T(128)S(6)} %copy.23.count_ref, bf16[272,256]{1,0:T(8,128)(2,1)S(1)} %collective-permute-done.6.refs_0_, s32[4,8,256,128]{3,2,1,0:T(8,128)S(1)} %windows.1.refs_1_, ...), custom_call_target="tpu_custom_call" | custom-call | flops 3000000000 | bytes 4000000 | tf_op jit(solution)/shard_map/sources/pallas_call | solution.py:318
  29.0 4.7 %all-to-all-start = ((bf16[8,80,128]{2,1,0:T(8,128)(2,1)}), bf16[8,80,128]{2,1,0:T(8,128)(2,1)S(1)}, u32[]{:S(2)}, u32[]{:S(2)}) async-start(bf16[8,80,128]{2,1,0:T(8,128)(2,1)} %get-tuple-element.39), calls=%async_computation | async-start | bytes 327680 | tf_op jit(solution)/shard_map/all_to_all | solution.py:471
  33.7 2.0 %collective-permute-start.7 = (bf16[136,128]{1,0:T(8,128)(2,1)S(1)}, bf16[136,128]{1,0:T(8,128)(2,1)S(1)}, u32[]{:S(2)}, u32[]{:S(2)}) collective-permute-start(bf16[136,128]{1,0:T(8,128)(2,1)S(1)} %get-tuple-element.40), channel_id=1, source_target_pairs={{0,1},{1,2},{2,3},{3,4},{4,5},{5,6},{6,7},{7,0},{8,9},{9,10},{10,1... | collective-permute-start | bytes 104456 | tf_op jit(solution)/shard_map/ppermute | solution.py:472
  35.7 1.5 %nodes.1 = (f32[1032,128]{1,0:T(8,128)}, f32[136,128]{1,0:T(8,128)S(1)}) custom-call(bf16[1168,1024]{1,0:T(8,128)(2,1)S(1)} %corners.1.refs_7_.corner_ref, bf16[1024,128]{1,0:T(8,128)(2,1)S(1)} %get-tuple-element.41.loading_ref), custom_call_target="tpu_custom_call" | custom-call | flops 2000000000 | bytes 4000000 | tf_op jit(solution)/shard_map/nodes/pallas_call | solution.py:337
  37.2 5.6 %collective-permute-done.7.rim_ref = bf16[136,128]{1,0:T(8,128)(2,1)S(1)} collective-permute-done((bf16[136,128]{1,0:T(8,128)(2,1)S(1)}, bf16[136,128]{1,0:T(8,128)(2,1)S(1)}, u32[]{:S(2)}, u32[]{:S(2)}) %collective-permute-start.7) | collective-permute-done | bytes 34848 | tf_op jit(solution)/shard_map/ppermute | solution.py:472
  42.8 0.9 %finish.1 = (f32[1032,128]{1,0:T(8,128)}, f32[256,128]{1,0:T(8,128)}) custom-call(bf16[8,80,128]{2,1,0:T(8,128)(2,1)S(1)} %all-to-all-done.message_ref, bf16[136,128]{1,0:T(8,128)(2,1)S(1)} %collective-permute-done.7.rim_ref, f32[136,128]{1,0:T(8,128)S(1)} %get-tuple-element.42.head_ref, ...), custom_call_target="tpu_custom_call", output_to_operand_aliasing={{0}: (3, {})} | custom-call | flops 1000000 | bytes 4000000 | tf_op jit(solution)/shard_map/finish/pallas_call | solution.py:374
  (19 shorter events, 0.2 us)
Async XLA Ops:
  0.6 7.1 %copy-start = (bf16[32,256]{1,0:T(8,128)(2,1)S(1)}, bf16[32,256]{1,0:T(8,128)(2,1)}, u32[]{:S(2)}) copy-start(bf16[32,256]{1,0:T(8,128)(2,1)} %refs_0_.1) | copy-start | bytes 49156
  0.6 7.1 %copy-start.1 = (bf16[32,3]{0,1:T(4,128)(2,1)S(1)}, bf16[32,3]{0,1:T(4,128)(2,1)}, u32[]{:S(2)}) copy-start(bf16[32,3]{0,1:T(4,128)(2,1)} %param.8) | copy-start | bytes 580
  0.7 5.3 %collective-permute-start.1 = (bf16[3,32]{1,0:T(4,128)(2,1)}, bf16[3,32]{1,0:T(4,128)(2,1)S(1)}, u32[]{:S(2)}, u32[]{:S(2)}) collective-permute-start(bf16[3,32]{1,0:T(4,128)(2,1)} %bitcast.2), channel_id=1, source_target_pairs={{0,2},{1,3},{2,0},{3,1},{4,6},{5,7},{6,4},{7,5},{8,10},{9,11},{10,... | collective-permute-start | bytes 584 | tf_op jit(solution)/shard_map/ppermute | solution.py:390
  3.7 3.9 %collective-permute-start = (bf16[32,256]{1,0:T(8,128)(2,1)}, bf16[32,256]{1,0:T(8,128)(2,1)S(1)}, u32[]{:S(2)}, u32[]{:S(2)}) collective-permute-start(bf16[32,256]{1,0:T(8,128)(2,1)} %refs_0_.1), channel_id=1, source_target_pairs={{0,2},{1,3},{2,0},{3,1},{4,6},{5,7},{6,4},{7,5},{8,10},{9,11},{10,... | collective-permute-start | bytes 49160 | tf_op jit(solution)/shard_map/ppermute | solution.py:390
  3.8 0.8 %copy-start.2 = (s32[8,1024]{1,0:T(8,128)S(1)}, s32[8,1024]{1,0:T(8,128)}, u32[]{:S(2)}) copy-start(s32[8,1024]{1,0:T(8,128)} %delay_ref.1) | copy-start | bytes 98308
  4.6 5.8 %copy-start.3 = (f32[7,1024]{1,0:T(8,128)S(1)}, f32[7,1024]{1,0:T(8,128)}, u32[]{:S(2)}) copy-start(f32[7,1024]{1,0:T(8,128)} %geometry_ref) | copy-start | bytes 86020
  4.6 5.8 %copy-start.5 = (s32[1024]{0:T(1024)S(1)}, s32[1024]{0:T(1024)}, u32[]{:S(2)}) copy-start(s32[1024]{0:T(1024)} %param.13) | copy-start | bytes 12292
  7.8 5.1 %collective-permute-start.2 = (bf16[80,256]{1,0:T(8,128)(2,1)S(1)}, bf16[80,256]{1,0:T(8,128)(2,1)S(1)}, u32[]{:S(2)}, u32[]{:S(2)}) collective-permute-start(bf16[80,256]{1,0:T(8,128)(2,1)S(1)} %first.1.mine_ref), channel_id=1, source_target_pairs={{0,4},{1,5},{2,6},{3,7},{4,0},{5,1},{6,2},{7,3},{8,12},{9,13},{10,... | collective-permute-start | bytes 122888 | tf_op jit(solution)/shard_map/ppermute | solution.py:390
  12.9 4.4 %collective-permute-start.3 = (bf16[144,256]{1,0:T(8,128)(2,1)S(1)}, bf16[144,256]{1,0:T(8,128)(2,1)S(1)}, u32[]{:S(2)}, u32[]{:S(2)}) collective-permute-start(bf16[144,256]{1,0:T(8,128)(2,1)S(1)} %join.2.mine_ref.refs_0_), channel_id=1, source_target_pairs={{0,1},{1,0},{2,3},{3,2},{4,5},{5,4},{6,7},{7,6},{8,9},{9,8},{10,11... | collective-permute-start | bytes 221192 | tf_op jit(solution)/shard_map/ppermute | solution.py:390
  14.6 1.2 %copy-start.4 = (s32[4,1024]{1,0:T(4,128)S(1)}, s32[4,1024]{1,0:T(4,128)}, u32[]{:S(2)}) copy-start(s32[4,1024]{1,0:T(4,128)} %conn_ref) | copy-start | bytes 49156
  17.3 3.1 %collective-permute-start.5 = (bf16[272,256]{1,0:T(8,128)(2,1)S(1)}, bf16[272,256]{1,0:T(8,128)(2,1)S(1)}, u32[]{:S(2)}, u32[]{:S(2)}) collective-permute-start(bf16[272,256]{1,0:T(8,128)(2,1)S(1)} %join.3), channel_id=1, source_target_pairs={{0,8},{8,0},{16,24},{24,16},{1,9},{9,1},{17,25},{25,17},{2,10},{10... | collective-permute-start | bytes 417800 | tf_op jit(solution)/shard_map/ppermute | solution.py:390
  17.4 6.1 %collective-permute-start.4 = (bf16[272,256]{1,0:T(8,128)(2,1)S(1)}, bf16[272,256]{1,0:T(8,128)(2,1)S(1)}, u32[]{:S(2)}, u32[]{:S(2)}) collective-permute-start(bf16[272,256]{1,0:T(8,128)(2,1)S(1)} %join.3), channel_id=1, source_target_pairs={{0,16},{8,24},{16,0},{24,8},{1,17},{9,25},{17,1},{25,9},{2,18},{10... | collective-permute-start | bytes 417800 | tf_op jit(solution)/shard_map/ppermute | solution.py:390
  23.4 2.2 %collective-permute-start.6 = (bf16[272,256]{1,0:T(8,128)(2,1)S(1)}, bf16[272,256]{1,0:T(8,128)(2,1)S(1)}, u32[]{:S(2)}, u32[]{:S(2)}) collective-permute-start(bf16[272,256]{1,0:T(8,128)(2,1)S(1)} %collective-permute-done.4.refs_0_), channel_id=1, source_target_pairs={{0,8},{8,0},{16,24},{24,16},{1,9},{9,1},{17,25},{25,17},{2,10},{10... | collective-permute-start | bytes 417800 | tf_op jit(solution)/shard_map/ppermute | solution.py:390
  29.0 13.8 %all-to-all-start = ((bf16[8,80,128]{2,1,0:T(8,128)(2,1)}), bf16[8,80,128]{2,1,0:T(8,128)(2,1)S(1)}, u32[]{:S(2)}, u32[]{:S(2)}) async-start(bf16[8,80,128]{2,1,0:T(8,128)(2,1)} %get-tuple-element.39), calls=%async_computation | async-start | bytes 327680 | tf_op jit(solution)/shard_map/all_to_all | solution.py:471
  33.7 9.1 %collective-permute-start.7 = (bf16[136,128]{1,0:T(8,128)(2,1)S(1)}, bf16[136,128]{1,0:T(8,128)(2,1)S(1)}, u32[]{:S(2)}, u32[]{:S(2)}) collective-permute-start(bf16[136,128]{1,0:T(8,128)(2,1)S(1)} %get-tuple-element.40), channel_id=1, source_target_pairs={{0,1},{1,2},{2,3},{3,4},{4,5},{5,6},{6,7},{7,0},{8,9},{9,10},{10,1... | collective-permute-start | bytes 104456 | tf_op jit(solution)/shard_map/ppermute | solution.py:472

commit v7 on v6

--- a/solution.py
+++ b/solution.py
@@ -40,10 +40,8 @@
     )
 
 
-def window_kernel(sections, paired, delay_ref, source_ref):
+def window_kernel(delay_ref, source_ref):
     groups, blocks, span, _ = source_ref.shape
-    count = span // sections
-    piece_rows = count if paired else 128
     padded = -(-blocks // 16) * 16
     delay = delay_ref[...].astype(F32)
     delay = jnp.concatenate([delay, jnp.zeros((padded - blocks, delay.shape[1]), F32)], 0).astype(BF16)
@@ -57,21 +55,14 @@
         )
         for block in range(blocks):
             source = columns[:, block * 128 : (block + 1) * 128].astype(jnp.int32) + lanes
-            for part in range(128 // piece_rows):
-                row = piece * 128 + part * piece_rows
-                begin = row % span
-                if paired:
-                    apart = lax.axis_index("sect") ^ (begin // count)
-                    begin = pl.multiple_of((apart // 2 + apart % 2 * (sections // 2)) * count, count)
-                source_ref[row // span, block, pl.ds(begin, piece_rows), :] = source[
-                    part * piece_rows : (part + 1) * piece_rows
-                ]
-
-
-def window_index(sections, groups, paired, delays):
+            begin = piece * 128 % span
+            source_ref[piece * 128 // span, block, begin : begin + 128, :] = source
+
+
+def window_index(groups, delays):
     blocks, observers = delays.shape
     return call(
-        functools.partial(window_kernel, sections, paired),
+        window_kernel,
         "windows",
         jax.ShapeDtypeStruct((groups, blocks, observers // groups, 128), jnp.int32),
         [WHOLE],
@@ -175,28 +166,27 @@
     )(counts, connectivity)
 
 
-def first_join_kernel(*refs):
-    *inputs, chunk_ref, wide_ref = refs
-    parts = len(inputs) // 2
-    count = inputs[0].shape[0]
+def pack_kernel(signal_ref, point_ref, message_ref, wide_ref):
+    count = signal_ref.shape[0]
     wide_ref[...] = jnp.zeros_like(wide_ref)
-    total = jnp.zeros(wide_ref.shape, F32)
-    for part in range(parts):
-        chunk_ref[part * count : (part + 1) * count, :] = inputs[part][...]
-        wide_ref[:3, :count] = inputs[parts + part][...].astype(F32)
-        total = total + (pltpu.roll(wide_ref[...], part * count, 1) if part else wide_ref[...])
-    chunk_ref[parts * count :, :] = total.astype(BF16)
-
-
-def join_kernel(mine_ref, other_ref, chunk_ref):
-    span = mine_ref.shape[0] - EXTRA
-    chunk_ref[:span, :] = mine_ref[:span, :]
-    chunk_ref[span : 2 * span, :] = other_ref[:span, :]
-    moved = pltpu.roll(other_ref[span:, :].astype(F32), span, 1)
-    chunk_ref[2 * span :, :] = (mine_ref[span:, :].astype(F32) + moved).astype(BF16)
-
-
-def sources_kernel(places, first, last, count_ref, *refs):
+    wide_ref[:3, :count] = point_ref[...].astype(F32)
+    extra = pltpu.roll(wide_ref[...], lax.axis_index("sect") * count, 1).astype(BF16)
+    for section in range(message_ref.shape[0]):
+        message_ref[section, :count, :] = signal_ref[...]
+        message_ref[section, count:, :] = extra
+
+
+def join_kernel(message_ref, chunk_ref):
+    sections = message_ref.shape[0]
+    count = message_ref.shape[1] - EXTRA
+    total = jnp.zeros((EXTRA, message_ref.shape[2]), F32)
+    for section in range(sections):
+        chunk_ref[section * count : (section + 1) * count, :] = message_ref[section, :count, :]
+        total = total + message_ref[section, count:, :].astype(F32)
+    chunk_ref[sections * count :, :] = total.astype(BF16)
+
+
+def sources_kernel(offsets, first, last, count_ref, *refs):
     refs = list(refs)
 
     def take(number):
@@ -204,7 +194,7 @@
         del refs[:number]
         return taken
 
-    parts = len(places)
+    parts = len(offsets)
     chunks = take(parts)
     source_ref, panel_ref = take(2)
     if last:
@@ -232,11 +222,11 @@
 
     lanes = lax.broadcasted_iota(jnp.int32, (128, 128), 1)
     for block in range(blocks):
-        for number, (offset, begin) in enumerate(places):
+        for number, offset in enumerate(offsets):
             group = lax.axis_index("azim") ^ offset
             for piece in range(span // 128):
                 here = number * span + piece * 128
-                source = source_ref[group, block, begin + piece * 128 : begin + (piece + 1) * 128, :]
+                source = source_ref[group, block, piece * 128 : (piece + 1) * 128, :]
                 at = source & 127
                 code = jnp.take_along_axis(code_ref[here : here + 128, :], at, axis=1, mode="promise_in_bounds")
                 scale = scale_ref[here : here + 128, :]
@@ -247,22 +237,23 @@
                 window_ref[block, here : here + 128, :] = current
                 window_ref[block, observers + here : observers + here + 128, :] = following - current
 
-                at_x, at_y, at_z = (points[number][i : i + 1, piece * 128 : piece * 128 + 128] for i in range(3))
-                for strip in range(BLK // 16):
-                    rows = slice(strip * 16, strip * 16 + 16)
-                    delta_x = at_x - panel_ref[block, 0, rows, :]
-                    delta_y = at_y - panel_ref[block, 1, rows, :]
-                    delta_z = at_z - panel_ref[block, 2, rows, :]
-                    inverse = lax.rsqrt(delta_x * delta_x + delta_y * delta_y + delta_z * delta_z)
-                    flux = (
-                        panel_ref[block, 3, rows, :] * delta_x
-                        + panel_ref[block, 4, rows, :] * delta_y
-                        + panel_ref[block, 5, rows, :] * delta_z
-                    )
-                    far = flux * inverse * inverse
-                    pair_ref[block, rows, here : here + 128] = (far * inverse).astype(BF16)
-                    pair_ref[block, rows, observers + here : observers + here + 128] = far.astype(BF16)
-                    mass_ref[block, rows, here : here + 128] = (panel_ref[block, 6, rows, :] * inverse).astype(BF16)
+        for strip in range(BLK // 16):
+            rows = slice(strip * 16, strip * 16 + 16)
+            x, y, z, normal_x, normal_y, normal_z, area = (panel_ref[block, i, rows, :] for i in range(7))
+            for piece in range(observers // 128):
+                here = piece * 128
+                at_x, at_y, at_z = (
+                    points[here // span][i : i + 1, here % span : here % span + 128] for i in range(3)
+                )
+                delta_x = at_x - x
+                delta_y = at_y - y
+                delta_z = at_z - z
+                inverse = lax.rsqrt(delta_x * delta_x + delta_y * delta_y + delta_z * delta_z)
+                flux = normal_x * delta_x + normal_y * delta_y + normal_z * delta_z
+                far = flux * inverse * inverse
+                pair_ref[block, rows, here : here + 128] = (far * inverse).astype(BF16)
+                pair_ref[block, rows, observers + here : observers + here + 128] = far.astype(BF16)
+                mass_ref[block, rows, here : here + 128] = (area * inverse).astype(BF16)
         rows = slice(block * BLK, (block + 1) * BLK)
         thick = jnp.dot(mass_ref[block], window_ref[block, observers:, :], preferred_element_type=F32)
         loading = jnp.dot(pair_ref[block], window_ref[block], preferred_element_type=F32)
@@ -288,10 +279,10 @@
         rim_ref[...] = rim[8:].astype(BF16)
 
 
-def sources(places, counts, chunks, source, panel_values, sums=(), slots=None, sections=None):
+def sources(offsets, counts, chunks, source, panel_values, sums=(), slots=None, sections=None):
     blocks = source.shape[1]
     panels = panel_values.shape[0] * BLK
-    observers = len(places) * (chunks[0].shape[0] - EXTRA)
+    observers = len(offsets) * (chunks[0].shape[0] - EXTRA)
     last = slots is not None
     operands = [counts, *chunks, source, panel_values, *sums]
     scratch = [
@@ -316,7 +307,7 @@
         if sums:
             aliases = {len(operands) - 2: 0, len(operands) - 1: 1}
     return call(
-        functools.partial(sources_kernel, places, not sums, last),
+        functools.partial(sources_kernel, offsets, not sums, last),
         "sources",
         out_shape,
         [SMEM] + [WHOLE] * (len(operands) - 1),
@@ -390,64 +381,41 @@
     return lax.ppermute(array, axis, [(i, i ^ bit) for i in range(peers)])
 
 
-def joined(mine, other):
-    span = mine.shape[0] - EXTRA
-    shape = jax.ShapeDtypeStruct((2 * span + EXTRA, mine.shape[1]), BF16)
-    return call(join_kernel, "join", shape, [WHOLE] * 2, WHOLE)(mine, other)
-
-
-def half_chunk(signals, xyz, sections):
-    count, width = signals.shape
-    turned = xyz.T
-    shape = jax.ShapeDtypeStruct((2 * count + EXTRA, width), BF16)
-    chunk = call(first_join_kernel, "first", shape, [WHOLE] * 4, WHOLE, [VMEM((EXTRA, width), F32)])(
-        signals, swapped(signals, "sect", 2), turned, swapped(turned, "sect", 2)
-    )
-    bit = 4
-    while bit < sections:
-        chunk = joined(chunk, swapped(chunk, "sect", bit))
-        bit *= 2
-    return chunk
-
-
 def after(array, other):
     return lax.optimization_barrier((array, other))[0]
 
 
-def spread_chunk(signals, xyz, sections):
+def section_chunk(signals, xyz, sections):
     count, width = signals.shape
-    extra = jnp.zeros((EXTRA, width), BF16)
-    extra = lax.dynamic_update_slice(extra, xyz.T, (0, lax.axis_index("sect") * count))
-    payload = jnp.concatenate([signals, extra], 0)
-    everyone = jnp.broadcast_to(payload[None], (sections,) + payload.shape)
-    received = lax.all_to_all(everyone, "sect", split_axis=0, concat_axis=0, tiled=True)
+    span = sections * count
+    kernels = count % 16 == 0
+    if kernels:
+        shape = jax.ShapeDtypeStruct((sections, count + EXTRA, width), BF16)
+        message = call(pack_kernel, "pack", shape, [WHOLE] * 2, WHOLE, [VMEM((EXTRA, width), F32)])(signals, xyz.T)
+    else:
+        extra = jnp.zeros((EXTRA, width), BF16)
+        extra = lax.dynamic_update_slice(extra, xyz.T, (0, lax.axis_index("sect") * count))
+        message = jnp.broadcast_to(jnp.concatenate([signals, extra], 0), (sections, count + EXTRA, width))
+    message = lax.all_to_all(message, "sect", split_axis=0, concat_axis=0, tiled=True)
+    if kernels:
+        return call(join_kernel, "join", jax.ShapeDtypeStruct((span + EXTRA, width), BF16), [WHOLE], WHOLE)(message)
     return jnp.concatenate(
-        [received[:, :count].reshape(sections * count, -1), received[:, count:].astype(F32).sum(0).astype(BF16)], 0
+        [message[:, :count].reshape(span, width), message[:, count:].astype(F32).sum(0).astype(BF16)], 0
     )
 
 
 def per_device(signals, observer_xyz, panel_geometry, delays, counts, connectivity, owners):
     sections = lax.axis_size("sect")
     groups = lax.axis_size("azim")
-    count = signals.shape[0]
-    paired = count % 16 == 0 and sections % 2 == 0 and sections // 2 * count == 128
-
-    source = window_index(sections, groups, paired, delays)
-    panel_values, slots, ids = panel_columns(sections, counts, after(panel_geometry, source), owners)
-
-    def add(sums, places, chunks, *rest):
-        return sources(places, counts, chunks, source, panel_values, sums, *rest)
-
-    if paired:
-        half = half_chunk(signals, observer_xyz, sections)
-        other = swapped(half, "sect", 1)
-        corners = corner_matrix(counts, after(connectivity, half))
-        sums = add((), [(0, 0)], [half])
-        sums = after(sums, corners)
-        chunk = joined(half, other)
-    else:
-        chunk = spread_chunk(signals, observer_xyz, sections)
-        corners = corner_matrix(counts, connectivity)
+
+    source = window_index(groups, delays)
+    panel_values, slots, ids = panel_columns(sections, counts, panel_geometry, owners)
+    corners = corner_matrix(counts, connectivity)
+
+    def add(sums, offsets, chunks, *rest):
+        return sources(offsets, counts, chunks, source, panel_values, sums, *rest)
+
+    chunk = section_chunk(signals, observer_xyz, sections)
     near = swapped(chunk, "azim", 1)
     chunks = {0: chunk}
     bit = groups // 2
@@ -455,19 +423,16 @@
         for offset in list(chunks):
             chunks[offset ^ bit] = swapped(chunks[offset], "azim", bit)
         bit //= 2
-    if paired:
-        sums = add(sums, [(0, 128)], [other])
-    else:
-        sums = add((), [(0, 0)], [chunk])
-    sums = add(sums, [(1, 0)], [near])
+    sums = add((), [0], [chunk])
+    sums = add(sums, [1], [near])
     rest = [offset for offset in chunks if offset]
     for offset in rest:
         chunks[offset] = after(chunks[offset], sums[0])
         chunks[offset ^ 1] = swapped(chunks[offset], "azim", 1)
-    sums = add(sums, [(o, 0) for o in rest], [chunks[o] for o in rest])
+    sums = add(sums, rest, [chunks[o] for o in rest])
     rest = [offset ^ 1 for offset in rest]
     matrices = [slots, ids, corners]
-    loading, message, rim = add(sums, [(o, 0) for o in rest], [chunks[o] for o in rest], matrices, sections)
+    loading, message, rim = add(sums, rest, [chunks[o] for o in rest], matrices, sections)
     message = lax.all_to_all(message, "sect", split_axis=0, concat_axis=0, tiled=True)
     rim = lax.ppermute(rim, "sect", [(i, (i + 1) % sections) for i in range(sections)])
     nodes, head = node_sums(corners, loading)

time: 44 us -> 53.1 us (1.21)
  local copies, waits for them, and re-layouts: 0.78 us -> 13.7 us
  waiting for transfers between devices: 9.97 us -> 4.51 us
  starting transfers between devices: 16 us -> 17.1 us
    unnamed x12 -> x30, local copies, waits for them, and re-layouts: 0.78 us -> 13.7 us
    ppermute x7 -> x3, starting transfers between devices: 9.29 us -> 1.86 us  [swapped(): return lax.ppermute(array, axis, [(i, i ^ bit) for i in range(peers)])]
    all_to_all x0 -> x1, starting transfers between devices: none -> 7.28 us  [section_chunk(): lax.all_to_all(message, 'sect', split_axis=0, concat_axis=0, tiled=True)]
    ppermute x7 -> x3, waiting for transfers between devices: 4.4 us -> 0.01 us  [swapped(): return lax.ppermute(array, axis, [(i, i ^ bit) for i in range(peers)])]
    all_to_all x1, starting transfers between devices: 4.68 us -> 5.95 us  [per_device(): lax.all_to_all(message, 'sect', split_axis=0, concat_axis=0, tiled=True)]
    ppermute x1, waiting for transfers between devices: 5.57 us -> 4.46 us  [per_device(): lax.ppermute(rim, 'sect', [(i, (i + 1) % sections) for i in range(section...]
    pallas_call x9 -> x7, Pallas kernels: 11.1 us -> 11.3 us  [the longest x4 8.86 us: sources(): call(functools.partial(sources_kernel, offsets, not sums, last), 'sources...]
  transfers between devices with their start and end apart: 9 -> 6, of which waited for: 5 -> 1; matrix products, arithmetic and copies ran while one was open for 0% -> 0% of each run, Pallas kernels for 26% -> 20%
where the time goes in v7:
time: 53.1 us; the launch traced here: 52.5 us
  starting transfers between devices  17.1 us (32%)
  Pallas kernels  15.8 us (30%)
  local copies, waits for them, and re-layouts  13.7 us (26%)
  waiting for transfers between devices  4.51 us (8%)
  between operations  1.41 us (3%)
    unnamed x30, local copies, waits for them, and re-layouts  13.7 us
    pallas_call x4, Pallas kernels, sources(): call(functools.partial(sources_kernel, offsets, not sums, last), 'sources...  8.86 us
    all_to_all x1, starting transfers between devices, section_chunk(): lax.all_to_all(message, 'sect', split_axis=0, concat_axis=0, tiled=True)  7.28 us
    all_to_all x1, starting transfers between devices, per_device(): lax.all_to_all(message, 'sect', split_axis=0, concat_axis=0, tiled=True)  5.95 us
    ppermute x1, waiting for transfers between devices, per_device(): lax.ppermute(rim, 'sect', [(i, (i + 1) % sections) for i in range(section...  4.46 us
    ppermute x1, starting transfers between devices, per_device(): lax.ppermute(rim, 'sect', [(i, (i + 1) % sections) for i in range(section...  2.02 us
    ppermute x3, starting transfers between devices, swapped(): return lax.ppermute(array, axis, [(i, i ^ bit) for i in range(peers)])  1.86 us
    pallas_call x1, Pallas kernels, node_sums(): call(node_kernel, 'nodes', (jax.ShapeDtypeStruct((NODE_DEV, TW), F32), ja...  1.51 us
  transfers between devices with their start and end apart: 6, of which 1 were waited for; matrix products, arithmetic and copies ran while one was open for 0% of the time, Pallas kernels for 20%

profile of v7, /device:TPU:0, one launch (start us, length us, event | category | flops | bytes accessed | tf_op | source)
XLA Modules:
  0.0 52.5 jit_solution(6742211963999357054)
XLA Ops:
  0.6 0.7 %copy-done.7 = bf16[32,256]{1,0:T(8,128)(2,1)S(1)} copy-done((bf16[32,256]{1,0:T(8,128)(2,1)S(1)}, bf16[32,256]{1,0:T(8,128)(2,1)}, u32[]{:S(2)}) %copy-start.7) | copy-done | bytes 16408
  2.0 0.8 %pack.1 = bf16[8,48,256]{2,1,0:T(8,128)(2,1)} custom-call(bf16[32,256]{1,0:T(8,128)(2,1)S(1)} %copy-done.7, bf16[3,32]{1,0:T(4,128)(2,1)S(1)} %bitcast.2), custom_call_target="tpu_custom_call" | custom-call | flops 1000000 | bytes 4000000 | tf_op jit(solution)/shard_map/pack/pallas_call | solution.py:394
  2.8 7.3 %all-to-all-start = ((bf16[8,48,256]{2,1,0:T(8,128)(2,1)}), bf16[8,48,256]{2,1,0:T(8,128)(2,1)}, u32[]{:S(2)}, u32[]{:S(2)}) async-start(bf16[8,48,256]{2,1,0:T(8,128)(2,1)} %pack.1), calls=%async_computation | async-start | bytes 393216 | tf_op jit(solution)/shard_map/all_to_all | solution.py:399
  10.7 0.7 %copy-done.11 = s32[8,1024]{1,0:T(8,128)S(1)} copy-done((s32[8,1024]{1,0:T(8,128)S(1)}, s32[8,1024]{1,0:T(8,128)}, u32[]{:S(2)}) %copy-start.11) | copy-done | bytes 32792
  11.5 0.7 %windows.1.refs_1_ = s32[4,8,256,128]{3,2,1,0:T(8,128)S(1)} custom-call(s32[8,1024]{1,0:T(8,128)S(1)} %copy-done.11), custom_call_target="tpu_custom_call" | custom-call | flops 2000000000 | bytes 4000000 | tf_op jit(solution)/shard_map/windows/pallas_call | solution.py:64
  12.2 1.9 %copy-done = s32[4,8,256,128]{3,2,1,0:T(8,128)} copy-done((s32[4,8,256,128]{3,2,1,0:T(8,128)}, s32[4,8,256,128]{3,2,1,0:T(8,128)S(1)}, u32[]{:S(2)}) %copy-start) | copy-done | bytes 4194328
  14.2 1.0 %corners.1.refs_7_.corner_ref = bf16[1168,1024]{1,0:T(8,128)(2,1)S(1)} custom-call(s32[1]{0:T(128)S(6)} %copy.19.count_ref, s32[4,1024]{1,0:T(4,128)S(1)} %copy-done.13), custom_call_target="tpu_custom_call" | custom-call | flops 2000000000 | bytes 4000000 | tf_op jit(solution)/shard_map/corners/pallas_call | solution.py:159
  15.2 1.1 %columns.1 = (f32[8,7,128,128]{3,2,1,0:T(8,128)S(1)}, bf16[512,1024]{1,0:T(8,128)(2,1)S(1)}, f32[16,128]{1,0:T(8,128)S(1)}) custom-call(s32[1]{0:T(128)S(6)} %copy.19.count_ref, f32[7,1024]{1,0:T(8,128)S(1)} %copy-done.12, s32[1,1024]{1,0:T(1,128)S(1)} %bitcast.3), custom_call_target="tpu_custom_call" | custom-call | flops 2000000000 | bytes 4000000 | tf_op jit(solution)/shard_map/columns/pallas_call | solution.py:128
  16.3 1.8 %copy-done.3 = f32[8,7,128,128]{3,2,1,0:T(8,128)} copy-done((f32[8,7,128,128]{3,2,1,0:T(8,128)}, f32[8,7,128,128]{3,2,1,0:T(8,128)S(1)}, u32[]{:S(2)}) %copy-start.3) | copy-done | bytes 3670040
  18.1 0.9 %join.1.refs_0_ = bf16[272,256]{1,0:T(8,128)(2,1)S(1)} custom-call(bf16[8,48,256]{2,1,0:T(8,128)(2,1)} %all-to-all-done.message_ref), custom_call_target="tpu_custom_call" | custom-call | flops 1000000 | bytes 4000000 | tf_op jit(solution)/shard_map/join/pallas_call | solution.py:401
  19.2 1.6 %collective-permute-start = (bf16[272,256]{1,0:T(8,128)(2,1)S(1)}, bf16[272,256]{1,0:T(8,128)(2,1)S(1)}, u32[]{:S(2)}, u32[]{:S(2)}) collective-permute-start(bf16[272,256]{1,0:T(8,128)(2,1)S(1)} %join.1.refs_0_), channel_id=1, source_target_pairs={{0,16},{8,24},{16,0},{24,8},{1,17},{9,25},{17,1},{25,9},{2,18},{10... | collective-permute-start | bytes 417800 | tf_op jit(solution)/shard_map/ppermute | solution.py:381
  20.7 2.2 %copy-done.1 = s32[4,8,256,128]{3,2,1,0:T(8,128)S(1)} copy-done((s32[4,8,256,128]{3,2,1,0:T(8,128)S(1)}, s32[4,8,256,128]{3,2,1,0:T(8,128)}, u32[]{:S(2)}) %copy-start.1) | copy-done | bytes 4194328
  22.9 2.0 %copy-done.4 = f32[8,7,128,128]{3,2,1,0:T(8,128)S(1)} copy-done((f32[8,7,128,128]{3,2,1,0:T(8,128)S(1)}, f32[8,7,128,128]{3,2,1,0:T(8,128)}, u32[]{:S(2)}) %copy-start.4) | copy-done | bytes 3670040
  24.9 2.1 %sources.4 = (f32[1024,128]{1,0:T(8,128)S(1)}, f32[1024,128]{1,0:T(8,128)S(1)}) custom-call(s32[1]{0:T(128)S(6)} %copy.19.count_ref, bf16[272,256]{1,0:T(8,128)(2,1)S(1)} %join.1.refs_0_, s32[4,8,256,128]{3,2,1,0:T(8,128)S(1)} %copy-done.1, f32[8,7,128,128]{3,2,1,0:T(8,128)S(1)} %copy-done.4), custom_call_target="tpu_custom_call" | custom-call | flops 3000000000 | bytes 4000000 | tf_op jit(solution)/shard_map/sources/pallas_call | solution.py:309
  27.1 1.1 %copy-done.5 = f32[8,7,128,128]{3,2,1,0:T(8,128)S(1)} copy-done((f32[8,7,128,128]{3,2,1,0:T(8,128)S(1)}, f32[8,7,128,128]{3,2,1,0:T(8,128)}, u32[]{:S(2)}) %copy-start.5) | copy-done | bytes 3670040
  28.3 2.1 %sources.5 = (f32[1024,128]{1,0:T(8,128)S(1)}, f32[1024,128]{1,0:T(8,128)S(1)}) custom-call(s32[1]{0:T(128)S(6)} %copy.19.count_ref, bf16[272,256]{1,0:T(8,128)(2,1)S(1)} %collective-permute-done.1.refs_0_, s32[4,8,256,128]{3,2,1,0:T(8,128)S(1)} %copy-done.2, f32[8,7,128,128]{3,2,1,0:T(8,128)S(1)} %copy-done.5, ...), custom_call_target="tpu_custom_call", output_to_operand_aliasing={{0}: (4, {}), {1}: (5, {})} | custom-call | flops 3000000000 | bytes 4000000 | tf_op jit(solution)/shard_map/sources/pallas_call | solution.py:309
  30.6 2.1 %sources.6 = (f32[1024,128]{1,0:T(8,128)S(1)}, f32[1024,128]{1,0:T(8,128)S(1)}) custom-call(s32[1]{0:T(128)S(6)} %copy.19.count_ref, bf16[272,256]{1,0:T(8,128)(2,1)S(1)} %collective-permute-done.refs_0_, s32[4,8,256,128]{3,2,1,0:T(8,128)S(1)} %copy-done.2, f32[8,7,128,128]{3,2,1,0:T(8,128)S(1)} %copy-done.5, ...), custom_call_target="tpu_custom_call", output_to_operand_aliasing={{0}: (4, {}), {1}: (5, {})} | custom-call | flops 3000000000 | bytes 4000000 | tf_op jit(solution)/shard_map/sources/pallas_call | solution.py:309
  32.8 2.5 %sources.7 = (bf16[1024,128]{1,0:T(8,128)(2,1)S(1)}, bf16[8,80,128]{2,1,0:T(8,128)(2,1)S(1)}, bf16[136,128]{1,0:T(8,128)(2,1)S(1)}) custom-call(s32[1]{0:T(128)S(6)} %copy.19.count_ref, bf16[272,256]{1,0:T(8,128)(2,1)S(1)} %collective-permute-done.2.refs_0_, s32[4,8,256,128]{3,2,1,0:T(8,128)S(1)} %copy-done.2, f32[8,7,128,128]{3,2,1,0:T(8,128)S(1)} %copy-done.5, ...), custom_call_target="tpu_custom_call" | custom-call | flops 3000000000 | bytes 4000000 | tf_op jit(solution)/shard_map/sources/pallas_call | solution.py:309
  36.7 6.0 %all-to-all-start.1 = ((bf16[8,80,128]{2,1,0:T(8,128)(2,1)}), bf16[8,80,128]{2,1,0:T(8,128)(2,1)S(1)}, u32[]{:S(2)}, u32[]{:S(2)}) async-start(bf16[8,80,128]{2,1,0:T(8,128)(2,1)} %copy-done.6), calls=%async_computation.1 | async-start | bytes 327680 | tf_op jit(solution)/shard_map/all_to_all | solution.py:436
  42.7 2.0 %collective-permute-start.3 = (bf16[136,128]{1,0:T(8,128)(2,1)S(1)}, bf16[136,128]{1,0:T(8,128)(2,1)S(1)}, u32[]{:S(2)}, u32[]{:S(2)}) collective-permute-start(bf16[136,128]{1,0:T(8,128)(2,1)S(1)} %get-tuple-element.28), channel_id=1, source_target_pairs={{0,1},{1,2},{2,3},{3,4},{4,5},{5,6},{6,7},{7,0},{8,9},{9,10},{10,1... | collective-permute-start | bytes 104456 | tf_op jit(solution)/shard_map/ppermute | solution.py:437
  44.7 0.9 %copy-done.10 = bf16[1024,128]{1,0:T(8,128)(2,1)S(1)} copy-done((bf16[1024,128]{1,0:T(8,128)(2,1)S(1)}, bf16[1024,128]{1,0:T(8,128)(2,1)}, u32[]{:S(2)}) %copy-start.10) | copy-done | bytes 262168
  45.6 1.5 %nodes.1 = (f32[1032,128]{1,0:T(8,128)}, f32[136,128]{1,0:T(8,128)S(1)}) custom-call(bf16[1168,1024]{1,0:T(8,128)(2,1)S(1)} %corners.1.refs_7_.corner_ref, bf16[1024,128]{1,0:T(8,128)(2,1)S(1)} %copy-done.10), custom_call_target="tpu_custom_call" | custom-call | flops 2000000000 | bytes 4000000 | tf_op jit(solution)/shard_map/nodes/pallas_call | solution.py:328
  47.1 4.5 %collective-permute-done.3.rim_ref = bf16[136,128]{1,0:T(8,128)(2,1)S(1)} collective-permute-done((bf16[136,128]{1,0:T(8,128)(2,1)S(1)}, bf16[136,128]{1,0:T(8,128)(2,1)S(1)}, u32[]{:S(2)}, u32[]{:S(2)}) %collective-permute-start.3) | collective-permute-done | bytes 34848 | tf_op jit(solution)/shard_map/ppermute | solution.py:437
  51.6 0.9 %finish.1 = (f32[1032,128]{1,0:T(8,128)}, f32[256,128]{1,0:T(8,128)}) custom-call(bf16[8,80,128]{2,1,0:T(8,128)(2,1)S(1)} %all-to-all-done.1.message_ref, bf16[136,128]{1,0:T(8,128)(2,1)S(1)} %collective-permute-done.3.rim_ref, f32[136,128]{1,0:T(8,128)S(1)} %get-tuple-element.30.head_ref, ...), custom_call_target="tpu_custom_call", output_to_operand_aliasing={{0}: (3, {})} | custom-call | flops 1000000 | bytes 4000000 | tf_op jit(solution)/shard_map/finish/pallas_call | solution.py:365
  (29 shorter events, 2.5 us)
Async XLA Ops:
  0.6 0.7 %copy-start.7 = (bf16[32,256]{1,0:T(8,128)(2,1)S(1)}, bf16[32,256]{1,0:T(8,128)(2,1)}, u32[]{:S(2)}) copy-start(bf16[32,256]{1,0:T(8,128)(2,1)} %signal_ref.1) | copy-start | bytes 49156
  1.3 0.7 %copy-start.8 = (bf16[32,3]{0,1:T(4,128)(2,1)S(1)}, bf16[32,3]{0,1:T(4,128)(2,1)}, u32[]{:S(2)}) copy-start(bf16[32,3]{0,1:T(4,128)(2,1)} %param.8) | copy-start | bytes 580
  2.8 15.3 %all-to-all-start = ((bf16[8,48,256]{2,1,0:T(8,128)(2,1)}), bf16[8,48,256]{2,1,0:T(8,128)(2,1)}, u32[]{:S(2)}, u32[]{:S(2)}) async-start(bf16[8,48,256]{2,1,0:T(8,128)(2,1)} %pack.1), calls=%async_computation | async-start | bytes 393216 | tf_op jit(solution)/shard_map/all_to_all | solution.py:399
  10.7 0.8 %copy-start.11 = (s32[8,1024]{1,0:T(8,128)S(1)}, s32[8,1024]{1,0:T(8,128)}, u32[]{:S(2)}) copy-start(s32[8,1024]{1,0:T(8,128)} %delay_ref.1) | copy-start | bytes 98308
  11.5 2.7 %copy-start.13 = (s32[4,1024]{1,0:T(4,128)S(1)}, s32[4,1024]{1,0:T(4,128)}, u32[]{:S(2)}) copy-start(s32[4,1024]{1,0:T(4,128)} %conn_ref.1) | copy-start | bytes 49156
  12.2 1.9 %copy-start = (s32[4,8,256,128]{3,2,1,0:T(8,128)}, s32[4,8,256,128]{3,2,1,0:T(8,128)S(1)}, u32[]{:S(2)}) copy-start(s32[4,8,256,128]{3,2,1,0:T(8,128)S(1)} %windows.1.refs_1_) | copy-start | bytes 12582916
  14.2 1.0 %copy-start.12 = (f32[7,1024]{1,0:T(8,128)S(1)}, f32[7,1024]{1,0:T(8,128)}, u32[]{:S(2)}) copy-start(f32[7,1024]{1,0:T(8,128)} %geometry_ref.1) | copy-start | bytes 86020
  14.2 1.0 %copy-start.14 = (s32[1024]{0:T(1024)S(1)}, s32[1024]{0:T(1024)}, u32[]{:S(2)}) copy-start(s32[1024]{0:T(1024)} %param.13) | copy-start | bytes 12292
  16.3 1.8 %copy-start.3 = (f32[8,7,128,128]{3,2,1,0:T(8,128)}, f32[8,7,128,128]{3,2,1,0:T(8,128)S(1)}, u32[]{:S(2)}) copy-start(f32[8,7,128,128]{3,2,1,0:T(8,128)S(1)} %get-tuple-element.17.refs_2_) | copy-start | bytes 11010052
  19.1 7.9 %collective-permute-start.1 = (bf16[272,256]{1,0:T(8,128)(2,1)S(1)}, bf16[272,256]{1,0:T(8,128)(2,1)S(1)}, u32[]{:S(2)}, u32[]{:S(2)}) collective-permute-start(bf16[272,256]{1,0:T(8,128)(2,1)S(1)} %join.1.refs_0_), channel_id=1, source_target_pairs={{0,8},{8,0},{16,24},{24,16},{1,9},{9,1},{17,25},{25,17},{2,10},{10... | collective-permute-start | bytes 417800 | tf_op jit(solution)/shard_map/ppermute | solution.py:381
  19.2 11.2 %collective-permute-start = (bf16[272,256]{1,0:T(8,128)(2,1)S(1)}, bf16[272,256]{1,0:T(8,128)(2,1)S(1)}, u32[]{:S(2)}, u32[]{:S(2)}) collective-permute-start(bf16[272,256]{1,0:T(8,128)(2,1)S(1)} %join.1.refs_0_), channel_id=1, source_target_pairs={{0,16},{8,24},{16,0},{24,8},{1,17},{9,25},{17,1},{25,9},{2,18},{10... | collective-permute-start | bytes 417800 | tf_op jit(solution)/shard_map/ppermute | solution.py:381
  20.7 2.2 %copy-start.1 = (s32[4,8,256,128]{3,2,1,0:T(8,128)S(1)}, s32[4,8,256,128]{3,2,1,0:T(8,128)}, u32[]{:S(2)}) copy-start(s32[4,8,256,128]{3,2,1,0:T(8,128)} %copy-done) | copy-start | bytes 12582916
  22.9 2.0 %copy-start.4 = (f32[8,7,128,128]{3,2,1,0:T(8,128)S(1)}, f32[8,7,128,128]{3,2,1,0:T(8,128)}, u32[]{:S(2)}) copy-start(f32[8,7,128,128]{3,2,1,0:T(8,128)} %copy-done.3) | copy-start | bytes 11010052
  24.9 2.2 %copy-start.2 = (s32[4,8,256,128]{3,2,1,0:T(8,128)S(1)}, s32[4,8,256,128]{3,2,1,0:T(8,128)}, u32[]{:S(2)}) copy-start(s32[4,8,256,128]{3,2,1,0:T(8,128)} %copy-done) | copy-start | bytes 12582916
  24.9 3.3 %copy-start.5 = (f32[8,7,128,128]{3,2,1,0:T(8,128)S(1)}, f32[8,7,128,128]{3,2,1,0:T(8,128)}, u32[]{:S(2)}) copy-start(f32[8,7,128,128]{3,2,1,0:T(8,128)} %copy-done.3) | copy-start | bytes 11010052
  30.4 2.4 %collective-permute-start.2 = (bf16[272,256]{1,0:T(8,128)(2,1)S(1)}, bf16[272,256]{1,0:T(8,128)(2,1)S(1)}, u32[]{:S(2)}, u32[]{:S(2)}) collective-permute-start(bf16[272,256]{1,0:T(8,128)(2,1)S(1)} %collective-permute-done.refs_0_), channel_id=1, source_target_pairs={{0,8},{8,0},{16,24},{24,16},{1,9},{9,1},{17,25},{25,17},{2,10},{10... | collective-permute-start | bytes 417800 | tf_op jit(solution)/shard_map/ppermute | solution.py:381
  35.3 0.7 %copy-start.6 = (bf16[8,80,128]{2,1,0:T(8,128)(2,1)}, bf16[8,80,128]{2,1,0:T(8,128)(2,1)S(1)}, u32[]{:S(2)}) copy-start(bf16[8,80,128]{2,1,0:T(8,128)(2,1)S(1)} %get-tuple-element.27) | copy-start | bytes 491524
  36.0 0.7 %copy-start.9 = (bf16[1024,128]{1,0:T(8,128)(2,1)}, bf16[1024,128]{1,0:T(8,128)(2,1)S(1)}, u32[]{:S(2)}) copy-start(bf16[1024,128]{1,0:T(8,128)(2,1)S(1)} %get-tuple-element.29.loading_ref) | copy-start | bytes 786436
  36.7 14.9 %all-to-all-start.1 = ((bf16[8,80,128]{2,1,0:T(8,128)(2,1)}), bf16[8,80,128]{2,1,0:T(8,128)(2,1)S(1)}, u32[]{:S(2)}, u32[]{:S(2)}) async-start(bf16[8,80,128]{2,1,0:T(8,128)(2,1)} %copy-done.6), calls=%async_computation.1 | async-start | bytes 327680 | tf_op jit(solution)/shard_map/all_to_all | solution.py:436
  42.7 8.9 %collective-permute-start.3 = (bf16[136,128]{1,0:T(8,128)(2,1)S(1)}, bf16[136,128]{1,0:T(8,128)(2,1)S(1)}, u32[]{:S(2)}, u32[]{:S(2)}) collective-permute-start(bf16[136,128]{1,0:T(8,128)(2,1)S(1)} %get-tuple-element.28), channel_id=1, source_target_pairs={{0,1},{1,2},{2,3},{3,4},{4,5},{5,6},{6,7},{7,0},{8,9},{9,10},{10,1... | collective-permute-start | bytes 104456 | tf_op jit(solution)/shard_map/ppermute | solution.py:437
  44.7 0.9 %copy-start.10 = (bf16[1024,128]{1,0:T(8,128)(2,1)S(1)}, bf16[1024,128]{1,0:T(8,128)(2,1)}, u32[]{:S(2)}) copy-start(bf16[1024,128]{1,0:T(8,128)(2,1)} %copy-done.9) | copy-start | bytes 786436

commit v8 on v6

--- a/solution.py
+++ b/solution.py
@@ -62,7 +62,8 @@
                 begin = row % span
                 if paired:
                     apart = lax.axis_index("sect") ^ (begin // count)
-                    begin = pl.multiple_of((apart // 2 + apart % 2 * (sections // 2)) * count, count)
+                    turned = apart // 4 + apart // 2 % 2 * 2 + apart % 2 * 4
+                    begin = pl.multiple_of(turned * count, count)
                 source_ref[row // span, block, pl.ds(begin, piece_rows), :] = source[
                     part * piece_rows : (part + 1) * piece_rows
                 ]
@@ -247,22 +248,23 @@
                 window_ref[block, here : here + 128, :] = current
                 window_ref[block, observers + here : observers + here + 128, :] = following - current
 
-                at_x, at_y, at_z = (points[number][i : i + 1, piece * 128 : piece * 128 + 128] for i in range(3))
-                for strip in range(BLK // 16):
-                    rows = slice(strip * 16, strip * 16 + 16)
-                    delta_x = at_x - panel_ref[block, 0, rows, :]
-                    delta_y = at_y - panel_ref[block, 1, rows, :]
-                    delta_z = at_z - panel_ref[block, 2, rows, :]
-                    inverse = lax.rsqrt(delta_x * delta_x + delta_y * delta_y + delta_z * delta_z)
-                    flux = (
-                        panel_ref[block, 3, rows, :] * delta_x
-                        + panel_ref[block, 4, rows, :] * delta_y
-                        + panel_ref[block, 5, rows, :] * delta_z
-                    )
-                    far = flux * inverse * inverse
-                    pair_ref[block, rows, here : here + 128] = (far * inverse).astype(BF16)
-                    pair_ref[block, rows, observers + here : observers + here + 128] = far.astype(BF16)
-                    mass_ref[block, rows, here : here + 128] = (panel_ref[block, 6, rows, :] * inverse).astype(BF16)
+        for strip in range(BLK // 16):
+            rows = slice(strip * 16, strip * 16 + 16)
+            x, y, z, normal_x, normal_y, normal_z, area = (panel_ref[block, i, rows, :] for i in range(7))
+            for piece in range(observers // 128):
+                here = piece * 128
+                at_x, at_y, at_z = (
+                    points[here // span][i : i + 1, here % span : here % span + 128] for i in range(3)
+                )
+                delta_x = at_x - x
+                delta_y = at_y - y
+                delta_z = at_z - z
+                inverse = lax.rsqrt(delta_x * delta_x + delta_y * delta_y + delta_z * delta_z)
+                flux = normal_x * delta_x + normal_y * delta_y + normal_z * delta_z
+                far = flux * inverse * inverse
+                pair_ref[block, rows, here : here + 128] = (far * inverse).astype(BF16)
+                pair_ref[block, rows, observers + here : observers + here + 128] = far.astype(BF16)
+                mass_ref[block, rows, here : here + 128] = (area * inverse).astype(BF16)
         rows = slice(block * BLK, (block + 1) * BLK)
         thick = jnp.dot(mass_ref[block], window_ref[block, observers:, :], preferred_element_type=F32)
         loading = jnp.dot(pair_ref[block], window_ref[block], preferred_element_type=F32)
@@ -396,18 +398,14 @@
     return call(join_kernel, "join", shape, [WHOLE] * 2, WHOLE)(mine, other)
 
 
-def half_chunk(signals, xyz, sections):
+def half_chunk(signals, xyz):
     count, width = signals.shape
     turned = xyz.T
     shape = jax.ShapeDtypeStruct((2 * count + EXTRA, width), BF16)
     chunk = call(first_join_kernel, "first", shape, [WHOLE] * 4, WHOLE, [VMEM((EXTRA, width), F32)])(
-        signals, swapped(signals, "sect", 2), turned, swapped(turned, "sect", 2)
+        signals, swapped(signals, "sect", 4), turned, swapped(turned, "sect", 4)
     )
-    bit = 4
-    while bit < sections:
-        chunk = joined(chunk, swapped(chunk, "sect", bit))
-        bit *= 2
-    return chunk
+    return joined(chunk, swapped(chunk, "sect", 2))
 
 
 def after(array, other):
@@ -430,44 +428,41 @@
     sections = lax.axis_size("sect")
     groups = lax.axis_size("azim")
     count = signals.shape[0]
-    paired = count % 16 == 0 and sections % 2 == 0 and sections // 2 * count == 128
+    paired = sections == 8 and groups == 4 and count % 16 == 0
 
     source = window_index(sections, groups, paired, delays)
     panel_values, slots, ids = panel_columns(sections, counts, after(panel_geometry, source), owners)
 
-    def add(sums, places, chunks, *rest):
-        return sources(places, counts, chunks, source, panel_values, sums, *rest)
+    def add(sums, *parts, matrices=None):
+        places, chunks = [part[:2] for part in parts], [part[2] for part in parts]
+        return sources(places, counts, chunks, source, panel_values, sums, matrices, sections)
 
     if paired:
-        half = half_chunk(signals, observer_xyz, sections)
+        half = half_chunk(signals, observer_xyz)
         other = swapped(half, "sect", 1)
-        corners = corner_matrix(counts, after(connectivity, half))
-        sums = add((), [(0, 0)], [half])
-        sums = after(sums, corners)
-        chunk = joined(half, other)
+        near = swapped(half, "azim", 1)
+        sums = add((), (0, 0, half))
+        far = swapped(after(half, sums[0]), "azim", 2)
+        sums = add(sums, (1, 0, near))
+        far = after(far, sums[0])
+        far_near = swapped(far, "azim", 1)
+        other_near, other_far = swapped(other, "azim", 1), swapped(other, "azim", 2)
+        sums = add(sums, (0, 128, other), (1, 128, other_near), (2, 0, far), (3, 0, far_near))
+        corners = corner_matrix(counts, after(connectivity, sums[0]))
+        other_far = after(other_far, sums[0])
+        last = (3, 128, swapped(other_far, "azim", 1))
+        sums = add(sums, (2, 128, other_far))
     else:
         chunk = spread_chunk(signals, observer_xyz, sections)
         corners = corner_matrix(counts, connectivity)
-    near = swapped(chunk, "azim", 1)
-    chunks = {0: chunk}
-    bit = groups // 2
-    while bit > 1:
-        for offset in list(chunks):
-            chunks[offset ^ bit] = swapped(chunks[offset], "azim", bit)
-        bit //= 2
-    if paired:
-        sums = add(sums, [(0, 128)], [other])
-    else:
-        sums = add((), [(0, 0)], [chunk])
-    sums = add(sums, [(1, 0)], [near])
-    rest = [offset for offset in chunks if offset]
-    for offset in rest:
-        chunks[offset] = after(chunks[offset], sums[0])
-        chunks[offset ^ 1] = swapped(chunks[offset], "azim", 1)
-    sums = add(sums, [(o, 0) for o in rest], [chunks[o] for o in rest])
-    rest = [offset ^ 1 for offset in rest]
-    matrices = [slots, ids, corners]
-    loading, message, rim = add(sums, [(o, 0) for o in rest], [chunks[o] for o in rest], matrices, sections)
+        parts = [(0, 0, chunk)]
+        bit = groups // 2
+        while bit:
+            parts += [(offset ^ bit, 0, swapped(array, "azim", bit)) for offset, _, array in parts]
+            bit //= 2
+        *parts, last = parts
+        sums = add((), *parts)
+    loading, message, rim = add(sums, last, matrices=[slots, ids, corners])
     message = lax.all_to_all(message, "sect", split_axis=0, concat_axis=0, tiled=True)
     rim = lax.ppermute(rim, "sect", [(i, (i + 1) % sections) for i in range(sections)])
     nodes, head = node_sums(corners, loading)

time: 44 us -> 46 us (1.045)
  waiting for transfers between devices: 9.97 us -> 11.4 us
    ppermute x7 -> x10, starting transfers between devices: 9.29 us -> 11 us  [swapped(): return lax.ppermute(array, axis, [(i, i ^ bit) for i in range(peers)])]
    all_to_all x1, starting transfers between devices: 4.68 us -> 3.38 us  [per_device(): lax.all_to_all(message, 'sect', split_axis=0, concat_axis=0, tiled=True)]
    ppermute x7 -> x10, waiting for transfers between devices: 4.4 us -> 5.53 us  [swapped(): return lax.ppermute(array, axis, [(i, i ^ bit) for i in range(peers)])]
  transfers between devices with their start and end apart: 9 -> 12, of which waited for: 5 -> 4; matrix products, arithmetic and copies ran while one was open for 0% -> 0% of each run, Pallas kernels for 26% -> 27%
where the time goes in v8:
time: 46 us; the launch traced here: 45.7 us
  starting transfers between devices  16.3 us (35%)
  Pallas kernels  15.8 us (34%)
  waiting for transfers between devices  11.4 us (25%)
  between operations  1.42 us (3%)
  local copies, waits for them, and re-layouts  0.78 us (2%)
    ppermute x10, starting transfers between devices, swapped(): return lax.ppermute(array, axis, [(i, i ^ bit) for i in range(peers)])  11 us
    pallas_call x5, Pallas kernels, sources(): call(functools.partial(sources_kernel, places, not sums, last), 'sources'...  10.4 us
    ppermute x1, waiting for transfers between devices, per_device(): lax.ppermute(rim, 'sect', [(i, (i + 1) % sections) for i in range(section...  5.86 us
    ppermute x10, waiting for transfers between devices, swapped(): return lax.ppermute(array, axis, [(i, i ^ bit) for i in range(peers)])  5.53 us
    all_to_all x1, starting transfers between devices, per_device(): lax.all_to_all(message, 'sect', split_axis=0, concat_axis=0, tiled=True)  3.38 us
    ppermute x1, starting transfers between devices, per_device(): lax.ppermute(rim, 'sect', [(i, (i + 1) % sections) for i in range(section...  1.92 us
    pallas_call x1, Pallas kernels, node_sums(): call(node_kernel, 'nodes', (jax.ShapeDtypeStruct((NODE_DEV, TW), F32), ja...  1.51 us
    pallas_call x1, Pallas kernels, panel_columns(): call(functools.partial(column_kernel, sections), 'columns', (jax.ShapeDty...  1.11 us
  transfers between devices with their start and end apart: 12, of which 4 were waited for; matrix products, arithmetic and copies ran while one was open for 0% of the time, Pallas kernels for 27%

profile of v8, /device:TPU:0, one launch (start us, length us, event | category | flops | bytes accessed | tf_op | source)
XLA Modules:
  0.0 45.7 jit_solution(4492573511630689425)
XLA Ops:
  0.7 4.1 %collective-permute-start.1 = (bf16[3,32]{1,0:T(4,128)(2,1)}, bf16[3,32]{1,0:T(4,128)(2,1)S(1)}, u32[]{:S(2)}, u32[]{:S(2)}) collective-permute-start(bf16[3,32]{1,0:T(4,128)(2,1)} %bitcast.2), channel_id=1, source_target_pairs={{0,4},{1,5},{2,6},{3,7},{4,0},{5,1},{6,2},{7,3},{8,12},{9,13},{10,... | collective-permute-start | bytes 584 | tf_op jit(solution)/shard_map/ppermute | solution.py:392
  4.8 0.1 collective-permute-start
  4.8 0.8 %copy-done.2 = s32[8,1024]{1,0:T(8,128)S(1)} copy-done((s32[8,1024]{1,0:T(8,128)S(1)}, s32[8,1024]{1,0:T(8,128)}, u32[]{:S(2)}) %copy-start.2) | copy-done | bytes 32792
  5.6 0.7 %windows.1.refs_1_.refs_4_ = s32[4,8,256,128]{3,2,1,0:T(8,128)S(1)} custom-call(s32[8,1024]{1,0:T(8,128)S(1)} %copy-done.2), custom_call_target="tpu_custom_call" | custom-call | flops 2000000000 | bytes 4000000 | tf_op jit(solution)/shard_map/windows/pallas_call | solution.py:74
  7.0 2.6 %collective-permute-done.refs_1_ = bf16[32,256]{1,0:T(8,128)(2,1)S(1)} collective-permute-done((bf16[32,256]{1,0:T(8,128)(2,1)}, bf16[32,256]{1,0:T(8,128)(2,1)S(1)}, u32[]{:S(2)}, u32[]{:S(2)}) %collective-permute-start) | collective-permute-done | bytes 16416 | tf_op jit(solution)/shard_map/ppermute | solution.py:392
  9.7 1.6 %collective-permute-start.2 = (bf16[80,256]{1,0:T(8,128)(2,1)S(1)}, bf16[80,256]{1,0:T(8,128)(2,1)S(1)}, u32[]{:S(2)}, u32[]{:S(2)}) collective-permute-start(bf16[80,256]{1,0:T(8,128)(2,1)S(1)} %first.1.mine_ref), channel_id=1, source_target_pairs={{0,2},{1,3},{2,0},{3,1},{4,6},{5,7},{6,4},{7,5},{8,10},{9,11},{10,... | collective-permute-start | bytes 122888 | tf_op jit(solution)/shard_map/ppermute | solution.py:392
  11.3 1.1 %columns.1 = (f32[8,7,128,128]{3,2,1,0:T(8,128)S(1)}, bf16[512,1024]{1,0:T(8,128)(2,1)S(1)}, f32[16,128]{1,0:T(8,128)S(1)}) custom-call(s32[1]{0:T(128)S(6)} %copy.23.count_ref, f32[7,1024]{1,0:T(8,128)S(1)} %copy-done.3, s32[1,1024]{1,0:T(1,128)S(1)} %bitcast.4), custom_call_target="tpu_custom_call" | custom-call | flops 2000000000 | bytes 4000000 | tf_op jit(solution)/shard_map/columns/pallas_call | solution.py:138
  12.4 1.3 %collective-permute-done.2.other_ref = bf16[80,256]{1,0:T(8,128)(2,1)S(1)} collective-permute-done((bf16[80,256]{1,0:T(8,128)(2,1)S(1)}, bf16[80,256]{1,0:T(8,128)(2,1)S(1)}, u32[]{:S(2)}, u32[]{:S(2)}) %collective-permute-start.2) | collective-permute-done | bytes 40992 | tf_op jit(solution)/shard_map/ppermute | solution.py:392
  13.8 1.6 %collective-permute-start.3 = (bf16[144,256]{1,0:T(8,128)(2,1)S(1)}, bf16[144,256]{1,0:T(8,128)(2,1)S(1)}, u32[]{:S(2)}, u32[]{:S(2)}) collective-permute-start(bf16[144,256]{1,0:T(8,128)(2,1)S(1)} %join.1.refs_0_), channel_id=1, source_target_pairs={{0,1},{1,0},{2,3},{3,2},{4,5},{5,4},{6,7},{7,6},{8,9},{9,8},{10,11... | collective-permute-start | bytes 221192 | tf_op jit(solution)/shard_map/ppermute | solution.py:392
  15.4 1.2 %sources.5 = (f32[1024,128]{1,0:T(8,128)S(1)}, f32[1024,128]{1,0:T(8,128)S(1)}) custom-call(s32[1]{0:T(128)S(6)} %copy.23.count_ref, bf16[144,256]{1,0:T(8,128)(2,1)S(1)} %join.1.refs_0_, s32[4,8,256,128]{3,2,1,0:T(8,128)S(1)} %windows.1.refs_1_.refs_4_, f32[8,7,128,128]{3,2,1,0:T(8,128)S(1)} %get-tuple-element.24.refs_2_.refs_5_), custom_call_target="tpu_custom_call" | custom-call | flops 3000000000 | bytes 4000000 | tf_op jit(solution)/shard_map/sources/pallas_call | solution.py:320
  16.5 1.6 %collective-permute-start.6 = (bf16[144,256]{1,0:T(8,128)(2,1)S(1)}, bf16[144,256]{1,0:T(8,128)(2,1)S(1)}, u32[]{:S(2)}, u32[]{:S(2)}) collective-permute-start(bf16[144,256]{1,0:T(8,128)(2,1)S(1)} %join.1.refs_0_), channel_id=1, source_target_pairs={{0,16},{8,24},{16,0},{24,8},{1,17},{9,25},{17,1},{25,9},{2,18},{10... | collective-permute-start | bytes 221192 | tf_op jit(solution)/shard_map/ppermute | solution.py:392
  18.1 1.2 %sources.6 = (f32[1024,128]{1,0:T(8,128)S(1)}, f32[1024,128]{1,0:T(8,128)S(1)}) custom-call(s32[1]{0:T(128)S(6)} %copy.23.count_ref, bf16[144,256]{1,0:T(8,128)(2,1)S(1)} %collective-permute-done.7.refs_0_, s32[4,8,256,128]{3,2,1,0:T(8,128)S(1)} %windows.1.refs_1_.refs_4_, ...), custom_call_target="tpu_custom_call", output_to_operand_aliasing={{0}: (4, {}), {1}: (5, {})} | custom-call | flops 3000000000 | bytes 4000000 | tf_op jit(solution)/shard_map/sources/pallas_call | solution.py:320
  19.4 1.6 %collective-permute-done.6.refs_2_ = bf16[144,256]{1,0:T(8,128)(2,1)S(1)} collective-permute-done((bf16[144,256]{1,0:T(8,128)(2,1)S(1)}, bf16[144,256]{1,0:T(8,128)(2,1)S(1)}, u32[]{:S(2)}, u32[]{:S(2)}) %collective-permute-start.6) | collective-permute-done | bytes 73760 | tf_op jit(solution)/shard_map/ppermute | solution.py:392
  21.0 0.5 %collective-permute-start.8 = (bf16[144,256]{1,0:T(8,128)(2,1)S(1)}, bf16[144,256]{1,0:T(8,128)(2,1)S(1)}, u32[]{:S(2)}, u32[]{:S(2)}) collective-permute-start(bf16[144,256]{1,0:T(8,128)(2,1)S(1)} %collective-permute-done.6.refs_2_), channel_id=1, source_target_pairs={{0,8},{8,0},{16,24},{24,16},{1,9},{9,1},{17,25},{25,17},{2,10},{10... | collective-permute-start | bytes 221192 | tf_op jit(solution)/shard_map/ppermute | solution.py:392
  21.5 1.5 %collective-permute-start.4 = (bf16[144,256]{1,0:T(8,128)(2,1)S(1)}, bf16[144,256]{1,0:T(8,128)(2,1)S(1)}, u32[]{:S(2)}, u32[]{:S(2)}) collective-permute-start(bf16[144,256]{1,0:T(8,128)(2,1)S(1)} %collective-permute-done.3.refs_0_), channel_id=1, source_target_pairs={{0,16},{8,24},{16,0},{24,8},{1,17},{9,25},{17,1},{25,9},{2,18},{10... | collective-permute-start | bytes 221192 | tf_op jit(solution)/shard_map/ppermute | solution.py:392
  23.0 4.6 %sources.7 = (f32[1024,128]{1,0:T(8,128)S(1)}, f32[1024,128]{1,0:T(8,128)S(1)}) custom-call(s32[1]{0:T(128)S(6)} %copy.23.count_ref, bf16[144,256]{1,0:T(8,128)(2,1)S(1)} %collective-permute-done.3.refs_0_, bf16[144,256]{1,0:T(8,128)(2,1)S(1)} %collective-permute-done.5.refs_1_, ...), custom_call_target="tpu_custom_call", output_to_operand_aliasing={{0}: (7, {}), {1}: (8, {})} | custom-call | flops 3000000000 | bytes 4000000 | tf_op jit(solution)/shard_map/sources/pallas_call | solution.py:320
  27.6 1.2 %sources.8 = (f32[1024,128]{1,0:T(8,128)S(1)}, f32[1024,128]{1,0:T(8,128)S(1)}) custom-call(s32[1]{0:T(128)S(6)} %copy.23.count_ref, bf16[144,256]{1,0:T(8,128)(2,1)S(1)} %collective-permute-done.4.refs_0_, s32[4,8,256,128]{3,2,1,0:T(8,128)S(1)} %windows.1.refs_1_.refs_4_, ...), custom_call_target="tpu_custom_call", output_to_operand_aliasing={{0}: (4, {}), {1}: (5, {})} | custom-call | flops 3000000000 | bytes 4000000 | tf_op jit(solution)/shard_map/sources/pallas_call | solution.py:320
  28.9 1.0 %corners.1.refs_7_.corner_ref = bf16[1168,1024]{1,0:T(8,128)(2,1)S(1)} custom-call(s32[1]{0:T(128)S(6)} %copy.23.count_ref, s32[4,1024]{1,0:T(4,128)S(1)} %copy-done.4), custom_call_target="tpu_custom_call" | custom-call | flops 2000000000 | bytes 4000000 | tf_op jit(solution)/shard_map/corners/pallas_call | solution.py:169
  29.9 2.2 %sources.9 = (bf16[1024,128]{1,0:T(8,128)(2,1)S(1)}, bf16[8,80,128]{2,1,0:T(8,128)(2,1)}, bf16[136,128]{1,0:T(8,128)(2,1)S(1)}) custom-call(s32[1]{0:T(128)S(6)} %copy.23.count_ref, bf16[144,256]{1,0:T(8,128)(2,1)S(1)} %collective-permute-done.9.refs_0_, s32[4,8,256,128]{3,2,1,0:T(8,128)S(1)} %windows.1.refs_1_.refs_4_, ...), custom_call_target="tpu_custom_call" | custom-call | flops 3000000000 | bytes 4000000 | tf_op jit(solution)/shard_map/sources/pallas_call | solution.py:320
  32.1 3.4 %all-to-all-start = ((bf16[8,80,128]{2,1,0:T(8,128)(2,1)}), bf16[8,80,128]{2,1,0:T(8,128)(2,1)S(1)}, u32[]{:S(2)}, u32[]{:S(2)}) async-start(bf16[8,80,128]{2,1,0:T(8,128)(2,1)} %get-tuple-element.39), calls=%async_computation | async-start | bytes 327680 | tf_op jit(solution)/shard_map/all_to_all | solution.py:466
  35.5 1.9 %collective-permute-start.10 = (bf16[136,128]{1,0:T(8,128)(2,1)S(1)}, bf16[136,128]{1,0:T(8,128)(2,1)S(1)}, u32[]{:S(2)}, u32[]{:S(2)}) collective-permute-start(bf16[136,128]{1,0:T(8,128)(2,1)S(1)} %get-tuple-element.40), channel_id=1, source_target_pairs={{0,1},{1,2},{2,3},{3,4},{4,5},{5,6},{6,7},{7,0},{8,9},{9,10},{10,1... | collective-permute-start | bytes 104456 | tf_op jit(solution)/shard_map/ppermute | solution.py:467
  37.4 1.5 %nodes.1 = (f32[1032,128]{1,0:T(8,128)}, f32[136,128]{1,0:T(8,128)S(1)}) custom-call(bf16[1168,1024]{1,0:T(8,128)(2,1)S(1)} %corners.1.refs_7_.corner_ref, bf16[1024,128]{1,0:T(8,128)(2,1)S(1)} %get-tuple-element.41.loading_ref), custom_call_target="tpu_custom_call" | custom-call | flops 2000000000 | bytes 4000000 | tf_op jit(solution)/shard_map/nodes/pallas_call | solution.py:339
  38.9 5.9 %collective-permute-done.10.rim_ref = bf16[136,128]{1,0:T(8,128)(2,1)S(1)} collective-permute-done((bf16[136,128]{1,0:T(8,128)(2,1)S(1)}, bf16[136,128]{1,0:T(8,128)(2,1)S(1)}, u32[]{:S(2)}, u32[]{:S(2)}) %collective-permute-start.10) | collective-permute-done | bytes 34848 | tf_op jit(solution)/shard_map/ppermute | solution.py:467
  44.8 0.9 %finish.1 = (f32[1032,128]{1,0:T(8,128)}, f32[256,128]{1,0:T(8,128)}) custom-call(bf16[8,80,128]{2,1,0:T(8,128)(2,1)S(1)} %all-to-all-done.message_ref, bf16[136,128]{1,0:T(8,128)(2,1)S(1)} %collective-permute-done.10.rim_ref, f32[136,128]{1,0:T(8,128)S(1)} %get-tuple-element.42.head_ref, ...), custom_call_target="tpu_custom_call", output_to_operand_aliasing={{0}: (3, {})} | custom-call | flops 1000000 | bytes 4000000 | tf_op jit(solution)/shard_map/finish/pallas_call | solution.py:376
  (24 shorter events, 0.3 us)
Async XLA Ops:
  0.6 9.0 %copy-start = (bf16[32,256]{1,0:T(8,128)(2,1)S(1)}, bf16[32,256]{1,0:T(8,128)(2,1)}, u32[]{:S(2)}) copy-start(bf16[32,256]{1,0:T(8,128)(2,1)} %refs_0_.1) | copy-start | bytes 49156
  0.6 9.0 %copy-start.1 = (bf16[32,3]{0,1:T(4,128)(2,1)S(1)}, bf16[32,3]{0,1:T(4,128)(2,1)}, u32[]{:S(2)}) copy-start(bf16[32,3]{0,1:T(4,128)(2,1)} %param.8) | copy-start | bytes 580
  0.7 6.3 %collective-permute-start.1 = (bf16[3,32]{1,0:T(4,128)(2,1)}, bf16[3,32]{1,0:T(4,128)(2,1)S(1)}, u32[]{:S(2)}, u32[]{:S(2)}) collective-permute-start(bf16[3,32]{1,0:T(4,128)(2,1)} %bitcast.2), channel_id=1, source_target_pairs={{0,4},{1,5},{2,6},{3,7},{4,0},{5,1},{6,2},{7,3},{8,12},{9,13},{10,... | collective-permute-start | bytes 584 | tf_op jit(solution)/shard_map/ppermute | solution.py:392
  4.8 4.8 %collective-permute-start = (bf16[32,256]{1,0:T(8,128)(2,1)}, bf16[32,256]{1,0:T(8,128)(2,1)S(1)}, u32[]{:S(2)}, u32[]{:S(2)}) collective-permute-start(bf16[32,256]{1,0:T(8,128)(2,1)} %refs_0_.1), channel_id=1, source_target_pairs={{0,4},{1,5},{2,6},{3,7},{4,0},{5,1},{6,2},{7,3},{8,12},{9,13},{10,... | collective-permute-start | bytes 49160 | tf_op jit(solution)/shard_map/ppermute | solution.py:392
  4.8 0.8 %copy-start.2 = (s32[8,1024]{1,0:T(8,128)S(1)}, s32[8,1024]{1,0:T(8,128)}, u32[]{:S(2)}) copy-start(s32[8,1024]{1,0:T(8,128)} %delay_ref.1) | copy-start | bytes 98308
  5.6 5.7 %copy-start.3 = (f32[7,1024]{1,0:T(8,128)S(1)}, f32[7,1024]{1,0:T(8,128)}, u32[]{:S(2)}) copy-start(f32[7,1024]{1,0:T(8,128)} %geometry_ref) | copy-start | bytes 86020
  5.6 5.7 %copy-start.5 = (s32[1024]{0:T(1024)S(1)}, s32[1024]{0:T(1024)}, u32[]{:S(2)}) copy-start(s32[1024]{0:T(1024)} %param.13) | copy-start | bytes 12292
  9.7 4.0 %collective-permute-start.2 = (bf16[80,256]{1,0:T(8,128)(2,1)S(1)}, bf16[80,256]{1,0:T(8,128)(2,1)S(1)}, u32[]{:S(2)}, u32[]{:S(2)}) collective-permute-start(bf16[80,256]{1,0:T(8,128)(2,1)S(1)} %first.1.mine_ref), channel_id=1, source_target_pairs={{0,2},{1,3},{2,0},{3,1},{4,6},{5,7},{6,4},{7,5},{8,10},{9,11},{10,... | collective-permute-start | bytes 122888 | tf_op jit(solution)/shard_map/ppermute | solution.py:392
  13.8 4.3 %collective-permute-start.7 = (bf16[144,256]{1,0:T(8,128)(2,1)S(1)}, bf16[144,256]{1,0:T(8,128)(2,1)S(1)}, u32[]{:S(2)}, u32[]{:S(2)}) collective-permute-start(bf16[144,256]{1,0:T(8,128)(2,1)S(1)} %join.1.refs_0_), channel_id=1, source_target_pairs={{0,8},{8,0},{16,24},{24,16},{1,9},{9,1},{17,25},{25,17},{2,10},{10... | collective-permute-start | bytes 221192 | tf_op jit(solution)/shard_map/ppermute | solution.py:392
  13.8 7.2 %collective-permute-start.3 = (bf16[144,256]{1,0:T(8,128)(2,1)S(1)}, bf16[144,256]{1,0:T(8,128)(2,1)S(1)}, u32[]{:S(2)}, u32[]{:S(2)}) collective-permute-start(bf16[144,256]{1,0:T(8,128)(2,1)S(1)} %join.1.refs_0_), channel_id=1, source_target_pairs={{0,1},{1,0},{2,3},{3,2},{4,5},{5,4},{6,7},{7,6},{8,9},{9,8},{10,11... | collective-permute-start | bytes 221192 | tf_op jit(solution)/shard_map/ppermute | solution.py:392
  16.5 4.4 %collective-permute-start.6 = (bf16[144,256]{1,0:T(8,128)(2,1)S(1)}, bf16[144,256]{1,0:T(8,128)(2,1)S(1)}, u32[]{:S(2)}, u32[]{:S(2)}) collective-permute-start(bf16[144,256]{1,0:T(8,128)(2,1)S(1)} %join.1.refs_0_), channel_id=1, source_target_pairs={{0,16},{8,24},{16,0},{24,8},{1,17},{9,25},{17,1},{25,9},{2,18},{10... | collective-permute-start | bytes 221192 | tf_op jit(solution)/shard_map/ppermute | solution.py:392
  21.0 2.0 %collective-permute-start.5 = (bf16[144,256]{1,0:T(8,128)(2,1)S(1)}, bf16[144,256]{1,0:T(8,128)(2,1)S(1)}, u32[]{:S(2)}, u32[]{:S(2)}) collective-permute-start(bf16[144,256]{1,0:T(8,128)(2,1)S(1)} %collective-permute-done.3.refs_0_), channel_id=1, source_target_pairs={{0,8},{8,0},{16,24},{24,16},{1,9},{9,1},{17,25},{25,17},{2,10},{10... | collective-permute-start | bytes 221192 | tf_op jit(solution)/shard_map/ppermute | solution.py:392
  21.0 2.0 %collective-permute-start.8 = (bf16[144,256]{1,0:T(8,128)(2,1)S(1)}, bf16[144,256]{1,0:T(8,128)(2,1)S(1)}, u32[]{:S(2)}, u32[]{:S(2)}) collective-permute-start(bf16[144,256]{1,0:T(8,128)(2,1)S(1)} %collective-permute-done.6.refs_2_), channel_id=1, source_target_pairs={{0,8},{8,0},{16,24},{24,16},{1,9},{9,1},{17,25},{25,17},{2,10},{10... | collective-permute-start | bytes 221192 | tf_op jit(solution)/shard_map/ppermute | solution.py:392
  21.5 6.1 %collective-permute-start.4 = (bf16[144,256]{1,0:T(8,128)(2,1)S(1)}, bf16[144,256]{1,0:T(8,128)(2,1)S(1)}, u32[]{:S(2)}, u32[]{:S(2)}) collective-permute-start(bf16[144,256]{1,0:T(8,128)(2,1)S(1)} %collective-permute-done.3.refs_0_), channel_id=1, source_target_pairs={{0,16},{8,24},{16,0},{24,8},{1,17},{9,25},{17,1},{25,9},{2,18},{10... | collective-permute-start | bytes 221192 | tf_op jit(solution)/shard_map/ppermute | solution.py:392
  27.5 2.3 %collective-permute-start.9 = (bf16[144,256]{1,0:T(8,128)(2,1)S(1)}, bf16[144,256]{1,0:T(8,128)(2,1)S(1)}, u32[]{:S(2)}, u32[]{:S(2)}) collective-permute-start(bf16[144,256]{1,0:T(8,128)(2,1)S(1)} %collective-permute-done.4.refs_0_), channel_id=1, source_target_pairs={{0,8},{8,0},{16,24},{24,16},{1,9},{9,1},{17,25},{25,17},{2,10},{10... | collective-permute-start | bytes 221192 | tf_op jit(solution)/shard_map/ppermute | solution.py:392
  27.6 1.3 %copy-start.4 = (s32[4,1024]{1,0:T(4,128)S(1)}, s32[4,1024]{1,0:T(4,128)}, u32[]{:S(2)}) copy-start(s32[4,1024]{1,0:T(4,128)} %conn_ref) | copy-start | bytes 49156
  32.1 12.7 %all-to-all-start = ((bf16[8,80,128]{2,1,0:T(8,128)(2,1)}), bf16[8,80,128]{2,1,0:T(8,128)(2,1)S(1)}, u32[]{:S(2)}, u32[]{:S(2)}) async-start(bf16[8,80,128]{2,1,0:T(8,128)(2,1)} %get-tuple-element.39), calls=%async_computation | async-start | bytes 327680 | tf_op jit(solution)/shard_map/all_to_all | solution.py:466
  35.5 9.3 %collective-permute-start.10 = (bf16[136,128]{1,0:T(8,128)(2,1)S(1)}, bf16[136,128]{1,0:T(8,128)(2,1)S(1)}, u32[]{:S(2)}, u32[]{:S(2)}) collective-permute-start(bf16[136,128]{1,0:T(8,128)(2,1)S(1)} %get-tuple-element.40), channel_id=1, source_target_pairs={{0,1},{1,2},{2,3},{3,4},{4,5},{5,6},{6,7},{7,0},{8,9},{9,10},{10,1... | collective-permute-start | bytes 104456 | tf_op jit(solution)/shard_map/ppermute | solution.py:467

commit v9 on v6

--- a/solution.py
+++ b/solution.py
@@ -247,22 +247,23 @@
                 window_ref[block, here : here + 128, :] = current
                 window_ref[block, observers + here : observers + here + 128, :] = following - current
 
-                at_x, at_y, at_z = (points[number][i : i + 1, piece * 128 : piece * 128 + 128] for i in range(3))
-                for strip in range(BLK // 16):
-                    rows = slice(strip * 16, strip * 16 + 16)
-                    delta_x = at_x - panel_ref[block, 0, rows, :]
-                    delta_y = at_y - panel_ref[block, 1, rows, :]
-                    delta_z = at_z - panel_ref[block, 2, rows, :]
-                    inverse = lax.rsqrt(delta_x * delta_x + delta_y * delta_y + delta_z * delta_z)
-                    flux = (
-                        panel_ref[block, 3, rows, :] * delta_x
-                        + panel_ref[block, 4, rows, :] * delta_y
-                        + panel_ref[block, 5, rows, :] * delta_z
-                    )
-                    far = flux * inverse * inverse
-                    pair_ref[block, rows, here : here + 128] = (far * inverse).astype(BF16)
-                    pair_ref[block, rows, observers + here : observers + here + 128] = far.astype(BF16)
-                    mass_ref[block, rows, here : here + 128] = (panel_ref[block, 6, rows, :] * inverse).astype(BF16)
+        for strip in range(BLK // 16):
+            rows = slice(strip * 16, strip * 16 + 16)
+            x, y, z, normal_x, normal_y, normal_z, area = (panel_ref[block, i, rows, :] for i in range(7))
+            for piece in range(observers // 128):
+                here = piece * 128
+                at_x, at_y, at_z = (
+                    points[here // span][i : i + 1, here % span : here % span + 128] for i in range(3)
+                )
+                delta_x = at_x - x
+                delta_y = at_y - y
+                delta_z = at_z - z
+                inverse = lax.rsqrt(delta_x * delta_x + delta_y * delta_y + delta_z * delta_z)
+                flux = normal_x * delta_x + normal_y * delta_y + normal_z * delta_z
+                far = flux * inverse * inverse
+                pair_ref[block, rows, here : here + 128] = (far * inverse).astype(BF16)
+                pair_ref[block, rows, observers + here : observers + here + 128] = far.astype(BF16)
+                mass_ref[block, rows, here : here + 128] = (area * inverse).astype(BF16)
         rows = slice(block * BLK, (block + 1) * BLK)
         thick = jnp.dot(mass_ref[block], window_ref[block, observers:, :], preferred_element_type=F32)
         loading = jnp.dot(pair_ref[block], window_ref[block], preferred_element_type=F32)

time: 44 us -> 44 us (level)
  no operation moved by 1% of the time
where the time goes in v9:
time: 44 us; the launch traced here: 43.7 us
  starting transfers between devices  16 us (36%)
  Pallas kernels  15.5 us (35%)
  waiting for transfers between devices  10 us (23%)
  between operations  1.39 us (3%)
  local copies, waits for them, and re-layouts  0.78 us (2%)
    pallas_call x5, Pallas kernels, sources(): call(functools.partial(sources_kernel, places, not sums, last), 'sources'...  10.1 us
    ppermute x7, starting transfers between devices, swapped(): return lax.ppermute(array, axis, [(i, i ^ bit) for i in range(peers)])  9.29 us
    ppermute x1, waiting for transfers between devices, per_device(): lax.ppermute(rim, 'sect', [(i, (i + 1) % sections) for i in range(section...  5.57 us
    all_to_all x1, starting transfers between devices, per_device(): lax.all_to_all(message, 'sect', split_axis=0, concat_axis=0, tiled=True)  4.68 us
    ppermute x7, waiting for transfers between devices, swapped(): return lax.ppermute(array, axis, [(i, i ^ bit) for i in range(peers)])  4.43 us
    ppermute x1, starting transfers between devices, per_device(): lax.ppermute(rim, 'sect', [(i, (i + 1) % sections) for i in range(section...  2.02 us
    pallas_call x1, Pallas kernels, node_sums(): call(node_kernel, 'nodes', (jax.ShapeDtypeStruct((NODE_DEV, TW), F32), ja...  1.51 us
    pallas_call x1, Pallas kernels, panel_columns(): call(functools.partial(column_kernel, sections), 'columns', (jax.ShapeDty...  1.11 us
  transfers between devices with their start and end apart: 9, of which 5 were waited for; matrix products, arithmetic and copies ran while one was open for 0% of the time, Pallas kernels for 26%

profile of v9, /device:TPU:0, one launch (start us, length us, event | category | flops | bytes accessed | tf_op | source)
XLA Modules:
  0.0 43.7 jit_solution(3464250701805177462)
XLA Ops:
  0.7 3.1 %collective-permute-start.1 = (bf16[3,32]{1,0:T(4,128)(2,1)}, bf16[3,32]{1,0:T(4,128)(2,1)S(1)}, u32[]{:S(2)}, u32[]{:S(2)}) collective-permute-start(bf16[3,32]{1,0:T(4,128)(2,1)} %bitcast.2), channel_id=1, source_target_pairs={{0,2},{1,3},{2,0},{3,1},{4,6},{5,7},{6,4},{7,5},{8,10},{9,11},{10,... | collective-permute-start | bytes 584 | tf_op jit(solution)/shard_map/ppermute | solution.py:391
  3.7 0.1 collective-permute-start
  3.8 0.8 %copy-done.2 = s32[8,1024]{1,0:T(8,128)S(1)} copy-done((s32[8,1024]{1,0:T(8,128)S(1)}, s32[8,1024]{1,0:T(8,128)}, u32[]{:S(2)}) %copy-start.2) | copy-done | bytes 32792
  4.6 0.7 %windows.1.refs_1_ = s32[4,8,256,128]{3,2,1,0:T(8,128)S(1)} custom-call(s32[8,1024]{1,0:T(8,128)S(1)} %copy-done.2), custom_call_target="tpu_custom_call" | custom-call | flops 2000000000 | bytes 4000000 | tf_op jit(solution)/shard_map/windows/pallas_call | solution.py:73
  6.0 1.7 %collective-permute-done.refs_1_ = bf16[32,256]{1,0:T(8,128)(2,1)S(1)} collective-permute-done((bf16[32,256]{1,0:T(8,128)(2,1)}, bf16[32,256]{1,0:T(8,128)(2,1)S(1)}, u32[]{:S(2)}, u32[]{:S(2)}) %collective-permute-start) | collective-permute-done | bytes 16416 | tf_op jit(solution)/shard_map/ppermute | solution.py:391
  7.8 2.6 %collective-permute-start.2 = (bf16[80,256]{1,0:T(8,128)(2,1)S(1)}, bf16[80,256]{1,0:T(8,128)(2,1)S(1)}, u32[]{:S(2)}, u32[]{:S(2)}) collective-permute-start(bf16[80,256]{1,0:T(8,128)(2,1)S(1)} %first.1.mine_ref), channel_id=1, source_target_pairs={{0,4},{1,5},{2,6},{3,7},{4,0},{5,1},{6,2},{7,3},{8,12},{9,13},{10,... | collective-permute-start | bytes 122888 | tf_op jit(solution)/shard_map/ppermute | solution.py:391
  10.4 1.1 %columns.1 = (f32[8,7,128,128]{3,2,1,0:T(8,128)S(1)}, bf16[512,1024]{1,0:T(8,128)(2,1)S(1)}, f32[16,128]{1,0:T(8,128)S(1)}) custom-call(s32[1]{0:T(128)S(6)} %copy.23.count_ref, f32[7,1024]{1,0:T(8,128)S(1)} %copy-done.3, s32[1,1024]{1,0:T(1,128)S(1)} %bitcast.4), custom_call_target="tpu_custom_call" | custom-call | flops 2000000000 | bytes 4000000 | tf_op jit(solution)/shard_map/columns/pallas_call | solution.py:137
  11.5 1.3 %collective-permute-done.2.other_ref = bf16[80,256]{1,0:T(8,128)(2,1)S(1)} collective-permute-done((bf16[80,256]{1,0:T(8,128)(2,1)S(1)}, bf16[80,256]{1,0:T(8,128)(2,1)S(1)}, u32[]{:S(2)}, u32[]{:S(2)}) %collective-permute-start.2) | collective-permute-done | bytes 40992 | tf_op jit(solution)/shard_map/ppermute | solution.py:391
  12.8 0.1 join.2.mine_ref.refs_0_
  12.9 1.7 %collective-permute-start.3 = (bf16[144,256]{1,0:T(8,128)(2,1)S(1)}, bf16[144,256]{1,0:T(8,128)(2,1)S(1)}, u32[]{:S(2)}, u32[]{:S(2)}) collective-permute-start(bf16[144,256]{1,0:T(8,128)(2,1)S(1)} %join.2.mine_ref.refs_0_), channel_id=1, source_target_pairs={{0,1},{1,0},{2,3},{3,2},{4,5},{5,4},{6,7},{7,6},{8,9},{9,8},{10,11... | collective-permute-start | bytes 221192 | tf_op jit(solution)/shard_map/ppermute | solution.py:391
  14.6 1.2 %sources.5 = (f32[1024,128]{1,0:T(8,128)S(1)}, f32[1024,128]{1,0:T(8,128)S(1)}) custom-call(s32[1]{0:T(128)S(6)} %copy.23.count_ref, bf16[144,256]{1,0:T(8,128)(2,1)S(1)} %join.2.mine_ref.refs_0_, s32[4,8,256,128]{3,2,1,0:T(8,128)S(1)} %windows.1.refs_1_, f32[8,7,128,128]{3,2,1,0:T(8,128)S(1)} %get-tuple-element.24.refs_2_), custom_call_target="tpu_custom_call" | custom-call | flops 3000000000 | bytes 4000000 | tf_op jit(solution)/shard_map/sources/pallas_call | solution.py:319
  15.8 1.0 %corners.1.refs_7_.corner_ref = bf16[1168,1024]{1,0:T(8,128)(2,1)S(1)} custom-call(s32[1]{0:T(128)S(6)} %copy.23.count_ref, s32[4,1024]{1,0:T(4,128)S(1)} %copy-done.4), custom_call_target="tpu_custom_call" | custom-call | flops 2000000000 | bytes 4000000 | tf_op jit(solution)/shard_map/corners/pallas_call | solution.py:168
  16.8 0.5 %collective-permute-done.3.other_ref.refs_0_ = bf16[144,256]{1,0:T(8,128)(2,1)S(1)} collective-permute-done((bf16[144,256]{1,0:T(8,128)(2,1)S(1)}, bf16[144,256]{1,0:T(8,128)(2,1)S(1)}, u32[]{:S(2)}, u32[]{:S(2)}) %collective-permute-start.3) | collective-permute-done | bytes 73760 | tf_op jit(solution)/shard_map/ppermute | solution.py:391
  17.4 1.7 %collective-permute-start.4 = (bf16[272,256]{1,0:T(8,128)(2,1)S(1)}, bf16[272,256]{1,0:T(8,128)(2,1)S(1)}, u32[]{:S(2)}, u32[]{:S(2)}) collective-permute-start(bf16[272,256]{1,0:T(8,128)(2,1)S(1)} %join.3), channel_id=1, source_target_pairs={{0,16},{8,24},{16,0},{24,8},{1,17},{9,25},{17,1},{25,9},{2,18},{10... | collective-permute-start | bytes 417800 | tf_op jit(solution)/shard_map/ppermute | solution.py:391
  19.1 1.2 %sources.6 = (f32[1024,128]{1,0:T(8,128)S(1)}, f32[1024,128]{1,0:T(8,128)S(1)}) custom-call(s32[1]{0:T(128)S(6)} %copy.23.count_ref, bf16[144,256]{1,0:T(8,128)(2,1)S(1)} %collective-permute-done.3.other_ref.refs_0_, s32[4,8,256,128]{3,2,1,0:T(8,128)S(1)} %windows.1.refs_1_, ...), custom_call_target="tpu_custom_call", output_to_operand_aliasing={{0}: (4, {}), {1}: (5, {})} | custom-call | flops 3000000000 | bytes 4000000 | tf_op jit(solution)/shard_map/sources/pallas_call | solution.py:319
  20.4 2.2 %sources.7 = (f32[1024,128]{1,0:T(8,128)S(1)}, f32[1024,128]{1,0:T(8,128)S(1)}) custom-call(s32[1]{0:T(128)S(6)} %copy.23.count_ref, bf16[272,256]{1,0:T(8,128)(2,1)S(1)} %collective-permute-done.5.refs_0_, s32[4,8,256,128]{3,2,1,0:T(8,128)S(1)} %windows.1.refs_1_, ...), custom_call_target="tpu_custom_call", output_to_operand_aliasing={{0}: (4, {}), {1}: (5, {})} | custom-call | flops 3000000000 | bytes 4000000 | tf_op jit(solution)/shard_map/sources/pallas_call | solution.py:319
  22.6 0.9 %collective-permute-done.4.refs_0_ = bf16[272,256]{1,0:T(8,128)(2,1)S(1)} collective-permute-done((bf16[272,256]{1,0:T(8,128)(2,1)S(1)}, bf16[272,256]{1,0:T(8,128)(2,1)S(1)}, u32[]{:S(2)}, u32[]{:S(2)}) %collective-permute-start.4) | collective-permute-done | bytes 139296 | tf_op jit(solution)/shard_map/ppermute | solution.py:391
  23.5 2.2 %sources.8 = (f32[1024,128]{1,0:T(8,128)S(1)}, f32[1024,128]{1,0:T(8,128)S(1)}) custom-call(s32[1]{0:T(128)S(6)} %copy.23.count_ref, bf16[272,256]{1,0:T(8,128)(2,1)S(1)} %collective-permute-done.4.refs_0_, s32[4,8,256,128]{3,2,1,0:T(8,128)S(1)} %windows.1.refs_1_, ...), custom_call_target="tpu_custom_call", output_to_operand_aliasing={{0}: (4, {}), {1}: (5, {})} | custom-call | flops 3000000000 | bytes 4000000 | tf_op jit(solution)/shard_map/sources/pallas_call | solution.py:319
  25.7 3.3 %sources.9 = (bf16[1024,128]{1,0:T(8,128)(2,1)S(1)}, bf16[8,80,128]{2,1,0:T(8,128)(2,1)}, bf16[136,128]{1,0:T(8,128)(2,1)S(1)}) custom-call(s32[1]{0:T(128)S(6)} %copy.23.count_ref, bf16[272,256]{1,0:T(8,128)(2,1)S(1)} %collective-permute-done.6.refs_0_, s32[4,8,256,128]{3,2,1,0:T(8,128)S(1)} %windows.1.refs_1_, ...), custom_call_target="tpu_custom_call" | custom-call | flops 3000000000 | bytes 4000000 | tf_op jit(solution)/shard_map/sources/pallas_call | solution.py:319
  29.0 4.7 %all-to-all-start = ((bf16[8,80,128]{2,1,0:T(8,128)(2,1)}), bf16[8,80,128]{2,1,0:T(8,128)(2,1)S(1)}, u32[]{:S(2)}, u32[]{:S(2)}) async-start(bf16[8,80,128]{2,1,0:T(8,128)(2,1)} %get-tuple-element.39), calls=%async_computation | async-start | bytes 327680 | tf_op jit(solution)/shard_map/all_to_all | solution.py:472
  33.7 2.0 %collective-permute-start.7 = (bf16[136,128]{1,0:T(8,128)(2,1)S(1)}, bf16[136,128]{1,0:T(8,128)(2,1)S(1)}, u32[]{:S(2)}, u32[]{:S(2)}) collective-permute-start(bf16[136,128]{1,0:T(8,128)(2,1)S(1)} %get-tuple-element.40), channel_id=1, source_target_pairs={{0,1},{1,2},{2,3},{3,4},{4,5},{5,6},{6,7},{7,0},{8,9},{9,10},{10,1... | collective-permute-start | bytes 104456 | tf_op jit(solution)/shard_map/ppermute | solution.py:473
  35.7 1.5 %nodes.1 = (f32[1032,128]{1,0:T(8,128)}, f32[136,128]{1,0:T(8,128)S(1)}) custom-call(bf16[1168,1024]{1,0:T(8,128)(2,1)S(1)} %corners.1.refs_7_.corner_ref, bf16[1024,128]{1,0:T(8,128)(2,1)S(1)} %get-tuple-element.41.loading_ref), custom_call_target="tpu_custom_call" | custom-call | flops 2000000000 | bytes 4000000 | tf_op jit(solution)/shard_map/nodes/pallas_call | solution.py:338
  37.2 5.6 %collective-permute-done.7.rim_ref = bf16[136,128]{1,0:T(8,128)(2,1)S(1)} collective-permute-done((bf16[136,128]{1,0:T(8,128)(2,1)S(1)}, bf16[136,128]{1,0:T(8,128)(2,1)S(1)}, u32[]{:S(2)}, u32[]{:S(2)}) %collective-permute-start.7) | collective-permute-done | bytes 34848 | tf_op jit(solution)/shard_map/ppermute | solution.py:473
  42.8 0.9 %finish.1 = (f32[1032,128]{1,0:T(8,128)}, f32[256,128]{1,0:T(8,128)}) custom-call(bf16[8,80,128]{2,1,0:T(8,128)(2,1)S(1)} %all-to-all-done.message_ref, bf16[136,128]{1,0:T(8,128)(2,1)S(1)} %collective-permute-done.7.rim_ref, f32[136,128]{1,0:T(8,128)S(1)} %get-tuple-element.42.head_ref, ...), custom_call_target="tpu_custom_call", output_to_operand_aliasing={{0}: (3, {})} | custom-call | flops 1000000 | bytes 4000000 | tf_op jit(solution)/shard_map/finish/pallas_call | solution.py:375
  (19 shorter events, 0.2 us)
Async XLA Ops:
  0.6 7.1 %copy-start = (bf16[32,256]{1,0:T(8,128)(2,1)S(1)}, bf16[32,256]{1,0:T(8,128)(2,1)}, u32[]{:S(2)}) copy-start(bf16[32,256]{1,0:T(8,128)(2,1)} %refs_0_.1) | copy-start | bytes 49156
  0.6 7.1 %copy-start.1 = (bf16[32,3]{0,1:T(4,128)(2,1)S(1)}, bf16[32,3]{0,1:T(4,128)(2,1)}, u32[]{:S(2)}) copy-start(bf16[32,3]{0,1:T(4,128)(2,1)} %param.8) | copy-start | bytes 580
  0.7 5.3 %collective-permute-start.1 = (bf16[3,32]{1,0:T(4,128)(2,1)}, bf16[3,32]{1,0:T(4,128)(2,1)S(1)}, u32[]{:S(2)}, u32[]{:S(2)}) collective-permute-start(bf16[3,32]{1,0:T(4,128)(2,1)} %bitcast.2), channel_id=1, source_target_pairs={{0,2},{1,3},{2,0},{3,1},{4,6},{5,7},{6,4},{7,5},{8,10},{9,11},{10,... | collective-permute-start | bytes 584 | tf_op jit(solution)/shard_map/ppermute | solution.py:391
  3.7 3.9 %collective-permute-start = (bf16[32,256]{1,0:T(8,128)(2,1)}, bf16[32,256]{1,0:T(8,128)(2,1)S(1)}, u32[]{:S(2)}, u32[]{:S(2)}) collective-permute-start(bf16[32,256]{1,0:T(8,128)(2,1)} %refs_0_.1), channel_id=1, source_target_pairs={{0,2},{1,3},{2,0},{3,1},{4,6},{5,7},{6,4},{7,5},{8,10},{9,11},{10,... | collective-permute-start | bytes 49160 | tf_op jit(solution)/shard_map/ppermute | solution.py:391
  3.8 0.8 %copy-start.2 = (s32[8,1024]{1,0:T(8,128)S(1)}, s32[8,1024]{1,0:T(8,128)}, u32[]{:S(2)}) copy-start(s32[8,1024]{1,0:T(8,128)} %delay_ref.1) | copy-start | bytes 98308
  4.6 5.8 %copy-start.3 = (f32[7,1024]{1,0:T(8,128)S(1)}, f32[7,1024]{1,0:T(8,128)}, u32[]{:S(2)}) copy-start(f32[7,1024]{1,0:T(8,128)} %geometry_ref) | copy-start | bytes 86020
  4.6 5.8 %copy-start.5 = (s32[1024]{0:T(1024)S(1)}, s32[1024]{0:T(1024)}, u32[]{:S(2)}) copy-start(s32[1024]{0:T(1024)} %param.13) | copy-start | bytes 12292
  7.8 5.1 %collective-permute-start.2 = (bf16[80,256]{1,0:T(8,128)(2,1)S(1)}, bf16[80,256]{1,0:T(8,128)(2,1)S(1)}, u32[]{:S(2)}, u32[]{:S(2)}) collective-permute-start(bf16[80,256]{1,0:T(8,128)(2,1)S(1)} %first.1.mine_ref), channel_id=1, source_target_pairs={{0,4},{1,5},{2,6},{3,7},{4,0},{5,1},{6,2},{7,3},{8,12},{9,13},{10,... | collective-permute-start | bytes 122888 | tf_op jit(solution)/shard_map/ppermute | solution.py:391
  12.9 4.4 %collective-permute-start.3 = (bf16[144,256]{1,0:T(8,128)(2,1)S(1)}, bf16[144,256]{1,0:T(8,128)(2,1)S(1)}, u32[]{:S(2)}, u32[]{:S(2)}) collective-permute-start(bf16[144,256]{1,0:T(8,128)(2,1)S(1)} %join.2.mine_ref.refs_0_), channel_id=1, source_target_pairs={{0,1},{1,0},{2,3},{3,2},{4,5},{5,4},{6,7},{7,6},{8,9},{9,8},{10,11... | collective-permute-start | bytes 221192 | tf_op jit(solution)/shard_map/ppermute | solution.py:391
  14.6 1.2 %copy-start.4 = (s32[4,1024]{1,0:T(4,128)S(1)}, s32[4,1024]{1,0:T(4,128)}, u32[]{:S(2)}) copy-start(s32[4,1024]{1,0:T(4,128)} %conn_ref) | copy-start | bytes 49156
  17.3 3.1 %collective-permute-start.5 = (bf16[272,256]{1,0:T(8,128)(2,1)S(1)}, bf16[272,256]{1,0:T(8,128)(2,1)S(1)}, u32[]{:S(2)}, u32[]{:S(2)}) collective-permute-start(bf16[272,256]{1,0:T(8,128)(2,1)S(1)} %join.3), channel_id=1, source_target_pairs={{0,8},{8,0},{16,24},{24,16},{1,9},{9,1},{17,25},{25,17},{2,10},{10... | collective-permute-start | bytes 417800 | tf_op jit(solution)/shard_map/ppermute | solution.py:391
  17.4 6.1 %collective-permute-start.4 = (bf16[272,256]{1,0:T(8,128)(2,1)S(1)}, bf16[272,256]{1,0:T(8,128)(2,1)S(1)}, u32[]{:S(2)}, u32[]{:S(2)}) collective-permute-start(bf16[272,256]{1,0:T(8,128)(2,1)S(1)} %join.3), channel_id=1, source_target_pairs={{0,16},{8,24},{16,0},{24,8},{1,17},{9,25},{17,1},{25,9},{2,18},{10... | collective-permute-start | bytes 417800 | tf_op jit(solution)/shard_map/ppermute | solution.py:391
  23.4 2.2 %collective-permute-start.6 = (bf16[272,256]{1,0:T(8,128)(2,1)S(1)}, bf16[272,256]{1,0:T(8,128)(2,1)S(1)}, u32[]{:S(2)}, u32[]{:S(2)}) collective-permute-start(bf16[272,256]{1,0:T(8,128)(2,1)S(1)} %collective-permute-done.4.refs_0_), channel_id=1, source_target_pairs={{0,8},{8,0},{16,24},{24,16},{1,9},{9,1},{17,25},{25,17},{2,10},{10... | collective-permute-start | bytes 417800 | tf_op jit(solution)/shard_map/ppermute | solution.py:391
  29.0 13.8 %all-to-all-start = ((bf16[8,80,128]{2,1,0:T(8,128)(2,1)}), bf16[8,80,128]{2,1,0:T(8,128)(2,1)S(1)}, u32[]{:S(2)}, u32[]{:S(2)}) async-start(bf16[8,80,128]{2,1,0:T(8,128)(2,1)} %get-tuple-element.39), calls=%async_computation | async-start | bytes 327680 | tf_op jit(solution)/shard_map/all_to_all | solution.py:472
  33.7 9.1 %collective-permute-start.7 = (bf16[136,128]{1,0:T(8,128)(2,1)S(1)}, bf16[136,128]{1,0:T(8,128)(2,1)S(1)}, u32[]{:S(2)}, u32[]{:S(2)}) collective-permute-start(bf16[136,128]{1,0:T(8,128)(2,1)S(1)} %get-tuple-element.40), channel_id=1, source_target_pairs={{0,1},{1,2},{2,3},{3,4},{4,5},{5,6},{6,7},{7,0},{8,9},{9,10},{10,1... | collective-permute-start | bytes 104456 | tf_op jit(solution)/shard_map/ppermute | solution.py:473

commit v10 on v9

--- a/solution.py
+++ b/solution.py
@@ -148,7 +148,7 @@
     )(counts, geometry, owners.reshape(1, panels))
 
 
-def corner_kernel(count_ref, conn_ref, corner_ref):
+def corner_kernel(count_ref, conn_ref, corner_ref, edge_ref):
     panels = conn_ref.shape[1]
     live = lax.broadcasted_iota(jnp.int32, (16, panels), 1) < count_ref[0]
     corners = [
@@ -161,16 +161,22 @@
         total = jnp.where(corners[0] == node, share, zero)
         for corner in corners[1:]:
             total = total + jnp.where(corner == node, share, zero)
-        corner_ref[row : row + 16, :] = total
+        if row < NODE_DEV + 8:
+            corner_ref[row : row + 16, :] = total
+        if row + 16 > NODE_DEV:
+            edge_ref[row - NODE_DEV + 8 : row - NODE_DEV + 24, :] = total
 
 
 def corner_matrix(counts, connectivity):
     return call(
         corner_kernel,
         "corners",
-        jax.ShapeDtypeStruct((NODE_ROWS, connectivity.shape[1]), BF16),
+        (
+            jax.ShapeDtypeStruct((NODE_DEV + 8, connectivity.shape[1]), BF16),
+            jax.ShapeDtypeStruct((HEAD + 8, connectivity.shape[1]), BF16),
+        ),
         [SMEM, WHOLE],
-        WHOLE,
+        [WHOLE] * 2,
         work=2_000_000_000,
     )(counts, connectivity)
 
@@ -208,12 +214,12 @@
     chunks = take(parts)
     source_ref, panel_ref = take(2)
     if last:
-        loading_in, thick_in, slot_ref, ids_ref, corner_ref = take(5)
+        loading_in, thick_in, slot_ref, ids_ref, edge_ref = take(5)
         loading_ref, message_ref, rim_ref, thick_ref = take(4)
     else:
         loading_in, thick_in = (None, None) if first else take(2)
         loading_ref, thick_ref = take(2)
-    code_ref, scale_ref, mass_ref, pair_ref, window_ref = take(5)
+    code_ref, scale_ref, weight_ref, window_ref = take(4)
 
     blocks = source_ref.shape[1]
     span = chunks[0].shape[0] - EXTRA
@@ -244,8 +250,8 @@
                 following = (jnp.where(lanes == 0, code, current).astype(F32) * scale).astype(BF16)
                 following = pltpu.roll(following, 127, 1)
                 current = (current.astype(F32) * scale).astype(BF16)
-                window_ref[block, here : here + 128, :] = current
-                window_ref[block, observers + here : observers + here + 128, :] = following - current
+                window_ref[block, here : here + 128, :TW] = current
+                window_ref[block, here : here + 128, TW:] = following - current
 
         for strip in range(BLK // 16):
             rows = slice(strip * 16, strip * 16 + 16)
@@ -261,12 +267,14 @@
                 inverse = lax.rsqrt(delta_x * delta_x + delta_y * delta_y + delta_z * delta_z)
                 flux = normal_x * delta_x + normal_y * delta_y + normal_z * delta_z
                 far = flux * inverse * inverse
-                pair_ref[block, rows, here : here + 128] = (far * inverse).astype(BF16)
-                pair_ref[block, rows, observers + here : observers + here + 128] = far.astype(BF16)
-                mass_ref[block, rows, here : here + 128] = (area * inverse).astype(BF16)
+                cols = slice(here, here + 128)
+                weight_ref[block, rows, cols] = (far * inverse).astype(BF16)
+                weight_ref[block, BLK + strip * 16 : BLK + strip * 16 + 16, cols] = far.astype(BF16)
+                weight_ref[block, 2 * BLK + strip * 16 : 2 * BLK + strip * 16 + 16, cols] = (area * inverse).astype(BF16)
         rows = slice(block * BLK, (block + 1) * BLK)
-        thick = jnp.dot(mass_ref[block], window_ref[block, observers:, :], preferred_element_type=F32)
-        loading = jnp.dot(pair_ref[block], window_ref[block], preferred_element_type=F32)
+        products = jnp.dot(weight_ref[block], window_ref[block], preferred_element_type=F32)
+        thick = products[2 * BLK :, TW:]
+        loading = products[:BLK, :TW] + products[BLK : 2 * BLK, TW:]
         if not first:
             thick = thick + thick_in[rows, :]
             loading = loading + loading_in[rows, :]
@@ -285,7 +293,7 @@
             message_ref[section, :cap, :] = slots[section * cap : (section + 1) * cap]
             ids = jnp.broadcast_to(ids_ref[section : section + 1, :], (EXTRA, 128))
             message_ref[section, cap:, :] = ids.astype(BF16)
-        rim = jnp.dot(corner_ref[NODE_DEV - 8 :, :], loading_ref[...], preferred_element_type=F32)
+        rim = jnp.dot(edge_ref[...], loading_ref[...], preferred_element_type=F32)
         rim_ref[...] = rim[8:].astype(BF16)
 
 
@@ -298,9 +306,8 @@
     scratch = [
         VMEM((observers, 128), jnp.int32),
         VMEM((observers, 128), F32),
-        VMEM((blocks, BLK, observers), BF16),
-        VMEM((blocks, BLK, 2 * observers), BF16),
-        VMEM((blocks, 2 * observers, TW), BF16),
+        VMEM((blocks, 3 * BLK, observers), BF16),
+        VMEM((blocks, observers, 2 * TW), BF16),
     ]
     aliases = {}
     if last:
@@ -329,7 +336,7 @@
 
 
 def node_kernel(corner_ref, loading_ref, node_ref, head_ref):
-    nodes = jnp.dot(corner_ref[: NODE_DEV + 8, :], loading_ref[...], preferred_element_type=F32)
+    nodes = jnp.dot(corner_ref[...], loading_ref[...], preferred_element_type=F32)
     head_ref[...] = nodes[:HEAD]
     node_ref[...] = nodes[:NODE_DEV]
 
@@ -442,13 +449,13 @@
     if paired:
         half = half_chunk(signals, observer_xyz, sections)
         other = swapped(half, "sect", 1)
-        corners = corner_matrix(counts, after(connectivity, half))
+        corners, edges = corner_matrix(counts, after(connectivity, half))
         sums = add((), [(0, 0)], [half])
-        sums = after(sums, corners)
+        sums = after(sums, edges)
         chunk = joined(half, other)
     else:
         chunk = spread_chunk(signals, observer_xyz, sections)
-        corners = corner_matrix(counts, connectivity)
+        corners, edges = corner_matrix(counts, connectivity)
     near = swapped(chunk, "azim", 1)
     chunks = {0: chunk}
     bit = groups // 2
@@ -467,7 +474,7 @@
         chunks[offset ^ 1] = swapped(chunks[offset], "azim", 1)
     sums = add(sums, [(o, 0) for o in rest], [chunks[o] for o in rest])
     rest = [offset ^ 1 for offset in rest]
-    matrices = [slots, ids, corners]
+    matrices = [slots, ids, edges]
     loading, message, rim = add(sums, [(o, 0) for o in rest], [chunks[o] for o in rest], matrices, sections)
     message = lax.all_to_all(message, "sect", split_axis=0, concat_axis=0, tiled=True)
     rim = lax.ppermute(rim, "sect", [(i, (i + 1) % sections) for i in range(sections)])

time: 44 us -> 44 us (level)
  no operation moved by 1% of the time
where the time goes in v10:
time: 44 us; the launch traced here: 43.7 us
  starting transfers between devices  16 us (36%)
  Pallas kernels  15.9 us (36%)
  waiting for transfers between devices  9.66 us (22%)
  between operations  1.4 us (3%)
  local copies, waits for them, and re-layouts  0.78 us (2%)
    pallas_call x5, Pallas kernels, sources(): call(functools.partial(sources_kernel, places, not sums, last), 'sources'...  10.5 us
    ppermute x7, starting transfers between devices, swapped(): return lax.ppermute(array, axis, [(i, i ^ bit) for i in range(peers)])  9.29 us
    ppermute x1, waiting for transfers between devices, per_device(): lax.ppermute(rim, 'sect', [(i, (i + 1) % sections) for i in range(section...  5.57 us
    all_to_all x1, starting transfers between devices, per_device(): lax.all_to_all(message, 'sect', split_axis=0, concat_axis=0, tiled=True)  4.67 us
    ppermute x7, waiting for transfers between devices, swapped(): return lax.ppermute(array, axis, [(i, i ^ bit) for i in range(peers)])  4.09 us
    ppermute x1, starting transfers between devices, per_device(): lax.ppermute(rim, 'sect', [(i, (i + 1) % sections) for i in range(section...  2.02 us
    pallas_call x1, Pallas kernels, node_sums(): call(node_kernel, 'nodes', (jax.ShapeDtypeStruct((NODE_DEV, TW), F32), ja...  1.51 us
    pallas_call x1, Pallas kernels, panel_columns(): call(functools.partial(column_kernel, sections), 'columns', (jax.ShapeDty...  1.11 us
  transfers between devices with their start and end apart: 9, of which 5 were waited for; matrix products, arithmetic and copies ran while one was open for 0% of the time, Pallas kernels for 26%

profile of v10, /device:TPU:0, one launch (start us, length us, event | category | flops | bytes accessed | tf_op | source)
XLA Modules:
  0.0 43.7 jit_solution(16626786852942944973)
XLA Ops:
  0.7 3.1 %collective-permute-start.1 = (bf16[3,32]{1,0:T(4,128)(2,1)}, bf16[3,32]{1,0:T(4,128)(2,1)S(1)}, u32[]{:S(2)}, u32[]{:S(2)}) collective-permute-start(bf16[3,32]{1,0:T(4,128)(2,1)} %bitcast.2), channel_id=1, source_target_pairs={{0,2},{1,3},{2,0},{3,1},{4,6},{5,7},{6,4},{7,5},{8,10},{9,11},{10,... | collective-permute-start | bytes 584 | tf_op jit(solution)/shard_map/ppermute | solution.py:398
  3.7 0.1 collective-permute-start
  3.8 0.8 %copy-done.2 = s32[8,1024]{1,0:T(8,128)S(1)} copy-done((s32[8,1024]{1,0:T(8,128)S(1)}, s32[8,1024]{1,0:T(8,128)}, u32[]{:S(2)}) %copy-start.2) | copy-done | bytes 32792
  4.6 0.7 %windows.1.refs_1_ = s32[4,8,256,128]{3,2,1,0:T(8,128)S(1)} custom-call(s32[8,1024]{1,0:T(8,128)S(1)} %copy-done.2), custom_call_target="tpu_custom_call" | custom-call | flops 2000000000 | bytes 4000000 | tf_op jit(solution)/shard_map/windows/pallas_call | solution.py:73
  6.0 1.7 %collective-permute-done.refs_1_ = bf16[32,256]{1,0:T(8,128)(2,1)S(1)} collective-permute-done((bf16[32,256]{1,0:T(8,128)(2,1)}, bf16[32,256]{1,0:T(8,128)(2,1)S(1)}, u32[]{:S(2)}, u32[]{:S(2)}) %collective-permute-start) | collective-permute-done | bytes 16416 | tf_op jit(solution)/shard_map/ppermute | solution.py:398
  7.8 2.6 %collective-permute-start.2 = (bf16[80,256]{1,0:T(8,128)(2,1)S(1)}, bf16[80,256]{1,0:T(8,128)(2,1)S(1)}, u32[]{:S(2)}, u32[]{:S(2)}) collective-permute-start(bf16[80,256]{1,0:T(8,128)(2,1)S(1)} %first.1.mine_ref), channel_id=1, source_target_pairs={{0,4},{1,5},{2,6},{3,7},{4,0},{5,1},{6,2},{7,3},{8,12},{9,13},{10,... | collective-permute-start | bytes 122888 | tf_op jit(solution)/shard_map/ppermute | solution.py:398
  10.4 1.1 %columns.1 = (f32[8,7,128,128]{3,2,1,0:T(8,128)S(1)}, bf16[512,1024]{1,0:T(8,128)(2,1)S(1)}, f32[16,128]{1,0:T(8,128)S(1)}) custom-call(s32[1]{0:T(128)S(6)} %copy.23.count_ref, f32[7,1024]{1,0:T(8,128)S(1)} %copy-done.3, s32[1,1024]{1,0:T(1,128)S(1)} %bitcast.4), custom_call_target="tpu_custom_call" | custom-call | flops 2000000000 | bytes 4000000 | tf_op jit(solution)/shard_map/columns/pallas_call | solution.py:137
  11.5 1.3 %collective-permute-done.2.other_ref = bf16[80,256]{1,0:T(8,128)(2,1)S(1)} collective-permute-done((bf16[80,256]{1,0:T(8,128)(2,1)S(1)}, bf16[80,256]{1,0:T(8,128)(2,1)S(1)}, u32[]{:S(2)}, u32[]{:S(2)}) %collective-permute-start.2) | collective-permute-done | bytes 40992 | tf_op jit(solution)/shard_map/ppermute | solution.py:398
  12.8 0.1 join.2.mine_ref.refs_0_
  12.9 1.7 %collective-permute-start.3 = (bf16[144,256]{1,0:T(8,128)(2,1)S(1)}, bf16[144,256]{1,0:T(8,128)(2,1)S(1)}, u32[]{:S(2)}, u32[]{:S(2)}) collective-permute-start(bf16[144,256]{1,0:T(8,128)(2,1)S(1)} %join.2.mine_ref.refs_0_), channel_id=1, source_target_pairs={{0,1},{1,0},{2,3},{3,2},{4,5},{5,4},{6,7},{7,6},{8,9},{9,8},{10,11... | collective-permute-start | bytes 221192 | tf_op jit(solution)/shard_map/ppermute | solution.py:398
  14.6 1.3 %sources.5 = (f32[1024,128]{1,0:T(8,128)S(1)}, f32[1024,128]{1,0:T(8,128)S(1)}) custom-call(s32[1]{0:T(128)S(6)} %copy.23.count_ref, bf16[144,256]{1,0:T(8,128)(2,1)S(1)} %join.2.mine_ref.refs_0_, s32[4,8,256,128]{3,2,1,0:T(8,128)S(1)} %windows.1.refs_1_, f32[8,7,128,128]{3,2,1,0:T(8,128)S(1)} %get-tuple-element.26.refs_2_), custom_call_target="tpu_custom_call" | custom-call | flops 3000000000 | bytes 4000000 | tf_op jit(solution)/shard_map/sources/pallas_call | solution.py:326
  15.9 1.0 %corners.1 = (bf16[1040,1024]{1,0:T(8,128)(2,1)S(1)}, bf16[144,1024]{1,0:T(8,128)(2,1)S(1)}) custom-call(s32[1]{0:T(128)S(6)} %copy.23.count_ref, s32[4,1024]{1,0:T(4,128)S(1)} %copy-done.4), custom_call_target="tpu_custom_call" | custom-call | flops 2000000000 | bytes 4000000 | tf_op jit(solution)/shard_map/corners/pallas_call | solution.py:171
  16.9 0.4 collective-permute-done.3.other_ref.refs_0_
  17.4 1.7 %collective-permute-start.4 = (bf16[272,256]{1,0:T(8,128)(2,1)S(1)}, bf16[272,256]{1,0:T(8,128)(2,1)S(1)}, u32[]{:S(2)}, u32[]{:S(2)}) collective-permute-start(bf16[272,256]{1,0:T(8,128)(2,1)S(1)} %join.3), channel_id=1, source_target_pairs={{0,16},{8,24},{16,0},{24,8},{1,17},{9,25},{17,1},{25,9},{2,18},{10... | collective-permute-start | bytes 417800 | tf_op jit(solution)/shard_map/ppermute | solution.py:398
  19.1 1.4 %sources.6 = (f32[1024,128]{1,0:T(8,128)S(1)}, f32[1024,128]{1,0:T(8,128)S(1)}) custom-call(s32[1]{0:T(128)S(6)} %copy.23.count_ref, bf16[144,256]{1,0:T(8,128)(2,1)S(1)} %collective-permute-done.3.other_ref.refs_0_, s32[4,8,256,128]{3,2,1,0:T(8,128)S(1)} %windows.1.refs_1_, ...), custom_call_target="tpu_custom_call", output_to_operand_aliasing={{0}: (4, {}), {1}: (5, {})} | custom-call | flops 3000000000 | bytes 4000000 | tf_op jit(solution)/shard_map/sources/pallas_call | solution.py:326
  20.5 2.3 %sources.7 = (f32[1024,128]{1,0:T(8,128)S(1)}, f32[1024,128]{1,0:T(8,128)S(1)}) custom-call(s32[1]{0:T(128)S(6)} %copy.23.count_ref, bf16[272,256]{1,0:T(8,128)(2,1)S(1)} %collective-permute-done.5.refs_0_, s32[4,8,256,128]{3,2,1,0:T(8,128)S(1)} %windows.1.refs_1_, ...), custom_call_target="tpu_custom_call", output_to_operand_aliasing={{0}: (4, {}), {1}: (5, {})} | custom-call | flops 3000000000 | bytes 4000000 | tf_op jit(solution)/shard_map/sources/pallas_call | solution.py:326
  22.8 0.6 %collective-permute-done.4.refs_0_ = bf16[272,256]{1,0:T(8,128)(2,1)S(1)} collective-permute-done((bf16[272,256]{1,0:T(8,128)(2,1)S(1)}, bf16[272,256]{1,0:T(8,128)(2,1)S(1)}, u32[]{:S(2)}, u32[]{:S(2)}) %collective-permute-start.4) | collective-permute-done | bytes 139296 | tf_op jit(solution)/shard_map/ppermute | solution.py:398
  23.5 2.3 %sources.8 = (f32[1024,128]{1,0:T(8,128)S(1)}, f32[1024,128]{1,0:T(8,128)S(1)}) custom-call(s32[1]{0:T(128)S(6)} %copy.23.count_ref, bf16[272,256]{1,0:T(8,128)(2,1)S(1)} %collective-permute-done.4.refs_0_, s32[4,8,256,128]{3,2,1,0:T(8,128)S(1)} %windows.1.refs_1_, ...), custom_call_target="tpu_custom_call", output_to_operand_aliasing={{0}: (4, {}), {1}: (5, {})} | custom-call | flops 3000000000 | bytes 4000000 | tf_op jit(solution)/shard_map/sources/pallas_call | solution.py:326
  25.8 3.2 %sources.9 = (bf16[1024,128]{1,0:T(8,128)(2,1)S(1)}, bf16[8,80,128]{2,1,0:T(8,128)(2,1)}, bf16[136,128]{1,0:T(8,128)(2,1)S(1)}) custom-call(s32[1]{0:T(128)S(6)} %copy.23.count_ref, bf16[272,256]{1,0:T(8,128)(2,1)S(1)} %collective-permute-done.6.refs_0_, s32[4,8,256,128]{3,2,1,0:T(8,128)S(1)} %windows.1.refs_1_, ...), custom_call_target="tpu_custom_call" | custom-call | flops 3000000000 | bytes 4000000 | tf_op jit(solution)/shard_map/sources/pallas_call | solution.py:326
  29.0 4.7 %all-to-all-start = ((bf16[8,80,128]{2,1,0:T(8,128)(2,1)}), bf16[8,80,128]{2,1,0:T(8,128)(2,1)S(1)}, u32[]{:S(2)}, u32[]{:S(2)}) async-start(bf16[8,80,128]{2,1,0:T(8,128)(2,1)} %get-tuple-element.42), calls=%async_computation | async-start | bytes 327680 | tf_op jit(solution)/shard_map/all_to_all | solution.py:479
  33.7 2.0 %collective-permute-start.7 = (bf16[136,128]{1,0:T(8,128)(2,1)S(1)}, bf16[136,128]{1,0:T(8,128)(2,1)S(1)}, u32[]{:S(2)}, u32[]{:S(2)}) collective-permute-start(bf16[136,128]{1,0:T(8,128)(2,1)S(1)} %get-tuple-element.43), channel_id=1, source_target_pairs={{0,1},{1,2},{2,3},{3,4},{4,5},{5,6},{6,7},{7,0},{8,9},{9,10},{10,1... | collective-permute-start | bytes 104456 | tf_op jit(solution)/shard_map/ppermute | solution.py:480
  35.7 1.5 %nodes.1 = (f32[1032,128]{1,0:T(8,128)}, f32[136,128]{1,0:T(8,128)S(1)}) custom-call(bf16[1040,1024]{1,0:T(8,128)(2,1)S(1)} %get-tuple-element.44.corner_ref, bf16[1024,128]{1,0:T(8,128)(2,1)S(1)} %get-tuple-element.45.loading_ref), custom_call_target="tpu_custom_call" | custom-call | flops 2000000000 | bytes 4000000 | tf_op jit(solution)/shard_map/nodes/pallas_call | solution.py:345
  37.2 5.6 %collective-permute-done.7.rim_ref = bf16[136,128]{1,0:T(8,128)(2,1)S(1)} collective-permute-done((bf16[136,128]{1,0:T(8,128)(2,1)S(1)}, bf16[136,128]{1,0:T(8,128)(2,1)S(1)}, u32[]{:S(2)}, u32[]{:S(2)}) %collective-permute-start.7) | collective-permute-done | bytes 34848 | tf_op jit(solution)/shard_map/ppermute | solution.py:480
  42.8 0.9 %finish.1 = (f32[1032,128]{1,0:T(8,128)}, f32[256,128]{1,0:T(8,128)}) custom-call(bf16[8,80,128]{2,1,0:T(8,128)(2,1)S(1)} %all-to-all-done.message_ref, bf16[136,128]{1,0:T(8,128)(2,1)S(1)} %collective-permute-done.7.rim_ref, f32[136,128]{1,0:T(8,128)S(1)} %get-tuple-element.46.head_ref, ...), custom_call_target="tpu_custom_call", output_to_operand_aliasing={{0}: (3, {})} | custom-call | flops 1000000 | bytes 4000000 | tf_op jit(solution)/shard_map/finish/pallas_call | solution.py:382
  (19 shorter events, 0.2 us)
Async XLA Ops:
  0.6 7.1 %copy-start = (bf16[32,256]{1,0:T(8,128)(2,1)S(1)}, bf16[32,256]{1,0:T(8,128)(2,1)}, u32[]{:S(2)}) copy-start(bf16[32,256]{1,0:T(8,128)(2,1)} %refs_0_.1) | copy-start | bytes 49156
  0.6 7.1 %copy-start.1 = (bf16[32,3]{0,1:T(4,128)(2,1)S(1)}, bf16[32,3]{0,1:T(4,128)(2,1)}, u32[]{:S(2)}) copy-start(bf16[32,3]{0,1:T(4,128)(2,1)} %param.8) | copy-start | bytes 580
  0.7 5.3 %collective-permute-start.1 = (bf16[3,32]{1,0:T(4,128)(2,1)}, bf16[3,32]{1,0:T(4,128)(2,1)S(1)}, u32[]{:S(2)}, u32[]{:S(2)}) collective-permute-start(bf16[3,32]{1,0:T(4,128)(2,1)} %bitcast.2), channel_id=1, source_target_pairs={{0,2},{1,3},{2,0},{3,1},{4,6},{5,7},{6,4},{7,5},{8,10},{9,11},{10,... | collective-permute-start | bytes 584 | tf_op jit(solution)/shard_map/ppermute | solution.py:398
  3.7 3.9 %collective-permute-start = (bf16[32,256]{1,0:T(8,128)(2,1)}, bf16[32,256]{1,0:T(8,128)(2,1)S(1)}, u32[]{:S(2)}, u32[]{:S(2)}) collective-permute-start(bf16[32,256]{1,0:T(8,128)(2,1)} %refs_0_.1), channel_id=1, source_target_pairs={{0,2},{1,3},{2,0},{3,1},{4,6},{5,7},{6,4},{7,5},{8,10},{9,11},{10,... | collective-permute-start | bytes 49160 | tf_op jit(solution)/shard_map/ppermute | solution.py:398
  3.8 0.8 %copy-start.2 = (s32[8,1024]{1,0:T(8,128)S(1)}, s32[8,1024]{1,0:T(8,128)}, u32[]{:S(2)}) copy-start(s32[8,1024]{1,0:T(8,128)} %delay_ref.1) | copy-start | bytes 98308
  4.6 5.8 %copy-start.3 = (f32[7,1024]{1,0:T(8,128)S(1)}, f32[7,1024]{1,0:T(8,128)}, u32[]{:S(2)}) copy-start(f32[7,1024]{1,0:T(8,128)} %geometry_ref) | copy-start | bytes 86020
  4.6 5.8 %copy-start.5 = (s32[1024]{0:T(1024)S(1)}, s32[1024]{0:T(1024)}, u32[]{:S(2)}) copy-start(s32[1024]{0:T(1024)} %param.13) | copy-start | bytes 12292
  7.8 5.1 %collective-permute-start.2 = (bf16[80,256]{1,0:T(8,128)(2,1)S(1)}, bf16[80,256]{1,0:T(8,128)(2,1)S(1)}, u32[]{:S(2)}, u32[]{:S(2)}) collective-permute-start(bf16[80,256]{1,0:T(8,128)(2,1)S(1)} %first.1.mine_ref), channel_id=1, source_target_pairs={{0,4},{1,5},{2,6},{3,7},{4,0},{5,1},{6,2},{7,3},{8,12},{9,13},{10,... | collective-permute-start | bytes 122888 | tf_op jit(solution)/shard_map/ppermute | solution.py:398
  12.9 4.4 %collective-permute-start.3 = (bf16[144,256]{1,0:T(8,128)(2,1)S(1)}, bf16[144,256]{1,0:T(8,128)(2,1)S(1)}, u32[]{:S(2)}, u32[]{:S(2)}) collective-permute-start(bf16[144,256]{1,0:T(8,128)(2,1)S(1)} %join.2.mine_ref.refs_0_), channel_id=1, source_target_pairs={{0,1},{1,0},{2,3},{3,2},{4,5},{5,4},{6,7},{7,6},{8,9},{9,8},{10,11... | collective-permute-start | bytes 221192 | tf_op jit(solution)/shard_map/ppermute | solution.py:398
  14.6 1.3 %copy-start.4 = (s32[4,1024]{1,0:T(4,128)S(1)}, s32[4,1024]{1,0:T(4,128)}, u32[]{:S(2)}) copy-start(s32[4,1024]{1,0:T(4,128)} %conn_ref) | copy-start | bytes 49156
  17.3 3.2 %collective-permute-start.5 = (bf16[272,256]{1,0:T(8,128)(2,1)S(1)}, bf16[272,256]{1,0:T(8,128)(2,1)S(1)}, u32[]{:S(2)}, u32[]{:S(2)}) collective-permute-start(bf16[272,256]{1,0:T(8,128)(2,1)S(1)} %join.3), channel_id=1, source_target_pairs={{0,8},{8,0},{16,24},{24,16},{1,9},{9,1},{17,25},{25,17},{2,10},{10... | collective-permute-start | bytes 417800 | tf_op jit(solution)/shard_map/ppermute | solution.py:398
  17.4 6.1 %collective-permute-start.4 = (bf16[272,256]{1,0:T(8,128)(2,1)S(1)}, bf16[272,256]{1,0:T(8,128)(2,1)S(1)}, u32[]{:S(2)}, u32[]{:S(2)}) collective-permute-start(bf16[272,256]{1,0:T(8,128)(2,1)S(1)} %join.3), channel_id=1, source_target_pairs={{0,16},{8,24},{16,0},{24,8},{1,17},{9,25},{17,1},{25,9},{2,18},{10... | collective-permute-start | bytes 417800 | tf_op jit(solution)/shard_map/ppermute | solution.py:398
  23.4 2.3 %collective-permute-start.6 = (bf16[272,256]{1,0:T(8,128)(2,1)S(1)}, bf16[272,256]{1,0:T(8,128)(2,1)S(1)}, u32[]{:S(2)}, u32[]{:S(2)}) collective-permute-start(bf16[272,256]{1,0:T(8,128)(2,1)S(1)} %collective-permute-done.4.refs_0_), channel_id=1, source_target_pairs={{0,8},{8,0},{16,24},{24,16},{1,9},{9,1},{17,25},{25,17},{2,10},{10... | collective-permute-start | bytes 417800 | tf_op jit(solution)/shard_map/ppermute | solution.py:398
  29.0 13.8 %all-to-all-start = ((bf16[8,80,128]{2,1,0:T(8,128)(2,1)}), bf16[8,80,128]{2,1,0:T(8,128)(2,1)S(1)}, u32[]{:S(2)}, u32[]{:S(2)}) async-start(bf16[8,80,128]{2,1,0:T(8,128)(2,1)} %get-tuple-element.42), calls=%async_computation | async-start | bytes 327680 | tf_op jit(solution)/shard_map/all_to_all | solution.py:479
  33.7 9.1 %collective-permute-start.7 = (bf16[136,128]{1,0:T(8,128)(2,1)S(1)}, bf16[136,128]{1,0:T(8,128)(2,1)S(1)}, u32[]{:S(2)}, u32[]{:S(2)}) collective-permute-start(bf16[136,128]{1,0:T(8,128)(2,1)S(1)} %get-tuple-element.43), channel_id=1, source_target_pairs={{0,1},{1,2},{2,3},{3,4},{4,5},{5,6},{6,7},{7,0},{8,9},{9,10},{10,1... | collective-permute-start | bytes 104456 | tf_op jit(solution)/shard_map/ppermute | solution.py:480

commit v11 on v10

--- a/solution.py
+++ b/solution.py
@@ -181,19 +181,6 @@
     )(counts, connectivity)
 
 
-def first_join_kernel(*refs):
-    *inputs, chunk_ref, wide_ref = refs
-    parts = len(inputs) // 2
-    count = inputs[0].shape[0]
-    wide_ref[...] = jnp.zeros_like(wide_ref)
-    total = jnp.zeros(wide_ref.shape, F32)
-    for part in range(parts):
-        chunk_ref[part * count : (part + 1) * count, :] = inputs[part][...]
-        wide_ref[:3, :count] = inputs[parts + part][...].astype(F32)
-        total = total + (pltpu.roll(wide_ref[...], part * count, 1) if part else wide_ref[...])
-    chunk_ref[parts * count :, :] = total.astype(BF16)
-
-
 def join_kernel(mine_ref, other_ref, chunk_ref):
     span = mine_ref.shape[0] - EXTRA
     chunk_ref[:span, :] = mine_ref[:span, :]
@@ -215,7 +202,7 @@
     source_ref, panel_ref = take(2)
     if last:
         loading_in, thick_in, slot_ref, ids_ref, edge_ref = take(5)
-        loading_ref, message_ref, rim_ref, thick_ref = take(4)
+        loading_ref, message_at, rim_ref, thick_ref, message_ref, sem = take(6)
     else:
         loading_in, thick_in = (None, None) if first else take(2)
         loading_ref, thick_ref = take(2)
@@ -272,16 +259,17 @@
                 weight_ref[block, BLK + strip * 16 : BLK + strip * 16 + 16, cols] = far.astype(BF16)
                 weight_ref[block, 2 * BLK + strip * 16 : 2 * BLK + strip * 16 + 16, cols] = (area * inverse).astype(BF16)
         rows = slice(block * BLK, (block + 1) * BLK)
+        if last:
+            alive = block * BLK + lax.broadcasted_iota(jnp.int32, (BLK, TW), 0) < count_ref[0]
+            thick = jnp.dot(weight_ref[block, 2 * BLK :, :], window_ref[block, :, TW:], preferred_element_type=F32)
+            thick_ref[rows, :] = jnp.where(alive, thick + thick_in[rows, :], 0.0).astype(BF16)
+            continue
         products = jnp.dot(weight_ref[block], window_ref[block], preferred_element_type=F32)
         thick = products[2 * BLK :, TW:]
         loading = products[:BLK, :TW] + products[BLK : 2 * BLK, TW:]
         if not first:
             thick = thick + thick_in[rows, :]
             loading = loading + loading_in[rows, :]
-        if last:
-            alive = block * BLK + lax.broadcasted_iota(jnp.int32, (BLK, TW), 0) < count_ref[0]
-            thick = jnp.where(alive, thick, 0.0).astype(BF16)
-            loading = jnp.where(alive, loading, 0.0).astype(BF16)
         thick_ref[rows, :] = thick
         loading_ref[rows, :] = loading
 
@@ -293,8 +281,20 @@
             message_ref[section, :cap, :] = slots[section * cap : (section + 1) * cap]
             ids = jnp.broadcast_to(ids_ref[section : section + 1, :], (EXTRA, 128))
             message_ref[section, cap:, :] = ids.astype(BF16)
+        copy = pltpu.make_async_copy(message_ref, message_at, sem.at[0])
+        copy.start()
+        for block in range(blocks):
+            rows = slice(block * BLK, (block + 1) * BLK)
+            alive = block * BLK + lax.broadcasted_iota(jnp.int32, (BLK, TW), 0) < count_ref[0]
+            loading = loading_in[rows, :]
+            for half in range(2):
+                weight = weight_ref[block, half * BLK : (half + 1) * BLK, :]
+                window = window_ref[block, :, half * TW : (half + 1) * TW]
+                loading = loading + jnp.dot(weight, window, preferred_element_type=F32)
+            loading_ref[rows, :] = jnp.where(alive, loading, 0.0).astype(BF16)
         rim = jnp.dot(edge_ref[...], loading_ref[...], preferred_element_type=F32)
         rim_ref[...] = rim[8:].astype(BF16)
+        copy.wait()
 
 
 def sources(places, counts, chunks, source, panel_values, sums=(), slots=None, sections=None):
@@ -318,17 +318,20 @@
             jax.ShapeDtypeStruct((sections, cap + EXTRA, TW), BF16),
             jax.ShapeDtypeStruct((HEAD, TW), BF16),
         ]
-        scratch = [VMEM((panels, TW), BF16)] + scratch
+        scratch = [VMEM((panels, TW), BF16), VMEM(out_shape[1].shape, BF16), COPY((1,))] + scratch
     else:
         out_shape = [jax.ShapeDtypeStruct((panels, TW), F32)] * 2
         if sums:
             aliases = {len(operands) - 2: 0, len(operands) - 1: 1}
+    out_specs = [WHOLE] * len(out_shape)
+    if last:
+        out_specs[1] = PLACE
     return call(
         functools.partial(sources_kernel, places, not sums, last),
         "sources",
         out_shape,
         [SMEM] + [WHOLE] * (len(operands) - 1),
-        [WHOLE] * len(out_shape),
+        out_specs,
         scratch,
         aliases,
         work=3_000_000_000,
@@ -406,12 +409,9 @@
 
 def half_chunk(signals, xyz, sections):
     count, width = signals.shape
-    turned = xyz.T
-    shape = jax.ShapeDtypeStruct((2 * count + EXTRA, width), BF16)
-    chunk = call(first_join_kernel, "first", shape, [WHOLE] * 4, WHOLE, [VMEM((EXTRA, width), F32)])(
-        signals, swapped(signals, "sect", 2), turned, swapped(turned, "sect", 2)
-    )
-    bit = 4
+    extra = jnp.pad(xyz.T, ((0, EXTRA - 3), (0, width - count)))
+    chunk = jnp.concatenate([signals, extra], 0)
+    bit = 2
     while bit < sections:
         chunk = joined(chunk, swapped(chunk, "sect", bit))
         bit *= 2

time: 44 us -> 44.4 us (level)
  waiting for transfers between devices: 9.66 us -> 7.95 us
  starting transfers between devices: 16 us -> 17.3 us
  other arithmetic: 0 us -> 0.74 us
    ppermute x7 -> x6, waiting for transfers between devices: 4.09 us -> 2.38 us  [swapped(): return lax.ppermute(array, axis, [(i, i ^ bit) for i in range(peers)])]
    all_to_all x1, starting transfers between devices: 4.67 us -> 6.25 us  [per_device(): lax.all_to_all(message, 'sect', split_axis=0, concat_axis=0, tiled=True)]
    concatenate x0 -> x1, other arithmetic: none -> 0.74 us  [half_chunk(): chunk = jnp.concatenate([signals, extra], 0)]
    ppermute x7 -> x6, starting transfers between devices: 9.29 us -> 8.99 us  [swapped(): return lax.ppermute(array, axis, [(i, i ^ bit) for i in range(peers)])]
  transfers between devices with their start and end apart: 9 -> 8, of which waited for: 5 -> 4; matrix products, arithmetic and copies ran while one was open for 0% -> 0% of each run, Pallas kernels for 26% -> 26%
where the time goes in v11:
time: 44.4 us; the launch traced here: 44.1 us
  starting transfers between devices  17.3 us (39%)
  Pallas kernels  16 us (36%)
  waiting for transfers between devices  7.95 us (18%)
  between operations  1.38 us (3%)
  local copies, waits for them, and re-layouts  0.77 us (2%)
  other arithmetic  0.74 us (2%)
    pallas_call x5, Pallas kernels, sources(): call(functools.partial(sources_kernel, places, not sums, last), 'sources'...  10.6 us
    ppermute x6, starting transfers between devices, swapped(): return lax.ppermute(array, axis, [(i, i ^ bit) for i in range(peers)])  8.99 us
    all_to_all x1, starting transfers between devices, per_device(): lax.all_to_all(message, 'sect', split_axis=0, concat_axis=0, tiled=True)  6.25 us
    ppermute x1, waiting for transfers between devices, per_device(): lax.ppermute(rim, 'sect', [(i, (i + 1) % sections) for i in range(section...  5.57 us
    ppermute x6, waiting for transfers between devices, swapped(): return lax.ppermute(array, axis, [(i, i ^ bit) for i in range(peers)])  2.38 us
    ppermute x1, starting transfers between devices, per_device(): lax.ppermute(rim, 'sect', [(i, (i + 1) % sections) for i in range(section...  2.02 us
    pallas_call x1, Pallas kernels, node_sums(): call(node_kernel, 'nodes', (jax.ShapeDtypeStruct((NODE_DEV, TW), F32), ja...  1.51 us
    pallas_call x1, Pallas kernels, panel_columns(): call(functools.partial(column_kernel, sections), 'columns', (jax.ShapeDty...  1.11 us
  transfers between devices with their start and end apart: 8, of which 4 were waited for; matrix products, arithmetic and copies ran while one was open for 0% of the time, Pallas kernels for 26%

profile of v11, /device:TPU:0, one launch (start us, length us, event | category | flops | bytes accessed | tf_op | source)
XLA Modules:
  0.0 44.1 jit_solution(9981149456050195261)
XLA Ops:
  0.6 0.7 %fusion.1.mine_ref = bf16[48,256]{1,0:T(8,128)(2,1)S(1)} fusion(bf16[3,32]{1,0:T(4,128)(2,1)} %bitcast.3, bf16[32,256]{1,0:T(8,128)(2,1)} %param.7), kind=kLoop, calls=%fused_computation.2 | loop fusion | flops 73728 | bytes 41152 | tf_op jit(solution)/shard_map/concatenate | solution.py:413
  1.4 3.0 %collective-permute-start = (bf16[48,256]{1,0:T(8,128)(2,1)S(1)}, bf16[48,256]{1,0:T(8,128)(2,1)S(1)}, u32[]{:S(2)}, u32[]{:S(2)}) collective-permute-start(bf16[48,256]{1,0:T(8,128)(2,1)S(1)} %fusion.1.mine_ref), channel_id=1, source_target_pairs={{0,2},{1,3},{2,0},{3,1},{4,6},{5,7},{6,4},{7,5},{8,10},{9,11},{10,... | collective-permute-start | bytes 73736 | tf_op jit(solution)/shard_map/ppermute | solution.py:401
  4.4 0.8 %copy-done = s32[8,1024]{1,0:T(8,128)S(1)} copy-done((s32[8,1024]{1,0:T(8,128)S(1)}, s32[8,1024]{1,0:T(8,128)}, u32[]{:S(2)}) %copy-start) | copy-done | bytes 32792
  5.2 0.7 %windows.1.refs_1_ = s32[4,8,256,128]{3,2,1,0:T(8,128)S(1)} custom-call(s32[8,1024]{1,0:T(8,128)S(1)} %copy-done), custom_call_target="tpu_custom_call" | custom-call | flops 2000000000 | bytes 4000000 | tf_op jit(solution)/shard_map/windows/pallas_call | solution.py:73
  6.6 0.1 join.3.mine_ref
  6.6 2.7 %collective-permute-start.1 = (bf16[80,256]{1,0:T(8,128)(2,1)S(1)}, bf16[80,256]{1,0:T(8,128)(2,1)S(1)}, u32[]{:S(2)}, u32[]{:S(2)}) collective-permute-start(bf16[80,256]{1,0:T(8,128)(2,1)S(1)} %join.3.mine_ref), channel_id=1, source_target_pairs={{0,4},{1,5},{2,6},{3,7},{4,0},{5,1},{6,2},{7,3},{8,12},{9,13},{10,... | collective-permute-start | bytes 122888 | tf_op jit(solution)/shard_map/ppermute | solution.py:401
  9.3 1.1 %columns.1 = (f32[8,7,128,128]{3,2,1,0:T(8,128)S(1)}, bf16[512,1024]{1,0:T(8,128)(2,1)S(1)}, f32[16,128]{1,0:T(8,128)S(1)}) custom-call(s32[1]{0:T(128)S(6)} %copy.23.count_ref, f32[7,1024]{1,0:T(8,128)S(1)} %copy-done.1, s32[1,1024]{1,0:T(1,128)S(1)} %bitcast.2), custom_call_target="tpu_custom_call" | custom-call | flops 2000000000 | bytes 4000000 | tf_op jit(solution)/shard_map/columns/pallas_call | solution.py:137
  10.4 1.1 %collective-permute-done.1.other_ref = bf16[80,256]{1,0:T(8,128)(2,1)S(1)} collective-permute-done((bf16[80,256]{1,0:T(8,128)(2,1)S(1)}, bf16[80,256]{1,0:T(8,128)(2,1)S(1)}, u32[]{:S(2)}, u32[]{:S(2)}) %collective-permute-start.1) | collective-permute-done | bytes 40992 | tf_op jit(solution)/shard_map/ppermute | solution.py:401
  11.6 0.1 join.4.mine_ref.refs_0_
  11.6 1.6 %collective-permute-start.2 = (bf16[144,256]{1,0:T(8,128)(2,1)S(1)}, bf16[144,256]{1,0:T(8,128)(2,1)S(1)}, u32[]{:S(2)}, u32[]{:S(2)}) collective-permute-start(bf16[144,256]{1,0:T(8,128)(2,1)S(1)} %join.4.mine_ref.refs_0_), channel_id=1, source_target_pairs={{0,1},{1,0},{2,3},{3,2},{4,5},{5,4},{6,7},{7,6},{8,9},{9,8},{10,11... | collective-permute-start | bytes 221192 | tf_op jit(solution)/shard_map/ppermute | solution.py:401
  13.2 1.3 %sources.5 = (f32[1024,128]{1,0:T(8,128)S(1)}, f32[1024,128]{1,0:T(8,128)S(1)}) custom-call(s32[1]{0:T(128)S(6)} %copy.23.count_ref, bf16[144,256]{1,0:T(8,128)(2,1)S(1)} %join.4.mine_ref.refs_0_, s32[4,8,256,128]{3,2,1,0:T(8,128)S(1)} %windows.1.refs_1_, f32[8,7,128,128]{3,2,1,0:T(8,128)S(1)} %get-tuple-element.26.refs_2_), custom_call_target="tpu_custom_call" | custom-call | flops 3000000000 | bytes 4000000 | tf_op jit(solution)/shard_map/sources/pallas_call | solution.py:329
  14.5 1.0 %corners.1 = (bf16[1040,1024]{1,0:T(8,128)(2,1)S(1)}, bf16[144,1024]{1,0:T(8,128)(2,1)S(1)}) custom-call(s32[1]{0:T(128)S(6)} %copy.23.count_ref, s32[4,1024]{1,0:T(4,128)S(1)} %copy-done.2), custom_call_target="tpu_custom_call" | custom-call | flops 2000000000 | bytes 4000000 | tf_op jit(solution)/shard_map/corners/pallas_call | solution.py:171
  15.5 0.5 %collective-permute-done.2.other_ref.refs_0_ = bf16[144,256]{1,0:T(8,128)(2,1)S(1)} collective-permute-done((bf16[144,256]{1,0:T(8,128)(2,1)S(1)}, bf16[144,256]{1,0:T(8,128)(2,1)S(1)}, u32[]{:S(2)}, u32[]{:S(2)}) %collective-permute-start.2) | collective-permute-done | bytes 73760 | tf_op jit(solution)/shard_map/ppermute | solution.py:401
  16.1 1.6 %collective-permute-start.3 = (bf16[272,256]{1,0:T(8,128)(2,1)S(1)}, bf16[272,256]{1,0:T(8,128)(2,1)S(1)}, u32[]{:S(2)}, u32[]{:S(2)}) collective-permute-start(bf16[272,256]{1,0:T(8,128)(2,1)S(1)} %join.5), channel_id=1, source_target_pairs={{0,16},{8,24},{16,0},{24,8},{1,17},{9,25},{17,1},{25,9},{2,18},{10... | collective-permute-start | bytes 417800 | tf_op jit(solution)/shard_map/ppermute | solution.py:401
  17.7 1.4 %sources.6 = (f32[1024,128]{1,0:T(8,128)S(1)}, f32[1024,128]{1,0:T(8,128)S(1)}) custom-call(s32[1]{0:T(128)S(6)} %copy.23.count_ref, bf16[144,256]{1,0:T(8,128)(2,1)S(1)} %collective-permute-done.2.other_ref.refs_0_, s32[4,8,256,128]{3,2,1,0:T(8,128)S(1)} %windows.1.refs_1_, ...), custom_call_target="tpu_custom_call", output_to_operand_aliasing={{0}: (4, {}), {1}: (5, {})} | custom-call | flops 3000000000 | bytes 4000000 | tf_op jit(solution)/shard_map/sources/pallas_call | solution.py:329
  19.1 2.3 %sources.7 = (f32[1024,128]{1,0:T(8,128)S(1)}, f32[1024,128]{1,0:T(8,128)S(1)}) custom-call(s32[1]{0:T(128)S(6)} %copy.23.count_ref, bf16[272,256]{1,0:T(8,128)(2,1)S(1)} %collective-permute-done.4.refs_0_, s32[4,8,256,128]{3,2,1,0:T(8,128)S(1)} %windows.1.refs_1_, ...), custom_call_target="tpu_custom_call", output_to_operand_aliasing={{0}: (4, {}), {1}: (5, {})} | custom-call | flops 3000000000 | bytes 4000000 | tf_op jit(solution)/shard_map/sources/pallas_call | solution.py:329
  21.4 0.7 %collective-permute-done.3.refs_0_ = bf16[272,256]{1,0:T(8,128)(2,1)S(1)} collective-permute-done((bf16[272,256]{1,0:T(8,128)(2,1)S(1)}, bf16[272,256]{1,0:T(8,128)(2,1)S(1)}, u32[]{:S(2)}, u32[]{:S(2)}) %collective-permute-start.3) | collective-permute-done | bytes 139296 | tf_op jit(solution)/shard_map/ppermute | solution.py:401
  22.2 2.3 %sources.8 = (f32[1024,128]{1,0:T(8,128)S(1)}, f32[1024,128]{1,0:T(8,128)S(1)}) custom-call(s32[1]{0:T(128)S(6)} %copy.23.count_ref, bf16[272,256]{1,0:T(8,128)(2,1)S(1)} %collective-permute-done.3.refs_0_, s32[4,8,256,128]{3,2,1,0:T(8,128)S(1)} %windows.1.refs_1_, ...), custom_call_target="tpu_custom_call", output_to_operand_aliasing={{0}: (4, {}), {1}: (5, {})} | custom-call | flops 3000000000 | bytes 4000000 | tf_op jit(solution)/shard_map/sources/pallas_call | solution.py:329
  24.5 3.3 %sources.9 = (bf16[1024,128]{1,0:T(8,128)(2,1)S(1)}, bf16[8,80,128]{2,1,0:T(8,128)(2,1)}, bf16[136,128]{1,0:T(8,128)(2,1)S(1)}) custom-call(s32[1]{0:T(128)S(6)} %copy.23.count_ref, bf16[272,256]{1,0:T(8,128)(2,1)S(1)} %collective-permute-done.5.refs_0_, s32[4,8,256,128]{3,2,1,0:T(8,128)S(1)} %windows.1.refs_1_, ...), custom_call_target="tpu_custom_call" | custom-call | flops 3000000000 | bytes 4000000 | tf_op jit(solution)/shard_map/sources/pallas_call | solution.py:329
  27.8 6.2 %all-to-all-start = ((bf16[8,80,128]{2,1,0:T(8,128)(2,1)}), bf16[8,80,128]{2,1,0:T(8,128)(2,1)S(1)}, u32[]{:S(2)}, u32[]{:S(2)}) async-start(bf16[8,80,128]{2,1,0:T(8,128)(2,1)} %get-tuple-element.42), calls=%async_computation | async-start | bytes 327680 | tf_op jit(solution)/shard_map/all_to_all | solution.py:479
  34.1 2.0 %collective-permute-start.6 = (bf16[136,128]{1,0:T(8,128)(2,1)S(1)}, bf16[136,128]{1,0:T(8,128)(2,1)S(1)}, u32[]{:S(2)}, u32[]{:S(2)}) collective-permute-start(bf16[136,128]{1,0:T(8,128)(2,1)S(1)} %get-tuple-element.43), channel_id=1, source_target_pairs={{0,1},{1,2},{2,3},{3,4},{4,5},{5,6},{6,7},{7,0},{8,9},{9,10},{10,1... | collective-permute-start | bytes 104456 | tf_op jit(solution)/shard_map/ppermute | solution.py:480
  36.1 1.5 %nodes.1 = (f32[1032,128]{1,0:T(8,128)}, f32[136,128]{1,0:T(8,128)S(1)}) custom-call(bf16[1040,1024]{1,0:T(8,128)(2,1)S(1)} %get-tuple-element.44.corner_ref, bf16[1024,128]{1,0:T(8,128)(2,1)S(1)} %get-tuple-element.45.loading_ref), custom_call_target="tpu_custom_call" | custom-call | flops 2000000000 | bytes 4000000 | tf_op jit(solution)/shard_map/nodes/pallas_call | solution.py:348
  37.6 5.6 %collective-permute-done.6.rim_ref = bf16[136,128]{1,0:T(8,128)(2,1)S(1)} collective-permute-done((bf16[136,128]{1,0:T(8,128)(2,1)S(1)}, bf16[136,128]{1,0:T(8,128)(2,1)S(1)}, u32[]{:S(2)}, u32[]{:S(2)}) %collective-permute-start.6) | collective-permute-done | bytes 34848 | tf_op jit(solution)/shard_map/ppermute | solution.py:480
  43.2 0.9 %finish.1 = (f32[1032,128]{1,0:T(8,128)}, f32[256,128]{1,0:T(8,128)}) custom-call(bf16[8,80,128]{2,1,0:T(8,128)(2,1)S(1)} %all-to-all-done.message_ref, bf16[136,128]{1,0:T(8,128)(2,1)S(1)} %collective-permute-done.6.rim_ref, f32[136,128]{1,0:T(8,128)S(1)} %get-tuple-element.46.head_ref, ...), custom_call_target="tpu_custom_call", output_to_operand_aliasing={{0}: (3, {})} | custom-call | flops 1000000 | bytes 4000000 | tf_op jit(solution)/shard_map/finish/pallas_call | solution.py:385
  (14 shorter events, 0.1 us)
Async XLA Ops:
  1.4 5.2 %collective-permute-start = (bf16[48,256]{1,0:T(8,128)(2,1)S(1)}, bf16[48,256]{1,0:T(8,128)(2,1)S(1)}, u32[]{:S(2)}, u32[]{:S(2)}) collective-permute-start(bf16[48,256]{1,0:T(8,128)(2,1)S(1)} %fusion.1.mine_ref), channel_id=1, source_target_pairs={{0,2},{1,3},{2,0},{3,1},{4,6},{5,7},{6,4},{7,5},{8,10},{9,11},{10,... | collective-permute-start | bytes 73736 | tf_op jit(solution)/shard_map/ppermute | solution.py:401
  4.4 0.8 %copy-start = (s32[8,1024]{1,0:T(8,128)S(1)}, s32[8,1024]{1,0:T(8,128)}, u32[]{:S(2)}) copy-start(s32[8,1024]{1,0:T(8,128)} %delay_ref.1) | copy-start | bytes 98308
  5.2 4.2 %copy-start.1 = (f32[7,1024]{1,0:T(8,128)S(1)}, f32[7,1024]{1,0:T(8,128)}, u32[]{:S(2)}) copy-start(f32[7,1024]{1,0:T(8,128)} %geometry_ref) | copy-start | bytes 86020
  5.2 4.2 %copy-start.3 = (s32[1024]{0:T(1024)S(1)}, s32[1024]{0:T(1024)}, u32[]{:S(2)}) copy-start(s32[1024]{0:T(1024)} %param.13) | copy-start | bytes 12292
  6.6 4.9 %collective-permute-start.1 = (bf16[80,256]{1,0:T(8,128)(2,1)S(1)}, bf16[80,256]{1,0:T(8,128)(2,1)S(1)}, u32[]{:S(2)}, u32[]{:S(2)}) collective-permute-start(bf16[80,256]{1,0:T(8,128)(2,1)S(1)} %join.3.mine_ref), channel_id=1, source_target_pairs={{0,4},{1,5},{2,6},{3,7},{4,0},{5,1},{6,2},{7,3},{8,12},{9,13},{10,... | collective-permute-start | bytes 122888 | tf_op jit(solution)/shard_map/ppermute | solution.py:401
  11.6 4.4 %collective-permute-start.2 = (bf16[144,256]{1,0:T(8,128)(2,1)S(1)}, bf16[144,256]{1,0:T(8,128)(2,1)S(1)}, u32[]{:S(2)}, u32[]{:S(2)}) collective-permute-start(bf16[144,256]{1,0:T(8,128)(2,1)S(1)} %join.4.mine_ref.refs_0_), channel_id=1, source_target_pairs={{0,1},{1,0},{2,3},{3,2},{4,5},{5,4},{6,7},{7,6},{8,9},{9,8},{10,11... | collective-permute-start | bytes 221192 | tf_op jit(solution)/shard_map/ppermute | solution.py:401
  13.2 1.3 %copy-start.2 = (s32[4,1024]{1,0:T(4,128)S(1)}, s32[4,1024]{1,0:T(4,128)}, u32[]{:S(2)}) copy-start(s32[4,1024]{1,0:T(4,128)} %conn_ref) | copy-start | bytes 49156
  16.0 3.1 %collective-permute-start.4 = (bf16[272,256]{1,0:T(8,128)(2,1)S(1)}, bf16[272,256]{1,0:T(8,128)(2,1)S(1)}, u32[]{:S(2)}, u32[]{:S(2)}) collective-permute-start(bf16[272,256]{1,0:T(8,128)(2,1)S(1)} %join.5), channel_id=1, source_target_pairs={{0,8},{8,0},{16,24},{24,16},{1,9},{9,1},{17,25},{25,17},{2,10},{10... | collective-permute-start | bytes 417800 | tf_op jit(solution)/shard_map/ppermute | solution.py:401
  16.1 6.1 %collective-permute-start.3 = (bf16[272,256]{1,0:T(8,128)(2,1)S(1)}, bf16[272,256]{1,0:T(8,128)(2,1)S(1)}, u32[]{:S(2)}, u32[]{:S(2)}) collective-permute-start(bf16[272,256]{1,0:T(8,128)(2,1)S(1)} %join.5), channel_id=1, source_target_pairs={{0,16},{8,24},{16,0},{24,8},{1,17},{9,25},{17,1},{25,9},{2,18},{10... | collective-permute-start | bytes 417800 | tf_op jit(solution)/shard_map/ppermute | solution.py:401
  22.2 2.3 %collective-permute-start.5 = (bf16[272,256]{1,0:T(8,128)(2,1)S(1)}, bf16[272,256]{1,0:T(8,128)(2,1)S(1)}, u32[]{:S(2)}, u32[]{:S(2)}) collective-permute-start(bf16[272,256]{1,0:T(8,128)(2,1)S(1)} %collective-permute-done.3.refs_0_), channel_id=1, source_target_pairs={{0,8},{8,0},{16,24},{24,16},{1,9},{9,1},{17,25},{25,17},{2,10},{10... | collective-permute-start | bytes 417800 | tf_op jit(solution)/shard_map/ppermute | solution.py:401
  27.8 15.4 %all-to-all-start = ((bf16[8,80,128]{2,1,0:T(8,128)(2,1)}), bf16[8,80,128]{2,1,0:T(8,128)(2,1)S(1)}, u32[]{:S(2)}, u32[]{:S(2)}) async-start(bf16[8,80,128]{2,1,0:T(8,128)(2,1)} %get-tuple-element.42), calls=%async_computation | async-start | bytes 327680 | tf_op jit(solution)/shard_map/all_to_all | solution.py:479
  34.1 9.1 %collective-permute-start.6 = (bf16[136,128]{1,0:T(8,128)(2,1)S(1)}, bf16[136,128]{1,0:T(8,128)(2,1)S(1)}, u32[]{:S(2)}, u32[]{:S(2)}) collective-permute-start(bf16[136,128]{1,0:T(8,128)(2,1)S(1)} %get-tuple-element.43), channel_id=1, source_target_pairs={{0,1},{1,2},{2,3},{3,4},{4,5},{5,6},{6,7},{7,0},{8,9},{9,10},{10,1... | collective-permute-start | bytes 104456 | tf_op jit(solution)/shard_map/ppermute | solution.py:480

commit v12 on v10

--- a/solution.py
+++ b/solution.py
@@ -335,30 +335,27 @@
     )(*operands)
 
 
-def node_kernel(corner_ref, loading_ref, node_ref, head_ref):
+def node_kernel(corner_ref, loading_ref, rim_ref, node_ref):
     nodes = jnp.dot(corner_ref[...], loading_ref[...], preferred_element_type=F32)
-    head_ref[...] = nodes[:HEAD]
-    node_ref[...] = nodes[:NODE_DEV]
-
-
-def node_sums(corners, loading):
+    node_ref[:HEAD, :] = nodes[:HEAD] + rim_ref[...].astype(F32)
+    node_ref[HEAD:, :] = nodes[HEAD:NODE_DEV]
+
+
+def node_sums(corners, loading, rim):
     return call(
         node_kernel,
         "nodes",
-        (jax.ShapeDtypeStruct((NODE_DEV, TW), F32), jax.ShapeDtypeStruct((HEAD, TW), F32)),
-        [WHOLE] * 2,
-        [WHOLE] * 2,
-        work=2_000_000_000,
-    )(corners, loading)
-
-
-def finish_kernel(message_ref, rim_ref, head_ref, _, node_ref, cell_ref, rows_ref, top_ref, total_ref, sems):
+        jax.ShapeDtypeStruct((NODE_DEV, TW), F32),
+        [WHOLE] * 3,
+        WHOLE,
+        work=20_000_000_000,
+    )(corners, loading, rim)
+
+
+def cell_kernel(message_ref, cell_ref, rows_ref):
     sections = message_ref.shape[0]
     cap = message_ref.shape[1] - EXTRA
     per = 128 // cap
-    top_ref[...] = head_ref[...] + rim_ref[...].astype(F32)
-    top_copy = pltpu.make_async_copy(top_ref, node_ref.at[pl.ds(0, HEAD), :], sems.at[0])
-    top_copy.start()
     total = jnp.zeros((CELL_DEV, TW), F32)
     cell = lax.broadcasted_iota(jnp.int32, (CELL_DEV, 128), 0).astype(F32)
     for group in range(sections // per):
@@ -369,28 +366,20 @@
             rows_ref[section * cap : (section + 1) * cap, :] = message_ref[section, :cap, :]
         match = jnp.where(ids[:1] == cell, 1.0, 0.0).astype(BF16)
         total = total + jnp.dot(match, rows_ref[group * 128 : (group + 1) * 128, :], preferred_element_type=F32)
-    total_ref[...] = total
-    cell_copy = pltpu.make_async_copy(total_ref, cell_ref, sems.at[1])
-    cell_copy.start()
-    top_copy.wait()
-    cell_copy.wait()
-
-
-def finish(message, rim, head, nodes):
+    cell_ref[...] = total
+
+
+def cell_sums(message):
     sections = message.shape[0]
     cap = message.shape[1] - EXTRA
     return call(
-        finish_kernel,
-        "finish",
-        (
-            jax.ShapeDtypeStruct((NODE_DEV, TW), F32),
-            jax.ShapeDtypeStruct((CELL_DEV, TW), F32),
-        ),
-        [WHOLE] * 3 + [PLACE],
-        [PLACE] * 2,
-        [VMEM((sections * cap, TW), BF16), VMEM((HEAD, TW), F32), VMEM((CELL_DEV, TW), F32), COPY((2,))],
-        {3: 0},
-    )(message, rim, head, nodes)
+        cell_kernel,
+        "cells",
+        jax.ShapeDtypeStruct((CELL_DEV, TW), F32),
+        [WHOLE],
+        WHOLE,
+        [VMEM((sections * cap, TW), BF16)],
+    )(message)
 
 
 def swapped(array, axis, bit):
@@ -478,8 +467,7 @@
     loading, message, rim = add(sums, [(o, 0) for o in rest], [chunks[o] for o in rest], matrices, sections)
     message = lax.all_to_all(message, "sect", split_axis=0, concat_axis=0, tiled=True)
     rim = lax.ppermute(rim, "sect", [(i, (i + 1) % sections) for i in range(sections)])
-    nodes, head = node_sums(corners, loading)
-    return finish(message, rim, head, nodes)
+    return node_sums(corners, loading, rim), cell_sums(message)
 
 
 def solution(mesh):

time: 44 us -> 44 us (level)
  waiting for transfers between devices: 9.66 us -> 10.4 us
  starting transfers between devices: 16 us -> 15.3 us
    all_to_all x1, waiting for transfers between devices: 0.01 us -> 5.7 us  [per_device(): lax.all_to_all(message, 'sect', split_axis=0, concat_axis=0, tiled=True)]
    ppermute x1, waiting for transfers between devices: 5.57 us -> 0.63 us  [per_device(): lax.ppermute(rim, 'sect', [(i, (i + 1) % sections) for i in range(section...]
  transfers between devices with their start and end apart: 9 -> 9, of which waited for: 5 -> 6; matrix products, arithmetic and copies ran while one was open for 0% -> 0% of each run, Pallas kernels for 26% -> 26%
where the time goes in v12:
time: 44 us; the launch traced here: 43.7 us
  Pallas kernels  15.8 us (36%)
  starting transfers between devices  15.3 us (35%)
  waiting for transfers between devices  10.4 us (24%)
  between operations  1.4 us (3%)
  local copies, waits for them, and re-layouts  0.78 us (2%)
    pallas_call x5, Pallas kernels, sources(): call(functools.partial(sources_kernel, places, not sums, last), 'sources'...  10.5 us
    ppermute x7, starting transfers between devices, swapped(): return lax.ppermute(array, axis, [(i, i ^ bit) for i in range(peers)])  9.29 us
    all_to_all x1, waiting for transfers between devices, per_device(): lax.all_to_all(message, 'sect', split_axis=0, concat_axis=0, tiled=True)  5.7 us
    all_to_all x1, starting transfers between devices, per_device(): lax.all_to_all(message, 'sect', split_axis=0, concat_axis=0, tiled=True)  4.3 us
    ppermute x7, waiting for transfers between devices, swapped(): return lax.ppermute(array, axis, [(i, i ^ bit) for i in range(peers)])  4.09 us
    ppermute x1, starting transfers between devices, per_device(): lax.ppermute(rim, 'sect', [(i, (i + 1) % sections) for i in range(section...  1.69 us
    pallas_call x1, Pallas kernels, node_sums(): call(node_kernel, 'nodes', jax.ShapeDtypeStruct((NODE_DEV, TW), F32), [WH...  1.51 us
    pallas_call x1, Pallas kernels, panel_columns(): call(functools.partial(column_kernel, sections), 'columns', (jax.ShapeDty...  1.11 us
  transfers between devices with their start and end apart: 9, of which 6 were waited for; matrix products, arithmetic and copies ran while one was open for 0% of the time, Pallas kernels for 26%

profile of v12, /device:TPU:0, one launch (start us, length us, event | category | flops | bytes accessed | tf_op | source)
XLA Modules:
  0.0 43.7 jit_solution(17122825351404308128)
XLA Ops:
  0.7 3.1 %collective-permute-start.1 = (bf16[3,32]{1,0:T(4,128)(2,1)}, bf16[3,32]{1,0:T(4,128)(2,1)S(1)}, u32[]{:S(2)}, u32[]{:S(2)}) collective-permute-start(bf16[3,32]{1,0:T(4,128)(2,1)} %bitcast.2), channel_id=1, source_target_pairs={{0,2},{1,3},{2,0},{3,1},{4,6},{5,7},{6,4},{7,5},{8,10},{9,11},{10,... | collective-permute-start | bytes 584 | tf_op jit(solution)/shard_map/ppermute | solution.py:387
  3.7 0.1 collective-permute-start
  3.8 0.8 %copy-done.2 = s32[8,1024]{1,0:T(8,128)S(1)} copy-done((s32[8,1024]{1,0:T(8,128)S(1)}, s32[8,1024]{1,0:T(8,128)}, u32[]{:S(2)}) %copy-start.2) | copy-done | bytes 32792
  4.6 0.7 %windows.1.refs_1_ = s32[4,8,256,128]{3,2,1,0:T(8,128)S(1)} custom-call(s32[8,1024]{1,0:T(8,128)S(1)} %copy-done.2), custom_call_target="tpu_custom_call" | custom-call | flops 2000000000 | bytes 4000000 | tf_op jit(solution)/shard_map/windows/pallas_call | solution.py:73
  6.0 1.7 %collective-permute-done.refs_1_ = bf16[32,256]{1,0:T(8,128)(2,1)S(1)} collective-permute-done((bf16[32,256]{1,0:T(8,128)(2,1)}, bf16[32,256]{1,0:T(8,128)(2,1)S(1)}, u32[]{:S(2)}, u32[]{:S(2)}) %collective-permute-start) | collective-permute-done | bytes 16416 | tf_op jit(solution)/shard_map/ppermute | solution.py:387
  7.8 2.6 %collective-permute-start.2 = (bf16[80,256]{1,0:T(8,128)(2,1)S(1)}, bf16[80,256]{1,0:T(8,128)(2,1)S(1)}, u32[]{:S(2)}, u32[]{:S(2)}) collective-permute-start(bf16[80,256]{1,0:T(8,128)(2,1)S(1)} %first.1.mine_ref), channel_id=1, source_target_pairs={{0,4},{1,5},{2,6},{3,7},{4,0},{5,1},{6,2},{7,3},{8,12},{9,13},{10,... | collective-permute-start | bytes 122888 | tf_op jit(solution)/shard_map/ppermute | solution.py:387
  10.4 1.1 %columns.1 = (f32[8,7,128,128]{3,2,1,0:T(8,128)S(1)}, bf16[512,1024]{1,0:T(8,128)(2,1)S(1)}, f32[16,128]{1,0:T(8,128)S(1)}) custom-call(s32[1]{0:T(128)S(6)} %copy.21.count_ref, f32[7,1024]{1,0:T(8,128)S(1)} %copy-done.3, s32[1,1024]{1,0:T(1,128)S(1)} %bitcast.4), custom_call_target="tpu_custom_call" | custom-call | flops 2000000000 | bytes 4000000 | tf_op jit(solution)/shard_map/columns/pallas_call | solution.py:137
  11.5 1.3 %collective-permute-done.2.other_ref = bf16[80,256]{1,0:T(8,128)(2,1)S(1)} collective-permute-done((bf16[80,256]{1,0:T(8,128)(2,1)S(1)}, bf16[80,256]{1,0:T(8,128)(2,1)S(1)}, u32[]{:S(2)}, u32[]{:S(2)}) %collective-permute-start.2) | collective-permute-done | bytes 40992 | tf_op jit(solution)/shard_map/ppermute | solution.py:387
  12.9 1.7 %collective-permute-start.3 = (bf16[144,256]{1,0:T(8,128)(2,1)S(1)}, bf16[144,256]{1,0:T(8,128)(2,1)S(1)}, u32[]{:S(2)}, u32[]{:S(2)}) collective-permute-start(bf16[144,256]{1,0:T(8,128)(2,1)S(1)} %join.2.mine_ref.refs_0_), channel_id=1, source_target_pairs={{0,1},{1,0},{2,3},{3,2},{4,5},{5,4},{6,7},{7,6},{8,9},{9,8},{10,11... | collective-permute-start | bytes 221192 | tf_op jit(solution)/shard_map/ppermute | solution.py:387
  14.6 1.3 %sources.5 = (f32[1024,128]{1,0:T(8,128)S(1)}, f32[1024,128]{1,0:T(8,128)S(1)}) custom-call(s32[1]{0:T(128)S(6)} %copy.21.count_ref, bf16[144,256]{1,0:T(8,128)(2,1)S(1)} %join.2.mine_ref.refs_0_, s32[4,8,256,128]{3,2,1,0:T(8,128)S(1)} %windows.1.refs_1_, f32[8,7,128,128]{3,2,1,0:T(8,128)S(1)} %get-tuple-element.26.refs_2_), custom_call_target="tpu_custom_call" | custom-call | flops 3000000000 | bytes 4000000 | tf_op jit(solution)/shard_map/sources/pallas_call | solution.py:326
  15.9 1.0 %corners.1 = (bf16[1040,1024]{1,0:T(8,128)(2,1)S(1)}, bf16[144,1024]{1,0:T(8,128)(2,1)S(1)}) custom-call(s32[1]{0:T(128)S(6)} %copy.21.count_ref, s32[4,1024]{1,0:T(4,128)S(1)} %copy-done.4), custom_call_target="tpu_custom_call" | custom-call | flops 2000000000 | bytes 4000000 | tf_op jit(solution)/shard_map/corners/pallas_call | solution.py:171
  16.9 0.4 collective-permute-done.3.other_ref.refs_0_
  17.4 1.7 %collective-permute-start.4 = (bf16[272,256]{1,0:T(8,128)(2,1)S(1)}, bf16[272,256]{1,0:T(8,128)(2,1)S(1)}, u32[]{:S(2)}, u32[]{:S(2)}) collective-permute-start(bf16[272,256]{1,0:T(8,128)(2,1)S(1)} %join.3), channel_id=1, source_target_pairs={{0,16},{8,24},{16,0},{24,8},{1,17},{9,25},{17,1},{25,9},{2,18},{10... | collective-permute-start | bytes 417800 | tf_op jit(solution)/shard_map/ppermute | solution.py:387
  19.1 1.4 %sources.6 = (f32[1024,128]{1,0:T(8,128)S(1)}, f32[1024,128]{1,0:T(8,128)S(1)}) custom-call(s32[1]{0:T(128)S(6)} %copy.21.count_ref, bf16[144,256]{1,0:T(8,128)(2,1)S(1)} %collective-permute-done.3.other_ref.refs_0_, s32[4,8,256,128]{3,2,1,0:T(8,128)S(1)} %windows.1.refs_1_, ...), custom_call_target="tpu_custom_call", output_to_operand_aliasing={{0}: (4, {}), {1}: (5, {})} | custom-call | flops 3000000000 | bytes 4000000 | tf_op jit(solution)/shard_map/sources/pallas_call | solution.py:326
  20.5 2.3 %sources.7 = (f32[1024,128]{1,0:T(8,128)S(1)}, f32[1024,128]{1,0:T(8,128)S(1)}) custom-call(s32[1]{0:T(128)S(6)} %copy.21.count_ref, bf16[272,256]{1,0:T(8,128)(2,1)S(1)} %collective-permute-done.5.refs_0_, s32[4,8,256,128]{3,2,1,0:T(8,128)S(1)} %windows.1.refs_1_, ...), custom_call_target="tpu_custom_call", output_to_operand_aliasing={{0}: (4, {}), {1}: (5, {})} | custom-call | flops 3000000000 | bytes 4000000 | tf_op jit(solution)/shard_map/sources/pallas_call | solution.py:326
  22.8 0.6 %collective-permute-done.4.refs_0_ = bf16[272,256]{1,0:T(8,128)(2,1)S(1)} collective-permute-done((bf16[272,256]{1,0:T(8,128)(2,1)S(1)}, bf16[272,256]{1,0:T(8,128)(2,1)S(1)}, u32[]{:S(2)}, u32[]{:S(2)}) %collective-permute-start.4) | collective-permute-done | bytes 139296 | tf_op jit(solution)/shard_map/ppermute | solution.py:387
  23.5 2.3 %sources.8 = (f32[1024,128]{1,0:T(8,128)S(1)}, f32[1024,128]{1,0:T(8,128)S(1)}) custom-call(s32[1]{0:T(128)S(6)} %copy.21.count_ref, bf16[272,256]{1,0:T(8,128)(2,1)S(1)} %collective-permute-done.4.refs_0_, s32[4,8,256,128]{3,2,1,0:T(8,128)S(1)} %windows.1.refs_1_, ...), custom_call_target="tpu_custom_call", output_to_operand_aliasing={{0}: (4, {}), {1}: (5, {})} | custom-call | flops 3000000000 | bytes 4000000 | tf_op jit(solution)/shard_map/sources/pallas_call | solution.py:326
  25.8 3.2 %sources.9 = (bf16[1024,128]{1,0:T(8,128)(2,1)S(1)}, bf16[8,80,128]{2,1,0:T(8,128)(2,1)}, bf16[136,128]{1,0:T(8,128)(2,1)S(1)}) custom-call(s32[1]{0:T(128)S(6)} %copy.21.count_ref, bf16[272,256]{1,0:T(8,128)(2,1)S(1)} %collective-permute-done.6.refs_0_, s32[4,8,256,128]{3,2,1,0:T(8,128)S(1)} %windows.1.refs_1_, ...), custom_call_target="tpu_custom_call" | custom-call | flops 3000000000 | bytes 4000000 | tf_op jit(solution)/shard_map/sources/pallas_call | solution.py:326
  29.0 1.7 %collective-permute-start.7 = (bf16[136,128]{1,0:T(8,128)(2,1)S(1)}, bf16[136,128]{1,0:T(8,128)(2,1)S(1)}, u32[]{:S(2)}, u32[]{:S(2)}) collective-permute-start(bf16[136,128]{1,0:T(8,128)(2,1)S(1)} %get-tuple-element.42), channel_id=1, source_target_pairs={{0,1},{1,2},{2,3},{3,4},{4,5},{5,6},{6,7},{7,0},{8,9},{9,10},{10,1... | collective-permute-start | bytes 104456 | tf_op jit(solution)/shard_map/ppermute | solution.py:469
  30.7 4.3 %all-to-all-start = ((bf16[8,80,128]{2,1,0:T(8,128)(2,1)}), bf16[8,80,128]{2,1,0:T(8,128)(2,1)S(1)}, u32[]{:S(2)}, u32[]{:S(2)}) async-start(bf16[8,80,128]{2,1,0:T(8,128)(2,1)} %get-tuple-element.43), calls=%async_computation | async-start | bytes 327680 | tf_op jit(solution)/shard_map/all_to_all | solution.py:468
  35.0 0.6 %collective-permute-done.7.rim_ref = bf16[136,128]{1,0:T(8,128)(2,1)S(1)} collective-permute-done((bf16[136,128]{1,0:T(8,128)(2,1)S(1)}, bf16[136,128]{1,0:T(8,128)(2,1)S(1)}, u32[]{:S(2)}, u32[]{:S(2)}) %collective-permute-start.7) | collective-permute-done | bytes 34848 | tf_op jit(solution)/shard_map/ppermute | solution.py:469
  35.6 1.5 %nodes.1 = f32[1032,128]{1,0:T(8,128)} custom-call(bf16[1040,1024]{1,0:T(8,128)(2,1)S(1)} %get-tuple-element.24.corner_ref, bf16[1024,128]{1,0:T(8,128)(2,1)S(1)} %get-tuple-element.41.loading_ref, bf16[136,128]{1,0:T(8,128)(2,1)S(1)} %collective-permute-done.7.rim_ref), custom_call_target="tpu_custom_call" | custom-call | flops 20000000000 | bytes 4000000 | tf_op jit(solution)/shard_map/nodes/pallas_call | solution.py:345
  37.1 5.7 %all-to-all-done.message_ref = bf16[8,80,128]{2,1,0:T(8,128)(2,1)S(1)} async-done(((bf16[8,80,128]{2,1,0:T(8,128)(2,1)}), bf16[8,80,128]{2,1,0:T(8,128)(2,1)S(1)}, u32[]{:S(2)}, u32[]{:S(2)}) %all-to-all-start) | async-done | bytes 163872 | tf_op jit(solution)/shard_map/all_to_all | solution.py:468
  42.8 0.9 %cells.1 = f32[256,128]{1,0:T(8,128)} custom-call(bf16[8,80,128]{2,1,0:T(8,128)(2,1)S(1)} %all-to-all-done.message_ref), custom_call_target="tpu_custom_call" | custom-call | flops 1000000 | bytes 4000000 | tf_op jit(solution)/shard_map/cells/pallas_call | solution.py:375
  (19 shorter events, 0.3 us)
Async XLA Ops:
  0.6 7.1 %copy-start = (bf16[32,256]{1,0:T(8,128)(2,1)S(1)}, bf16[32,256]{1,0:T(8,128)(2,1)}, u32[]{:S(2)}) copy-start(bf16[32,256]{1,0:T(8,128)(2,1)} %refs_0_.1) | copy-start | bytes 49156
  0.6 7.1 %copy-start.1 = (bf16[32,3]{0,1:T(4,128)(2,1)S(1)}, bf16[32,3]{0,1:T(4,128)(2,1)}, u32[]{:S(2)}) copy-start(bf16[32,3]{0,1:T(4,128)(2,1)} %param.8) | copy-start | bytes 580
  0.7 5.3 %collective-permute-start.1 = (bf16[3,32]{1,0:T(4,128)(2,1)}, bf16[3,32]{1,0:T(4,128)(2,1)S(1)}, u32[]{:S(2)}, u32[]{:S(2)}) collective-permute-start(bf16[3,32]{1,0:T(4,128)(2,1)} %bitcast.2), channel_id=1, source_target_pairs={{0,2},{1,3},{2,0},{3,1},{4,6},{5,7},{6,4},{7,5},{8,10},{9,11},{10,... | collective-permute-start | bytes 584 | tf_op jit(solution)/shard_map/ppermute | solution.py:387
  3.7 3.9 %collective-permute-start = (bf16[32,256]{1,0:T(8,128)(2,1)}, bf16[32,256]{1,0:T(8,128)(2,1)S(1)}, u32[]{:S(2)}, u32[]{:S(2)}) collective-permute-start(bf16[32,256]{1,0:T(8,128)(2,1)} %refs_0_.1), channel_id=1, source_target_pairs={{0,2},{1,3},{2,0},{3,1},{4,6},{5,7},{6,4},{7,5},{8,10},{9,11},{10,... | collective-permute-start | bytes 49160 | tf_op jit(solution)/shard_map/ppermute | solution.py:387
  3.8 0.8 %copy-start.2 = (s32[8,1024]{1,0:T(8,128)S(1)}, s32[8,1024]{1,0:T(8,128)}, u32[]{:S(2)}) copy-start(s32[8,1024]{1,0:T(8,128)} %delay_ref.1) | copy-start | bytes 98308
  4.6 5.8 %copy-start.3 = (f32[7,1024]{1,0:T(8,128)S(1)}, f32[7,1024]{1,0:T(8,128)}, u32[]{:S(2)}) copy-start(f32[7,1024]{1,0:T(8,128)} %geometry_ref) | copy-start | bytes 86020
  4.6 5.8 %copy-start.5 = (s32[1024]{0:T(1024)S(1)}, s32[1024]{0:T(1024)}, u32[]{:S(2)}) copy-start(s32[1024]{0:T(1024)} %param.13) | copy-start | bytes 12292
  7.8 5.1 %collective-permute-start.2 = (bf16[80,256]{1,0:T(8,128)(2,1)S(1)}, bf16[80,256]{1,0:T(8,128)(2,1)S(1)}, u32[]{:S(2)}, u32[]{:S(2)}) collective-permute-start(bf16[80,256]{1,0:T(8,128)(2,1)S(1)} %first.1.mine_ref), channel_id=1, source_target_pairs={{0,4},{1,5},{2,6},{3,7},{4,0},{5,1},{6,2},{7,3},{8,12},{9,13},{10,... | collective-permute-start | bytes 122888 | tf_op jit(solution)/shard_map/ppermute | solution.py:387
  12.9 4.4 %collective-permute-start.3 = (bf16[144,256]{1,0:T(8,128)(2,1)S(1)}, bf16[144,256]{1,0:T(8,128)(2,1)S(1)}, u32[]{:S(2)}, u32[]{:S(2)}) collective-permute-start(bf16[144,256]{1,0:T(8,128)(2,1)S(1)} %join.2.mine_ref.refs_0_), channel_id=1, source_target_pairs={{0,1},{1,0},{2,3},{3,2},{4,5},{5,4},{6,7},{7,6},{8,9},{9,8},{10,11... | collective-permute-start | bytes 221192 | tf_op jit(solution)/shard_map/ppermute | solution.py:387
  14.6 1.3 %copy-start.4 = (s32[4,1024]{1,0:T(4,128)S(1)}, s32[4,1024]{1,0:T(4,128)}, u32[]{:S(2)}) copy-start(s32[4,1024]{1,0:T(4,128)} %conn_ref) | copy-start | bytes 49156
  17.3 3.2 %collective-permute-start.5 = (bf16[272,256]{1,0:T(8,128)(2,1)S(1)}, bf16[272,256]{1,0:T(8,128)(2,1)S(1)}, u32[]{:S(2)}, u32[]{:S(2)}) collective-permute-start(bf16[272,256]{1,0:T(8,128)(2,1)S(1)} %join.3), channel_id=1, source_target_pairs={{0,8},{8,0},{16,24},{24,16},{1,9},{9,1},{17,25},{25,17},{2,10},{10... | collective-permute-start | bytes 417800 | tf_op jit(solution)/shard_map/ppermute | solution.py:387
  17.4 6.1 %collective-permute-start.4 = (bf16[272,256]{1,0:T(8,128)(2,1)S(1)}, bf16[272,256]{1,0:T(8,128)(2,1)S(1)}, u32[]{:S(2)}, u32[]{:S(2)}) collective-permute-start(bf16[272,256]{1,0:T(8,128)(2,1)S(1)} %join.3), channel_id=1, source_target_pairs={{0,16},{8,24},{16,0},{24,8},{1,17},{9,25},{17,1},{25,9},{2,18},{10... | collective-permute-start | bytes 417800 | tf_op jit(solution)/shard_map/ppermute | solution.py:387
  23.4 2.3 %collective-permute-start.6 = (bf16[272,256]{1,0:T(8,128)(2,1)S(1)}, bf16[272,256]{1,0:T(8,128)(2,1)S(1)}, u32[]{:S(2)}, u32[]{:S(2)}) collective-permute-start(bf16[272,256]{1,0:T(8,128)(2,1)S(1)} %collective-permute-done.4.refs_0_), channel_id=1, source_target_pairs={{0,8},{8,0},{16,24},{24,16},{1,9},{9,1},{17,25},{25,17},{2,10},{10... | collective-permute-start | bytes 417800 | tf_op jit(solution)/shard_map/ppermute | solution.py:387
  29.0 6.6 %collective-permute-start.7 = (bf16[136,128]{1,0:T(8,128)(2,1)S(1)}, bf16[136,128]{1,0:T(8,128)(2,1)S(1)}, u32[]{:S(2)}, u32[]{:S(2)}) collective-permute-start(bf16[136,128]{1,0:T(8,128)(2,1)S(1)} %get-tuple-element.42), channel_id=1, source_target_pairs={{0,1},{1,2},{2,3},{3,4},{4,5},{5,6},{6,7},{7,0},{8,9},{9,10},{10,1... | collective-permute-start | bytes 104456 | tf_op jit(solution)/shard_map/ppermute | solution.py:469
  30.7 12.2 %all-to-all-start = ((bf16[8,80,128]{2,1,0:T(8,128)(2,1)}), bf16[8,80,128]{2,1,0:T(8,128)(2,1)S(1)}, u32[]{:S(2)}, u32[]{:S(2)}) async-start(bf16[8,80,128]{2,1,0:T(8,128)(2,1)} %get-tuple-element.43), calls=%async_computation | async-start | bytes 327680 | tf_op jit(solution)/shard_map/all_to_all | solution.py:468

commit v13 on v12

--- a/solution.py
+++ b/solution.py
@@ -335,21 +335,21 @@
     )(*operands)
 
 
-def node_kernel(corner_ref, loading_ref, rim_ref, node_ref):
+def node_kernel(corner_ref, loading_ref, node_ref, head_ref):
     nodes = jnp.dot(corner_ref[...], loading_ref[...], preferred_element_type=F32)
-    node_ref[:HEAD, :] = nodes[:HEAD] + rim_ref[...].astype(F32)
-    node_ref[HEAD:, :] = nodes[HEAD:NODE_DEV]
-
-
-def node_sums(corners, loading, rim):
+    head_ref[...] = nodes[:HEAD]
+    node_ref[...] = nodes[:NODE_DEV]
+
+
+def node_sums(corners, loading):
     return call(
         node_kernel,
         "nodes",
-        jax.ShapeDtypeStruct((NODE_DEV, TW), F32),
-        [WHOLE] * 3,
-        WHOLE,
-        work=20_000_000_000,
-    )(corners, loading, rim)
+        (jax.ShapeDtypeStruct((NODE_DEV, TW), F32), jax.ShapeDtypeStruct((HEAD, TW), F32)),
+        [WHOLE] * 2,
+        [WHOLE] * 2,
+        work=2_000_000_000,
+    )(corners, loading)
 
 
 def cell_kernel(message_ref, cell_ref, rows_ref):
@@ -380,6 +380,25 @@
         WHOLE,
         [VMEM((sections * cap, TW), BF16)],
     )(message)
+
+
+def head_kernel(rim_ref, head_ref, _, node_ref, top_ref, sems):
+    top_ref[...] = head_ref[...] + rim_ref[...].astype(F32)
+    copy = pltpu.make_async_copy(top_ref, node_ref.at[pl.ds(0, HEAD), :], sems.at[0])
+    copy.start()
+    copy.wait()
+
+
+def with_rim(rim, head, nodes):
+    return call(
+        head_kernel,
+        "head",
+        jax.ShapeDtypeStruct((NODE_DEV, TW), F32),
+        [WHOLE] * 2 + [PLACE],
+        PLACE,
+        [VMEM((HEAD, TW), F32), COPY((1,))],
+        {2: 0},
+    )(rim, head, nodes)
 
 
 def swapped(array, axis, bit):
@@ -467,7 +486,10 @@
     loading, message, rim = add(sums, [(o, 0) for o in rest], [chunks[o] for o in rest], matrices, sections)
     message = lax.all_to_all(message, "sect", split_axis=0, concat_axis=0, tiled=True)
     rim = lax.ppermute(rim, "sect", [(i, (i + 1) % sections) for i in range(sections)])
-    return node_sums(corners, loading, rim), cell_sums(message)
+    nodes, head = node_sums(corners, loading)
+    cells = cell_sums(message)
+    rim, cells = lax.optimization_barrier((rim, cells))
+    return with_rim(rim, head, nodes), cells
 
 
 def solution(mesh):

time: 44 us -> 44 us (level)
  waiting for transfers between devices: 10.4 us -> 9.07 us
  Pallas kernels: 15.8 us -> 16.5 us
  starting transfers between devices: 15.3 us -> 16 us
    all_to_all x1, waiting for transfers between devices: 5.7 us -> 4.98 us  [per_device(): lax.all_to_all(message, 'sect', split_axis=0, concat_axis=0, tiled=True)]
    pallas_call x1 -> x2, Pallas kernels: 1.51 us -> 2.16 us  [the longest x1 1.51 us: node_sums(): call(node_kernel, 'nodes', (jax.ShapeDtypeStruct((NODE_DEV, TW), F32), ja...]
    ppermute x1, waiting for transfers between devices: 0.63 us -> 0.01 us  [per_device(): lax.ppermute(rim, 'sect', [(i, (i + 1) % sections) for i in range(section...]
  transfers between devices with their start and end apart: 9 -> 9, of which waited for: 6 -> 5; matrix products, arithmetic and copies ran while one was open for 0% -> 0% of each run, Pallas kernels for 26% -> 28%
where the time goes in v13:
time: 44 us; the launch traced here: 43.7 us
  Pallas kernels  16.5 us (38%)
  starting transfers between devices  16 us (36%)
  waiting for transfers between devices  9.07 us (21%)
  between operations  1.4 us (3%)
  local copies, waits for them, and re-layouts  0.78 us (2%)
    pallas_call x5, Pallas kernels, sources(): call(functools.partial(sources_kernel, places, not sums, last), 'sources'...  10.5 us
    ppermute x7, starting transfers between devices, swapped(): return lax.ppermute(array, axis, [(i, i ^ bit) for i in range(peers)])  9.29 us
    all_to_all x1, waiting for transfers between devices, per_device(): lax.all_to_all(message, 'sect', split_axis=0, concat_axis=0, tiled=True)  4.98 us
    all_to_all x1, starting transfers between devices, per_device(): lax.all_to_all(message, 'sect', split_axis=0, concat_axis=0, tiled=True)  4.67 us
    ppermute x7, waiting for transfers between devices, swapped(): return lax.ppermute(array, axis, [(i, i ^ bit) for i in range(peers)])  4.09 us
    ppermute x1, starting transfers between devices, per_device(): lax.ppermute(rim, 'sect', [(i, (i + 1) % sections) for i in range(section...  2.02 us
    pallas_call x1, Pallas kernels, node_sums(): call(node_kernel, 'nodes', (jax.ShapeDtypeStruct((NODE_DEV, TW), F32), ja...  1.51 us
    pallas_call x1, Pallas kernels, panel_columns(): call(functools.partial(column_kernel, sections), 'columns', (jax.ShapeDty...  1.11 us
  transfers between devices with their start and end apart: 9, of which 5 were waited for; matrix products, arithmetic and copies ran while one was open for 0% of the time, Pallas kernels for 28%

profile of v13, /device:TPU:0, one launch (start us, length us, event | category | flops | bytes accessed | tf_op | source)
XLA Modules:
  0.0 43.7 jit_solution(17463996184233313231)
XLA Ops:
  0.7 3.1 %collective-permute-start.1 = (bf16[3,32]{1,0:T(4,128)(2,1)}, bf16[3,32]{1,0:T(4,128)(2,1)S(1)}, u32[]{:S(2)}, u32[]{:S(2)}) collective-permute-start(bf16[3,32]{1,0:T(4,128)(2,1)} %bitcast.2), channel_id=1, source_target_pairs={{0,2},{1,3},{2,0},{3,1},{4,6},{5,7},{6,4},{7,5},{8,10},{9,11},{10,... | collective-permute-start | bytes 584 | tf_op jit(solution)/shard_map/ppermute | solution.py:406
  3.7 0.1 collective-permute-start
  3.8 0.8 %copy-done.2 = s32[8,1024]{1,0:T(8,128)S(1)} copy-done((s32[8,1024]{1,0:T(8,128)S(1)}, s32[8,1024]{1,0:T(8,128)}, u32[]{:S(2)}) %copy-start.2) | copy-done | bytes 32792
  4.6 0.7 %windows.1.refs_1_ = s32[4,8,256,128]{3,2,1,0:T(8,128)S(1)} custom-call(s32[8,1024]{1,0:T(8,128)S(1)} %copy-done.2), custom_call_target="tpu_custom_call" | custom-call | flops 2000000000 | bytes 4000000 | tf_op jit(solution)/shard_map/windows/pallas_call | solution.py:73
  6.0 1.7 %collective-permute-done.refs_1_ = bf16[32,256]{1,0:T(8,128)(2,1)S(1)} collective-permute-done((bf16[32,256]{1,0:T(8,128)(2,1)}, bf16[32,256]{1,0:T(8,128)(2,1)S(1)}, u32[]{:S(2)}, u32[]{:S(2)}) %collective-permute-start) | collective-permute-done | bytes 16416 | tf_op jit(solution)/shard_map/ppermute | solution.py:406
  7.8 2.6 %collective-permute-start.2 = (bf16[80,256]{1,0:T(8,128)(2,1)S(1)}, bf16[80,256]{1,0:T(8,128)(2,1)S(1)}, u32[]{:S(2)}, u32[]{:S(2)}) collective-permute-start(bf16[80,256]{1,0:T(8,128)(2,1)S(1)} %first.1.mine_ref), channel_id=1, source_target_pairs={{0,4},{1,5},{2,6},{3,7},{4,0},{5,1},{6,2},{7,3},{8,12},{9,13},{10,... | collective-permute-start | bytes 122888 | tf_op jit(solution)/shard_map/ppermute | solution.py:406
  10.4 1.1 %columns.1 = (f32[8,7,128,128]{3,2,1,0:T(8,128)S(1)}, bf16[512,1024]{1,0:T(8,128)(2,1)S(1)}, f32[16,128]{1,0:T(8,128)S(1)}) custom-call(s32[1]{0:T(128)S(6)} %copy.23.count_ref, f32[7,1024]{1,0:T(8,128)S(1)} %copy-done.3, s32[1,1024]{1,0:T(1,128)S(1)} %bitcast.4), custom_call_target="tpu_custom_call" | custom-call | flops 2000000000 | bytes 4000000 | tf_op jit(solution)/shard_map/columns/pallas_call | solution.py:137
  11.5 1.3 %collective-permute-done.2.other_ref = bf16[80,256]{1,0:T(8,128)(2,1)S(1)} collective-permute-done((bf16[80,256]{1,0:T(8,128)(2,1)S(1)}, bf16[80,256]{1,0:T(8,128)(2,1)S(1)}, u32[]{:S(2)}, u32[]{:S(2)}) %collective-permute-start.2) | collective-permute-done | bytes 40992 | tf_op jit(solution)/shard_map/ppermute | solution.py:406
  12.9 1.7 %collective-permute-start.3 = (bf16[144,256]{1,0:T(8,128)(2,1)S(1)}, bf16[144,256]{1,0:T(8,128)(2,1)S(1)}, u32[]{:S(2)}, u32[]{:S(2)}) collective-permute-start(bf16[144,256]{1,0:T(8,128)(2,1)S(1)} %join.2.mine_ref.refs_0_), channel_id=1, source_target_pairs={{0,1},{1,0},{2,3},{3,2},{4,5},{5,4},{6,7},{7,6},{8,9},{9,8},{10,11... | collective-permute-start | bytes 221192 | tf_op jit(solution)/shard_map/ppermute | solution.py:406
  14.6 1.3 %sources.5 = (f32[1024,128]{1,0:T(8,128)S(1)}, f32[1024,128]{1,0:T(8,128)S(1)}) custom-call(s32[1]{0:T(128)S(6)} %copy.23.count_ref, bf16[144,256]{1,0:T(8,128)(2,1)S(1)} %join.2.mine_ref.refs_0_, s32[4,8,256,128]{3,2,1,0:T(8,128)S(1)} %windows.1.refs_1_, f32[8,7,128,128]{3,2,1,0:T(8,128)S(1)} %get-tuple-element.28.refs_2_), custom_call_target="tpu_custom_call" | custom-call | flops 3000000000 | bytes 4000000 | tf_op jit(solution)/shard_map/sources/pallas_call | solution.py:326
  15.9 1.0 %corners.1 = (bf16[1040,1024]{1,0:T(8,128)(2,1)S(1)}, bf16[144,1024]{1,0:T(8,128)(2,1)S(1)}) custom-call(s32[1]{0:T(128)S(6)} %copy.23.count_ref, s32[4,1024]{1,0:T(4,128)S(1)} %copy-done.4), custom_call_target="tpu_custom_call" | custom-call | flops 2000000000 | bytes 4000000 | tf_op jit(solution)/shard_map/corners/pallas_call | solution.py:171
  16.9 0.4 collective-permute-done.3.other_ref.refs_0_
  17.4 1.7 %collective-permute-start.4 = (bf16[272,256]{1,0:T(8,128)(2,1)S(1)}, bf16[272,256]{1,0:T(8,128)(2,1)S(1)}, u32[]{:S(2)}, u32[]{:S(2)}) collective-permute-start(bf16[272,256]{1,0:T(8,128)(2,1)S(1)} %join.3), channel_id=1, source_target_pairs={{0,16},{8,24},{16,0},{24,8},{1,17},{9,25},{17,1},{25,9},{2,18},{10... | collective-permute-start | bytes 417800 | tf_op jit(solution)/shard_map/ppermute | solution.py:406
  19.1 1.4 %sources.6 = (f32[1024,128]{1,0:T(8,128)S(1)}, f32[1024,128]{1,0:T(8,128)S(1)}) custom-call(s32[1]{0:T(128)S(6)} %copy.23.count_ref, bf16[144,256]{1,0:T(8,128)(2,1)S(1)} %collective-permute-done.3.other_ref.refs_0_, s32[4,8,256,128]{3,2,1,0:T(8,128)S(1)} %windows.1.refs_1_, ...), custom_call_target="tpu_custom_call", output_to_operand_aliasing={{0}: (4, {}), {1}: (5, {})} | custom-call | flops 3000000000 | bytes 4000000 | tf_op jit(solution)/shard_map/sources/pallas_call | solution.py:326
  20.5 2.3 %sources.7 = (f32[1024,128]{1,0:T(8,128)S(1)}, f32[1024,128]{1,0:T(8,128)S(1)}) custom-call(s32[1]{0:T(128)S(6)} %copy.23.count_ref, bf16[272,256]{1,0:T(8,128)(2,1)S(1)} %collective-permute-done.5.refs_0_, s32[4,8,256,128]{3,2,1,0:T(8,128)S(1)} %windows.1.refs_1_, ...), custom_call_target="tpu_custom_call", output_to_operand_aliasing={{0}: (4, {}), {1}: (5, {})} | custom-call | flops 3000000000 | bytes 4000000 | tf_op jit(solution)/shard_map/sources/pallas_call | solution.py:326
  22.8 0.6 %collective-permute-done.4.refs_0_ = bf16[272,256]{1,0:T(8,128)(2,1)S(1)} collective-permute-done((bf16[272,256]{1,0:T(8,128)(2,1)S(1)}, bf16[272,256]{1,0:T(8,128)(2,1)S(1)}, u32[]{:S(2)}, u32[]{:S(2)}) %collective-permute-start.4) | collective-permute-done | bytes 139296 | tf_op jit(solution)/shard_map/ppermute | solution.py:406
  23.5 2.3 %sources.8 = (f32[1024,128]{1,0:T(8,128)S(1)}, f32[1024,128]{1,0:T(8,128)S(1)}) custom-call(s32[1]{0:T(128)S(6)} %copy.23.count_ref, bf16[272,256]{1,0:T(8,128)(2,1)S(1)} %collective-permute-done.4.refs_0_, s32[4,8,256,128]{3,2,1,0:T(8,128)S(1)} %windows.1.refs_1_, ...), custom_call_target="tpu_custom_call", output_to_operand_aliasing={{0}: (4, {}), {1}: (5, {})} | custom-call | flops 3000000000 | bytes 4000000 | tf_op jit(solution)/shard_map/sources/pallas_call | solution.py:326
  25.8 3.2 %sources.9 = (bf16[1024,128]{1,0:T(8,128)(2,1)S(1)}, bf16[8,80,128]{2,1,0:T(8,128)(2,1)}, bf16[136,128]{1,0:T(8,128)(2,1)S(1)}) custom-call(s32[1]{0:T(128)S(6)} %copy.23.count_ref, bf16[272,256]{1,0:T(8,128)(2,1)S(1)} %collective-permute-done.6.refs_0_, s32[4,8,256,128]{3,2,1,0:T(8,128)S(1)} %windows.1.refs_1_, ...), custom_call_target="tpu_custom_call" | custom-call | flops 3000000000 | bytes 4000000 | tf_op jit(solution)/shard_map/sources/pallas_call | solution.py:326
  29.0 4.7 %all-to-all-start = ((bf16[8,80,128]{2,1,0:T(8,128)(2,1)}), bf16[8,80,128]{2,1,0:T(8,128)(2,1)S(1)}, u32[]{:S(2)}, u32[]{:S(2)}) async-start(bf16[8,80,128]{2,1,0:T(8,128)(2,1)} %get-tuple-element.45), calls=%async_computation | async-start | bytes 327680 | tf_op jit(solution)/shard_map/all_to_all | solution.py:487
  33.7 2.0 %collective-permute-start.7 = (bf16[136,128]{1,0:T(8,128)(2,1)S(1)}, bf16[136,128]{1,0:T(8,128)(2,1)S(1)}, u32[]{:S(2)}, u32[]{:S(2)}) collective-permute-start(bf16[136,128]{1,0:T(8,128)(2,1)S(1)} %get-tuple-element.44), channel_id=1, source_target_pairs={{0,1},{1,2},{2,3},{3,4},{4,5},{5,6},{6,7},{7,0},{8,9},{9,10},{10,1... | collective-permute-start | bytes 104456 | tf_op jit(solution)/shard_map/ppermute | solution.py:488
  35.7 1.5 %nodes.1 = (f32[1032,128]{1,0:T(8,128)}, f32[136,128]{1,0:T(8,128)S(1)}) custom-call(bf16[1040,1024]{1,0:T(8,128)(2,1)S(1)} %get-tuple-element.47.corner_ref, bf16[1024,128]{1,0:T(8,128)(2,1)S(1)} %get-tuple-element.48.loading_ref), custom_call_target="tpu_custom_call" | custom-call | flops 2000000000 | bytes 4000000 | tf_op jit(solution)/shard_map/nodes/pallas_call | solution.py:345
  37.2 5.0 %all-to-all-done.message_ref = bf16[8,80,128]{2,1,0:T(8,128)(2,1)S(1)} async-done(((bf16[8,80,128]{2,1,0:T(8,128)(2,1)}), bf16[8,80,128]{2,1,0:T(8,128)(2,1)S(1)}, u32[]{:S(2)}, u32[]{:S(2)}) %all-to-all-start) | async-done | bytes 163872 | tf_op jit(solution)/shard_map/all_to_all | solution.py:487
  42.2 0.9 %cells.1 = f32[256,128]{1,0:T(8,128)} custom-call(bf16[8,80,128]{2,1,0:T(8,128)(2,1)S(1)} %all-to-all-done.message_ref), custom_call_target="tpu_custom_call" | custom-call | flops 1000000 | bytes 4000000 | tf_op jit(solution)/shard_map/cells/pallas_call | solution.py:375
  43.1 0.6 %head.1 = f32[1032,128]{1,0:T(8,128)} custom-call(bf16[136,128]{1,0:T(8,128)(2,1)S(1)} %collective-permute-done.7.rim_ref, f32[136,128]{1,0:T(8,128)S(1)} %get-tuple-element.49.head_ref, f32[1032,128]{1,0:T(8,128)} %get-tuple-element.50._), custom_call_target="tpu_custom_call", output_to_operand_aliasing={{}: (2, {})} | custom-call | flops 1000000 | bytes 4000000 | tf_op jit(solution)/shard_map/head/pallas_call | solution.py:393
  (20 shorter events, 0.3 us)
Async XLA Ops:
  0.6 7.1 %copy-start = (bf16[32,256]{1,0:T(8,128)(2,1)S(1)}, bf16[32,256]{1,0:T(8,128)(2,1)}, u32[]{:S(2)}) copy-start(bf16[32,256]{1,0:T(8,128)(2,1)} %refs_0_.1) | copy-start | bytes 49156
  0.6 7.1 %copy-start.1 = (bf16[32,3]{0,1:T(4,128)(2,1)S(1)}, bf16[32,3]{0,1:T(4,128)(2,1)}, u32[]{:S(2)}) copy-start(bf16[32,3]{0,1:T(4,128)(2,1)} %param.8) | copy-start | bytes 580
  0.7 5.3 %collective-permute-start.1 = (bf16[3,32]{1,0:T(4,128)(2,1)}, bf16[3,32]{1,0:T(4,128)(2,1)S(1)}, u32[]{:S(2)}, u32[]{:S(2)}) collective-permute-start(bf16[3,32]{1,0:T(4,128)(2,1)} %bitcast.2), channel_id=1, source_target_pairs={{0,2},{1,3},{2,0},{3,1},{4,6},{5,7},{6,4},{7,5},{8,10},{9,11},{10,... | collective-permute-start | bytes 584 | tf_op jit(solution)/shard_map/ppermute | solution.py:406
  3.7 3.9 %collective-permute-start = (bf16[32,256]{1,0:T(8,128)(2,1)}, bf16[32,256]{1,0:T(8,128)(2,1)S(1)}, u32[]{:S(2)}, u32[]{:S(2)}) collective-permute-start(bf16[32,256]{1,0:T(8,128)(2,1)} %refs_0_.1), channel_id=1, source_target_pairs={{0,2},{1,3},{2,0},{3,1},{4,6},{5,7},{6,4},{7,5},{8,10},{9,11},{10,... | collective-permute-start | bytes 49160 | tf_op jit(solution)/shard_map/ppermute | solution.py:406
  3.8 0.8 %copy-start.2 = (s32[8,1024]{1,0:T(8,128)S(1)}, s32[8,1024]{1,0:T(8,128)}, u32[]{:S(2)}) copy-start(s32[8,1024]{1,0:T(8,128)} %delay_ref.1) | copy-start | bytes 98308
  4.6 5.8 %copy-start.3 = (f32[7,1024]{1,0:T(8,128)S(1)}, f32[7,1024]{1,0:T(8,128)}, u32[]{:S(2)}) copy-start(f32[7,1024]{1,0:T(8,128)} %geometry_ref) | copy-start | bytes 86020
  4.6 5.8 %copy-start.5 = (s32[1024]{0:T(1024)S(1)}, s32[1024]{0:T(1024)}, u32[]{:S(2)}) copy-start(s32[1024]{0:T(1024)} %param.13) | copy-start | bytes 12292
  7.8 5.1 %collective-permute-start.2 = (bf16[80,256]{1,0:T(8,128)(2,1)S(1)}, bf16[80,256]{1,0:T(8,128)(2,1)S(1)}, u32[]{:S(2)}, u32[]{:S(2)}) collective-permute-start(bf16[80,256]{1,0:T(8,128)(2,1)S(1)} %first.1.mine_ref), channel_id=1, source_target_pairs={{0,4},{1,5},{2,6},{3,7},{4,0},{5,1},{6,2},{7,3},{8,12},{9,13},{10,... | collective-permute-start | bytes 122888 | tf_op jit(solution)/shard_map/ppermute | solution.py:406
  12.9 4.4 %collective-permute-start.3 = (bf16[144,256]{1,0:T(8,128)(2,1)S(1)}, bf16[144,256]{1,0:T(8,128)(2,1)S(1)}, u32[]{:S(2)}, u32[]{:S(2)}) collective-permute-start(bf16[144,256]{1,0:T(8,128)(2,1)S(1)} %join.2.mine_ref.refs_0_), channel_id=1, source_target_pairs={{0,1},{1,0},{2,3},{3,2},{4,5},{5,4},{6,7},{7,6},{8,9},{9,8},{10,11... | collective-permute-start | bytes 221192 | tf_op jit(solution)/shard_map/ppermute | solution.py:406
  14.6 1.3 %copy-start.4 = (s32[4,1024]{1,0:T(4,128)S(1)}, s32[4,1024]{1,0:T(4,128)}, u32[]{:S(2)}) copy-start(s32[4,1024]{1,0:T(4,128)} %conn_ref) | copy-start | bytes 49156
  17.3 3.2 %collective-permute-start.5 = (bf16[272,256]{1,0:T(8,128)(2,1)S(1)}, bf16[272,256]{1,0:T(8,128)(2,1)S(1)}, u32[]{:S(2)}, u32[]{:S(2)}) collective-permute-start(bf16[272,256]{1,0:T(8,128)(2,1)S(1)} %join.3), channel_id=1, source_target_pairs={{0,8},{8,0},{16,24},{24,16},{1,9},{9,1},{17,25},{25,17},{2,10},{10... | collective-permute-start | bytes 417800 | tf_op jit(solution)/shard_map/ppermute | solution.py:406
  17.4 6.1 %collective-permute-start.4 = (bf16[272,256]{1,0:T(8,128)(2,1)S(1)}, bf16[272,256]{1,0:T(8,128)(2,1)S(1)}, u32[]{:S(2)}, u32[]{:S(2)}) collective-permute-start(bf16[272,256]{1,0:T(8,128)(2,1)S(1)} %join.3), channel_id=1, source_target_pairs={{0,16},{8,24},{16,0},{24,8},{1,17},{9,25},{17,1},{25,9},{2,18},{10... | collective-permute-start | bytes 417800 | tf_op jit(solution)/shard_map/ppermute | solution.py:406
  23.4 2.3 %collective-permute-start.6 = (bf16[272,256]{1,0:T(8,128)(2,1)S(1)}, bf16[272,256]{1,0:T(8,128)(2,1)S(1)}, u32[]{:S(2)}, u32[]{:S(2)}) collective-permute-start(bf16[272,256]{1,0:T(8,128)(2,1)S(1)} %collective-permute-done.4.refs_0_), channel_id=1, source_target_pairs={{0,8},{8,0},{16,24},{24,16},{1,9},{9,1},{17,25},{25,17},{2,10},{10... | collective-permute-start | bytes 417800 | tf_op jit(solution)/shard_map/ppermute | solution.py:406
  29.0 13.2 %all-to-all-start = ((bf16[8,80,128]{2,1,0:T(8,128)(2,1)}), bf16[8,80,128]{2,1,0:T(8,128)(2,1)S(1)}, u32[]{:S(2)}, u32[]{:S(2)}) async-start(bf16[8,80,128]{2,1,0:T(8,128)(2,1)} %get-tuple-element.45), calls=%async_computation | async-start | bytes 327680 | tf_op jit(solution)/shard_map/all_to_all | solution.py:487
  33.7 9.4 %collective-permute-start.7 = (bf16[136,128]{1,0:T(8,128)(2,1)S(1)}, bf16[136,128]{1,0:T(8,128)(2,1)S(1)}, u32[]{:S(2)}, u32[]{:S(2)}) collective-permute-start(bf16[136,128]{1,0:T(8,128)(2,1)S(1)} %get-tuple-element.44), channel_id=1, source_target_pairs={{0,1},{1,2},{2,3},{3,4},{4,5},{5,6},{6,7},{7,0},{8,9},{9,10},{10,1... | collective-permute-start | bytes 104456 | tf_op jit(solution)/shard_map/ppermute | solution.py:488
